TPU v7x, 32 devices: a whole 2x2x4 slice. The times are simulated.
32 devices in a mesh: dp: 8 (over y, x, core), ctx: 4 (over z).
Axes of the slice: x: 2, y: 2, z: 4, core: 2. Of those that a mesh axis runs over, the one named last changes fastest.
Arguments:
- inputs: bfloat16 [8192, 2048], P(('dp', 'ctx')), may hold values from -6 to 6
- span_table: int32 [4, 2], replicated, may hold values from 0 to 7, as said below
- ln_gain: bfloat16 [2048], P(('dp', 'ctx')), may hold values from 0.5 to 1.5
- ln_bias: bfloat16 [2048], P(('dp', 'ctx')), may hold values from -2 to 2
- qkv_weight: bfloat16 [2048, 6144], P(('dp', 'ctx')), may hold values from -0.125 to 0.125
- qkv_bias: bfloat16 [6144], P(('dp', 'ctx')), may hold values from -0.19921875 to 0.19921875
- out_weight: bfloat16 [2048, 2048], P(('dp', 'ctx')), may hold values from -2 to 2
- out_bias: bfloat16 [2048], P(('dp', 'ctx')), may hold values from -2 to 2
- fc1_weight: bfloat16 [2048, 8192], P(('dp', 'ctx')), may hold values from -0.125 to 0.125
- fc1_bias: bfloat16 [8192], P(('dp', 'ctx')), may hold values from -2 to 2
- fc2_weight: bfloat16 [8192, 2048], P(('dp', 'ctx')), may hold values from -0.0625 to 0.0625
- fc2_bias: bfloat16 [2048], P(('dp', 'ctx')), may hold values from -2 to 2
- cotangent: bfloat16 [8192, 2048], P(('dp', 'ctx')), may hold values from -6 to 6
Outputs:
- output: bfloat16 [8192, 2048], P(('dp', 'ctx'))
- input_grad: bfloat16 [8192, 2048], P(('dp', 'ctx'))
- ln_gain_grad: float32 [2048], P(('dp', 'ctx'))
- ln_bias_grad: float32 [2048], P(('dp', 'ctx'))
- qkv_weight_grad: float32 [2048, 6144], P(('dp', 'ctx'))
- qkv_bias_grad: float32 [6144], P(('dp', 'ctx'))
- out_weight_grad: float32 [2048, 2048], P(('dp', 'ctx'))
- out_bias_grad: float32 [2048], P(('dp', 'ctx'))
- fc1_weight_grad: float32 [2048, 8192], P(('dp', 'ctx'))
- fc1_bias_grad: float32 [8192], P(('dp', 'ctx'))
- fc2_weight_grad: float32 [8192, 2048], P(('dp', 'ctx'))
- fc2_bias_grad: float32 [2048], P(('dp', 'ctx'))
Inputs may be any that keep to these rules, and one draw needn't show every extreme that they name: `span_table`: row i names two spans c and 7 - c for some c, in either order; every span of 0 to 7 appears once.
All inputs are finite; a program needn't handle non-finite values.
Results may differ from a plain program's by a relative error of at most 0.013.
Values may be sent and summed in bfloat16 or wider, within the bound.
No kernel may reach another device: no remote copies, remote signals or barrier semaphores. Data moves between devices by JAX's collectives and lax.ppermute only.
A program may use at most 248 MiB of HBM per device.

v0:
```python
from functools import partial
import math

import jax
import jax.numpy as jnp
from jax import lax
from jax.sharding import PartitionSpec as P

HEADS = 32
ROT = 32


EPS = 1e-05
NEG = -1e30


def layer_norm(values, gain, bias):
    mean = jnp.mean(values, axis=-1, keepdims=True)
    centred = values - mean
    spread = jnp.mean(centred * centred, axis=-1, keepdims=True)
    return centred * lax.rsqrt(spread + EPS) * gain + bias


def span_positions(spans, span_len):
    starts = spans.reshape(-1)[:, None] * span_len
    return (starts + jnp.arange(span_len, dtype=jnp.int32)[None, :]).reshape(-1)


def rotary_tables(positions, rot_dims):
    half = rot_dims // 2
    freqs = jnp.exp(jnp.arange(half, dtype=jnp.float32) * (-2.0 * math.log(10000.0) / rot_dims))
    angles = positions.astype(jnp.float32)[:, None] * freqs[None, :]
    cosine = jnp.cos(angles)
    sine = jnp.sin(angles)
    return (jnp.concatenate([cosine, cosine], 1), jnp.concatenate([sine, sine], 1))


def rotate(values, cosine, sine):
    rot_dims = cosine.shape[1]
    half = rot_dims // 2
    front = values[..., :rot_dims]
    turned = jnp.concatenate([-front[..., half:], front[..., :half]], -1)
    moved = front * cosine[:, None, :] + turned * sine[:, None, :]
    return jnp.concatenate([moved, values[..., rot_dims:]], -1)


def per_device(
    inputs,
    span_table,
    ln_gain,
    ln_bias,
    qkv_weight,
    qkv_bias,
    out_weight,
    out_bias,
    fc1_weight,
    fc1_bias,
    fc2_weight,
    fc2_bias,
    cotangent,
):
    rows, width = inputs.shape
    head_dim = width // HEADS
    span_len = rows // 2
    seq_len = rows * lax.axis_size("ctx")
    block = math.gcd(seq_len, 512)
    count = seq_len // block
    scale = head_dim ** (-0.5)
    rank = lax.axis_index("ctx")
    own_spans = lax.dynamic_slice_in_dim(span_table, rank, 1, 0)
    query_pos = span_positions(own_spans, span_len)
    key_pos = span_positions(span_table, span_len).reshape(count, block)
    cosine, sine = rotary_tables(query_pos, ROT)
    gain, shift, w_qkv, b_qkv, w_out, b_out = (
        lax.all_gather(ln_gain, ("dp", "ctx"), axis=0, tiled=True),
        lax.all_gather(ln_bias, ("dp", "ctx"), axis=0, tiled=True),
        lax.all_gather(qkv_weight, ("dp", "ctx"), axis=0, tiled=True),
        lax.all_gather(qkv_bias, ("dp", "ctx"), axis=0, tiled=True),
        lax.all_gather(out_weight, ("dp", "ctx"), axis=0, tiled=True),
        lax.all_gather(out_bias, ("dp", "ctx"), axis=0, tiled=True),
    )
    w_up, b_up, w_down, b_down = (
        lax.all_gather(fc1_weight, ("dp", "ctx"), axis=0, tiled=True),
        lax.all_gather(fc1_bias, ("dp", "ctx"), axis=0, tiled=True),
        lax.all_gather(fc2_weight, ("dp", "ctx"), axis=0, tiled=True),
        lax.all_gather(fc2_bias, ("dp", "ctx"), axis=0, tiled=True),
    )
    x = inputs.astype(jnp.float32)
    normed, norm_back = jax.vjp(layer_norm, x, gain.astype(jnp.float32), shift.astype(jnp.float32))
    hidden = normed.astype(jnp.bfloat16)
    qkv = jnp.dot(hidden, w_qkv, preferred_element_type=jnp.float32) + b_qkv.astype(jnp.float32)
    q_raw = qkv[:, :width].reshape(rows, HEADS, head_dim)
    k_raw = qkv[:, width : 2 * width].reshape(rows, HEADS, head_dim)

    def rotate_pair(q_in, k_in):
        return (rotate(q_in, cosine, sine), rotate(k_in, cosine, sine))

    (q_turned, k_turned), rotate_back = jax.vjp(rotate_pair, q_raw, k_raw)
    queries = q_turned.astype(jnp.bfloat16)
    keys = k_turned.reshape(rows, width).astype(jnp.bfloat16)
    values = qkv[:, 2 * width :].astype(jnp.bfloat16)
    keys_all, values_all = (
        lax.all_gather(keys, "ctx", axis=0, tiled=True),
        lax.all_gather(values, "ctx", axis=0, tiled=True),
    )

    def block_scores(key_block, pos_block):
        scores = (
            jnp.einsum("thd,khd->htk", queries, key_block, preferred_element_type=jnp.float32)
            * scale
        )
        allowed = pos_block[None, None, :] <= query_pos[None, :, None]
        return (scores, allowed)

    def running(carry, item):
        top, total = carry
        key_block, pos_block = item
        scores, allowed = block_scores(key_block, pos_block)
        masked = jnp.where(allowed, scores, NEG)
        new_top = jnp.maximum(top, jnp.max(masked, -1))
        fresh = jnp.where(allowed, jnp.exp(masked - new_top[..., None]), 0.0)
        total = total * jnp.exp(top - new_top) + jnp.sum(fresh, -1)
        return ((new_top, total), None)

    key_blocks = keys_all.reshape(count, block, HEADS, head_dim)
    value_blocks = values_all.reshape(count, block, HEADS, head_dim)
    start = (jnp.full((HEADS, rows), NEG, jnp.float32), jnp.zeros((HEADS, rows), jnp.float32))
    (top, total), _ = lax.scan(running, start, (key_blocks, key_pos))
    log_total = top + jnp.log(total)

    def weighted(acc, item):
        key_block, value_block, pos_block = item
        scores, allowed = block_scores(key_block, pos_block)
        probs = jnp.where(allowed, jnp.exp(scores - log_total[..., None]), 0.0)
        return (
            acc
            + jnp.einsum(
                "htk,khd->thd",
                probs.astype(jnp.bfloat16),
                value_block,
                preferred_element_type=jnp.float32,
            ),
            None,
        )

    attended, _ = lax.scan(
        weighted,
        jnp.zeros((rows, HEADS, head_dim), jnp.float32),
        (key_blocks, value_blocks, key_pos),
    )
    attended_low = attended.reshape(rows, width).astype(jnp.bfloat16)
    pre = jnp.dot(hidden, w_up, preferred_element_type=jnp.float32) + b_up.astype(jnp.float32)
    activated, gelu_back = jax.vjp(partial(jax.nn.gelu, approximate=True), pre)
    act = activated.astype(jnp.bfloat16)
    attn_branch = jnp.dot(attended_low, w_out, preferred_element_type=jnp.float32) + b_out.astype(
        jnp.float32
    )
    mlp_branch = jnp.dot(act, w_down, preferred_element_type=jnp.float32) + b_down.astype(
        jnp.float32
    )
    output = (x + attn_branch + mlp_branch).astype(jnp.bfloat16)
    grad_out = cotangent.astype(jnp.float32)
    bias_grad = jnp.sum(grad_out, 0)
    fresh_up, fresh_down, held = lax.optimization_barrier((fc1_weight, fc2_weight, cotangent))
    w_up, w_down = (
        lax.all_gather(fresh_up, ("dp", "ctx"), axis=0, tiled=True),
        lax.all_gather(fresh_down, ("dp", "ctx"), axis=0, tiled=True),
    )
    act_grad = jnp.dot(cotangent, w_down.T, preferred_element_type=jnp.float32)
    pre_grad = gelu_back(act_grad)[0].astype(jnp.bfloat16)
    normed_grad = jnp.dot(pre_grad, w_up.T, preferred_element_type=jnp.float32)
    down_grad = jnp.dot(act.T, cotangent, preferred_element_type=jnp.float32)
    up_grad = jnp.dot(hidden.T, pre_grad, preferred_element_type=jnp.float32)
    up_bias_grad = jnp.sum(pre_grad.astype(jnp.float32), 0)
    fc1_weight_grad, fc1_bias_grad, fc2_weight_grad, fc2_bias_grad = (
        lax.psum_scatter(up_grad, ("dp", "ctx"), scatter_dimension=0, tiled=True),
        lax.psum_scatter(up_bias_grad, ("dp", "ctx"), scatter_dimension=0, tiled=True),
        lax.psum_scatter(down_grad, ("dp", "ctx"), scatter_dimension=0, tiled=True),
        lax.psum_scatter(bias_grad, ("dp", "ctx"), scatter_dimension=0, tiled=True),
    )
    fresh_qkv, fresh_out, held = lax.optimization_barrier((qkv_weight, out_weight, fc1_weight_grad))
    w_qkv, w_out = (
        lax.all_gather(fresh_qkv, ("dp", "ctx"), axis=0, tiled=True),
        lax.all_gather(fresh_out, ("dp", "ctx"), axis=0, tiled=True),
    )
    out_grad = jnp.dot(attended_low.T, cotangent, preferred_element_type=jnp.float32)
    attended_grad = (
        jnp.dot(cotangent, w_out.T, preferred_element_type=jnp.float32)
        .astype(jnp.bfloat16)
        .reshape(rows, HEADS, head_dim)
    )
    delta = jnp.sum(attended_grad.astype(jnp.float32) * attended, -1).T
    fresh_keys, fresh_values, held = lax.optimization_barrier((keys, values, attended_grad))
    keys_all, values_all = (
        lax.all_gather(fresh_keys, "ctx", axis=0, tiled=True),
        lax.all_gather(fresh_values, "ctx", axis=0, tiled=True),
    )
    key_blocks = keys_all.reshape(count, block, HEADS, head_dim)
    value_blocks = values_all.reshape(count, block, HEADS, head_dim)

    def backward_block(query_sum, item):
        key_block, value_block, pos_block = item
        scores, allowed = block_scores(key_block, pos_block)
        probs = jnp.where(allowed, jnp.exp(scores - log_total[..., None]), 0.0)
        probs_grad = jnp.einsum(
            "thd,khd->htk", attended_grad, value_block, preferred_element_type=jnp.float32
        )
        score_grad = (probs * (probs_grad - delta[..., None])).astype(jnp.bfloat16)
        value_part = jnp.einsum(
            "htk,thd->khd",
            probs.astype(jnp.bfloat16),
            attended_grad,
            preferred_element_type=jnp.float32,
        )
        key_part = (
            jnp.einsum("htk,thd->khd", score_grad, queries, preferred_element_type=jnp.float32)
            * scale
        )
        query_sum = query_sum + jnp.einsum(
            "htk,khd->thd", score_grad, key_block, preferred_element_type=jnp.float32
        )
        return (query_sum, (key_part.reshape(block, width), value_part.reshape(block, width)))

    query_sum, (key_parts, value_parts) = lax.scan(
        backward_block,
        jnp.zeros((rows, HEADS, head_dim), jnp.float32),
        (key_blocks, value_blocks, key_pos),
    )
    key_own, value_own = (
        lax.psum_scatter(
            key_parts.reshape(seq_len, width).astype(jnp.bfloat16),
            "ctx",
            scatter_dimension=0,
            tiled=True,
        ).astype(jnp.float32),
        lax.psum_scatter(
            value_parts.reshape(seq_len, width).astype(jnp.bfloat16),
            "ctx",
            scatter_dimension=0,
            tiled=True,
        ).astype(jnp.float32),
    )
    query_back, key_back = rotate_back((query_sum * scale, key_own.reshape(rows, HEADS, head_dim)))
    qkv_grad = jnp.concatenate(
        [query_back.reshape(rows, width), key_back.reshape(rows, width), value_own], 1
    ).astype(jnp.bfloat16)
    qkv_term = jnp.dot(hidden.T, qkv_grad, preferred_element_type=jnp.float32)
    qkv_bias_term = jnp.sum(qkv_grad.astype(jnp.float32), 0)
    normed_grad = normed_grad + jnp.dot(qkv_grad, w_qkv.T, preferred_element_type=jnp.float32)
    x_grad, gain_grad, shift_grad = norm_back(normed_grad)
    input_grad = (grad_out + x_grad).astype(jnp.bfloat16)
    ln_gain_grad, ln_bias_grad, qkv_weight_grad, qkv_bias_grad, out_weight_grad, out_bias_grad = (
        lax.psum_scatter(gain_grad, ("dp", "ctx"), scatter_dimension=0, tiled=True),
        lax.psum_scatter(shift_grad, ("dp", "ctx"), scatter_dimension=0, tiled=True),
        lax.psum_scatter(qkv_term, ("dp", "ctx"), scatter_dimension=0, tiled=True),
        lax.psum_scatter(qkv_bias_term, ("dp", "ctx"), scatter_dimension=0, tiled=True),
        lax.psum_scatter(out_grad, ("dp", "ctx"), scatter_dimension=0, tiled=True),
        lax.psum_scatter(bias_grad, ("dp", "ctx"), scatter_dimension=0, tiled=True),
    )
    return (
        output,
        input_grad,
        ln_gain_grad,
        ln_bias_grad,
        qkv_weight_grad,
        qkv_bias_grad,
        out_weight_grad,
        out_bias_grad,
        fc1_weight_grad,
        fc1_bias_grad,
        fc2_weight_grad,
        fc2_bias_grad,
    )


def solution(mesh):
    placed = (
        P(("dp", "ctx"), None),
        P(),
        P(("dp", "ctx")),
        P(("dp", "ctx")),
        P(("dp", "ctx"), None),
        P(("dp", "ctx")),
        P(("dp", "ctx"), None),
        P(("dp", "ctx")),
        P(("dp", "ctx"), None),
        P(("dp", "ctx")),
        P(("dp", "ctx"), None),
        P(("dp", "ctx")),
        P(("dp", "ctx"), None),
    )
    return jax.shard_map(
        per_device,
        mesh=mesh,
        in_specs=placed,
        out_specs=(
            P(("dp", "ctx"), None),
            P(("dp", "ctx"), None),
            P(("dp", "ctx")),
            P(("dp", "ctx")),
            P(("dp", "ctx"), None),
            P(("dp", "ctx")),
            P(("dp", "ctx"), None),
            P(("dp", "ctx")),
            P(("dp", "ctx"), None),
            P(("dp", "ctx")),
            P(("dp", "ctx"), None),
            P(("dp", "ctx")),
        ),
        check_vma=False,
    )
```

profile of v0, /device:TPU:0, one launch (start us, length us, event | category | flops | bytes accessed | tf_op | source)
XLA Modules:
  0.0 5522.4 jit_solution(3456154045438133219)
XLA Ops:
  13.7 44.6 all-reduce.19
  59.0 67.8 %all-gather = bf16[32,1,256]{2,1,0:T(2,128)(2,1)S(1)} all-gather(bf16[1,1,256]{2,1,0:T(2,128)(2,1)S(1)} %reshape.292), channel_id=1, replica_groups=mesh['dp'=8,'ctx'=4] {'dp','ctx'}, dimensions={0}, use_global_device_ids=true | all-gather | bytes 16896 | tf_op jit(solution)/shard_map/all_gather | solution.py:84
  128.7 81.2 %all-gather.22.cloned.1.call-done = bf16[2048,8192]{1,0:T(8,128)(2,1)} async-done(((bf16[64,8192]{1,0:T(8,128)(2,1)}), bf16[2048,8192]{1,0:T(8,128)(2,1)}) %all-gather.22.cloned.1.call-update) | async-done | bytes 33554448 | tf_op jit(solution)/shard_map/all_gather | solution.py:83
  209.9 18.0 convolution_add_fusion
  228.0 177.9 %all-gather.26.cloned.1.call-done = bf16[8192,2048]{1,0:T(8,128)(2,1)} async-done(((bf16[256,2048]{1,0:T(8,128)(2,1)}), bf16[8192,2048]{1,0:T(8,128)(2,1)}) %all-gather.26.cloned.1.call-update) | async-done | bytes 33554448 | tf_op jit(solution)/shard_map/all_gather | solution.py:167
  405.9 22.4 convert_reduce_fusion
  428.3 26.4 fusion.81
  455.8 105.8 %all-gather.14.cloned.1.call-done = bf16[2048,6144]{1,0:T(8,128)(2,1)} async-done(((bf16[64,6144]{1,0:T(8,128)(2,1)}), bf16[2048,6144]{1,0:T(8,128)(2,1)}) %all-gather.14.cloned.1.call-update) | async-done | bytes 25165840 | tf_op jit(solution)/shard_map/all_gather | solution.py:77
  588.7 1384.5 %reduce-scatter.7.cloned.1.call-done = f32[64,8192]{1,0:T(8,128)} async-done(((f32[2048,8192]{1,0:T(8,128)}), f32[64,8192]{1,0:T(8,128)}) %reduce-scatter.7.cloned.1.call-update) | async-done | bytes 2097168 | tf_op jit(solution)/shard_map/reduce_scatter | solution.py:176
  1973.8 82.1 %all-gather.18.cloned.1.call-done = bf16[1024,2048]{0,1:T(8,128)(2,1)} async-done(((bf16[256,2048]{0,1:T(8,128)(2,1)}), bf16[1024,2048]{0,1:T(8,128)(2,1)}) %all-gather.18.cloned.1.call-update) | async-done | bytes 4194320 | tf_op jit(solution)/shard_map/all_gather | solution.py:103
  2069.6 67.2 %all-gather.16.cloned.1.call-done = bf16[1024,2048]{1,0:T(8,128)(2,1)} async-done(((bf16[256,2048]{1,0:T(8,128)(2,1)}), bf16[1024,2048]{1,0:T(8,128)(2,1)}) %all-gather.16.cloned.1.call-update) | async-done | bytes 4194320 | tf_op jit(solution)/shard_map/all_gather | solution.py:104
  2136.8 12.9 reshape.295
  2159.5 38.0 while.39
  2197.6 18.2 while.40
  2225.3 78.1 %all-gather.34.cloned.1.call-done = bf16[1024,2048]{1,0:T(8,128)(2,1)} async-done(((bf16[256,2048]{1,0:T(8,128)(2,1)}), bf16[1024,2048]{1,0:T(8,128)(2,1)}) %all-gather.34.cloned.1.call-update) | async-done | bytes 4194320 | tf_op jit(solution)/shard_map/all_gather | solution.py:196
  2326.1 58.5 %all-gather.32.cloned.1.call-done = bf16[1024,2048]{0,1:T(8,128)(2,1)} async-done(((bf16[256,2048]{0,1:T(8,128)(2,1)}), bf16[1024,2048]{0,1:T(8,128)(2,1)}) %all-gather.32.cloned.1.call-update) | async-done | bytes 4194320 | tf_op jit(solution)/shard_map/all_gather | solution.py:195
  2398.3 112.4 %while.41 = (s32[]{:T(128)}, f32[256,32,64]{0,2,1:T(8,128)}, bf16[2,512,2048]{2,1,0:T(8,128)(2,1)}, bf16[2,512,2048]{2,1,0:T(8,128)(2,1)}, bf16[2,512,32,64]{1,3...) while((s32[]{:T(128)}, f32[256,32,64]{0,2,1:T(8,128)}, ...), condition=%wide.region_11.12_spmd.clone, body=%wide.region_10.11_spmd.clone.sunk | while | flops 2729574656 | bytes 153594112 | solution.py:224
  2479.6 15.1 fusion.154
  2513.3 67.2 %all-gather.28.cloned.1.call-done = bf16[2048,8192]{1,0:T(8,128)(2,1)} async-done(((bf16[64,8192]{1,0:T(8,128)(2,1)}), bf16[2048,8192]{1,0:T(8,128)(2,1)}) %all-gather.28.cloned.1.call-update) | async-done | bytes 33554448 | tf_op jit(solution)/shard_map/all_gather | solution.py:166
  2580.5 17.3 fusion.91
  2600.5 57.2 %reduce-scatter.9.cloned.1.call-done = bf16[256,2048]{1,0:T(8,128)(2,1)} async-done(((bf16[1024,2048]{1,0:T(8,128)(2,1)}), bf16[256,2048]{1,0:T(8,128)(2,1)}) %reduce-scatter.9.cloned.1.call-update) | async-done | bytes 1048592 | tf_op jit(solution)/shard_map/reduce_scatter | solution.py:230
  2670.5 66.8 %reduce-scatter.11.cloned.1.call-done = bf16[256,2048]{1,0:T(8,128)(2,1)} async-done(((bf16[1024,2048]{1,0:T(8,128)(2,1)}), bf16[256,2048]{1,0:T(8,128)(2,1)}) %reduce-scatter.11.cloned.1.call-update) | async-done | bytes 1048592 | tf_op jit(solution)/shard_map/reduce_scatter | solution.py:236
  2739.5 155.9 %all-gather.36.cloned.1.call-done = bf16[2048,6144]{1,0:T(8,128)(2,1)} async-done(((bf16[64,6144]{1,0:T(8,128)(2,1)}), bf16[2048,6144]{1,0:T(8,128)(2,1)}) %all-gather.36.cloned.1.call-update) | async-done | bytes 25165840 | tf_op jit(solution)/shard_map/all_gather | solution.py:183
  2895.4 14.3 fusion.85
  2915.7 28.1 fusion.79
  2954.9 21.5 fusion.77
  2984.7 185.3 %all-gather.24.cloned.1.call-done = bf16[8192,2048]{1,0:T(8,128)(2,1)} async-done(((bf16[256,2048]{1,0:T(8,128)(2,1)}), bf16[8192,2048]{1,0:T(8,128)(2,1)}) %all-gather.24.cloned.1.call-update) | async-done | bytes 33554448 | tf_op jit(solution)/shard_map/all_gather | solution.py:85
  3170.0 19.8 fusion.63
  3189.8 107.0 %all-reduce.22.cloned.1.call-done = (f32[2048]{0:T(1024)}, f32[2048]{0:T(1024)}, f32[6144]{0:T(1024)}, f32[2048]{0:T(1024)}, f32[8192]{0:T(1024)}) async-done(((f32[2048]{0:T(1024)}, f32[2048]{0:T(1024)}, f32[6144]{0:T(1024)}, f32[2048]{0:T(1024)}, f32[8192]{0:T(1024)}), (f32[2048]{0:T(1024)}, f32[2048]{0:T(1024)}, f32[6144]{0:T(1024)}, f32[2048]{0:T(1024)}, f32[8192]{0:T(1024)})) %all-reduce.22.cloned.1.call-update) | async-done | bytes 81936
  3302.7 1408.8 %reduce-scatter.17.cloned.1.call-done = f32[256,2048]{1,0:T(8,128)} async-done(((f32[8192,2048]{1,0:T(8,128)}), f32[256,2048]{1,0:T(8,128)}) %reduce-scatter.17.cloned.1.call-update) | async-done | bytes 2097168 | tf_op jit(solution)/shard_map/reduce_scatter | solution.py:178
  4711.6 367.0 %reduce-scatter.15.cloned.1.call-done = f32[64,2048]{1,0:T(8,128)} async-done(((f32[2048,2048]{1,0:T(8,128)}), f32[64,2048]{1,0:T(8,128)}) %reduce-scatter.15.cloned.1.call-update) | async-done | bytes 524304 | tf_op jit(solution)/shard_map/reduce_scatter | solution.py:257
  5078.5 436.6 %reduce-scatter.13.cloned.1.call-done = f32[64,6144]{1,0:T(8,128)} async-done(((f32[2048,6144]{1,0:T(8,128)}), f32[64,6144]{1,0:T(8,128)}) %reduce-scatter.13.cloned.1.call-update) | async-done | bytes 1572880 | tf_op jit(solution)/shard_map/reduce_scatter | solution.py:255
  (245 shorter events, 311.5 us)
Async XLA Ops:
  7.2 202.8 %all-gather.22.cloned.1.call-start = ((), (), s32[]{:S(2)}) async-start(), calls=%async_computation.10 | async-start | bytes 34603008 | tf_op jit(solution)/shard_map/all_gather | solution.py:83
  7.9 398.0 %all-gather.26.cloned.1.call-start = ((), (), s32[]{:S(2)}) async-start(), calls=%async_computation.12 | async-start | bytes 34603008 | tf_op jit(solution)/shard_map/all_gather | solution.py:167
  8.7 553.0 %all-gather.14.cloned.1.call-start = ((), (), s32[]{:S(2)}) async-start(), calls=%async_computation.6 | async-start | bytes 25952256 | tf_op jit(solution)/shard_map/all_gather | solution.py:77
  9.4 1963.8 %reduce-scatter.7.cloned.1.call-start = ((), (), s32[]{:S(2)}) async-start(), calls=%async_computation.14 | async-start | bytes 69206016 | tf_op jit(solution)/shard_map/reduce_scatter | solution.py:176
  58.3 503.4 %copy-start.16 = (f32[2048]{0:T(1024)}, f32[2048]{0:T(1024)S(1)}, u32[]{:S(2)}) copy-start(f32[2048]{0:T(1024)S(1)} %convert_element_type.101) | copy-start | bytes 24580
  58.3 503.4 %copy-start.18 = (f32[2048]{0:T(1024)}, f32[2048]{0:T(1024)S(1)}, u32[]{:S(2)}) copy-start(f32[2048]{0:T(1024)S(1)} %convert_element_type.102) | copy-start | bytes 24580
  128.2 433.4 %copy-start.24 = (f32[256]{0:T(256)}, f32[256]{0:T(256)S(1)}, u32[]{:S(2)}) copy-start(f32[256]{0:T(256)S(1)} %broadcast_multiply_fusion.2) | copy-start | bytes 3076
  128.7 433.0 %copy-start.26 = (f32[256]{0:T(256)}, f32[256]{0:T(256)S(1)}, u32[]{:S(2)}) copy-start(f32[256]{0:T(256)S(1)} %fusion.76) | copy-start | bytes 3076
  209.9 195.9 %copy-start.8 = (bf16[256,2048]{1,0:T(8,128)(2,1)S(1)}, bf16[256,2048]{1,0:T(8,128)(2,1)}, u32[]{:S(2)}) copy-start(bf16[256,2048]{1,0:T(8,128)(2,1)} %param.31) | copy-start | bytes 3145732
  454.7 1601.1 %all-gather.18.cloned.1.call-start = ((), (), s32[]{:S(2)}) async-start(), calls=%async_computation.8 | async-start | bytes 5242880 | tf_op jit(solution)/shard_map/all_gather | solution.py:103
  455.8 128.4 %copy-start.20 = (f32[256,32]{0,1:T(8,128)}, f32[256,32]{0,1:T(8,128)S(1)}, u32[]{:S(2)}) copy-start(f32[256,32]{0,1:T(8,128)S(1)} %get-tuple-element.455) | copy-start | bytes 98308
  455.8 128.4 %copy-start.22 = (f32[256,32]{0,1:T(8,128)}, f32[256,32]{0,1:T(8,128)S(1)}, u32[]{:S(2)}) copy-start(f32[256,32]{0,1:T(8,128)S(1)} %get-tuple-element.454) | copy-start | bytes 98308
  585.9 1550.9 %all-gather.16.cloned.1.call-start = ((), (), s32[]{:S(2)}) async-start(), calls=%async_computation.7 | async-start | bytes 5242880 | tf_op jit(solution)/shard_map/all_gather | solution.py:104
  588.7 1627.0 %all-gather.30.cloned.1.call-start = ((), (), s32[]{:S(2)}) async-start(), calls=%async_computation.15 | async-start | bytes 8650752 | tf_op jit(solution)/shard_map/all_gather | solution.py:184
  1973.3 330.2 %all-gather.34.cloned.1.call-start = ((), (), s32[]{:S(2)}) async-start(), calls=%async_computation.17 | async-start | bytes 5242880 | tf_op jit(solution)/shard_map/all_gather | solution.py:196
  2223.9 160.7 %all-gather.32.cloned.1.call-start = ((), (), s32[]{:S(2)}) async-start(), calls=%async_computation.16 | async-start | bytes 5242880 | tf_op jit(solution)/shard_map/all_gather | solution.py:195
  2224.7 355.8 %all-gather.28.cloned.1.call-start = ((), (), s32[]{:S(2)}) async-start(), calls=%async_computation.13 | async-start | bytes 34603008 | tf_op jit(solution)/shard_map/all_gather | solution.py:166
  2225.3 432.5 %reduce-scatter.9.cloned.1.call-start = ((), (), s32[]{:S(2)}) async-start(), calls=%async_computation.18 | async-start | bytes 5242880 | tf_op jit(solution)/shard_map/reduce_scatter | solution.py:230
  2510.7 226.6 %reduce-scatter.11.cloned.1.call-start = ((), (), s32[]{:S(2)}) async-start(), calls=%async_computation.19 | async-start | bytes 5242880 | tf_op jit(solution)/shard_map/reduce_scatter | solution.py:236
  2511.3 384.1 %all-gather.36.cloned.1.call-start = ((), (), s32[]{:S(2)}) async-start(), calls=%async_computation.20 | async-start | bytes 25952256 | tf_op jit(solution)/shard_map/all_gather | solution.py:183
  2512.0 465.1 %all-gather.20.cloned.1.call-start = ((), (), s32[]{:S(2)}) async-start(), calls=%async_computation.9 | async-start | bytes 8650752 | tf_op jit(solution)/shard_map/all_gather | solution.py:79
  2512.6 657.4 %all-gather.24.cloned.1.call-start = ((), (), s32[]{:S(2)}) async-start(), calls=%async_computation.11 | async-start | bytes 34603008 | tf_op jit(solution)/shard_map/all_gather | solution.py:85
  2513.2 783.6 %all-reduce.22.cloned.1.call-start = ((), (), s32[]{:S(2)}) async-start(), calls=%async_computation.24 | async-start | bytes 163840
  2665.6 229.8 %copy-start.3 = (bf16[256,2048]{1,0:T(8,128)(2,1)S(1)}, bf16[256,2048]{1,0:T(8,128)(2,1)}, u32[]{:S(2)}) copy-start(bf16[256,2048]{1,0:T(8,128)(2,1)} %param.19) | copy-start | bytes 3145732
  2665.6 229.8 %copy-start.17 = (f32[2048]{0:T(1024)S(1)}, f32[2048]{0:T(1024)}, u32[]{:S(2)}) copy-start(f32[2048]{0:T(1024)} %copy-done.16) | copy-start | bytes 24580
  2665.6 229.7 %copy-start.25 = (f32[256]{0:T(256)S(1)}, f32[256]{0:T(256)}, u32[]{:S(2)}) copy-start(f32[256]{0:T(256)} %copy-done.24) | copy-start | bytes 3076
  2739.5 170.2 %copy-start.29 = (f32[256]{0:T(256)S(1)}, f32[256]{0:T(256)}, u32[]{:S(2)}) copy-start(f32[256]{0:T(256)} %copy-done.28) | copy-start | bytes 3076
  2739.5 170.2 %copy-start.27 = (f32[256]{0:T(256)S(1)}, f32[256]{0:T(256)}, u32[]{:S(2)}) copy-start(f32[256]{0:T(256)} %copy-done.26) | copy-start | bytes 3076
  2915.7 1795.9 %reduce-scatter.17.cloned.1.call-start = ((), (), s32[]{:S(2)}) async-start(), calls=%async_computation.23 | async-start | bytes 69206016 | tf_op jit(solution)/shard_map/reduce_scatter | solution.py:178
  2943.8 2134.7 %reduce-scatter.15.cloned.1.call-start = ((), (), s32[]{:S(2)}) async-start(), calls=%async_computation.22 | async-start | bytes 17301504 | tf_op jit(solution)/shard_map/reduce_scatter | solution.py:257
  2954.2 2560.9 %reduce-scatter.13.cloned.1.call-start = ((), (), s32[]{:S(2)}) async-start(), calls=%async_computation.21 | async-start | bytes 51904512 | tf_op jit(solution)/shard_map/reduce_scatter | solution.py:255
  3297.6 2218.1 %copy-start.35 = (f32[64]{0:T(128)}, f32[64]{0:T(128)S(1)}, u32[]{:S(2)}) copy-start(f32[64]{0:T(128)S(1)} %dynamic-slice.3) | copy-start | bytes 772
  (26 other events, 535.0 us)
Sparse Core Ops, SparseCore 0:
  11.0 198.9 all-gather.21
  212.9 192.9 all-gather.25
  408.8 152.8 all-gather.13
  564.4 1408.7 reduce-scatter.6
  1975.2 80.5 all-gather.17
  2057.8 78.9 all-gather.15
  2139.7 75.9 all-gather.29
  2224.1 79.3 all-gather.33
  2305.6 79.0 all-gather.31
  2387.5 192.9 all-gather.27
  2582.8 74.9 reduce-scatter.8
  2660.0 77.2 reduce-scatter.10
  2740.2 155.1 all-gather.35
  2898.1 75.6 all-gather.19
  2976.6 193.3 all-gather.23
  3176.3 120.4 all-reduce.21
  3299.6 1411.9 reduce-scatter.16
  4714.3 364.1 reduce-scatter.14
  5085.5 429.5 reduce-scatter.12
where the time goes:
time: 5530 us; the launch traced here: 5520 us
  waiting for transfers between devices  4890 us (88%)
  matrix products  334 us (6%)
  local copies, waits for them, and re-layouts  126 us (2%)
  blocking collectives  112 us (2%)
    reduce_scatter x1, waiting for transfers between devices, per_device(): lax.psum_scatter(down_grad, ('dp', 'ctx'), scatter_dimension=0, tiled=True)  1410 us
    reduce_scatter x1, waiting for transfers between devices, per_device(): lax.psum_scatter(up_grad, ('dp', 'ctx'), scatter_dimension=0, tiled=True)  1380 us
    reduce_scatter x1, waiting for transfers between devices, per_device(): lax.psum_scatter(qkv_term, ('dp', 'ctx'), scatter_dimension=0, tiled=True)  437 us
    reduce_scatter x1, waiting for transfers between devices, per_device(): lax.psum_scatter(out_grad, ('dp', 'ctx'), scatter_dimension=0, tiled=True)  367 us
    all_gather x1, waiting for transfers between devices, per_device(): lax.all_gather(fc2_weight, ('dp', 'ctx'), axis=0, tiled=True)  185 us
    all_gather x1, waiting for transfers between devices, per_device(): lax.all_gather(fresh_down, ('dp', 'ctx'), axis=0, tiled=True)  178 us
    all_gather x1, waiting for transfers between devices, per_device(): lax.all_gather(fresh_qkv, ('dp', 'ctx'), axis=0, tiled=True)  156 us
    unnamed x20, waiting for transfers between devices  113 us
  transfers between devices with their start and end apart: 19, of which 17 were waited for; matrix products, arithmetic and copies ran while one was open for 9% of the time, Pallas kernels for 0%

commit v1 on v0

v1 whole, which is shorter than its diff:
```python
from functools import partial
import math

import jax
import jax.numpy as jnp
from jax import lax
from jax.experimental import pallas as pl
from jax.experimental.pallas import tpu as pltpu
from jax.sharding import Mesh, PartitionSpec as P

HEADS = 32
ROT = 32
EPS = 1e-05
NEG = -1e30
BLOCK_Q = 256

BF = jnp.bfloat16
F32 = jnp.float32


def dot(a, b):
    return jnp.dot(a, b, preferred_element_type=F32)


def dot_t(a, b):
    return lax.dot_general(a, b, (((1,), (1,)), ((), ())), preferred_element_type=F32)


def t_dot(a, b):
    return lax.dot_general(a, b, (((0,), (0,)), ((), ())), preferred_element_type=F32)


def ring_pairs(order, step):
    n = len(order)
    return [(order[i], order[(i + step) % n]) for i in range(n)]


def ring_gather(own, axis, order):
    n = len(order)
    blocks = {0: own}
    up = down = own
    half = own.shape[0] // 2
    for step in range(1, n // 2 + 1):
        if 2 * step == n:
            first = lax.ppermute(up[:half], axis, ring_pairs(order, 1))
            second = lax.ppermute(down[half:], axis, ring_pairs(order, -1))
            blocks[step] = jnp.concatenate([first, second], 0)
        else:
            up = lax.ppermute(up, axis, ring_pairs(order, 1))
            down = lax.ppermute(down, axis, ring_pairs(order, -1))
            blocks[-step] = up
            blocks[step] = down
    return blocks


def ring_scatter(parts, axis, order):
    n = len(order)
    rows = parts[0].shape[0]
    half = rows // 2
    low = high = None
    for step in range(n // 2, 0, -1):
        if 2 * step == n:
            low = lax.ppermute(parts[step][:half].astype(BF), axis, ring_pairs(order, -1))
            high = lax.ppermute(parts[step][half:].astype(BF), axis, ring_pairs(order, 1))
        else:
            to_low = joined(parts[-step], low, True).astype(BF)
            to_high = joined(parts[step], high, False).astype(BF)
            low = lax.ppermute(to_low, axis, ring_pairs(order, -1))
            high = lax.ppermute(to_high, axis, ring_pairs(order, 1))
    return joined(joined(parts[0], low, True), high, False)


def joined(part, arrived, first):
    part = part.astype(F32)
    arrived = arrived.astype(F32)
    if arrived.shape[0] == part.shape[0]:
        return part + arrived
    half = arrived.shape[0]
    if first:
        return jnp.concatenate([part[:half] + arrived, part[half:]], 0)
    return jnp.concatenate([part[:half], part[half:] + arrived], 0)


def swap(value):
    return lax.ppermute(value, "core", [(0, 1), (1, 0)])


def turn(values, cosine, sine_a, sine_b):
    width = values.shape[1]
    return (
        values * cosine
        + pltpu.roll(values, width - ROT // 2, 1) * sine_a
        + pltpu.roll(values, ROT // 2, 1) * sine_b
    )


def head_mask(shape, head, head_dim):
    lane = lax.broadcasted_iota(jnp.int32, shape, 1)
    return (lane >= head * head_dim) & (lane < (head + 1) * head_dim)


def attend_kernel(heads, head_dim, span, order_ref, qkv_ref, cos_ref, sin_a_ref, sin_b_ref, att_ref, sorted_ref, out_scr):
    seq_len = qkv_ref.shape[1]
    width = heads * head_dim
    for slot in range(seq_len // span):
        rows = pl.ds(pl.multiple_of(order_ref[slot] * span, span), span)
        here = pl.ds(slot * span, span)
        tables = (cos_ref[here, :], sin_a_ref[here, :], sin_b_ref[here, :])
        query = turn(qkv_ref[0, rows, 0:width], *tables).astype(BF)
        sorted_ref[0, here, 0:width] = (query.astype(F32) * (head_dim**-0.5)).astype(BF)
        sorted_ref[0, here, width : 2 * width] = turn(qkv_ref[0, rows, width : 2 * width], *tables).astype(BF)
        sorted_ref[0, here, 2 * width :] = qkv_ref[0, rows, 2 * width :].astype(BF)
    block = min(BLOCK_Q, seq_len)
    for i in range(seq_len // block):
        extent = (i + 1) * block
        here = pl.ds(i * block, block)
        queries = sorted_ref[0, here, 0:width]
        keys = sorted_ref[0, 0:extent, width : 2 * width]
        values = sorted_ref[0, 0:extent, 2 * width :]
        row = lax.broadcasted_iota(jnp.int32, (block, extent), 0) + i * block
        col = lax.broadcasted_iota(jnp.int32, (block, extent), 1)
        total = jnp.zeros((block, width), F32)
        for head in range(heads):
            mask = head_mask((block, width), head, head_dim)
            scores = dot_t(jnp.where(mask, queries, jnp.zeros_like(queries)), keys)
            scores = jnp.where(col <= row, scores, NEG)
            top = jnp.max(scores, 1, keepdims=True)
            weights = jnp.exp(scores - top)
            norm = 1.0 / jnp.sum(weights, 1, keepdims=True)
            probs = (weights * norm).astype(BF)
            total = jnp.where(mask, dot(probs, values), total)
        out_scr[here, :] = total.astype(BF)
    for slot in range(seq_len // span):
        rows = pl.ds(pl.multiple_of(order_ref[slot] * span, span), span)
        att_ref[0, rows, :] = out_scr[slot * span : (slot + 1) * span, :]


def attend_back_kernel(
    heads, head_dim, span, order_ref, sorted_ref, grad_ref, cos_ref, sin_a_ref, sin_b_ref, out_ref, grad_scr, key_scr, value_scr
):
    seq_len = sorted_ref.shape[1]
    width = heads * head_dim
    for slot in range(seq_len // span):
        rows = pl.ds(pl.multiple_of(order_ref[slot] * span, span), span)
        grad_scr[slot * span : (slot + 1) * span, :] = grad_ref[0, rows, :]
    key_scr[...] = jnp.zeros_like(key_scr)
    value_scr[...] = jnp.zeros_like(value_scr)
    block = min(BLOCK_Q, seq_len)

    def put(slot, first, values):
        rows = pl.ds(pl.multiple_of(order_ref[slot] * span, span), span)
        out_ref[0, rows, first : first + width] = values.astype(BF)

    def tables(here):
        return (cos_ref[here, :], -sin_a_ref[here, :], -sin_b_ref[here, :])

    for i in range(seq_len // block):
        extent = (i + 1) * block
        here = pl.ds(i * block, block)
        queries = sorted_ref[0, here, 0:width]
        grads = grad_scr[here, :]
        keys = sorted_ref[0, 0:extent, width : 2 * width]
        values = sorted_ref[0, 0:extent, 2 * width :]
        key = lax.broadcasted_iota(jnp.int32, (extent, block), 0)
        query = lax.broadcasted_iota(jnp.int32, (extent, block), 1) + i * block
        query_grad = jnp.zeros((block, width), F32)
        for head in range(heads):
            mask = head_mask((block, width), head, head_dim)
            own_queries = jnp.where(mask, queries, jnp.zeros_like(queries))
            own_grads = jnp.where(mask, grads, jnp.zeros_like(grads))
            scores = jnp.where(key <= query, dot_t(keys, own_queries), NEG)
            weights = jnp.exp(scores - jnp.max(scores, 0, keepdims=True))
            probs = weights * (1.0 / jnp.sum(weights, 0, keepdims=True))
            probs_grad = dot_t(values, own_grads)
            delta = jnp.sum(probs * probs_grad, 0, keepdims=True)
            score_grad = (probs * (probs_grad - delta)).astype(BF)
            value_scr[0:extent, :] += dot(probs.astype(BF), own_grads)
            key_scr[0:extent, :] += dot(score_grad, own_queries)
            query_grad = jnp.where(mask, t_dot(score_grad, keys), query_grad)
        query_grad = turn(query_grad * (head_dim**-0.5), *tables(here))
        for j in range(block // span):
            put(i * (block // span) + j, 0, query_grad[j * span : (j + 1) * span])
    for slot in range(seq_len // span):
        here = pl.ds(slot * span, span)
        put(slot, width, turn(key_scr[here, :], *tables(here)))
        put(slot, 2 * width, value_scr[here, :])


def attend(order, qkv, tables, heads, head_dim, span):
    count, seq_len, wide = qkv.shape
    width = wide // 3
    whole = pl.BlockSpec((seq_len, width), lambda s, o: (0, 0))
    return pl.pallas_call(
        partial(attend_kernel, heads, head_dim, span),
        grid_spec=pltpu.PrefetchScalarGridSpec(
            num_scalar_prefetch=1,
            grid=(count,),
            in_specs=[pl.BlockSpec((1, seq_len, wide), lambda s, o: (s, 0, 0)), whole, whole, whole],
            out_specs=[
                pl.BlockSpec((1, seq_len, width), lambda s, o: (s, 0, 0)),
                pl.BlockSpec((1, seq_len, wide), lambda s, o: (s, 0, 0)),
            ],
            scratch_shapes=[pltpu.VMEM((seq_len, width), BF)],
        ),
        out_shape=[
            jax.ShapeDtypeStruct((count, seq_len, width), BF),
            jax.ShapeDtypeStruct((count, seq_len, wide), BF),
        ],
        compiler_params=pltpu.CompilerParams(vmem_limit_bytes=56 * 2**20),
        cost_estimate=pl.CostEstimate(
            flops=8 * count * heads * seq_len * seq_len * head_dim,
            bytes_accessed=count * seq_len * wide * 8,
            transcendentals=count * heads * seq_len * seq_len,
        ),
        name="attend",
    )(order, qkv, *tables)


def attend_back(order, kept, grads, tables, heads, head_dim, span):
    count, seq_len, wide = kept.shape
    width = wide // 3
    whole = pl.BlockSpec((seq_len, width), lambda s, o: (0, 0))
    return pl.pallas_call(
        partial(attend_back_kernel, heads, head_dim, span),
        grid_spec=pltpu.PrefetchScalarGridSpec(
            num_scalar_prefetch=1,
            grid=(count,),
            in_specs=[
                pl.BlockSpec((1, seq_len, wide), lambda s, o: (s, 0, 0)),
                pl.BlockSpec((1, seq_len, width), lambda s, o: (s, 0, 0)),
                whole,
                whole,
                whole,
            ],
            out_specs=pl.BlockSpec((1, seq_len, wide), lambda s, o: (s, 0, 0)),
            scratch_shapes=[
                pltpu.VMEM((seq_len, width), BF),
                pltpu.VMEM((seq_len, width), F32),
                pltpu.VMEM((seq_len, width), F32),
            ],
        ),
        out_shape=jax.ShapeDtypeStruct((count, seq_len, wide), BF),
        compiler_params=pltpu.CompilerParams(vmem_limit_bytes=56 * 2**20),
        cost_estimate=pl.CostEstimate(
            flops=20 * count * heads * seq_len * seq_len * head_dim,
            bytes_accessed=count * seq_len * wide * 6,
            transcendentals=count * heads * seq_len * seq_len,
        ),
        name="attend_back",
    )(order, kept, grads, *tables)


def norm_parts(rows):
    rows = rows.astype(F32)
    mean = jnp.mean(rows, -1, keepdims=True)
    centred = rows - mean
    scale = lax.rsqrt(jnp.mean(centred * centred, -1, keepdims=True) + EPS)
    return centred * scale, scale


def per_device(
    inputs,
    span_table,
    ln_gain,
    ln_bias,
    qkv_weight,
    qkv_bias,
    out_weight,
    out_bias,
    fc1_weight,
    fc1_bias,
    fc2_weight,
    fc2_bias,
    cotangent,
):
    rows, width = inputs.shape
    head_dim = width // HEADS
    n_q, n_z = lax.axis_size("q"), lax.axis_size("ctx")
    n_t = 2 * n_z
    n_all = n_q * n_t
    q, core, z = lax.axis_index("q"), lax.axis_index("core"), lax.axis_index("ctx")
    t = core * n_z + z
    span = rows // 2
    seq_len = rows * n_z
    heads = HEADS // n_t
    own_width = heads * head_dim
    hidden_all = fc2_weight.shape[0] * n_all
    units = fc2_weight.shape[0]
    own_units = units * n_q
    every = ("q", "core", "ctx")
    z_order = list(range(n_z))
    q_order = [0, 1, 3, 2] if n_q == 4 else list(range(n_q))
    places = jnp.array([q_order.index(i) for i in range(n_q)], jnp.int32)
    q_place = places[q]
    q_ring = jnp.array(q_order, jnp.int32)

    def q_at(offset):
        return q_ring[(q_place + offset) % n_q]

    small = jnp.concatenate([ln_gain, ln_bias, out_bias, fc2_bias, qkv_bias, fc1_bias])
    small = lax.all_gather(small, every, axis=0)
    cuts = [ln_gain.shape[0], ln_bias.shape[0], out_bias.shape[0], fc2_bias.shape[0], qkv_bias.shape[0], fc1_bias.shape[0]]
    starts = [sum(cuts[:i]) for i in range(len(cuts))]
    gain, shift, b_out, b_down, b_qkv, b_up = (
        small[:, s : s + c].astype(F32) for s, c in zip(starts, cuts)
    )
    gain, shift, b_out, b_down = (v.reshape(1, width) for v in (gain, shift, b_out, b_down))
    b_qkv = lax.dynamic_index_in_dim(b_qkv.reshape(3, heads, n_t, head_dim), t, 2, False).reshape(1, 3 * own_width)
    b_up = lax.dynamic_index_in_dim(b_up.reshape(n_q, n_t, units), t, 1, False).reshape(1, own_units)

    def q_gather(block):
        blocks = ring_gather(block, "q", q_order)
        whole = jnp.zeros((n_q,) + block.shape, block.dtype)
        for offset, value in blocks.items():
            whole = lax.dynamic_update_index_in_dim(whole, value, q_at(offset), 0)
        return whole.reshape((n_q * block.shape[0],) + block.shape[1:])

    def q_scatter(part):
        part = part.reshape((n_q, part.shape[0] // n_q) + part.shape[1:])
        offsets = [0] + [o for s in range(1, n_q // 2 + 1) for o in ((s,) if 2 * s == n_q else (-s, s))]
        parts = {o: lax.dynamic_index_in_dim(part, q_at(o), 0, False) for o in offsets}
        return ring_scatter(parts, "q", q_order)

    def rows_to_columns(blocks):
        _, r, c = blocks.shape
        blocks = blocks.reshape(2, n_z, r, c)
        mine = lax.dynamic_index_in_dim(blocks, core, 0, False)
        other = swap(lax.dynamic_index_in_dim(blocks, 1 - core, 0, False))
        both = jnp.stack([mine, other], 1)
        whole = jnp.zeros((2, n_z, r, c), blocks.dtype)
        for shift_by in range(n_z):
            piece = lax.dynamic_index_in_dim(both, (z + shift_by) % n_z, 0, False)
            if shift_by:
                piece = lax.ppermute(piece, "ctx", ring_pairs(z_order, shift_by))
            source = (z - shift_by) % n_z
            for rank, at in ((0, core), (1, 1 - core)):
                whole = lax.dynamic_update_slice(whole, piece[rank][None, None], (at, source, 0, 0))
        return whole.reshape(n_t * r, c)

    def columns_to_rows(part):
        c = part.shape[1]
        r = part.shape[0] // n_t
        part = part.reshape(2, n_z, r, c)
        mine = lax.dynamic_index_in_dim(part, core, 0, False)
        other = swap(lax.dynamic_index_in_dim(part, 1 - core, 0, False))
        both = jnp.stack([mine, other], 1)
        whole = jnp.zeros((2, n_z, r, c), part.dtype)
        for shift_by in range(n_z):
            piece = lax.dynamic_index_in_dim(both, (z + shift_by) % n_z, 0, False)
            if shift_by:
                piece = lax.ppermute(piece, "ctx", ring_pairs(z_order, shift_by))
            source = (z - shift_by) % n_z
            for rank, at in ((0, core), (1, 1 - core)):
                whole = lax.dynamic_update_slice(whole, piece[rank][None, None], (at, source, 0, 0))
        return whole.reshape(n_t, r, c)

    d_rows = qkv_weight.shape[0]
    qkv_blocks = qkv_weight.reshape(d_rows, 3, heads, n_t, head_dim).transpose(3, 0, 1, 2, 4).reshape(n_t, d_rows, 3 * own_width)
    up_blocks = fc1_weight.reshape(d_rows, n_q, n_t, units).transpose(2, 0, 1, 3).reshape(n_t, d_rows, own_units)
    w_qkv = q_gather(rows_to_columns(qkv_blocks))
    w_up = q_gather(rows_to_columns(up_blocks))
    whole_heads = out_weight.shape[0] == head_dim
    if whole_heads:
        w_out = q_gather(out_weight)
    else:
        w_out = lax.all_gather(out_weight, every, axis=0, tiled=True).reshape(heads, n_t, head_dim, width)
        w_out = lax.dynamic_index_in_dim(w_out, t, 1, False).reshape(own_width, width)
    w_down = q_gather(fc2_weight)

    offsets = [0] + [o for s in range(1, n_z // 2 + 1) for o in ((s,) if 2 * s == n_z else (-s, s))]

    def line_gather(block):
        blocks = ring_gather(block, "ctx", z_order)
        mine = [blocks[o] for o in offsets]
        return jnp.concatenate(mine + [swap(b) for b in mine], 0)

    def line_scatter(part):
        other = swap(part[seq_len:].astype(BF))
        mine = part[:seq_len].astype(F32) + other.astype(F32)
        parts = {o: mine[i * rows : (i + 1) * rows] for i, o in enumerate(offsets)}
        return ring_scatter(parts, "ctx", z_order)

    x_all = line_gather(inputs)
    g_all = line_gather(cotangent)

    spans = jnp.concatenate([lax.dynamic_index_in_dim(span_table, (z + o) % n_z, 0, False) for o in offsets])
    n_spans = 2 * n_z
    order = jnp.sum(
        jnp.where(spans[None, :] == jnp.arange(n_spans, dtype=jnp.int32)[:, None], jnp.arange(n_spans, dtype=jnp.int32)[None, :], 0),
        1,
        dtype=jnp.int32,
    )
    half = ROT // 2
    lane = jnp.arange(own_width, dtype=jnp.int32)[None, :] % head_dim
    position = jnp.arange(seq_len, dtype=jnp.int32).astype(F32)[:, None]
    freqs = jnp.where(lane < ROT, jnp.exp((lane % half).astype(F32) * (-2.0 * math.log(10000.0) / ROT)), 0.0)
    angles = position * freqs
    sine = jnp.sin(angles)
    tables = (jnp.cos(angles), jnp.where(lane < half, -sine, 0.0), jnp.where((lane >= half) & (lane < ROT), sine, 0.0))

    xhat, _ = norm_parts(x_all)
    hidden = (xhat * gain + shift).astype(BF)
    qkv = (dot(hidden, w_qkv) + b_qkv).reshape(2, seq_len, 3 * own_width)
    attended, kept = attend(order, qkv, tables, heads, head_dim, span)
    attended = attended.reshape(2 * seq_len, own_width)
    pre = dot(hidden, w_up) + b_up
    act, gelu_back = jax.vjp(partial(jax.nn.gelu, approximate=True), pre)
    act = act.astype(BF)
    out_part = dot(attended, w_out) + dot(act, w_down)
    x_own = inputs.astype(F32)
    output = (x_own + line_scatter(out_part.astype(BF)) + b_out + b_down).astype(BF)

    pre_grad = gelu_back(dot_t(g_all, w_down))[0].astype(BF)
    down_part = t_dot(act, g_all).astype(BF)
    up_part = t_dot(hidden, pre_grad).astype(BF)
    up_bias_part = jnp.sum(pre_grad.astype(F32), 0)

    attended_grad = dot_t(g_all, w_out).astype(BF).reshape(2, seq_len, own_width)
    out_w_part = t_dot(attended, g_all).astype(BF)
    qkv_grad = attend_back(order, kept, attended_grad, tables, heads, head_dim, span).reshape(2 * seq_len, 3 * own_width)
    normed_part = (dot_t(qkv_grad, w_qkv) + dot_t(pre_grad, w_up)).astype(BF)
    qkv_part = t_dot(hidden, qkv_grad).astype(BF)
    qkv_bias_part = jnp.sum(qkv_grad.astype(F32), 0)

    fc2_weight_grad = q_scatter(down_part)
    fc1_weight_grad = (
        columns_to_rows(q_scatter(up_part).astype(BF))
        .astype(F32)
        .reshape(n_t, d_rows, n_q, units)
        .transpose(1, 2, 0, 3)
        .reshape(d_rows, hidden_all)
    )
    qkv_weight_grad = (
        columns_to_rows(q_scatter(qkv_part).astype(BF))
        .astype(F32)
        .reshape(n_t, d_rows, 3, heads, head_dim)
        .transpose(1, 2, 3, 0, 4)
        .reshape(d_rows, 3 * width)
    )
    if whole_heads:
        out_weight_grad = q_scatter(out_w_part)
    else:
        spread = jnp.zeros((heads, n_t, head_dim, width), F32)
        spread = lax.dynamic_update_slice(spread, out_w_part.astype(F32).reshape(heads, 1, head_dim, width), (0, t, 0, 0))
        out_weight_grad = lax.psum_scatter(spread.reshape(width, width), every, scatter_dimension=0, tiled=True)

    normed_grad = line_scatter(normed_part)
    g_own = cotangent.astype(F32)
    xhat_own, scale_own = norm_parts(inputs)
    m = normed_grad * gain
    x_grad = (m - jnp.mean(m, -1, keepdims=True) - xhat_own * jnp.mean(m * xhat_own, -1, keepdims=True)) * scale_own
    input_grad = (g_own + x_grad).astype(BF)

    def by_owner(vector):
        return vector.reshape(n_all, vector.shape[0] // n_all)

    qkv_spread = lax.dynamic_update_slice(
        jnp.zeros((3, heads, n_t, head_dim), F32), qkv_bias_part.reshape(3, heads, 1, head_dim), (0, 0, t, 0)
    ).reshape(-1)
    up_spread = lax.dynamic_update_slice(jnp.zeros((n_q, n_t, units), F32), up_bias_part.reshape(n_q, 1, units), (0, t, 0)).reshape(-1)
    vectors = jnp.concatenate(
        [
            by_owner(jnp.sum(normed_grad * xhat_own, 0)),
            by_owner(jnp.sum(normed_grad, 0)),
            by_owner(jnp.sum(g_own, 0)),
            by_owner(qkv_spread),
            by_owner(up_spread),
        ],
        1,
    )
    wide = vectors.shape[1]
    cube = vectors.reshape(n_q, 2, n_z, wide)
    cube = lax.dynamic_index_in_dim(cube, core, 1, False) + swap(lax.dynamic_index_in_dim(cube, 1 - core, 1, False))
    line = sum_blocks(cube, "q", q, n_q)
    line = sum_blocks(line, "ctx", z, n_z)
    cuts = [ln_gain.shape[0], ln_bias.shape[0], out_bias.shape[0], qkv_bias.shape[0], fc1_bias.shape[0]]
    starts = [sum(cuts[:i]) for i in range(len(cuts))]
    gain_grad, shift_grad, bias_grad, qkv_bias_grad, fc1_bias_grad = (line[s : s + c] for s, c in zip(starts, cuts))
    return (
        output,
        input_grad,
        gain_grad,
        shift_grad,
        qkv_weight_grad,
        qkv_bias_grad,
        out_weight_grad,
        bias_grad,
        fc1_weight_grad,
        fc1_bias_grad,
        fc2_weight_grad,
        bias_grad,
    )


def sum_blocks(blocks, axis, index, n):
    total = lax.dynamic_index_in_dim(blocks, index, 0, False)
    for shift_by in range(1, n):
        piece = lax.dynamic_index_in_dim(blocks, (index + shift_by) % n, 0, False)
        total = total + lax.ppermute(piece, axis, ring_pairs(list(range(n)), shift_by))
    return total


def solution(mesh):
    n_dp, n_ctx = mesh.devices.shape
    inner = Mesh(mesh.devices.reshape(n_dp // 2, 2, n_ctx), ("q", "core", "ctx"))
    every = ("q", "core", "ctx")
    matrix, vector = P(every, None), P(every)
    return jax.shard_map(
        per_device,
        mesh=inner,
        in_specs=(
            matrix,
            P(),
            vector,
            vector,
            matrix,
            vector,
            matrix,
            vector,
            matrix,
            vector,
            matrix,
            vector,
            matrix,
        ),
        out_specs=(matrix, matrix, vector, vector, matrix, vector, matrix, vector, matrix, vector, matrix, vector),
        check_vma=False,
    )
```

time: 5530 us -> 911 us (0.16)
  waiting for transfers between devices: 4890 us -> 402 us
  matrix products: 334 us -> 140 us
  starting transfers between devices: 0.75 us -> 97.7 us
  blocking collectives: 112 us -> 47.1 us
    reduce_scatter x6 -> x0, waiting for transfers between devices: 3720 us -> none  [the longest x1 1410 us: per_device(): lax.psum_scatter(down_grad, ('dp', 'ctx'), scatter_dimension=0, tiled=True)]
    all_gather x12 -> x0, waiting for transfers between devices: 1060 us -> none  [the longest x1 185 us: per_device(): lax.all_gather(fc2_weight, ('dp', 'ctx'), axis=0, tiled=True)]
    ppermute x0 -> x81, waiting for transfers between devices: none -> 402 us  [the longest x6 84.1 us: rows_to_columns(): piece = lax.ppermute(piece, 'ctx', ring_pairs(z_order, shift_by))]
    dot_general x26 -> x12, matrix products: 334 us -> 140 us  [the longest x4 50 us: dot_t(): lax.dot_general(a, b, (((1,), (1,)), ((), ())), preferred_element_type=F32)]
    unnamed x20 -> x0, waiting for transfers between devices: 113 us -> none
    ppermute x0 -> x81, starting transfers between devices: none -> 97.7 us  [the longest x6 15.1 us: columns_to_rows(): piece = lax.ppermute(piece, 'ctx', ring_pairs(z_order, shift_by))]
    all_gather x1 -> x0, blocking collectives: 67.8 us -> none  [per_device(): lax.all_gather(fc1_bias, ('dp', 'ctx'), axis=0, tiled=True)]
  transfers between devices with their start and end apart: 19 -> 81, of which waited for: 17 -> 35; matrix products, arithmetic and copies ran while one was open for 9% -> 20% of each run, Pallas kernels for 0% -> 0%
where the time goes in v1:
time: 911 us; the launch traced here: 901 us
  waiting for transfers between devices  402 us (44%)
  matrix products  140 us (15%)
  starting transfers between devices  97.7 us (11%)
  local copies, waits for them, and re-layouts  91.1 us (10%)
  other arithmetic  60.7 us (7%)
  Pallas kernels  47.7 us (5%)
  blocking collectives  47.1 us (5%)
  between operations  14.3 us (2%)
    ppermute x6, waiting for transfers between devices, rows_to_columns(): piece = lax.ppermute(piece, 'ctx', ring_pairs(z_order, shift_by))  84.1 us
    ppermute x6, waiting for transfers between devices, ring_scatter(): low = lax.ppermute(to_low, axis, ring_pairs(order, -1))  57.8 us
    ppermute x6, waiting for transfers between devices, ring_scatter(): high = lax.ppermute(to_high, axis, ring_pairs(order, 1))  57.8 us
    dot_general x4, matrix products, dot_t(): lax.dot_general(a, b, (((1,), (1,)), ((), ())), preferred_element_type=F32)  50 us
    unnamed x1, blocking collectives  47.1 us
    dot_general x4, matrix products, t_dot(): lax.dot_general(a, b, (((0,), (0,)), ((), ())), preferred_element_type=F32)  45.4 us
    ppermute x6, waiting for transfers between devices, ring_scatter(): lax.ppermute(parts[step][:half].astype(BF), axis, ring_pairs(order, -1))  45.2 us
    dot_general x4, matrix products, dot(): return jnp.dot(a, b, preferred_element_type=F32)  44.7 us
  transfers between devices with their start and end apart: 81, of which 35 were waited for; matrix products, arithmetic and copies ran while one was open for 20% of the time, Pallas kernels for 0%

profile of v1, /device:TPU:0, one launch (start us, length us, event | category | flops | bytes accessed | tf_op | source)
XLA Modules:
  0.0 900.9 jit_solution(9408221574889822000)
XLA Ops:
  21.8 47.1 %all-reduce = bf16[22528]{0:T(1024)(128)(2,1)S(1)} all-reduce(bf16[22528]{0:T(1024)(128)(2,1)S(1)} %dynamic-update-slice), channel_id=2, replica_groups=mesh['q'=4,'core'=2,'ctx'=4] {'q','core','ctx'}, use_global_device_ids=true, to_apply=%add | all-reduce | flops 22528 | bytes 90112
  114.7 43.7 %collective-permute-done.9 = bf16[2,64,768]{2,1,0:T(8,128)(2,1)S(1)} collective-permute-done((bf16[2,64,768]{2,1,0:T(8,128)(2,1)S(1)}, bf16[2,64,768]{2,1,0:T(8,128)(2,1)S(1)}, u32[]{:S(2)}, u32[]{:S(2)}) %collective-permute-start.9) | collective-permute-done | bytes 196640 | tf_op jit(solution)/shard_map/ppermute | solution.py:334
  160.6 8.9 collective-permute-done.10
  178.1 9.2 %collective-permute-done.21 = bf16[2,64,1024]{2,1,0:T(8,128)(2,1)S(1)} collective-permute-done((bf16[2,64,1024]{2,1,0:T(8,128)(2,1)S(1)}, bf16[2,64,1024]{2,1,0:T(8,128)(2,1)S(1)}, u32[]{:S(2)}, u32[]{:S(2)}) %collective-permute-start.21) | collective-permute-done | bytes 262176 | tf_op jit(solution)/shard_map/ppermute | solution.py:334
  187.4 11.7 %collective-permute-done.22 = bf16[2,64,1024]{2,1,0:T(8,128)(2,1)S(1)} collective-permute-done((bf16[2,64,1024]{2,1,0:T(8,128)(2,1)S(1)}, bf16[2,64,1024]{2,1,0:T(8,128)(2,1)S(1)}, u32[]{:S(2)}, u32[]{:S(2)}) %collective-permute-start.22) | collective-permute-done | bytes 262176 | tf_op jit(solution)/shard_map/ppermute | solution.py:334
  215.5 20.3 %collective-permute-done = bf16[256,2048]{1,0:T(8,128)(2,1)S(1)} collective-permute-done((bf16[256,2048]{1,0:T(8,128)(2,1)S(1)}, bf16[256,2048]{1,0:T(8,128)(2,1)S(1)}, u32[]{:S(2)}, u32[]{:S(2)}) %collective-permute-start) | collective-permute-done | bytes 1048608 | tf_op jit(solution)/shard_map/ppermute | solution.py:49
  235.9 18.9 %collective-permute-done.1 = bf16[256,2048]{1,0:T(8,128)(2,1)S(1)} collective-permute-done((bf16[256,2048]{1,0:T(8,128)(2,1)S(1)}, bf16[256,2048]{1,0:T(8,128)(2,1)S(1)}, u32[]{:S(2)}, u32[]{:S(2)}) %collective-permute-start.1) | collective-permute-done | bytes 1048608 | tf_op jit(solution)/shard_map/ppermute | solution.py:50
  274.7 11.2 %collective-permute-done.39 = bf16[128,2048]{1,0:T(8,128)(2,1)S(1)} collective-permute-done((bf16[128,2048]{1,0:T(8,128)(2,1)S(1)}, bf16[128,2048]{1,0:T(8,128)(2,1)S(1)}, u32[]{:S(2)}, u32[]{:S(2)}) %collective-permute-start.39) | collective-permute-done | bytes 524320 | tf_op jit(solution)/shard_map/ppermute | solution.py:45
  308.7 12.2 %collective-permute-done.31 = bf16[128,2048]{1,0:T(8,128)(2,1)S(1)} collective-permute-done((bf16[128,2048]{1,0:T(8,128)(2,1)S(1)}, bf16[128,2048]{1,0:T(8,128)(2,1)S(1)}, u32[]{:S(2)}, u32[]{:S(2)}) %collective-permute-start.31) | collective-permute-done | bytes 524320 | tf_op jit(solution)/shard_map/ppermute | solution.py:46
  320.9 12.5 %collective-permute-done.30 = bf16[128,2048]{1,0:T(8,128)(2,1)S(1)} collective-permute-done((bf16[128,2048]{1,0:T(8,128)(2,1)S(1)}, bf16[128,2048]{1,0:T(8,128)(2,1)S(1)}, u32[]{:S(2)}, u32[]{:S(2)}) %collective-permute-start.30) | collective-permute-done | bytes 524320 | tf_op jit(solution)/shard_map/ppermute | solution.py:45
  334.9 8.7 collective-permute-done.14
  348.1 11.0 %collective-permute-done.27 = bf16[256,1024]{1,0:T(8,128)(2,1)S(1)} collective-permute-done((bf16[256,1024]{1,0:T(8,128)(2,1)S(1)}, bf16[256,1024]{1,0:T(8,128)(2,1)S(1)}, u32[]{:S(2)}, u32[]{:S(2)}) %collective-permute-start.27) | collective-permute-done | bytes 524320 | tf_op jit(solution)/shard_map/ppermute | solution.py:46
  369.3 11.0 %fusion.137 = f32[2048,1024]{1,0:T(8,128)} fusion(bf16[2048,2048]{1,0:T(8,128)(2,1)S(1)} %fusion.5, bf16[2048,1024]{1,0:T(8,128)(2,1)S(1)} %bitcast.372), kind=kOutput, calls=%fused_computation.364 | convolution fusion | flops 8589934592 | bytes 20971520 | tf_op jit(solution)/shard_map/dot_general | solution.py:22
  380.4 17.5 %convolution_convert_fusion = bf16[1024,2048]{1,0:T(8,128)(2,1)} fusion(bf16[2048,2048]{1,0:T(8,128)(2,1)S(1)} %constant_dynamic-update-slice_fusion.9, f32[2048,1024]{1,0:T(8,128)} %fusion.137, f32[1024]{0:T(1024)S(1)} %bitcast.397), kind=kOutput, calls=%fused_computation.24 | convolution fusion | flops 8613003264 | bytes 20975616 | tf_op jit(solution)/shard_map/dot_general | solution.py:30
  398.0 18.4 %convert_reduce_fusion.1 = (f32[1024]{0:T(1024)S(1)}, bf16[2048,1024]{1,0:T(8,128)(2,1)}) fusion(f32[2048,1024]{1,0:T(8,128)} %fusion.137, f32[1024]{0:T(1024)S(1)} %bitcast.398, bf16[2048,2048]{1,0:T(8,128)(2,1)S(1)} %constant_dynamic-update-slice_fusion.9, bf16[1024,2048]{1,0:T(8,128)(2,1)} %bitcast.56), kind=kOutput, calls=%fused_computation.19 | convolution fusion | flops 8638168064 | bytes 25174016 | tf_op jit(solution)/shard_map/dot_general | solution.py:26
  416.4 16.7 %fusion.130 = f32[2048,2048]{1,0:T(8,128)} fusion(bf16[1024,2048]{1,0:T(8,128)(2,1)} %bitcast.56, f32[2048,1024]{1,0:T(8,128)} %fusion.137, f32[1024]{0:T(1024)S(1)} %bitcast.399), kind=kOutput, calls=%fused_computation.359 | convolution fusion | flops 8610906112 | bytes 29364224 | tf_op jit(solution)/shard_map/dot_general | solution.py:22
  433.1 12.7 %convolution_convert_fusion.1 = bf16[2048,1024]{1,0:T(8,128)(2,1)} fusion(bf16[2048,2048]{1,0:T(8,128)(2,1)S(1)} %bitcast.356, bf16[2048,1024]{1,0:T(8,128)(2,1)} %get-tuple-element.29), kind=kOutput, calls=%fused_computation.25 | convolution fusion | flops 8592031744 | bytes 16777216 | tf_op jit(solution)/shard_map/dot_general | solution.py:30
  445.8 14.4 %fusion.138 = f32[2048,2048]{1,0:T(8,128)} fusion(bf16[2048,1024]{1,0:T(8,128)(2,1)} %get-tuple-element.29, bf16[2048,1024]{1,0:T(8,128)(2,1)S(1)} %bitcast.373), kind=kOutput, calls=%fused_computation.365 | convolution fusion | flops 8589934592 | bytes 25165824 | tf_op jit(solution)/shard_map/dot_general | solution.py:26
  472.1 18.0 %attend.1 = (bf16[2,1024,256]{2,1,0:T(8,128)(2,1)}, bf16[2,1024,768]{2,1,0:T(8,128)(2,1)}) custom-call(s32[8]{0:T(128)} %select_reduce_fusion.order_ref, f32[2,1024,768]{2,1,0:T(8,128)} %bitcast.401, f32[1024,256]{1,0:T(8,128)} %get-tuple-element.107.cos_ref, f32[1024,256]{1,0:T(8,128)} %get-tuple-element.106.sin_a_ref, f32[1024,256]{1,0:T(8,128)} %get-tuple-element.105.sin_b_ref), custom_call_target="tpu_custom_call" | custom-call | flops 4294967296 | bytes 12582912 | tf_op jit(solution)/shard_map/attend/pallas_call | solution.py:193
  490.1 29.7 %attend_back.1 = bf16[2,1024,768]{2,1,0:T(8,128)(2,1)} custom-call(s32[8]{0:T(128)} %select_reduce_fusion.order_ref, bf16[2,1024,768]{2,1,0:T(8,128)(2,1)} %get-tuple-element.15.sorted_ref, bf16[2,1024,256]{2,1,0:T(8,128)(2,1)} %bitcast.402, f32[1024,256]{1,0:T(8,128)} %get-tuple-element.107.cos_ref, f32[1024,256]{1,0:T(8,128)} %get-tuple-element.106.sin_a_ref, ...), custom_call_target="tpu_custom_call" | custom-call | flops 10737418240 | bytes 9437184 | tf_op jit(solution)/shard_map/attend_back/pallas_call | solution.py:223
  531.3 9.4 %convolution_convert_fusion.2 = bf16[2048,768]{1,0:T(8,128)(2,1)S(1)} fusion(bf16[2048,2048]{1,0:T(8,128)(2,1)} %copy-done.6, bf16[2048,768]{1,0:T(8,128)(2,1)S(1)} %bitcast.381), kind=kOutput, calls=%fused_computation.26 | convolution fusion | flops 6444023808 | bytes 14680064 | tf_op jit(solution)/shard_map/dot_general | solution.py:30
  548.3 13.8 %add_convert_fusion = bf16[2048,2048]{1,0:T(8,128)(2,1)} fusion(f32[2048,2048]{1,0:T(8,128)} %fusion.138, bf16[2048,768]{1,0:T(8,128)(2,1)S(1)} %bitcast.382, bf16[2048,768]{1,0:T(8,128)(2,1)} %bitcast.386), kind=kOutput, calls=%fused_computation.8 | convolution fusion | flops 6450839552 | bytes 31457280 | tf_op jit(solution)/shard_map/dot_general | solution.py:26
  616.2 14.7 %collective-permute-done.60 = bf16[512,768]{1,0:T(8,128)(2,1)S(1)} collective-permute-done((bf16[512,768]{1,0:T(8,128)(2,1)S(1)}, bf16[512,768]{1,0:T(8,128)(2,1)S(1)}, u32[]{:S(2)}, u32[]{:S(2)}) %collective-permute-start.60) | collective-permute-done | bytes 786464 | tf_op jit(solution)/shard_map/ppermute | solution.py:69
  633.5 19.9 %collective-permute-done.72 = bf16[512,1024]{1,0:T(8,128)(2,1)S(1)} collective-permute-done((bf16[512,1024]{1,0:T(8,128)(2,1)S(1)}, bf16[512,1024]{1,0:T(8,128)(2,1)S(1)}, u32[]{:S(2)}, u32[]{:S(2)}) %collective-permute-start.72) | collective-permute-done | bytes 1048608 | tf_op jit(solution)/shard_map/ppermute | solution.py:69
  654.6 18.8 %collective-permute-done.80 = bf16[256,2048]{1,0:T(8,128)(2,1)S(1)} collective-permute-done((bf16[256,2048]{1,0:T(8,128)(2,1)S(1)}, bf16[256,2048]{1,0:T(8,128)(2,1)S(1)}, u32[]{:S(2)}, u32[]{:S(2)}) %collective-permute-start.80) | collective-permute-done | bytes 1048608 | tf_op jit(solution)/shard_map/ppermute | solution.py:69
  692.5 9.0 collective-permute-done.63
  719.2 9.9 %collective-permute-done.74 = bf16[2,64,1024]{2,1,0:T(8,128)(2,1)S(1)} collective-permute-done((bf16[2,64,1024]{2,1,0:T(8,128)(2,1)S(1)}, bf16[2,64,1024]{2,1,0:T(8,128)(2,1)S(1)}, u32[]{:S(2)}, u32[]{:S(2)}) %collective-permute-start.74) | collective-permute-done | bytes 262176 | tf_op jit(solution)/shard_map/ppermute | solution.py:351
  730.5 9.1 %fusion.129 = (bf16[1024,2048]{1,0:T(8,128)(2,1)S(1)}, f32[1024,2048]{1,0:T(8,128)}) fusion(bf16[1024,2048]{1,0:T(8,128)(2,1)} %collective-permute-done.45, bf16[2048,2048]{1,0:T(8,128)(2,1)} %add_convert_fusion), kind=kLoop, calls=%fused_computation.358 | loop fusion | flops 8388608 | bytes 20971520 | tf_op jit(solution)/shard_map/convert.55
  753.5 11.0 %collective-permute-done.46 = bf16[128,2048]{1,0:T(8,128)(2,1)} collective-permute-done((bf16[128,2048]{1,0:T(8,128)(2,1)}, bf16[128,2048]{1,0:T(8,128)(2,1)}, u32[]{:S(2)}, u32[]{:S(2)}) %collective-permute-start.46) | collective-permute-done | bytes 524320 | tf_op jit(solution)/shard_map/ppermute | solution.py:63
  772.4 34.1 %collective-permute-done.33 = bf16[128,2048]{1,0:T(8,128)(2,1)S(1)} collective-permute-done((bf16[128,2048]{1,0:T(8,128)(2,1)S(1)}, bf16[128,2048]{1,0:T(8,128)(2,1)S(1)}, u32[]{:S(2)}, u32[]{:S(2)}) %collective-permute-start.33) | collective-permute-done | bytes 524320 | tf_op jit(solution)/shard_map/ppermute | solution.py:63
  814.1 42.2 %collective-permute-done.47 = bf16[256,2048]{1,0:T(8,128)(2,1)S(1)} collective-permute-done((bf16[256,2048]{1,0:T(8,128)(2,1)S(1)}, bf16[256,2048]{1,0:T(8,128)(2,1)S(1)}, u32[]{:S(2)}, u32[]{:S(2)}) %collective-permute-start.47) | collective-permute-done | bytes 1048608 | tf_op jit(solution)/shard_map/ppermute | solution.py:68
  859.3 15.6 %collective-permute-done.34 = bf16[256,2048]{1,0:T(8,128)(2,1)S(1)} collective-permute-done((bf16[256,2048]{1,0:T(8,128)(2,1)S(1)}, bf16[256,2048]{1,0:T(8,128)(2,1)S(1)}, u32[]{:S(2)}, u32[]{:S(2)}) %collective-permute-start.34) | collective-permute-done | bytes 1048608 | tf_op jit(solution)/shard_map/ppermute | solution.py:68
  (471 shorter events, 325.4 us)
Async XLA Ops:
  0.6 101.5 %collective-permute-start.17 = (bf16[64,2048]{1,0:T(8,128)(2,1)}, bf16[64,2048]{1,0:T(8,128)(2,1)}, u32[]{:S(2)}, u32[]{:S(2)}) collective-permute-start(bf16[64,2048]{1,0:T(8,128)(2,1)} %param.21), channel_id=1, source_target_pairs={{0,16},{8,0},{24,8},{16,24},{1,17},{9,1},{25,9},{17,25},{2,18},{10... | collective-permute-start | bytes 786440 | tf_op jit(solution)/shard_map/ppermute | solution.py:50
  3.7 101.7 %collective-permute-start.16 = (bf16[64,2048]{1,0:T(8,128)(2,1)}, bf16[64,2048]{1,0:T(8,128)(2,1)}, u32[]{:S(2)}, u32[]{:S(2)}) collective-permute-start(bf16[64,2048]{1,0:T(8,128)(2,1)} %param.21), channel_id=1, source_target_pairs={{0,8},{8,24},{24,16},{16,0},{1,9},{9,25},{25,17},{17,1},{2,10},{10... | collective-permute-start | bytes 786440 | tf_op jit(solution)/shard_map/ppermute | solution.py:49
  3.7 254.2 %collective-permute-start.29 = (bf16[256,2048]{1,0:T(8,128)(2,1)}, bf16[256,2048]{1,0:T(8,128)(2,1)}, u32[]{:S(2)}, u32[]{:S(2)}) collective-permute-start(bf16[256,2048]{1,0:T(8,128)(2,1)} %param.25), channel_id=1, source_target_pairs={{0,16},{8,0},{24,8},{16,24},{1,17},{9,1},{25,9},{17,25},{2,18},{10... | collective-permute-start | bytes 3145736 | tf_op jit(solution)/shard_map/ppermute | solution.py:50
  5.7 207.0 %collective-permute-start.28 = (bf16[256,2048]{1,0:T(8,128)(2,1)}, bf16[256,2048]{1,0:T(8,128)(2,1)}, u32[]{:S(2)}, u32[]{:S(2)}) collective-permute-start(bf16[256,2048]{1,0:T(8,128)(2,1)} %param.25), channel_id=1, source_target_pairs={{0,8},{8,24},{24,16},{16,0},{1,9},{9,25},{25,17},{17,1},{2,10},{10... | collective-permute-start | bytes 3145736 | tf_op jit(solution)/shard_map/ppermute | solution.py:49
  13.2 98.6 %collective-permute-start.8 = (bf16[4,64,768]{2,1,0:T(8,128)(2,1)}, bf16[4,64,768]{2,1,0:T(8,128)(2,1)}, u32[]{:S(2)}, u32[]{:S(2)}) collective-permute-start(bf16[4,64,768]{2,1,0:T(8,128)(2,1)} %get-tuple-element.96), channel_id=1, source_target_pairs={{0,4},{4,0},{1,5},{5,1},{2,6},{6,2},{3,7},{7,3},{8,12},{12,8},{9,1... | collective-permute-start | bytes 1179656 | tf_op jit(solution)/shard_map/ppermute | solution.py:85
  108.3 104.2 %collective-permute-start.38 = (bf16[256,2048]{1,0:T(8,128)(2,1)S(1)}, bf16[256,2048]{1,0:T(8,128)(2,1)S(1)}, u32[]{:S(2)}, u32[]{:S(2)}) collective-permute-start(bf16[256,2048]{1,0:T(8,128)(2,1)S(1)} %copy-done.8), channel_id=1, source_target_pairs={{0,3},{1,0},{2,1},{3,2},{4,7},{5,4},{6,5},{7,6},{8,11},{9,8},{10,9... | collective-permute-start | bytes 3145736 | tf_op jit(solution)/shard_map/ppermute | solution.py:50
  111.3 96.8 %collective-permute-start.37 = (bf16[256,2048]{1,0:T(8,128)(2,1)S(1)}, bf16[256,2048]{1,0:T(8,128)(2,1)S(1)}, u32[]{:S(2)}, u32[]{:S(2)}) collective-permute-start(bf16[256,2048]{1,0:T(8,128)(2,1)S(1)} %copy-done.8), channel_id=1, source_target_pairs={{0,1},{1,2},{2,3},{3,0},{4,5},{5,6},{6,7},{7,4},{8,9},{9,10},{10,1... | collective-permute-start | bytes 3145736 | tf_op jit(solution)/shard_map/ppermute | solution.py:49
  113.8 44.6 %collective-permute-start.9 = (bf16[2,64,768]{2,1,0:T(8,128)(2,1)S(1)}, bf16[2,64,768]{2,1,0:T(8,128)(2,1)S(1)}, u32[]{:S(2)}, u32[]{:S(2)}) collective-permute-start(bf16[2,64,768]{2,1,0:T(8,128)(2,1)S(1)} %get-tuple-element.94), channel_id=1, source_target_pairs={{0,1},{1,2},{2,3},{3,0},{4,5},{5,6},{6,7},{7,4},{8,9},{9,10},{10,1... | collective-permute-start | bytes 589832 | tf_op jit(solution)/shard_map/ppermute | solution.py:334
  208.1 46.7 %collective-permute-start.1 = (bf16[256,2048]{1,0:T(8,128)(2,1)S(1)}, bf16[256,2048]{1,0:T(8,128)(2,1)S(1)}, u32[]{:S(2)}, u32[]{:S(2)}) collective-permute-start(bf16[256,2048]{1,0:T(8,128)(2,1)S(1)} %copy-done.1), channel_id=1, source_target_pairs={{0,3},{1,0},{2,1},{3,2},{4,7},{5,4},{6,5},{7,6},{8,11},{9,8},{10,9... | collective-permute-start | bytes 3145736 | tf_op jit(solution)/shard_map/ppermute | solution.py:50
  212.5 93.9 %collective-permute-start.41 = (bf16[256,2048]{1,0:T(8,128)(2,1)S(1)}, bf16[256,2048]{1,0:T(8,128)(2,1)S(1)}, u32[]{:S(2)}, u32[]{:S(2)}) collective-permute-start(bf16[256,2048]{1,0:T(8,128)(2,1)S(1)} %copy-done.8), channel_id=1, source_target_pairs={{0,4},{4,0},{1,5},{5,1},{2,6},{6,2},{3,7},{7,3},{8,12},{12,8},{9,1... | collective-permute-start | bytes 3145736 | tf_op jit(solution)/shard_map/ppermute | solution.py:85
  212.7 95.7 %collective-permute-start.4 = (bf16[256,2048]{1,0:T(8,128)(2,1)S(1)}, bf16[256,2048]{1,0:T(8,128)(2,1)S(1)}, u32[]{:S(2)}, u32[]{:S(2)}) collective-permute-start(bf16[256,2048]{1,0:T(8,128)(2,1)S(1)} %copy-done.1), channel_id=1, source_target_pairs={{0,4},{4,0},{1,5},{5,1},{2,6},{6,2},{3,7},{7,3},{8,12},{12,8},{9,1... | collective-permute-start | bytes 3145736 | tf_op jit(solution)/shard_map/ppermute | solution.py:85
  289.7 54.8 %collective-permute-start.25 = (bf16[512,1024]{1,0:T(8,128)(2,1)S(1)}, bf16[512,1024]{1,0:T(8,128)(2,1)S(1)}, u32[]{:S(2)}, u32[]{:S(2)}) collective-permute-start(bf16[512,1024]{1,0:T(8,128)(2,1)S(1)} %bitcast.367), channel_id=1, source_target_pairs={{0,16},{8,0},{24,8},{16,24},{1,17},{9,1},{25,9},{17,25},{2,18},{10... | collective-permute-start | bytes 3145736 | tf_op jit(solution)/shard_map/ppermute | solution.py:50
  297.1 46.5 %collective-permute-start.24 = (bf16[512,1024]{1,0:T(8,128)(2,1)S(1)}, bf16[512,1024]{1,0:T(8,128)(2,1)S(1)}, u32[]{:S(2)}, u32[]{:S(2)}) collective-permute-start(bf16[512,1024]{1,0:T(8,128)(2,1)S(1)} %bitcast.368), channel_id=1, source_target_pairs={{0,8},{8,24},{24,16},{16,0},{1,9},{9,25},{25,17},{17,1},{2,10},{10... | collective-permute-start | bytes 3145736 | tf_op jit(solution)/shard_map/ppermute | solution.py:49
  529.3 53.0 %collective-permute-start.65 = (bf16[32,2048]{1,0:T(8,128)(2,1)}, bf16[32,2048]{1,0:T(8,128)(2,1)}, u32[]{:S(2)}, u32[]{:S(2)}) collective-permute-start(bf16[32,2048]{1,0:T(8,128)(2,1)} %get-tuple-element.73), channel_id=1, source_target_pairs={{0,16},{8,0},{24,8},{16,24},{1,17},{9,1},{25,9},{17,25},{2,18},{10... | collective-permute-start | bytes 393224 | tf_op jit(solution)/shard_map/ppermute | solution.py:63
  529.3 54.9 %collective-permute-start.67 = (bf16[32,2048]{1,0:T(8,128)(2,1)}, bf16[32,2048]{1,0:T(8,128)(2,1)}, u32[]{:S(2)}, u32[]{:S(2)}) collective-permute-start(bf16[32,2048]{1,0:T(8,128)(2,1)} %get-tuple-element.75), channel_id=1, source_target_pairs={{0,8},{8,24},{24,16},{16,0},{1,9},{9,25},{25,17},{17,1},{2,10},{10... | collective-permute-start | bytes 393224 | tf_op jit(solution)/shard_map/ppermute | solution.py:64
  543.4 42.1 %collective-permute-start.57 = (bf16[256,768]{1,0:T(8,128)(2,1)}, bf16[256,768]{1,0:T(8,128)(2,1)}, u32[]{:S(2)}, u32[]{:S(2)}) collective-permute-start(bf16[256,768]{1,0:T(8,128)(2,1)} %get-tuple-element.61), channel_id=1, source_target_pairs={{0,16},{8,0},{24,8},{16,24},{1,17},{9,1},{25,9},{17,25},{2,18},{10... | collective-permute-start | bytes 1179656 | tf_op jit(solution)/shard_map/ppermute | solution.py:63
  543.4 44.1 %collective-permute-start.59 = (bf16[256,768]{1,0:T(8,128)(2,1)}, bf16[256,768]{1,0:T(8,128)(2,1)}, u32[]{:S(2)}, u32[]{:S(2)}) collective-permute-start(bf16[256,768]{1,0:T(8,128)(2,1)} %get-tuple-element.63), channel_id=1, source_target_pairs={{0,8},{8,24},{24,16},{16,0},{1,9},{9,25},{25,17},{17,1},{2,10},{10... | collective-permute-start | bytes 1179656 | tf_op jit(solution)/shard_map/ppermute | solution.py:64
  548.3 41.8 %collective-permute-start.69 = (bf16[256,1024]{1,0:T(8,128)(2,1)}, bf16[256,1024]{1,0:T(8,128)(2,1)}, u32[]{:S(2)}, u32[]{:S(2)}) collective-permute-start(bf16[256,1024]{1,0:T(8,128)(2,1)} %get-tuple-element.47), channel_id=1, source_target_pairs={{0,16},{8,0},{24,8},{16,24},{1,17},{9,1},{25,9},{17,25},{2,18},{10... | collective-permute-start | bytes 1572872 | tf_op jit(solution)/shard_map/ppermute | solution.py:63
  608.4 44.9 %collective-permute-start.72 = (bf16[512,1024]{1,0:T(8,128)(2,1)S(1)}, bf16[512,1024]{1,0:T(8,128)(2,1)S(1)}, u32[]{:S(2)}, u32[]{:S(2)}) collective-permute-start(bf16[512,1024]{1,0:T(8,128)(2,1)S(1)} %pad_maximum_fusion.7), channel_id=1, source_target_pairs={{0,8},{8,24},{24,16},{16,0},{1,9},{9,25},{25,17},{17,1},{2,10},{10... | collective-permute-start | bytes 3145736 | tf_op jit(solution)/shard_map/ppermute | solution.py:69
  615.4 58.0 %collective-permute-start.80 = (bf16[256,2048]{1,0:T(8,128)(2,1)S(1)}, bf16[256,2048]{1,0:T(8,128)(2,1)S(1)}, u32[]{:S(2)}, u32[]{:S(2)}) collective-permute-start(bf16[256,2048]{1,0:T(8,128)(2,1)S(1)} %pad_maximum_fusion.9), channel_id=1, source_target_pairs={{0,8},{8,24},{24,16},{16,0},{1,9},{9,25},{25,17},{17,1},{2,10},{10... | collective-permute-start | bytes 3145736 | tf_op jit(solution)/shard_map/ppermute | solution.py:69
  630.9 42.5 %collective-permute-start.78 = (bf16[256,2048]{1,0:T(8,128)(2,1)S(1)}, bf16[256,2048]{1,0:T(8,128)(2,1)S(1)}, u32[]{:S(2)}, u32[]{:S(2)}) collective-permute-start(bf16[256,2048]{1,0:T(8,128)(2,1)S(1)} %pad_maximum_fusion.8), channel_id=1, source_target_pairs={{0,16},{8,0},{24,8},{16,24},{1,17},{9,1},{25,9},{17,25},{2,18},{10... | collective-permute-start | bytes 3145736 | tf_op jit(solution)/shard_map/ppermute | solution.py:68
  633.1 97.4 %collective-permute-start.45 = (bf16[1024,2048]{1,0:T(8,128)(2,1)}, bf16[1024,2048]{1,0:T(8,128)(2,1)}, u32[]{:S(2)}, u32[]{:S(2)}) collective-permute-start(bf16[1024,2048]{1,0:T(8,128)(2,1)} %slice.610), channel_id=1, source_target_pairs={{0,4},{4,0},{1,5},{5,1},{2,6},{6,2},{3,7},{7,3},{8,12},{12,8},{9,1... | collective-permute-start | bytes 12582920 | tf_op jit(solution)/shard_map/ppermute | solution.py:85
  653.4 89.2 %collective-permute-start.32 = (bf16[1024,2048]{1,0:T(8,128)(2,1)}, bf16[1024,2048]{1,0:T(8,128)(2,1)}, u32[]{:S(2)}, u32[]{:S(2)}) collective-permute-start(bf16[1024,2048]{1,0:T(8,128)(2,1)} %slice.597), channel_id=1, source_target_pairs={{0,4},{4,0},{1,5},{5,1},{2,6},{6,2},{3,7},{7,3},{8,12},{12,8},{9,1... | collective-permute-start | bytes 12582920 | tf_op jit(solution)/shard_map/ppermute | solution.py:85
  673.4 39.6 %collective-permute-start.73 = (bf16[4,64,1024]{2,1,0:T(8,128)(2,1)S(1)}, bf16[4,64,1024]{2,1,0:T(8,128)(2,1)S(1)}, u32[]{:S(2)}, u32[]{:S(2)}) collective-permute-start(bf16[4,64,1024]{2,1,0:T(8,128)(2,1)S(1)} %get-tuple-element.69), channel_id=1, source_target_pairs={{0,4},{4,0},{1,5},{5,1},{2,6},{6,2},{3,7},{7,3},{8,12},{12,8},{9,1... | collective-permute-start | bytes 1572872 | tf_op jit(solution)/shard_map/ppermute | solution.py:85
  713.8 169.9 %collective-permute-start.76 = (bf16[2,64,1024]{2,1,0:T(8,128)(2,1)S(1)}, bf16[2,64,1024]{2,1,0:T(8,128)(2,1)}, u32[]{:S(2)}, u32[]{:S(2)}) collective-permute-start(bf16[2,64,1024]{2,1,0:T(8,128)(2,1)S(1)} %get-tuple-element.65), channel_id=1, source_target_pairs={{0,3},{1,0},{2,1},{3,2},{4,7},{5,4},{6,5},{7,6},{8,11},{9,8},{10,9... | collective-permute-start | bytes 786440 | tf_op jit(solution)/shard_map/ppermute | solution.py:351
  716.2 94.2 %collective-permute-start.75 = (bf16[2,64,1024]{2,1,0:T(8,128)(2,1)}, bf16[2,64,1024]{2,1,0:T(8,128)(2,1)}, u32[]{:S(2)}, u32[]{:S(2)}) collective-permute-start(bf16[2,64,1024]{2,1,0:T(8,128)(2,1)} %get-tuple-element.68), channel_id=1, source_target_pairs={{0,2},{1,3},{2,0},{3,1},{4,6},{5,7},{6,4},{7,5},{8,10},{9,11},{10,... | collective-permute-start | bytes 786440 | tf_op jit(solution)/shard_map/ppermute | solution.py:351
  750.4 56.2 %collective-permute-start.33 = (bf16[128,2048]{1,0:T(8,128)(2,1)S(1)}, bf16[128,2048]{1,0:T(8,128)(2,1)S(1)}, u32[]{:S(2)}, u32[]{:S(2)}) collective-permute-start(bf16[128,2048]{1,0:T(8,128)(2,1)S(1)} %get-tuple-element.55), channel_id=1, source_target_pairs={{0,3},{1,0},{2,1},{3,2},{4,7},{5,4},{6,5},{7,6},{8,11},{9,8},{10,9... | collective-permute-start | bytes 1572872 | tf_op jit(solution)/shard_map/ppermute | solution.py:63
  764.6 42.0 %collective-permute-start.35 = (bf16[128,2048]{1,0:T(8,128)(2,1)S(1)}, bf16[128,2048]{1,0:T(8,128)(2,1)S(1)}, u32[]{:S(2)}, u32[]{:S(2)}) collective-permute-start(bf16[128,2048]{1,0:T(8,128)(2,1)S(1)} %get-tuple-element.56), channel_id=1, source_target_pairs={{0,1},{1,2},{2,3},{3,0},{4,5},{5,6},{6,7},{7,4},{8,9},{9,10},{10,1... | collective-permute-start | bytes 1572872 | tf_op jit(solution)/shard_map/ppermute | solution.py:64
  772.3 41.9 %collective-permute-start.49 = (bf16[256,2048]{1,0:T(8,128)(2,1)S(1)}, bf16[256,2048]{1,0:T(8,128)(2,1)S(1)}, u32[]{:S(2)}, u32[]{:S(2)}) collective-permute-start(bf16[256,2048]{1,0:T(8,128)(2,1)S(1)} %pad_maximum_fusion.5), channel_id=1, source_target_pairs={{0,1},{1,2},{2,3},{3,0},{4,5},{5,6},{6,7},{7,4},{8,9},{9,10},{10,1... | collective-permute-start | bytes 3145736 | tf_op jit(solution)/shard_map/ppermute | solution.py:69
  806.5 49.8 %collective-permute-start.47 = (bf16[256,2048]{1,0:T(8,128)(2,1)S(1)}, bf16[256,2048]{1,0:T(8,128)(2,1)S(1)}, u32[]{:S(2)}, u32[]{:S(2)}) collective-permute-start(bf16[256,2048]{1,0:T(8,128)(2,1)S(1)} %pad_maximum_fusion.4), channel_id=1, source_target_pairs={{0,3},{1,0},{2,1},{3,2},{4,7},{5,4},{6,5},{7,6},{8,11},{9,8},{10,9... | collective-permute-start | bytes 3145736 | tf_op jit(solution)/shard_map/ppermute | solution.py:68
  807.0 52.3 %collective-permute-start.36 = (bf16[256,2048]{1,0:T(8,128)(2,1)S(1)}, bf16[256,2048]{1,0:T(8,128)(2,1)S(1)}, u32[]{:S(2)}, u32[]{:S(2)}) collective-permute-start(bf16[256,2048]{1,0:T(8,128)(2,1)S(1)} %pad_maximum_fusion.2), channel_id=1, source_target_pairs={{0,1},{1,2},{2,3},{3,0},{4,5},{5,6},{6,7},{7,4},{8,9},{9,10},{10,1... | collective-permute-start | bytes 3145736 | tf_op jit(solution)/shard_map/ppermute | solution.py:69
  810.4 64.5 %collective-permute-start.34 = (bf16[256,2048]{1,0:T(8,128)(2,1)S(1)}, bf16[256,2048]{1,0:T(8,128)(2,1)S(1)}, u32[]{:S(2)}, u32[]{:S(2)}) collective-permute-start(bf16[256,2048]{1,0:T(8,128)(2,1)S(1)} %pad_maximum_fusion.1), channel_id=1, source_target_pairs={{0,3},{1,0},{2,1},{3,2},{4,7},{5,4},{6,5},{7,6},{8,11},{9,8},{10,9... | collective-permute-start | bytes 3145736 | tf_op jit(solution)/shard_map/ppermute | solution.py:68
  (111 other events, 2738.4 us)

commit v2 on v1

v2 whole, which is shorter than its diff:
```python
from functools import partial
import math

import jax
import jax.numpy as jnp
from jax import lax
from jax.experimental import pallas as pl
from jax.experimental.pallas import tpu as pltpu
from jax.sharding import Mesh, PartitionSpec as P

HEADS = 32
ROT = 32
EPS = 1e-05
NEG = -1e30
BLOCK_Q = 256

BF = jnp.bfloat16
F32 = jnp.float32


def dot(a, b):
    return jnp.dot(a, b, preferred_element_type=F32)


def dot_t(a, b):
    return lax.dot_general(a, b, (((1,), (1,)), ((), ())), preferred_element_type=F32)


def t_dot(a, b):
    return lax.dot_general(a, b, (((0,), (0,)), ((), ())), preferred_element_type=F32)


def ring_pairs(order, step):
    n = len(order)
    return [(order[i], order[(i + step) % n]) for i in range(n)]


def swap(value):
    return lax.ppermute(value, "core", [(0, 1), (1, 0)])


def turn(values, cosine, sine_a, sine_b):
    width = values.shape[1]
    return (
        values * cosine
        + pltpu.roll(values, width - ROT // 2, 1) * sine_a
        + pltpu.roll(values, ROT // 2, 1) * sine_b
    )


def head_mask(shape, head, head_dim):
    lane = lax.broadcasted_iota(jnp.int32, shape, 1)
    return (lane >= head * head_dim) & (lane < (head + 1) * head_dim)


def attend_kernel(heads, head_dim, span, order_ref, qkv_ref, cos_ref, sin_a_ref, sin_b_ref, att_ref, sorted_ref, out_scr):
    seq_len = qkv_ref.shape[1]
    width = heads * head_dim
    for slot in range(seq_len // span):
        rows = pl.ds(pl.multiple_of(order_ref[slot] * span, span), span)
        here = pl.ds(slot * span, span)
        tables = (cos_ref[here, :], sin_a_ref[here, :], sin_b_ref[here, :])
        query = turn(qkv_ref[0, rows, 0:width], *tables).astype(BF)
        sorted_ref[0, here, 0:width] = (query.astype(F32) * (head_dim**-0.5)).astype(BF)
        sorted_ref[0, here, width : 2 * width] = turn(qkv_ref[0, rows, width : 2 * width], *tables).astype(BF)
        sorted_ref[0, here, 2 * width :] = qkv_ref[0, rows, 2 * width :].astype(BF)
    block = min(BLOCK_Q, seq_len)
    for i in range(seq_len // block):
        extent = (i + 1) * block
        here = pl.ds(i * block, block)
        queries = sorted_ref[0, here, 0:width]
        keys = sorted_ref[0, 0:extent, width : 2 * width]
        values = sorted_ref[0, 0:extent, 2 * width :]
        row = lax.broadcasted_iota(jnp.int32, (block, extent), 0) + i * block
        col = lax.broadcasted_iota(jnp.int32, (block, extent), 1)
        total = jnp.zeros((block, width), F32)
        for head in range(heads):
            mask = head_mask((block, width), head, head_dim)
            scores = dot_t(jnp.where(mask, queries, jnp.zeros_like(queries)), keys)
            scores = jnp.where(col <= row, scores, NEG)
            top = jnp.max(scores, 1, keepdims=True)
            weights = jnp.exp(scores - top)
            norm = 1.0 / jnp.sum(weights, 1, keepdims=True)
            probs = (weights * norm).astype(BF)
            total = jnp.where(mask, dot(probs, values), total)
        out_scr[here, :] = total.astype(BF)
    for slot in range(seq_len // span):
        rows = pl.ds(pl.multiple_of(order_ref[slot] * span, span), span)
        att_ref[0, rows, :] = out_scr[slot * span : (slot + 1) * span, :]


def attend_back_kernel(
    heads, head_dim, span, order_ref, sorted_ref, grad_ref, cos_ref, sin_a_ref, sin_b_ref, out_ref, grad_scr, key_scr, value_scr
):
    seq_len = sorted_ref.shape[1]
    width = heads * head_dim
    for slot in range(seq_len // span):
        rows = pl.ds(pl.multiple_of(order_ref[slot] * span, span), span)
        grad_scr[slot * span : (slot + 1) * span, :] = grad_ref[0, rows, :]
    key_scr[...] = jnp.zeros_like(key_scr)
    value_scr[...] = jnp.zeros_like(value_scr)
    block = min(BLOCK_Q, seq_len)

    def put(slot, first, values):
        rows = pl.ds(pl.multiple_of(order_ref[slot] * span, span), span)
        out_ref[0, rows, first : first + width] = values.astype(BF)

    def tables(here):
        return (cos_ref[here, :], -sin_a_ref[here, :], -sin_b_ref[here, :])

    for i in range(seq_len // block):
        extent = (i + 1) * block
        here = pl.ds(i * block, block)
        queries = sorted_ref[0, here, 0:width]
        grads = grad_scr[here, :]
        keys = sorted_ref[0, 0:extent, width : 2 * width]
        values = sorted_ref[0, 0:extent, 2 * width :]
        key = lax.broadcasted_iota(jnp.int32, (extent, block), 0)
        query = lax.broadcasted_iota(jnp.int32, (extent, block), 1) + i * block
        query_grad = jnp.zeros((block, width), F32)
        for head in range(heads):
            mask = head_mask((block, width), head, head_dim)
            own_queries = jnp.where(mask, queries, jnp.zeros_like(queries))
            own_grads = jnp.where(mask, grads, jnp.zeros_like(grads))
            scores = jnp.where(key <= query, dot_t(keys, own_queries), NEG)
            weights = jnp.exp(scores - jnp.max(scores, 0, keepdims=True))
            probs = weights * (1.0 / jnp.sum(weights, 0, keepdims=True))
            probs_grad = dot_t(values, own_grads)
            delta = jnp.sum(probs * probs_grad, 0, keepdims=True)
            score_grad = (probs * (probs_grad - delta)).astype(BF)
            value_scr[0:extent, :] += dot(probs.astype(BF), own_grads)
            key_scr[0:extent, :] += dot(score_grad, own_queries)
            query_grad = jnp.where(mask, t_dot(score_grad, keys), query_grad)
        query_grad = turn(query_grad * (head_dim**-0.5), *tables(here))
        for j in range(block // span):
            put(i * (block // span) + j, 0, query_grad[j * span : (j + 1) * span])
    for slot in range(seq_len // span):
        here = pl.ds(slot * span, span)
        put(slot, width, turn(key_scr[here, :], *tables(here)))
        put(slot, 2 * width, value_scr[here, :])


def attend(order, qkv, tables, heads, head_dim, span):
    count, seq_len, wide = qkv.shape
    width = wide // 3
    whole = pl.BlockSpec((seq_len, width), lambda s, o: (0, 0))
    return pl.pallas_call(
        partial(attend_kernel, heads, head_dim, span),
        grid_spec=pltpu.PrefetchScalarGridSpec(
            num_scalar_prefetch=1,
            grid=(count,),
            in_specs=[pl.BlockSpec((1, seq_len, wide), lambda s, o: (s, 0, 0)), whole, whole, whole],
            out_specs=[
                pl.BlockSpec((1, seq_len, width), lambda s, o: (s, 0, 0)),
                pl.BlockSpec((1, seq_len, wide), lambda s, o: (s, 0, 0)),
            ],
            scratch_shapes=[pltpu.VMEM((seq_len, width), BF)],
        ),
        out_shape=[
            jax.ShapeDtypeStruct((count, seq_len, width), BF),
            jax.ShapeDtypeStruct((count, seq_len, wide), BF),
        ],
        compiler_params=pltpu.CompilerParams(vmem_limit_bytes=40 * 2**20),
        cost_estimate=pl.CostEstimate(
            flops=8 * count * heads * seq_len * seq_len * head_dim,
            bytes_accessed=count * seq_len * wide * 8,
            transcendentals=count * heads * seq_len * seq_len,
        ),
        name="attend",
    )(order, qkv, *tables)


def attend_back(order, kept, grads, tables, heads, head_dim, span):
    count, seq_len, wide = kept.shape
    width = wide // 3
    whole = pl.BlockSpec((seq_len, width), lambda s, o: (0, 0))
    return pl.pallas_call(
        partial(attend_back_kernel, heads, head_dim, span),
        grid_spec=pltpu.PrefetchScalarGridSpec(
            num_scalar_prefetch=1,
            grid=(count,),
            in_specs=[
                pl.BlockSpec((1, seq_len, wide), lambda s, o: (s, 0, 0)),
                pl.BlockSpec((1, seq_len, width), lambda s, o: (s, 0, 0)),
                whole,
                whole,
                whole,
            ],
            out_specs=pl.BlockSpec((1, seq_len, wide), lambda s, o: (s, 0, 0)),
            scratch_shapes=[
                pltpu.VMEM((seq_len, width), BF),
                pltpu.VMEM((seq_len, width), F32),
                pltpu.VMEM((seq_len, width), F32),
            ],
        ),
        out_shape=jax.ShapeDtypeStruct((count, seq_len, wide), BF),
        compiler_params=pltpu.CompilerParams(vmem_limit_bytes=40 * 2**20),
        cost_estimate=pl.CostEstimate(
            flops=20 * count * heads * seq_len * seq_len * head_dim,
            bytes_accessed=count * seq_len * wide * 6,
            transcendentals=count * heads * seq_len * seq_len,
        ),
        name="attend_back",
    )(order, kept, grads, *tables)


def after(value, *others):
    return lax.optimization_barrier((value,) + others)[0]


def whole_block(shape):
    return pl.BlockSpec(shape, lambda *_: (0,) * len(shape))


def params(limit):
    return pltpu.CompilerParams(vmem_limit_bytes=limit * 2**20)


def cost(flops, nbytes):
    return pl.CostEstimate(flops=flops, bytes_accessed=nbytes, transcendentals=0)


ANYWHERE = pl.BlockSpec(memory_space=pl.ANY)
SCALARS = pl.BlockSpec(memory_space=pltpu.SMEM)
VMEM = pl.BlockSpec(memory_space=pltpu.VMEM)
ROWS = 256


def gathered(own, axis, order):
    n = len(order)
    up_pairs, down_pairs = ring_pairs(order, 1), ring_pairs(order, -1)
    out = [(0, 0, own)]
    up = down = own
    half = own.shape[0] // 2
    for step in range(1, n // 2 + 1):
        if 2 * step == n:
            out.append((step, 0, lax.ppermute(up[:half], axis, up_pairs)))
            out.append((step, half, lax.ppermute(down[half:], axis, down_pairs)))
        else:
            up, down = lax.ppermute(up, axis, up_pairs), lax.ppermute(down, axis, down_pairs)
            out += [(-step, 0, up), (step, 0, down)]
    return out


def to_blocks_kernel(n_q, n_t, heads, head_dim, units, at_ref, qkv_ref, up_ref, *out_refs):
    n_z = n_t // 2
    width = heads * head_dim
    core, z = at_ref[0], at_ref[1]
    rows = qkv_ref.shape[0]
    low = lax.broadcasted_iota(jnp.int32, (rows, 128), 1) < head_dim
    per = 128 // head_dim
    for c in range(2):
        for s in range(n_z):
            out_ref = out_refs[c * n_z + s]
            t = lax.rem(core + c, 2) * n_z + lax.rem(z + s, n_z)
            odd = lax.rem(t, per)
            for which in range(3):
                for j in range(0, heads, per):
                    tiles = []
                    for i in range(per):
                        first = (which * heads + j + i) * n_t * head_dim + (t // per) * 128
                        tile = qkv_ref[:, pl.ds(pl.multiple_of(first, 128), 128)].astype(F32)
                        tiles.append(tile)
                    even = jnp.where(low, tiles[0], pltpu.roll(tiles[1], head_dim, 1))
                    uneven = jnp.where(low, pltpu.roll(tiles[0], head_dim, 1), tiles[1])
                    at = which * width + j * head_dim
                    out_ref[:, at : at + 128] = jnp.where(odd == 0, even, uneven).astype(BF)
            for q in range(n_q):
                at = 3 * width + q * units
                if units % 128 == 0:
                    first = pl.multiple_of((q * n_t + t) * units, 128)
                    out_ref[:, at : at + units] = up_ref[:, pl.ds(first, units)]
                else:
                    for k in range(n_t):

                        @pl.when(t == k)
                        def _(at=at, q=q, k=k):
                            first = (q * n_t + k) * units
                            out_ref[:, at : at + units] = up_ref[:, first : first + units]


def to_blocks(at, qkv, up, n_q, n_t, heads, head_dim, units):
    rows = qkv.shape[0]
    wide = 3 * heads * head_dim + n_q * units
    return pl.pallas_call(
        partial(to_blocks_kernel, n_q, n_t, heads, head_dim, units),
        in_specs=[SCALARS, VMEM, VMEM],
        out_specs=[VMEM] * n_t,
        out_shape=[jax.ShapeDtypeStruct((rows, wide), BF)] * n_t,
        compiler_params=params(16),
        cost_estimate=cost(0, 4 * rows * wide * n_t),
        name="to_blocks",
    )(at, qkv, up)


def stack_rows_kernel(n_z, at_ref, *refs):
    pieces, out_ref = refs[:-1], refs[-1]
    rows = pieces[0].shape[0]
    core, z = at_ref[0], at_ref[1]
    for c in range(2):
        for s in range(n_z):
            block = lax.rem(core + c, 2) * n_z + lax.rem(z - s + n_z, n_z)
            out_ref[pl.ds(pl.multiple_of(block * rows, 16), rows), :] = pieces[c * n_z + s][...]


def stack_rows(at, pieces):
    rows, columns = pieces[0].shape
    n_t = len(pieces)
    return pl.pallas_call(
        partial(stack_rows_kernel, n_t // 2),
        in_specs=[SCALARS] + [VMEM] * n_t,
        out_specs=VMEM,
        out_shape=jax.ShapeDtypeStruct((n_t * rows, columns), BF),
        compiler_params=params(16),
        cost_estimate=cost(0, 4 * n_t * rows * columns),
        name="stack_rows",
    )(at, *pieces)


def last_sum_kernel(n_z, at_ref, part_ref, low_ref, high_ref, *out_refs):
    rows = out_refs[0].shape[0]
    core, z = at_ref[0], at_ref[1]
    for c in range(2):
        for s in range(n_z):
            block = lax.rem(core + c, 2) * n_z + lax.rem(z + s, n_z)
            here = pl.ds(pl.multiple_of(block * rows, 16), rows)
            total = part_ref[here, :].astype(F32) + low_ref[here, :].astype(F32) + high_ref[here, :].astype(F32)
            out_refs[c * n_z + s][...] = total.astype(BF)


def last_sum(at, parts, low, high, n_t):
    count, columns = low.shape
    rows = count // n_t
    return pl.pallas_call(
        partial(last_sum_kernel, n_t // 2),
        grid=(1,),
        in_specs=[SCALARS] + [pl.BlockSpec((count, columns), lambda i: (0, 0))] * 3,
        out_specs=[pl.BlockSpec((rows, columns), lambda i: (0, 0))] * n_t,
        out_shape=[jax.ShapeDtypeStruct((rows, columns), BF)] * n_t,
        compiler_params=params(24),
        cost_estimate=cost(0, 8 * count * columns),
        name="last_sum",
    )(at, parts, low, high)


def from_blocks_kernel(groups, piece, n_t, at_ref, *refs):
    n_z = n_t // 2
    pieces, out_ref, held_ref = refs[:n_t], refs[n_t], refs[n_t + 1]
    core, z = at_ref[0], at_ref[1]
    for c in range(2):
        for s in range(n_z):
            block = lax.rem(core + c, 2) * n_z + lax.rem(z - s + n_z, n_z)
            held_ref[block] = pieces[c * n_z + s][...]
    for t in range(n_t):
        for j in range(groups):
            first = (j * n_t + t) * piece
            out_ref[:, first : first + piece] = held_ref[t, :, j * piece : (j + 1) * piece].astype(F32)


def from_blocks(at, pieces, groups, piece):
    n_t = len(pieces)
    rows = pieces[0].shape[0]
    return pl.pallas_call(
        partial(from_blocks_kernel, groups, piece, n_t),
        in_specs=[SCALARS] + [VMEM] * n_t,
        out_specs=VMEM,
        out_shape=jax.ShapeDtypeStruct((rows, groups * n_t * piece), F32),
        scratch_shapes=[pltpu.VMEM((n_t, rows, groups * piece), BF)],
        compiler_params=params(16),
        cost_estimate=cost(0, 8 * rows * groups * n_t * piece),
        name="from_blocks",
    )(at, *pieces)


def pass_on_kernel(half, low_part_ref, high_part_ref, low_ref, high_ref, to_low_ref, to_high_ref):
    rows = low_part_ref.shape[0]
    if half:
        cut = rows // 2
        to_low_ref[0:cut, :] = (low_part_ref[0:cut, :].astype(F32) + low_ref[...].astype(F32)).astype(BF)
        to_low_ref[cut:, :] = low_part_ref[cut:, :]
        to_high_ref[0:cut, :] = high_part_ref[0:cut, :]
        to_high_ref[cut:, :] = (high_part_ref[cut:, :].astype(F32) + high_ref[...].astype(F32)).astype(BF)
    else:
        to_low_ref[...] = (low_part_ref[...].astype(F32) + low_ref[...].astype(F32)).astype(BF)
        to_high_ref[...] = (high_part_ref[...].astype(F32) + high_ref[...].astype(F32)).astype(BF)


def pass_on(parts, low_slot, high_slot, low, high, rows):
    columns = parts.shape[1]
    half = low.shape[0] < rows
    wide = math.gcd(columns, 512)
    arrived = pl.BlockSpec((low.shape[0], wide), lambda i: (0, i))
    out = pl.BlockSpec((rows, wide), lambda i: (0, i))
    return pl.pallas_call(
        partial(pass_on_kernel, half),
        grid=(columns // wide,),
        in_specs=[
            pl.BlockSpec((rows, wide), lambda i: (low_slot, i)),
            pl.BlockSpec((rows, wide), lambda i: (high_slot, i)),
            arrived,
            arrived,
        ],
        out_specs=[out, out],
        out_shape=[jax.ShapeDtypeStruct((rows, columns), BF)] * 2,
        cost_estimate=pl.CostEstimate(flops=2 * rows * columns, bytes_accessed=12 * rows * columns, transcendentals=0),
        name="pass_on",
    )(parts, parts, low, high)


def ring_offsets(n):
    return [0] + [o for s in range(1, n // 2 + 1) for o in ((s,) if 2 * s == n else (-s, s))]


def ring_sum(parts, rows, axis, order):
    n = len(order)
    slots = {o: i for i, o in enumerate(ring_offsets(n))}
    down, up = ring_pairs(order, -1), ring_pairs(order, 1)
    low = high = None
    for step in range(n // 2, 0, -1):
        if 2 * step == n:
            first = slots[step] * rows
            to_low, to_high = parts[first : first + rows // 2], parts[first + rows // 2 : first + rows]
        else:
            to_low, to_high = pass_on(parts, slots[-step], slots[step], low, high, rows)
        low, high = lax.ppermute(to_low, axis, down), lax.ppermute(to_high, axis, up)
    return low, high, (to_low, to_high)


def load_pieces(plan, starts_ref, piece_refs, target, sem):
    copies = []
    for i, (piece, first, rows) in enumerate(plan):
        start = pl.multiple_of(starts_ref[i], 16)
        copies.append(pltpu.make_async_copy(piece_refs[piece].at[pl.ds(first, rows)], target.at[pl.ds(start, rows)], sem.at[i]))
    return copies


def slot_copies(plan, slot, piece_refs, target, sem):
    return [
        pltpu.make_async_copy(piece_refs[piece], target.at[pl.ds(first, rows)], sem)
        for piece, first, rows in plan[slot]
    ]


def fetch_slots(plan, piece_refs, buffers, sems):
    i = pl.program_id(0)
    for slot in range(len(plan)):

        @pl.when(i == slot)
        def _(slot=slot):
            if slot == 0:
                for copy in slot_copies(plan, 0, piece_refs, buffers.at[0], sems.at[0]):
                    copy.start()
            if slot + 1 < len(plan):
                for copy in slot_copies(plan, slot + 1, piece_refs, buffers.at[(slot + 1) % 2], sems.at[(slot + 1) % 2]):
                    copy.start()
            pltpu.make_async_copy(buffers.at[slot % 2], buffers.at[slot % 2], sems.at[slot % 2]).wait()


class Gathered:
    def __init__(self, arrays, plan, starts):
        self.arrays = arrays
        self.plan = tuple(plan)
        self.starts = jnp.stack([jnp.asarray(s, jnp.int32) for s in starts])
        self.rows = sum(rows for *_, rows in plan)
        self.columns = arrays[0].shape[1]

    def scratch(self):
        return [pltpu.VMEM((self.rows, self.columns), BF), pltpu.SemaphoreType.DMA((len(self.plan),))]

    def specs(self):
        return [ANYWHERE] * len(self.arrays)


def normed(rows):
    mean = jnp.mean(rows, -1, keepdims=True)
    centred = rows - mean
    scale = lax.rsqrt(jnp.mean(centred * centred, -1, keepdims=True) + EPS)
    return centred * scale, scale


def project_kernel(split, x_plan, n_x, w_plan, n_w, starts_ref, *refs):
    x_refs, refs = refs[:n_x], refs[n_x:]
    w_refs, refs = refs[:n_w], refs[n_w:]
    gain_ref, shift_ref, b_ref, x_out_ref, hidden_ref, qkv_ref, act_ref, slope_ref, w_ref, w_sem, x_buf, x_sem = refs

    @pl.when(pl.program_id(0) == 0)
    def _():
        for copy in load_pieces(w_plan, starts_ref, w_refs, w_ref, w_sem):
            copy.start()

    fetch_slots(x_plan, x_refs, x_buf, x_sem)
    x = x_buf[lax.rem(pl.program_id(0), 2)]
    x_out_ref[...] = x
    xhat, _ = normed(x.astype(F32))
    hidden = (xhat * gain_ref[...] + shift_ref[...]).astype(BF)
    hidden_ref[...] = hidden

    @pl.when(pl.program_id(0) == 0)
    def _():
        for copy in load_pieces(w_plan, starts_ref, w_refs, w_ref, w_sem):
            copy.wait()

    pre = dot(hidden, w_ref[:, split:]) + b_ref[:, split:]
    root = math.sqrt(2.0 / math.pi)
    square = pre * pre
    turned = jnp.tanh(root * pre * (1.0 + 0.044715 * square))
    act_ref[...] = (0.5 * pre * (1.0 + turned)).astype(BF)
    slope = 0.5 * (1.0 + turned) + 0.5 * pre * (1.0 - turned * turned) * (root * (1.0 + 3 * 0.044715 * square))
    slope_ref[...] = slope.astype(BF)
    qkv_ref[...] = dot(hidden, w_ref[:, :split]) + b_ref[:, :split]


def project(x_arrays, x_plan, gain, shift, w, b, split, rows):
    count, width = rows * len(x_plan), x_arrays[0].shape[1]
    wide = w.columns

    def block(columns):
        return pl.BlockSpec((rows, columns), lambda i, s: (i, 0))

    return pl.pallas_call(
        partial(project_kernel, split, x_plan, len(x_arrays), w.plan, len(w.arrays)),
        grid_spec=pltpu.PrefetchScalarGridSpec(
            num_scalar_prefetch=1,
            grid=(len(x_plan),),
            in_specs=[ANYWHERE] * len(x_arrays) + w.specs() + [whole_block((1, width))] * 2 + [whole_block(b.shape)],
            out_specs=[block(width), block(width), block(split), block(wide - split), block(wide - split)],
            scratch_shapes=w.scratch() + [pltpu.VMEM((2, rows, width), BF), pltpu.SemaphoreType.DMA((2,))],
        ),
        out_shape=[
            jax.ShapeDtypeStruct((count, width), BF),
            jax.ShapeDtypeStruct((count, width), BF),
            jax.ShapeDtypeStruct((count, split), F32),
            jax.ShapeDtypeStruct((count, wide - split), BF),
            jax.ShapeDtypeStruct((count, wide - split), BF),
        ],
        compiler_params=params(36),
        cost_estimate=cost(2 * count * width * wide, 8 * count * width + 2 * width * wide),
        name="project",
    )(w.starts, *x_arrays, *w.arrays, gain, shift, b)


def combine_kernel(split, w_plan, n_w, starts_ref, act_ref, att_ref, *refs):
    w_refs, refs = refs[:n_w], refs[n_w:]
    w_ref, w_sem = refs[-2:]

    @pl.when(pl.program_id(0) == 0)
    def _():
        copies = load_pieces(w_plan, starts_ref, w_refs, w_ref, w_sem)
        for copy in copies:
            copy.start()
        for copy in copies:
            copy.wait()

    total = dot(act_ref[...], w_ref[:split, :]) + dot(att_ref[...], w_ref[split:, :])
    if len(refs) == 4:
        total = total + refs[0][...].astype(F32)
    refs[-3][...] = total.astype(BF)


def combine(act, att, w, part, arrived=None):
    count, split = act.shape[0] // 2, act.shape[1]
    width = w.columns
    rows = math.gcd(count, ROWS)
    base = part * (count // rows)

    def block(columns):
        return pl.BlockSpec((rows, columns), lambda i, s: (i + base, 0))

    out = pl.BlockSpec((rows, width), lambda i, s: (i, 0))
    extra = [] if arrived is None else [arrived]
    return pl.pallas_call(
        partial(combine_kernel, split, w.plan, len(w.arrays)),
        grid_spec=pltpu.PrefetchScalarGridSpec(
            num_scalar_prefetch=1,
            grid=(count // rows,),
            in_specs=[block(split), block(att.shape[1])] + w.specs() + [out] * len(extra),
            out_specs=out,
            scratch_shapes=w.scratch(),
        ),
        out_shape=jax.ShapeDtypeStruct((count, width), BF),
        compiler_params=params(32),
        cost_estimate=cost(2 * count * width * w.rows, 4 * count * width + 2 * width * w.rows),
        name="combine",
    )(w.starts, act, att, *w.arrays, *extra)


def combine_back_kernel(split, g_plan, n_g, w_plan, n_w, starts_ref, *refs):
    g_refs, refs = refs[:n_g], refs[n_g:]
    w_refs, refs = refs[:n_w], refs[n_w:]
    slope_ref, g_out_ref, pre_grad_ref, att_grad_ref, w_ref, w_sem, g_buf, g_sem = refs

    @pl.when(pl.program_id(0) == 0)
    def _():
        for copy in load_pieces(w_plan, starts_ref, w_refs, w_ref, w_sem):
            copy.start()

    fetch_slots(g_plan, g_refs, g_buf, g_sem)

    @pl.when(pl.program_id(0) == 0)
    def _():
        for copy in load_pieces(w_plan, starts_ref, w_refs, w_ref, w_sem):
            copy.wait()

    grad = g_buf[lax.rem(pl.program_id(0), 2)]
    g_out_ref[...] = grad
    pre_grad_ref[...] = (dot_t(grad, w_ref[:split, :]) * slope_ref[...].astype(F32)).astype(BF)
    att_grad_ref[...] = dot_t(grad, w_ref[split:, :]).astype(BF)


def combine_back(g_arrays, g_plan, w, slope, rows):
    count, width = rows * len(g_plan), g_arrays[0].shape[1]
    split = slope.shape[1]
    rest = w.rows - split

    def block(columns):
        return pl.BlockSpec((rows, columns), lambda i, s: (i, 0))

    return pl.pallas_call(
        partial(combine_back_kernel, split, g_plan, len(g_arrays), w.plan, len(w.arrays)),
        grid_spec=pltpu.PrefetchScalarGridSpec(
            num_scalar_prefetch=1,
            grid=(len(g_plan),),
            in_specs=[ANYWHERE] * len(g_arrays) + w.specs() + [block(split)],
            out_specs=[block(width), block(split), block(rest)],
            scratch_shapes=w.scratch() + [pltpu.VMEM((2, rows, width), BF), pltpu.SemaphoreType.DMA((2,))],
        ),
        out_shape=[
            jax.ShapeDtypeStruct((count, width), BF),
            jax.ShapeDtypeStruct((count, split), BF),
            jax.ShapeDtypeStruct((count, rest), BF),
        ],
        compiler_params=params(32),
        cost_estimate=cost(2 * count * width * w.rows, 6 * count * width + 2 * width * w.rows),
        name="combine_back",
    )(w.starts, *g_arrays, *w.arrays, slope)


def project_back_kernel(split, w_plan, n_w, starts_ref, qkv_grad_ref, pre_grad_ref, x_ref, *refs):
    w_refs, refs = refs[:n_w], refs[n_w:]
    out_ref, sums_ref, w_ref, w_sem = refs[-4:]

    @pl.when(pl.program_id(0) == 0)
    def _():
        copies = load_pieces(w_plan, starts_ref, w_refs, w_ref, w_sem)
        for copy in copies:
            copy.start()
        sums_ref[...] = jnp.zeros_like(sums_ref)
        for copy in copies:
            copy.wait()

    grad = dot_t(qkv_grad_ref[...], w_ref[:, :split]) + dot_t(pre_grad_ref[...], w_ref[:, split:])
    xhat, _ = normed(x_ref[...].astype(F32))
    sums_ref[0:1, :] += jnp.sum(grad * xhat, 0, keepdims=True)
    sums_ref[1:2, :] += jnp.sum(grad, 0, keepdims=True)
    if len(refs) == 5:
        grad = grad + refs[0][...].astype(F32)
    out_ref[...] = grad.astype(BF)


def project_back(qkv_grad, pre_grad, w, x, part, arrived=None):
    count, width = x.shape[0] // 2, x.shape[1]
    split = qkv_grad.shape[1]
    rows = math.gcd(count, ROWS)
    base = part * (count // rows)

    def block(columns):
        return pl.BlockSpec((rows, columns), lambda i, s: (i + base, 0))

    out = pl.BlockSpec((rows, width), lambda i, s: (i, 0))
    extra = [] if arrived is None else [arrived]
    return pl.pallas_call(
        partial(project_back_kernel, split, w.plan, len(w.arrays)),
        grid_spec=pltpu.PrefetchScalarGridSpec(
            num_scalar_prefetch=1,
            grid=(count // rows,),
            in_specs=[block(split), block(pre_grad.shape[1]), block(width)] + w.specs() + [out] * len(extra),
            out_specs=[out, whole_block((8, width))],
            scratch_shapes=w.scratch(),
        ),
        out_shape=[jax.ShapeDtypeStruct((count, width), BF), jax.ShapeDtypeStruct((8, width), F32)],
        compiler_params=params(36),
        cost_estimate=cost(2 * count * width * w.columns, 6 * count * width + 2 * width * w.columns),
        name="project_back",
    )(w.starts, qkv_grad, pre_grad, x, *w.arrays, *extra)


def weight_grad_kernel(turns_ref, left_ref, right_ref, out_ref, sums_ref):
    out_ref[...] = t_dot(left_ref[...], right_ref[...]).astype(BF)

    @pl.when(pl.program_id(0) == 0)
    def _():
        sums_ref[...] = jnp.zeros_like(sums_ref)
        sums_ref[0:1, :] = jnp.sum(right_ref[...].astype(F32), 0, keepdims=True)


def weight_grad(turns, left, right):
    n_q = turns.shape[0]
    count, wide = left.shape
    columns = right.shape[1]
    part = wide // n_q
    return pl.pallas_call(
        weight_grad_kernel,
        grid_spec=pltpu.PrefetchScalarGridSpec(
            num_scalar_prefetch=1,
            grid=(n_q,),
            in_specs=[pl.BlockSpec((count, part), lambda k, s: (0, s[k])), whole_block(right.shape)],
            out_specs=[pl.BlockSpec((part, columns), lambda k, s: (k, 0)), whole_block((8, columns))],
        ),
        out_shape=[jax.ShapeDtypeStruct((wide, columns), BF), jax.ShapeDtypeStruct((8, columns), F32)],
        compiler_params=params(40),
        cost_estimate=cost(2 * count * wide * columns, 2 * count * (wide + columns) + 2 * wide * columns),
        name="weight_grad",
    )(turns, left, right)


def down_grad_kernel(head_rows, turns_ref, act_ref, att_ref, g_ref, out_ref, held_ref):
    units = act_ref.shape[1]
    k = pl.program_id(0)

    @pl.when(k == 0)
    def _():
        held_ref[...] = t_dot(att_ref[...], g_ref[...]).astype(BF)

    out_ref[0:units, :] = t_dot(act_ref[...], g_ref[...]).astype(BF)
    rows = pl.ds(pl.multiple_of(turns_ref[k] * head_rows, head_rows), head_rows)
    out_ref[units:, :] = held_ref[rows, :]


def down_grad(turns, act, att, g, head_rows):
    n_q = turns.shape[0]
    count, wide = act.shape
    own_width = att.shape[1]
    width = g.shape[1]
    units = wide // n_q
    if not head_rows:
        whole = t_dot(act, g).astype(BF).reshape(n_q, units, width)[turns]
        return whole.reshape(wide, width), t_dot(att, g)
    return pl.pallas_call(
        partial(down_grad_kernel, head_rows),
        grid_spec=pltpu.PrefetchScalarGridSpec(
            num_scalar_prefetch=1,
            grid=(n_q,),
            in_specs=[pl.BlockSpec((count, units), lambda k, s: (0, s[k])), whole_block(att.shape), whole_block(g.shape)],
            out_specs=pl.BlockSpec((units + head_rows, width), lambda k, s: (k, 0)),
            scratch_shapes=[pltpu.VMEM((own_width, width), BF)],
        ),
        out_shape=jax.ShapeDtypeStruct((n_q * (units + head_rows), width), BF),
        compiler_params=params(40),
        cost_estimate=cost(2 * count * (wide + own_width) * width, 2 * count * (wide + width) + 2 * wide * width),
        name="down_grad",
    )(turns, act, att, g), None


def finish_kernel(part_ref, low_ref, high_ref, x_ref, g_ref, gain_ref, out_ref):
    grad = part_ref[...].astype(F32) + low_ref[...].astype(F32) + high_ref[...].astype(F32)
    xhat, scale = normed(x_ref[...].astype(F32))
    m = grad * gain_ref[...]
    x_grad = (m - jnp.mean(m, -1, keepdims=True) - xhat * jnp.mean(m * xhat, -1, keepdims=True)) * scale
    out_ref[...] = (g_ref[...].astype(F32) + x_grad).astype(BF)


def finish(parts, low, high, x, g, gain):
    count, width = x.shape
    rows = math.gcd(count, 64)
    block = pl.BlockSpec((rows, width), lambda i: (i, 0))
    return pl.pallas_call(
        finish_kernel,
        grid=(count // rows,),
        in_specs=[block] * 5 + [whole_block((1, width))],
        out_specs=block,
        out_shape=jax.ShapeDtypeStruct((count, width), BF),
        cost_estimate=cost(20 * count * width, 12 * count * width),
        name="finish",
    )(parts, low, high, x, g, gain)


def per_device(
    inputs,
    span_table,
    ln_gain,
    ln_bias,
    qkv_weight,
    qkv_bias,
    out_weight,
    out_bias,
    fc1_weight,
    fc1_bias,
    fc2_weight,
    fc2_bias,
    cotangent,
):
    rows, width = inputs.shape
    head_dim = width // HEADS
    n_q, n_z = lax.axis_size("q"), lax.axis_size("ctx")
    n_t = 2 * n_z
    n_all = n_q * n_t
    q, core, z = lax.axis_index("q"), lax.axis_index("core"), lax.axis_index("ctx")
    t = core * n_z + z
    at = jnp.stack([core, z]).astype(jnp.int32)
    span = rows // 2
    seq_len = rows * n_z
    heads = HEADS // n_t
    own_width = heads * head_dim
    split = 3 * own_width
    units = fc2_weight.shape[0]
    own_units = units * n_q
    d_rows = qkv_weight.shape[0]
    every = ("q", "core", "ctx")
    z_order = list(range(n_z))
    q_order = [0, 1, 3, 2] if n_q == 4 else list(range(n_q))
    places = jnp.array([q_order.index(i) for i in range(n_q)], jnp.int32)
    q_ring = jnp.array(q_order, jnp.int32)
    q_offsets, z_offsets = ring_offsets(n_q), ring_offsets(n_z)
    turns = jnp.stack([q_ring[(places[q] + o) % n_q] for o in q_offsets])
    q_at = dict(zip(q_offsets, turns))
    whole_heads = out_weight.shape[0] == head_dim

    small = jnp.concatenate([ln_gain, ln_bias, out_bias, fc2_bias, qkv_bias, fc1_bias])
    small = jnp.pad(small, (0, 256 * 128 - small.shape[0])).reshape(256, 128)
    small = lax.all_gather(small, every, axis=0, tiled=True).reshape(n_all, 256 * 128)
    cuts = [ln_gain.shape[0], ln_bias.shape[0], out_bias.shape[0], fc2_bias.shape[0], qkv_bias.shape[0], fc1_bias.shape[0]]
    starts = [sum(cuts[:i]) for i in range(len(cuts))]
    gain, shift, b_out, b_down, b_qkv, b_up = (small[:, s : s + c].astype(F32) for s, c in zip(starts, cuts))
    gain, shift, b_out, b_down = (v.reshape(1, width) for v in (gain, shift, b_out, b_down))
    b_qkv = lax.dynamic_index_in_dim(b_qkv.reshape(3, heads, n_t, head_dim), t, 2, False).reshape(1, split)
    b_up = lax.dynamic_index_in_dim(b_up.reshape(n_q, n_t, units), t, 1, False).reshape(1, own_units)
    b_project = jnp.concatenate([b_qkv, b_up], 1)

    spans = jnp.concatenate([lax.dynamic_index_in_dim(span_table, (z + o) % n_z, 0, False) for o in z_offsets])
    n_spans = 2 * n_z
    slots = jnp.arange(n_spans, dtype=jnp.int32)
    order = jnp.sum(jnp.where(spans[None, :] == slots[:, None], slots[None, :], 0), 1, dtype=jnp.int32)
    half = ROT // 2
    lane = jnp.arange(own_width, dtype=jnp.int32)[None, :] % head_dim
    position = jnp.arange(seq_len, dtype=jnp.int32).astype(F32)[:, None]
    freqs = jnp.where(lane < ROT, jnp.exp((lane % half).astype(F32) * (-2.0 * math.log(10000.0) / ROT)), 0.0)
    angles = position * freqs
    sine = jnp.sin(angles)
    tables = (jnp.cos(angles), jnp.where(lane < half, -sine, 0.0), jnp.where((lane >= half) & (lane < ROT), sine, 0.0))

    def line_exchange(pieces):
        mine = pieces[:n_z]
        theirs = list(swap(jnp.concatenate(pieces[n_z:], 0)).reshape(n_z, *pieces[0].shape))
        return [
            lax.ppermute(p, "ctx", ring_pairs(z_order, s)) if s else p for c in (mine, theirs) for s, p in enumerate(c)
        ]

    w2_block = jnp.concatenate([fc2_weight, out_weight], 0) if whole_heads else fc2_weight
    w2_pieces = gathered(w2_block, "q", q_order)
    blocks = line_exchange(to_blocks(at, qkv_weight, fc1_weight, n_q, n_t, heads, head_dim, units))
    w1_block = stack_rows(at, [after(blocks[0], w2_pieces[1][2], w2_pieces[2][2])] + blocks[1:])
    plan, places_of = [], []
    for i, (offset, first, piece) in enumerate(w2_pieces):
        last = first + piece.shape[0]
        if first < units:
            plan.append((i, 0, min(last, units) - first))
            places_of.append(q_at[offset] * units + first)
        if last > units:
            begin = max(first, units)
            plan.append((i, begin - first, last - begin))
            places_of.append(own_units + q_at[offset] * head_dim + begin - units)
    w2_arrays = [piece for *_, piece in w2_pieces]
    if not whole_heads:
        w_out = lax.all_gather(out_weight, every, axis=0, tiled=True).reshape(heads, n_t, head_dim, width)
        w2_arrays.append(lax.dynamic_index_in_dim(w_out, t, 1, False).reshape(own_width, width))
        plan.append((len(w2_arrays) - 1, 0, own_width))
        places_of.append(own_units)
    w2 = Gathered(w2_arrays, plan, places_of)

    w1_pieces = gathered(w1_block, "q", q_order)
    block_rows = n_t * d_rows
    w1 = Gathered(
        [piece for *_, piece in w1_pieces],
        [(i, 0, piece.shape[0]) for i, (*_, piece) in enumerate(w1_pieces)],
        [q_at[offset] * block_rows + first for offset, first, _ in w1_pieces],
    )

    slot_of = {o: i for i, o in enumerate(z_offsets)}

    def line(block):
        pieces = gathered(block, "ctx", z_order)
        token_plan = [[] for _ in range(2 * n_z)]
        for i, (offset, first, piece) in enumerate(pieces):
            for c in range(2):
                token_plan[slot_of[offset] + c * n_z].append((i + c * len(pieces), first, piece.shape[0]))
        arrays = [piece for *_, piece in pieces]
        return arrays, arrays + [swap(piece) for piece in arrays], tuple(tuple(p) for p in token_plan)

    x_line, x_arrays, token_plan = line(after(inputs, *blocks[1:n_z], *blocks[n_z + 1 :]))
    g_line, g_arrays, _ = line(after(cotangent, *x_line[-2:]))

    x_all, hidden, qkv, act, slope = project(x_arrays, token_plan, gain, shift, w1, b_project, split, rows)
    att, kept = attend(order, qkv.reshape(2, seq_len, split), tables, heads, head_dim, span)
    att = after(att, *g_line[1:3]).reshape(2 * seq_len, own_width)
    out_other = combine(act, att, w2, 1)
    out_own = combine(act, after(att, out_other), w2, 0, swap(out_other))

    low, high, sent = ring_sum(after(out_own, *g_line[-2:]), rows, "ctx", z_order)
    x_here = inputs.astype(F32)
    output = (x_here + (out_own[:rows].astype(F32) + low.astype(F32) + high.astype(F32)) + (b_out + b_down)).astype(BF)

    def q_sum(part):
        return ring_sum(part, part.shape[0] // n_q, "q", q_order)

    g_all, pre_grad, att_grad = combine_back(g_arrays, token_plan, w2, after(slope, out_own), rows)
    up_part, up_sums = weight_grad(turns, hidden, pre_grad)
    up_low, up_high, up_sent = q_sum(up_part)
    att_grad = after(att_grad, up_part, *sent).reshape(2, seq_len, own_width)
    qkv_grad = attend_back(order, kept, att_grad, tables, heads, head_dim, span).reshape(2 * seq_len, split)
    part_other, sums_other = project_back(after(qkv_grad, *up_sent), pre_grad, w1, x_all, 1)
    qkv_part, qkv_sums = weight_grad(turns, after(hidden, part_other), qkv_grad)
    part_own, sums_own = project_back(after(qkv_grad, qkv_part, low, high), pre_grad, w1, x_all, 0, swap(part_other))
    qkv_low, qkv_high, qkv_sent = q_sum(qkv_part)
    n_low, n_high, n_sent = ring_sum(part_own, rows, "ctx", z_order)
    up_rows = last_sum(at, up_part, up_low, up_high, n_t)
    down, out_apart = down_grad(turns, after(act, part_own, *qkv_sent, *up_rows), att, g_all, head_dim if whole_heads else 0)

    fc1_weight_grad = from_blocks(at, line_exchange(up_rows), n_q, units)
    qkv_rows = last_sum(at, qkv_part, qkv_low, qkv_high, n_t)
    qkv_weight_grad = from_blocks(at, line_exchange(qkv_rows), 3 * heads, head_dim)
    down_low, down_high, _ = q_sum(down)
    down_rows = down_low.shape[0]
    down_sum = down[:down_rows].astype(F32) + down_low.astype(F32) + down_high.astype(F32)
    fc2_weight_grad = down_sum[:units]
    if whole_heads:
        out_weight_grad = down_sum[units:]
    else:
        spread = jnp.zeros((heads, n_t, head_dim, width), F32)
        spread = lax.dynamic_update_slice(spread, out_apart.reshape(heads, 1, head_dim, width), (0, t, 0, 0))
        out_weight_grad = lax.psum_scatter(spread.reshape(width, width), every, scatter_dimension=0, tiled=True)

    input_grad = finish(part_own, n_low, n_high, inputs, cotangent, gain)

    def by_owner(vector):
        return vector.reshape(n_all, vector.shape[0] // n_all)

    qkv_spread = lax.dynamic_update_slice(
        jnp.zeros((3, heads, n_t, head_dim), F32), qkv_sums[0].reshape(3, heads, 1, head_dim), (0, 0, t, 0)
    ).reshape(-1)
    up_spread = lax.dynamic_update_slice(jnp.zeros((n_q, n_t, units), F32), up_sums[0].reshape(n_q, 1, units), (0, t, 0)).reshape(-1)
    vectors = jnp.concatenate(
        [
            by_owner(sums_own[0] + sums_other[0]),
            by_owner(sums_own[1] + sums_other[1]),
            by_owner(jnp.sum(cotangent.astype(F32), 0)),
            by_owner(qkv_spread),
            by_owner(up_spread),
        ],
        1,
    )
    cube = vectors.reshape(n_q, 2, n_z, vectors.shape[1])
    cube = lax.dynamic_index_in_dim(cube, core, 1, False) + swap(lax.dynamic_index_in_dim(cube, 1 - core, 1, False))
    total = sum_blocks(cube, "q", q, n_q)
    total = sum_blocks(total, "ctx", z, n_z)
    cuts = [ln_gain.shape[0], ln_bias.shape[0], out_bias.shape[0], qkv_bias.shape[0], fc1_bias.shape[0]]
    starts = [sum(cuts[:i]) for i in range(len(cuts))]
    gain_grad, shift_grad, bias_grad, qkv_bias_grad, fc1_bias_grad = (total[s : s + c] for s, c in zip(starts, cuts))
    return (
        output,
        input_grad,
        gain_grad,
        shift_grad,
        qkv_weight_grad,
        qkv_bias_grad,
        out_weight_grad,
        bias_grad,
        fc1_weight_grad,
        fc1_bias_grad,
        fc2_weight_grad,
        bias_grad,
    )


def sum_blocks(blocks, axis, index, n):
    total = lax.dynamic_index_in_dim(blocks, index, 0, False)
    for shift_by in range(1, n):
        piece = lax.dynamic_index_in_dim(blocks, (index + shift_by) % n, 0, False)
        total = total + lax.ppermute(piece, axis, ring_pairs(list(range(n)), shift_by))
    return total


def solution(mesh):
    n_dp, n_ctx = mesh.devices.shape
    inner = Mesh(mesh.devices.reshape(n_dp // 2, 2, n_ctx), ("q", "core", "ctx"))
    every = ("q", "core", "ctx")
    matrix, vector = P(every, None), P(every)
    return jax.shard_map(
        per_device,
        mesh=inner,
        in_specs=(
            matrix,
            P(),
            vector,
            vector,
            matrix,
            vector,
            matrix,
            vector,
            matrix,
            vector,
            matrix,
            vector,
            matrix,
        ),
        out_specs=(matrix, matrix, vector, vector, matrix, vector, matrix, vector, matrix, vector, matrix, vector),
        check_vma=False,
    )
```

time: 911 us -> 647 us (0.71)
  waiting for transfers between devices: 402 us -> 243 us
  Pallas kernels: 47.7 us -> 205 us
  matrix products: 140 us -> 0 us
  blocking collectives: 47.1 us -> 0 us
  other arithmetic: 60.7 us -> 19.9 us
  local copies, waits for them, and re-layouts: 91.1 us -> 65.1 us
  starting transfers between devices: 97.7 us -> 81.1 us
  between operations: 14.3 us -> 26.9 us
    ppermute x60 -> x54, waiting for transfers between devices: 399 us -> 208 us  [the longest x10 52.8 us: ring_sum(): lax.ppermute(to_low, axis, down)]
    pallas_call x0 -> x21, Pallas kernels: none -> 165 us  [the longest x2 30.6 us: project_back(): pl.pallas_call(partial(project_back_kernel, split, w.plan, len(w.arrays))...]
    dot_general x12 -> x0, matrix products: 140 us -> none  [the longest x4 50 us: dot_t(): lax.dot_general(a, b, (((1,), (1,)), ((), ())), preferred_element_type=F32)]
    unnamed x1 -> x0, blocking collectives: 47.1 us -> none
    ppermute x6, waiting for transfers between devices: 1.62 us -> 34.8 us  [sum_blocks(): lax.ppermute(piece, axis, ring_pairs(list(range(n)), shift_by))]
    another operation x8 -> x2, other arithmetic: 23.5 us -> 2.74 us  [the longest x1 2.66 us: per_device(): turns = jnp.stack([q_ring[(places[q] + o) % n_q] for o in q_offsets])]
    unnamed x146 -> x130, local copies, waits for them, and re-layouts: 16 us -> 34.4 us
    ppermute x60 -> x54, starting transfers between devices: 88 us -> 69.9 us  [the longest x18 30.8 us: line_exchange(): lax.ppermute(p, 'ctx', ring_pairs(z_order, s))]
  transfers between devices with their start and end apart: 81 -> 77, of which waited for: 35 -> 22; matrix products, arithmetic and copies ran while one was open for 20% -> 7% of each run, Pallas kernels for 0% -> 28%
where the time goes in v2:
time: 647 us; the launch traced here: 641 us
  waiting for transfers between devices  243 us (38%)
  Pallas kernels  205 us (32%)
  starting transfers between devices  81.1 us (13%)
  local copies, waits for them, and re-layouts  65.1 us (10%)
  between operations  26.9 us (4%)
  other arithmetic  19.9 us (3%)
    ppermute x10, waiting for transfers between devices, ring_sum(): lax.ppermute(to_low, axis, down)  52.8 us
    ppermute x18, waiting for transfers between devices, line_exchange(): lax.ppermute(p, 'ctx', ring_pairs(z_order, s))  39.1 us
    ppermute x6, waiting for transfers between devices, sum_blocks(): lax.ppermute(piece, axis, ring_pairs(list(range(n)), shift_by))  34.8 us
    unnamed x130, local copies, waits for them, and re-layouts  34.4 us
    ppermute x4, waiting for transfers between devices, gathered(): out.append((step, half, lax.ppermute(down[half:], axis, down_pairs)))  33 us
    ppermute x4, waiting for transfers between devices, gathered(): lax.ppermute(down, axis, down_pairs)  31.3 us
    ppermute x18, starting transfers between devices, line_exchange(): lax.ppermute(p, 'ctx', ring_pairs(z_order, s))  30.8 us
    pallas_call x2, Pallas kernels, project_back(): pl.pallas_call(partial(project_back_kernel, split, w.plan, len(w.arrays))...  30.6 us
  transfers between devices with their start and end apart: 77, of which 22 were waited for; matrix products, arithmetic and copies ran while one was open for 7% of the time, Pallas kernels for 28%

profile of v2, /device:TPU:0, one launch (start us, length us, event | category | flops | bytes accessed | tf_op | source)
XLA Modules:
  0.0 640.5 jit_solution(11900547420498388510)
XLA Ops:
  25.9 5.0 collective-permute-done.refs_1_
  31.8 17.2 %collective-permute-done.17.refs_2_.refs_12_ = bf16[320,2048]{1,0:T(8,128)(2,1)S(1)} collective-permute-done((bf16[320,2048]{1,0:T(8,128)(2,1)S(1)}, bf16[320,2048]{1,0:T(8,128)(2,1)S(1)}, u32[]{:S(2)}, u32[]{:S(2)}) %collective-permute-start.17) | collective-permute-done | bytes 1310752 | tf_op jit(solution)/shard_map/ppermute | solution.py:240
  53.5 15.9 %collective-permute-done.5.refs_6_ = bf16[64,1792]{1,0:T(8,128)(2,1)S(1)} collective-permute-done((bf16[64,1792]{1,0:T(8,128)(2,1)S(1)}, bf16[64,1792]{1,0:T(8,128)(2,1)S(1)}, u32[]{:S(2)}, u32[]{:S(2)}) %collective-permute-start.5) | collective-permute-done | bytes 229408 | tf_op jit(solution)/shard_map/ppermute | solution.py:845
  87.6 14.0 %collective-permute-done.8.refs_2_ = bf16[256,2048]{1,0:T(8,128)(2,1)} collective-permute-done((bf16[256,2048]{1,0:T(8,128)(2,1)S(1)}, bf16[256,2048]{1,0:T(8,128)(2,1)}, u32[]{:S(2)}, u32[]{:S(2)}) %collective-permute-start.8) | collective-permute-done | bytes 1048608 | tf_op jit(solution)/shard_map/ppermute | solution.py:240
  102.7 4.5 collective-permute-start.10
  107.2 20.9 %collective-permute-done.7.refs_1_ = bf16[256,2048]{1,0:T(8,128)(2,1)} collective-permute-done((bf16[256,2048]{1,0:T(8,128)(2,1)S(1)}, bf16[256,2048]{1,0:T(8,128)(2,1)}, u32[]{:S(2)}, u32[]{:S(2)}) %collective-permute-start.7) | collective-permute-done | bytes 1048608 | tf_op jit(solution)/shard_map/ppermute | solution.py:240
  129.5 5.0 fusion
  137.3 11.6 %collective-permute-done.9.refs_3_ = bf16[128,2048]{1,0:T(8,128)(2,1)S(1)} collective-permute-done((bf16[128,2048]{1,0:T(8,128)(2,1)S(1)}, bf16[128,2048]{1,0:T(8,128)(2,1)S(1)}, u32[]{:S(2)}, u32[]{:S(2)}) %collective-permute-start.9) | collective-permute-done | bytes 524320 | tf_op jit(solution)/shard_map/ppermute | solution.py:237
  155.3 4.2 reshape.242
  165.7 9.4 %collective-permute-done.21.refs_14_.refs_4_ = bf16[256,1792]{1,0:T(8,128)(2,1)S(1)} collective-permute-done((bf16[256,1792]{1,0:T(8,128)(2,1)}, bf16[256,1792]{1,0:T(8,128)(2,1)S(1)}, u32[]{:S(2)}, u32[]{:S(2)}) %collective-permute-start.21) | collective-permute-done | bytes 917536 | tf_op jit(solution)/shard_map/ppermute | solution.py:238
  176.1 7.0 %collective-permute-done.20.refs_13_.refs_3_ = bf16[256,1792]{1,0:T(8,128)(2,1)} collective-permute-done((bf16[256,1792]{1,0:T(8,128)(2,1)}, bf16[256,1792]{1,0:T(8,128)(2,1)}, u32[]{:S(2)}, u32[]{:S(2)}) %collective-permute-start.20) | collective-permute-done | bytes 917536 | tf_op jit(solution)/shard_map/ppermute | solution.py:237
  186.9 30.3 %project.1 = (bf16[2048,2048]{1,0:T(8,128)(2,1)}, bf16[2048,2048]{1,0:T(8,128)(2,1)}, f32[2048,768]{1,0:T(8,128)}, bf16[2048,1024]{1,0:T(8,128)(2,1)}, bf16[2048,1024]{1,0:T(8,128)(2,1)}) custom-call(s32[5]{0:T(128)S(1)} %stack.13.starts_ref, bf16[256,2048]{1,0:T(8,128)(2,1)S(1)} %copy-done.7, bf16[256,2048]{1,0:T(8,128)(2,1)} %collective-permute-done.7.refs_1_, ...), custom_call_target="tpu_custom_call" | custom-call | flops 15032385536 | bytes 40894464 | tf_op jit(solution)/shard_map/project/pallas_call | solution.py:520
  220.0 14.5 %attend.1 = (bf16[2,1024,256]{2,1,0:T(8,128)(2,1)S(1)}, bf16[2,1024,768]{2,1,0:T(8,128)(2,1)S(1)}) custom-call(s32[8]{0:T(128)S(1)} %select_reduce_fusion.order_ref, f32[2,1024,768]{2,1,0:T(8,128)S(1)} %bitcast.39, f32[1024,256]{1,0:T(8,128)S(1)} %copy-done.18, f32[1024,256]{1,0:T(8,128)S(1)} %copy-done.16, f32[1024,256]{1,0:T(8,128)S(1)} %copy-done.15), custom_call_target="tpu_custom_call" | custom-call | flops 4294967296 | bytes 12582912 | tf_op jit(solution)/shard_map/attend/pallas_call | solution.py:147
  238.8 7.5 %combine.2 = bf16[1024,2048]{1,0:T(8,128)(2,1)S(1)} custom-call(s32[9]{0:T(128)S(1)} %stack.12.starts_ref, bf16[2048,1024]{1,0:T(8,128)(2,1)S(1)} %copy-done.50, bf16[2048,256]{1,0:T(8,128)(2,1)S(1)} %bitcast.43, bf16[320,2048]{1,0:T(8,128)(2,1)S(1)} %copy-done.21, bf16[320,2048]{1,0:T(8,128)(2,1)S(1)} %copy-done.30, bf16[320,2048]{1,0:T(8,128)(2,1)S(1)} %copy-done.27, ...), custom_call_target="tpu_custom_call" | custom-call | flops 5368709120 | bytes 13631488 | tf_op jit(solution)/shard_map/combine/pallas_call | solution.py:571
  250.1 22.7 %collective-permute-done.28.refs_4_ = bf16[128,2048]{1,0:T(8,128)(2,1)S(1)} collective-permute-done((bf16[128,2048]{1,0:T(8,128)(2,1)S(1)}, bf16[128,2048]{1,0:T(8,128)(2,1)S(1)}, u32[]{:S(2)}, u32[]{:S(2)}) %collective-permute-start.28) | collective-permute-done | bytes 524320 | tf_op jit(solution)/shard_map/ppermute | solution.py:238
  276.1 7.5 %combine.3.low_part_ref.high_part_ref = bf16[1024,2048]{1,0:T(8,128)(2,1)S(1)} custom-call(s32[9]{0:T(128)S(1)} %stack.12.starts_ref, bf16[2048,1024]{1,0:T(8,128)(2,1)S(1)} %copy-done.51, bf16[2048,256]{1,0:T(8,128)(2,1)S(1)} %bitcast.44, bf16[320,2048]{1,0:T(8,128)(2,1)S(1)} %copy-done.21, bf16[320,2048]{1,0:T(8,128)(2,1)S(1)} %copy-done.30, ...), custom_call_target="tpu_custom_call" | custom-call | flops 5368709120 | bytes 13631488 | tf_op jit(solution)/shard_map/combine/pallas_call | solution.py:571
  289.6 16.1 %combine_back.1 = (bf16[2048,2048]{1,0:T(8,128)(2,1)}, bf16[2048,1024]{1,0:T(8,128)(2,1)S(1)}, bf16[2048,256]{1,0:T(8,128)(2,1)S(1)}) custom-call(s32[9]{0:T(128)S(1)} %stack.12.starts_ref, bf16[256,2048]{1,0:T(8,128)(2,1)S(1)} %copy-done.9, bf16[256,2048]{1,0:T(8,128)(2,1)S(1)} %collective-permute-done.22.refs_1_, ...), custom_call_target="tpu_custom_call" | custom-call | flops 10737418240 | bytes 30408704 | tf_op jit(solution)/shard_map/combine_back/pallas_call | solution.py:618
  306.7 13.4 %weight_grad.2 = (bf16[2048,1024]{1,0:T(8,128)(2,1)S(1)}, f32[8,1024]{1,0:T(8,128)S(1)}) custom-call(s32[4]{0:T(128)S(1)} %pad_add_fusion.2.turns_ref, bf16[2048,2048]{1,0:T(8,128)(2,1)} %get-tuple-element.108.left_ref, bf16[2048,1024]{1,0:T(8,128)(2,1)S(1)} %get-tuple-element.100.right_ref.pre_grad_ref), custom_call_target="tpu_custom_call" | custom-call | flops 8589934592 | bytes 16777216 | tf_op jit(solution)/shard_map/weight_grad/pallas_call | solution.py:701
  332.6 25.6 %attend_back.1 = bf16[2,1024,768]{2,1,0:T(8,128)(2,1)S(1)} custom-call(s32[8]{0:T(128)S(1)} %select_reduce_fusion.order_ref, bf16[2,1024,768]{2,1,0:T(8,128)(2,1)S(1)} %copy-done.54, bf16[2,1024,256]{2,1,0:T(8,128)(2,1)S(1)} %bitcast.46, f32[1024,256]{1,0:T(8,128)S(1)} %copy-done.19, f32[1024,256]{1,0:T(8,128)S(1)} %copy-done.17, f32[1024,256]{1,0:T(8,128)S(1)} %copy-done.15), custom_call_target="tpu_custom_call" | custom-call | flops 10737418240 | bytes 9437184 | tf_op jit(solution)/shard_map/attend_back/pallas_call | solution.py:177
  365.0 15.0 %project_back.2 = (bf16[1024,2048]{1,0:T(8,128)(2,1)}, f32[8,2048]{1,0:T(8,128)S(1)}) custom-call(s32[5]{0:T(128)S(1)} %stack.13.starts_ref, bf16[2048,768]{1,0:T(8,128)(2,1)S(1)} %bitcast.40, bf16[2048,1024]{1,0:T(8,128)(2,1)} %copy-done.49, bf16[2048,2048]{1,0:T(8,128)(2,1)} %get-tuple-element.106.x_ref, bf16[512,1792]{1,0:T(8,128)(2,1)S(1)} %copy-done.12, ...), custom_call_target="tpu_custom_call" | custom-call | flops 7516192768 | bytes 19922944 | tf_op jit(solution)/shard_map/project_back/pallas_call | solution.py:671
  380.1 10.1 %weight_grad.3 = (bf16[2048,768]{1,0:T(8,128)(2,1)S(1)}, f32[8,768]{1,0:T(8,128)S(1)}) custom-call(s32[4]{0:T(128)S(1)} %pad_add_fusion.2.turns_ref, bf16[2048,2048]{1,0:T(8,128)(2,1)} %get-tuple-element.108.left_ref, bf16[2048,768]{1,0:T(8,128)(2,1)S(1)} %bitcast.41), custom_call_target="tpu_custom_call" | custom-call | flops 6442450944 | bytes 14680064 | tf_op jit(solution)/shard_map/weight_grad/pallas_call | solution.py:701
  392.4 9.6 %collective-permute-done.53.high_ref = bf16[256,768]{1,0:T(8,128)(2,1)} collective-permute-done((bf16[256,768]{1,0:T(8,128)(2,1)S(1)}, bf16[256,768]{1,0:T(8,128)(2,1)}, u32[]{:S(2)}, u32[]{:S(2)}) %collective-permute-start.53) | collective-permute-done | bytes 393248 | tf_op jit(solution)/shard_map/ppermute | solution.py:425
  409.8 16.6 %collective-permute-done.54.low_ref = bf16[512,768]{1,0:T(8,128)(2,1)S(1)} collective-permute-done((bf16[512,768]{1,0:T(8,128)(2,1)}, bf16[512,768]{1,0:T(8,128)(2,1)S(1)}, u32[]{:S(2)}, u32[]{:S(2)}) %collective-permute-start.54) | collective-permute-done | bytes 786464 | tf_op jit(solution)/shard_map/ppermute | solution.py:425
  435.5 11.9 %collective-permute-done.63.low_ref = bf16[512,1024]{1,0:T(8,128)(2,1)S(1)} collective-permute-done((bf16[512,1024]{1,0:T(8,128)(2,1)}, bf16[512,1024]{1,0:T(8,128)(2,1)S(1)}, u32[]{:S(2)}, u32[]{:S(2)}) %collective-permute-start.63) | collective-permute-done | bytes 1048608 | tf_op jit(solution)/shard_map/ppermute | solution.py:425
  451.9 24.1 %collective-permute-done.31 = bf16[256,2048]{1,0:T(8,128)(2,1)} collective-permute-done((bf16[256,2048]{1,0:T(8,128)(2,1)}, bf16[256,2048]{1,0:T(8,128)(2,1)}, u32[]{:S(2)}, u32[]{:S(2)}) %collective-permute-start.31) | collective-permute-done | bytes 1048608 | tf_op jit(solution)/shard_map/ppermute | solution.py:425
  479.9 15.6 %project_back.3 = (bf16[1024,2048]{1,0:T(8,128)(2,1)S(1)}, f32[8,2048]{1,0:T(8,128)S(1)}) custom-call(s32[5]{0:T(128)S(1)} %stack.13.starts_ref, bf16[2048,768]{1,0:T(8,128)(2,1)S(1)} %bitcast.42, bf16[2048,1024]{1,0:T(8,128)(2,1)} %copy-done.49, bf16[2048,2048]{1,0:T(8,128)(2,1)} %get-tuple-element.106.x_ref, bf16[512,1792]{1,0:T(8,128)(2,1)S(1)} %copy-done.13, ...), custom_call_target="tpu_custom_call" | custom-call | flops 7516192768 | bytes 19922944 | tf_op jit(solution)/shard_map/project_back/pallas_call | solution.py:671
  495.6 17.0 %down_grad.1.low_part_ref.high_part_ref = bf16[1280,2048]{1,0:T(8,128)(2,1)S(1)} custom-call(s32[4]{0:T(128)S(1)} %pad_add_fusion.2.turns_ref, bf16[2048,1024]{1,0:T(8,128)(2,1)S(1)} %copy-done.52, bf16[2048,256]{1,0:T(8,128)(2,1)S(1)} %bitcast.45, bf16[2048,2048]{1,0:T(8,128)(2,1)} %get-tuple-element.137.g_ref), custom_call_target="tpu_custom_call" | custom-call | flops 10737418240 | bytes 16777216 | tf_op jit(solution)/shard_map/down_grad/pallas_call | solution.py:738
  526.6 6.0 collective-permute-start.60
  541.2 11.0 %collective-permute-done.75.refs_7_ = bf16[64,1024]{1,0:T(8,128)(2,1)S(1)} collective-permute-done((bf16[64,1024]{1,0:T(8,128)(2,1)S(1)}, bf16[64,1024]{1,0:T(8,128)(2,1)S(1)}, u32[]{:S(2)}, u32[]{:S(2)}) %collective-permute-start.75) | collective-permute-done | bytes 131104 | tf_op jit(solution)/shard_map/ppermute | solution.py:845
  556.5 4.3 pass_on.9
  586.1 34.8 %collective-permute-done.50 = f32[640]{0:T(1024)S(1)} collective-permute-done((f32[640]{0:T(1024)S(1)}, f32[640]{0:T(1024)S(1)}, u32[]{:S(2)}, u32[]{:S(2)}) %collective-permute-start.50) | collective-permute-done | bytes 2592 | tf_op jit(solution)/shard_map/ppermute | solution.py:978
  622.7 5.1 finish.1
  (355 shorter events, 180.1 us)
Async XLA Ops:
  7.2 148.2 %all-gather.2.cloned.1.call-start = ((), (), s32[]{:S(2)}) async-start(), calls=%async_computation | async-start | bytes 2162688 | tf_op jit(solution)/shard_map/all_gather | solution.py:820
  16.8 32.3 %collective-permute-start.17 = (bf16[320,2048]{1,0:T(8,128)(2,1)S(1)}, bf16[320,2048]{1,0:T(8,128)(2,1)S(1)}, u32[]{:S(2)}, u32[]{:S(2)}) collective-permute-start(bf16[320,2048]{1,0:T(8,128)(2,1)S(1)} %constant_dynamic-update-slice_fusion.refs_0_.refs_10_), channel_id=1, source_target_pairs={{0,16},{8,0},{24,8},{16,24},{1,17},{9,1},{25,9},{17,25},{2,18},{10... | collective-permute-start | bytes 3932168 | tf_op jit(solution)/shard_map/ppermute | solution.py:240
  70.1 78.8 %collective-permute-start.19 = (bf16[512,1792]{1,0:T(8,128)(2,1)S(1)}, bf16[512,1792]{1,0:T(8,128)(2,1)}, u32[]{:S(2)}, u32[]{:S(2)}) collective-permute-start(bf16[512,1792]{1,0:T(8,128)(2,1)S(1)} %stack_rows.1.refs_10_.refs_0_), channel_id=1, source_target_pairs={{0,16},{8,0},{24,8},{16,24},{1,17},{9,1},{25,9},{17,25},{2,18},{10... | collective-permute-start | bytes 5505032 | tf_op jit(solution)/shard_map/ppermute | solution.py:240
  71.6 80.0 %collective-permute-start.18 = (bf16[512,1792]{1,0:T(8,128)(2,1)S(1)}, bf16[512,1792]{1,0:T(8,128)(2,1)}, u32[]{:S(2)}, u32[]{:S(2)}) collective-permute-start(bf16[512,1792]{1,0:T(8,128)(2,1)S(1)} %stack_rows.1.refs_10_.refs_0_), channel_id=1, source_target_pairs={{0,8},{8,24},{24,16},{16,0},{1,9},{9,25},{25,17},{17,1},{2,10},{10... | collective-permute-start | bytes 5505032 | tf_op jit(solution)/shard_map/ppermute | solution.py:240
  72.2 55.9 %collective-permute-start.7 = (bf16[256,2048]{1,0:T(8,128)(2,1)S(1)}, bf16[256,2048]{1,0:T(8,128)(2,1)}, u32[]{:S(2)}, u32[]{:S(2)}) collective-permute-start(bf16[256,2048]{1,0:T(8,128)(2,1)S(1)} %copy-done.7), channel_id=1, source_target_pairs={{0,1},{1,2},{2,3},{3,0},{4,5},{5,6},{6,7},{7,4},{8,9},{9,10},{10,1... | collective-permute-start | bytes 3145736 | tf_op jit(solution)/shard_map/ppermute | solution.py:240
  74.2 85.4 %collective-permute-start.11 = (bf16[256,2048]{1,0:T(8,128)(2,1)S(1)}, bf16[256,2048]{1,0:T(8,128)(2,1)}, u32[]{:S(2)}, u32[]{:S(2)}) collective-permute-start(bf16[256,2048]{1,0:T(8,128)(2,1)S(1)} %copy-done.7), channel_id=1, source_target_pairs={{0,4},{4,0},{1,5},{5,1},{2,6},{6,2},{3,7},{7,3},{8,12},{12,8},{9,1... | collective-permute-start | bytes 3145736 | tf_op jit(solution)/shard_map/ppermute | solution.py:39
  102.7 34.6 %collective-permute-start.10 = (bf16[128,2048]{1,0:T(8,128)(2,1)S(1)}, bf16[128,2048]{1,0:T(8,128)(2,1)}, u32[]{:S(2)}, u32[]{:S(2)}) collective-permute-start(bf16[128,2048]{1,0:T(8,128)(2,1)S(1)} %slice.169), channel_id=1, source_target_pairs={{0,3},{1,0},{2,1},{3,2},{4,7},{5,4},{6,5},{7,6},{8,11},{9,8},{10,9... | collective-permute-start | bytes 1572872 | tf_op jit(solution)/shard_map/ppermute | solution.py:238
  162.8 73.4 %collective-permute-start.25 = (bf16[160,2048]{1,0:T(8,128)(2,1)}, bf16[160,2048]{1,0:T(8,128)(2,1)S(1)}, u32[]{:S(2)}, u32[]{:S(2)}) collective-permute-start(bf16[160,2048]{1,0:T(8,128)(2,1)} %slice.177), channel_id=1, source_target_pairs={{0,16},{8,0},{24,8},{16,24},{1,17},{9,1},{25,9},{17,25},{2,18},{10... | collective-permute-start | bytes 1966088 | tf_op jit(solution)/shard_map/ppermute | solution.py:238
  164.5 71.8 %collective-permute-start.24 = (bf16[160,2048]{1,0:T(8,128)(2,1)}, bf16[160,2048]{1,0:T(8,128)(2,1)S(1)}, u32[]{:S(2)}, u32[]{:S(2)}) collective-permute-start(bf16[160,2048]{1,0:T(8,128)(2,1)} %slice.176), channel_id=1, source_target_pairs={{0,8},{8,24},{24,16},{16,0},{1,9},{9,25},{25,17},{17,1},{2,10},{10... | collective-permute-start | bytes 1966088 | tf_op jit(solution)/shard_map/ppermute | solution.py:237
  165.6 70.5 %collective-permute-start.23 = (bf16[256,2048]{1,0:T(8,128)(2,1)S(1)}, bf16[256,2048]{1,0:T(8,128)(2,1)S(1)}, u32[]{:S(2)}, u32[]{:S(2)}) collective-permute-start(bf16[256,2048]{1,0:T(8,128)(2,1)S(1)} %copy-done.9), channel_id=1, source_target_pairs={{0,3},{1,0},{2,1},{3,2},{4,7},{5,4},{6,5},{7,6},{8,11},{9,8},{10,9... | collective-permute-start | bytes 3145736 | tf_op jit(solution)/shard_map/ppermute | solution.py:240
  175.9 60.2 %collective-permute-start.22 = (bf16[256,2048]{1,0:T(8,128)(2,1)S(1)}, bf16[256,2048]{1,0:T(8,128)(2,1)S(1)}, u32[]{:S(2)}, u32[]{:S(2)}) collective-permute-start(bf16[256,2048]{1,0:T(8,128)(2,1)S(1)} %copy-done.9), channel_id=1, source_target_pairs={{0,1},{1,2},{2,3},{3,0},{4,5},{5,6},{6,7},{7,4},{8,9},{9,10},{10,1... | collective-permute-start | bytes 3145736 | tf_op jit(solution)/shard_map/ppermute | solution.py:240
  249.5 36.2 %collective-permute-start.33 = (bf16[256,2048]{1,0:T(8,128)(2,1)S(1)}, bf16[256,2048]{1,0:T(8,128)(2,1)S(1)}, u32[]{:S(2)}, u32[]{:S(2)}) collective-permute-start(bf16[256,2048]{1,0:T(8,128)(2,1)S(1)} %copy-done.9), channel_id=1, source_target_pairs={{0,4},{4,0},{1,5},{5,1},{2,6},{6,2},{3,7},{7,3},{8,12},{12,8},{9,1... | collective-permute-start | bytes 3145736 | tf_op jit(solution)/shard_map/ppermute | solution.py:39
  249.5 40.1 %collective-permute-start.35 = (bf16[256,2048]{1,0:T(8,128)(2,1)S(1)}, bf16[256,2048]{1,0:T(8,128)(2,1)S(1)}, u32[]{:S(2)}, u32[]{:S(2)}) collective-permute-start(bf16[256,2048]{1,0:T(8,128)(2,1)S(1)} %collective-permute-done.23.refs_2_), channel_id=1, source_target_pairs={{0,4},{4,0},{1,5},{5,1},{2,6},{6,2},{3,7},{7,3},{8,12},{12,8},{9,1... | collective-permute-start | bytes 3145736 | tf_op jit(solution)/shard_map/ppermute | solution.py:39
  285.7 39.8 %collective-permute-start.30 = (bf16[128,2048]{1,0:T(8,128)(2,1)S(1)}, bf16[128,2048]{1,0:T(8,128)(2,1)}, u32[]{:S(2)}, u32[]{:S(2)}) collective-permute-start(bf16[128,2048]{1,0:T(8,128)(2,1)S(1)} %get-tuple-element.156), channel_id=1, source_target_pairs={{0,1},{1,2},{2,3},{3,0},{4,5},{5,6},{6,7},{7,4},{8,9},{9,10},{10,1... | collective-permute-start | bytes 1572872 | tf_op jit(solution)/shard_map/ppermute | solution.py:425
  285.8 39.7 %collective-permute-start.29 = (bf16[128,2048]{1,0:T(8,128)(2,1)S(1)}, bf16[128,2048]{1,0:T(8,128)(2,1)}, u32[]{:S(2)}, u32[]{:S(2)}) collective-permute-start(bf16[128,2048]{1,0:T(8,128)(2,1)S(1)} %get-tuple-element.157), channel_id=1, source_target_pairs={{0,3},{1,0},{2,1},{3,2},{4,7},{5,4},{6,5},{7,6},{8,11},{9,8},{10,9... | collective-permute-start | bytes 1572872 | tf_op jit(solution)/shard_map/ppermute | solution.py:425
  323.1 36.8 %collective-permute-start.39 = (bf16[256,1024]{1,0:T(8,128)(2,1)}, bf16[256,1024]{1,0:T(8,128)(2,1)}, u32[]{:S(2)}, u32[]{:S(2)}) collective-permute-start(bf16[256,1024]{1,0:T(8,128)(2,1)} %get-tuple-element.154), channel_id=1, source_target_pairs={{0,8},{8,24},{24,16},{16,0},{1,9},{9,25},{25,17},{17,1},{2,10},{10... | collective-permute-start | bytes 1572872 | tf_op jit(solution)/shard_map/ppermute | solution.py:425
  323.5 36.4 %collective-permute-start.38 = (bf16[256,1024]{1,0:T(8,128)(2,1)}, bf16[256,1024]{1,0:T(8,128)(2,1)}, u32[]{:S(2)}, u32[]{:S(2)}) collective-permute-start(bf16[256,1024]{1,0:T(8,128)(2,1)} %get-tuple-element.155), channel_id=1, source_target_pairs={{0,16},{8,0},{24,8},{16,24},{1,17},{9,1},{25,9},{17,25},{2,18},{10... | collective-permute-start | bytes 1572872 | tf_op jit(solution)/shard_map/ppermute | solution.py:425
  380.0 99.5 %collective-permute-start.40 = (bf16[1024,2048]{1,0:T(8,128)(2,1)}, bf16[1024,2048]{1,0:T(8,128)(2,1)}, u32[]{:S(2)}, u32[]{:S(2)}) collective-permute-start(bf16[1024,2048]{1,0:T(8,128)(2,1)} %get-tuple-element.107), channel_id=1, source_target_pairs={{0,4},{4,0},{1,5},{5,1},{2,6},{6,2},{3,7},{7,3},{8,12},{12,8},{9,1... | collective-permute-start | bytes 12582920 | tf_op jit(solution)/shard_map/ppermute | solution.py:39
  407.8 39.6 %collective-permute-start.63 = (bf16[512,1024]{1,0:T(8,128)(2,1)}, bf16[512,1024]{1,0:T(8,128)(2,1)S(1)}, u32[]{:S(2)}, u32[]{:S(2)}) collective-permute-start(bf16[512,1024]{1,0:T(8,128)(2,1)} %get-tuple-element.103), channel_id=1, source_target_pairs={{0,16},{8,0},{24,8},{16,24},{1,17},{9,1},{25,9},{17,25},{2,18},{10... | collective-permute-start | bytes 3145736 | tf_op jit(solution)/shard_map/ppermute | solution.py:425
  409.4 39.3 %collective-permute-start.64 = (bf16[512,1024]{1,0:T(8,128)(2,1)}, bf16[512,1024]{1,0:T(8,128)(2,1)S(1)}, u32[]{:S(2)}, u32[]{:S(2)}) collective-permute-start(bf16[512,1024]{1,0:T(8,128)(2,1)} %get-tuple-element.104), channel_id=1, source_target_pairs={{0,8},{8,24},{24,16},{16,0},{1,9},{9,25},{25,17},{17,1},{2,10},{10... | collective-permute-start | bytes 3145736 | tf_op jit(solution)/shard_map/ppermute | solution.py:425
  426.5 49.4 %collective-permute-start.31 = (bf16[256,2048]{1,0:T(8,128)(2,1)}, bf16[256,2048]{1,0:T(8,128)(2,1)}, u32[]{:S(2)}, u32[]{:S(2)}) collective-permute-start(bf16[256,2048]{1,0:T(8,128)(2,1)} %get-tuple-element.93), channel_id=1, source_target_pairs={{0,3},{1,0},{2,1},{3,2},{4,7},{5,4},{6,5},{7,6},{8,11},{9,8},{10,9... | collective-permute-start | bytes 3145736 | tf_op jit(solution)/shard_map/ppermute | solution.py:425
  428.9 47.0 %collective-permute-start.32 = (bf16[256,2048]{1,0:T(8,128)(2,1)}, bf16[256,2048]{1,0:T(8,128)(2,1)}, u32[]{:S(2)}, u32[]{:S(2)}) collective-permute-start(bf16[256,2048]{1,0:T(8,128)(2,1)} %get-tuple-element.94), channel_id=1, source_target_pairs={{0,1},{1,2},{2,3},{3,0},{4,5},{5,6},{6,7},{7,4},{8,9},{9,10},{10,1... | collective-permute-start | bytes 3145736 | tf_op jit(solution)/shard_map/ppermute | solution.py:425
  451.8 63.8 %collective-permute-start.69 = (bf16[64,1024]{1,0:T(8,128)(2,1)S(1)}, bf16[64,1024]{1,0:T(8,128)(2,1)S(1)}, u32[]{:S(2)}, u32[]{:S(2)}) collective-permute-start(bf16[64,1024]{1,0:T(8,128)(2,1)S(1)} %get-tuple-element.129), channel_id=1, source_target_pairs={{0,1},{1,2},{2,3},{3,0},{4,5},{5,6},{6,7},{7,4},{8,9},{9,10},{10,1... | collective-permute-start | bytes 393224 | tf_op jit(solution)/shard_map/ppermute | solution.py:845
  475.9 42.2 %collective-permute-start.70 = (bf16[64,1024]{1,0:T(8,128)(2,1)S(1)}, bf16[64,1024]{1,0:T(8,128)(2,1)S(1)}, u32[]{:S(2)}, u32[]{:S(2)}) collective-permute-start(bf16[64,1024]{1,0:T(8,128)(2,1)S(1)} %get-tuple-element.130), channel_id=1, source_target_pairs={{0,2},{1,3},{2,0},{3,1},{4,6},{5,7},{6,4},{7,5},{8,10},{9,11},{10,... | collective-permute-start | bytes 393224 | tf_op jit(solution)/shard_map/ppermute | solution.py:845
  475.9 43.5 %collective-permute-start.71 = (bf16[64,1024]{1,0:T(8,128)(2,1)S(1)}, bf16[64,1024]{1,0:T(8,128)(2,1)S(1)}, u32[]{:S(2)}, u32[]{:S(2)}) collective-permute-start(bf16[64,1024]{1,0:T(8,128)(2,1)S(1)} %get-tuple-element.131), channel_id=1, source_target_pairs={{0,3},{1,0},{2,1},{3,2},{4,7},{5,4},{6,5},{7,6},{8,11},{9,8},{10,9... | collective-permute-start | bytes 393224 | tf_op jit(solution)/shard_map/ppermute | solution.py:845
  478.5 48.1 %collective-permute-start.72 = (bf16[256,1024]{1,0:T(8,128)(2,1)}, bf16[256,1024]{1,0:T(8,128)(2,1)S(1)}, u32[]{:S(2)}, u32[]{:S(2)}) collective-permute-start(bf16[256,1024]{1,0:T(8,128)(2,1)} %pad_maximum_fusion.1), channel_id=1, source_target_pairs={{0,4},{4,0},{1,5},{5,1},{2,6},{6,2},{3,7},{7,3},{8,12},{12,8},{9,1... | collective-permute-start | bytes 1572872 | tf_op jit(solution)/shard_map/ppermute | solution.py:39
  479.6 40.8 %collective-permute-start.56 = (bf16[64,768]{1,0:T(8,128)(2,1)S(1)}, bf16[64,768]{1,0:T(8,128)(2,1)S(1)}, u32[]{:S(2)}, u32[]{:S(2)}) collective-permute-start(bf16[64,768]{1,0:T(8,128)(2,1)S(1)} %get-tuple-element.121), channel_id=1, source_target_pairs={{0,1},{1,2},{2,3},{3,0},{4,5},{5,6},{6,7},{7,4},{8,9},{9,10},{10,1... | collective-permute-start | bytes 294920 | tf_op jit(solution)/shard_map/ppermute | solution.py:845
  563.4 64.5 %collective-permute-start.67 = (bf16[320,2048]{1,0:T(8,128)(2,1)}, bf16[320,2048]{1,0:T(8,128)(2,1)}, u32[]{:S(2)}, u32[]{:S(2)}) collective-permute-start(bf16[320,2048]{1,0:T(8,128)(2,1)} %get-tuple-element.138), channel_id=1, source_target_pairs={{0,16},{8,0},{24,8},{16,24},{1,17},{9,1},{25,9},{17,25},{2,18},{10... | collective-permute-start | bytes 3932168 | tf_op jit(solution)/shard_map/ppermute | solution.py:425
  564.1 63.8 %collective-permute-start.68 = (bf16[320,2048]{1,0:T(8,128)(2,1)}, bf16[320,2048]{1,0:T(8,128)(2,1)}, u32[]{:S(2)}, u32[]{:S(2)}) collective-permute-start(bf16[320,2048]{1,0:T(8,128)(2,1)} %get-tuple-element.139), channel_id=1, source_target_pairs={{0,8},{8,24},{24,16},{16,0},{1,9},{9,25},{25,17},{17,1},{2,10},{10... | collective-permute-start | bytes 3932168 | tf_op jit(solution)/shard_map/ppermute | solution.py:425
  573.5 49.2 %collective-permute-start.43 = (bf16[256,2048]{1,0:T(8,128)(2,1)}, bf16[256,2048]{1,0:T(8,128)(2,1)}, u32[]{:S(2)}, u32[]{:S(2)}) collective-permute-start(bf16[256,2048]{1,0:T(8,128)(2,1)} %get-tuple-element.112), channel_id=1, source_target_pairs={{0,3},{1,0},{2,1},{3,2},{4,7},{5,4},{6,5},{7,6},{8,11},{9,8},{10,9... | collective-permute-start | bytes 3145736 | tf_op jit(solution)/shard_map/ppermute | solution.py:425
  574.9 47.8 %collective-permute-start.44 = (bf16[256,2048]{1,0:T(8,128)(2,1)}, bf16[256,2048]{1,0:T(8,128)(2,1)}, u32[]{:S(2)}, u32[]{:S(2)}) collective-permute-start(bf16[256,2048]{1,0:T(8,128)(2,1)} %get-tuple-element.113), channel_id=1, source_target_pairs={{0,1},{1,2},{2,3},{3,0},{4,5},{5,6},{6,7},{7,4},{8,9},{9,10},{10,1... | collective-permute-start | bytes 3145736 | tf_op jit(solution)/shard_map/ppermute | solution.py:425
  576.4 44.5 %collective-permute-start.50 = (f32[640]{0:T(1024)S(1)}, f32[640]{0:T(1024)S(1)}, u32[]{:S(2)}, u32[]{:S(2)}) collective-permute-start(f32[640]{0:T(1024)S(1)} %get-tuple-element.144), channel_id=1, source_target_pairs={{0,2},{1,3},{2,0},{3,1},{4,6},{5,7},{6,4},{7,5},{8,10},{9,11},{10,... | collective-permute-start | bytes 7688 | tf_op jit(solution)/shard_map/ppermute | solution.py:978
  (107 other events, 1716.7 us)
Sparse Core Ops, SparseCore 0:
  12.1 84.6 all-gather.1

commit v3 on v2

v3 whole, which is shorter than its diff:
```python
from functools import partial
import math

import jax
import jax.numpy as jnp
from jax import lax
from jax.experimental import pallas as pl
from jax.experimental.pallas import tpu as pltpu
from jax.sharding import Mesh, PartitionSpec as P

HEADS = 32
ROT = 32
EPS = 1e-05
NEG = -1e30
BLOCK_Q = 256

BF = jnp.bfloat16
F32 = jnp.float32


def dot(a, b):
    return jnp.dot(a, b, preferred_element_type=F32)


def dot_t(a, b):
    return lax.dot_general(a, b, (((1,), (1,)), ((), ())), preferred_element_type=F32)


def t_dot(a, b):
    return lax.dot_general(a, b, (((0,), (0,)), ((), ())), preferred_element_type=F32)


def cost(flops, nbytes):
    return pl.CostEstimate(flops=flops // 1000, bytes_accessed=nbytes // 1000, transcendentals=0)


def across(value, axis, e):
    n = math.prod(lax.axis_size(a) for a in axis) if isinstance(axis, tuple) else lax.axis_size(axis)
    return lax.ppermute(value, axis, [(i, i ^ e) for i in range(n)])


def scattered(parts, axis):
    return [parts[0]] + [across(part, axis, e) for e, part in enumerate(parts) if e]


def ring_pairs(order, step):
    n = len(order)
    return [(order[i], order[(i + step) % n]) for i in range(n)]


def ring_offsets(n):
    return [0] + [o for s in range(1, n // 2) for o in (-s, s)] + [n // 2]


def half_of(rows):
    return rows // 32 * 16


def slot_plan(n, rows, first=0):
    plan = [((first + k, 0, rows),) for k in range(n - 1)]
    return plan + [((first + n - 1, 0, half_of(rows)), (first + n, half_of(rows), rows - half_of(rows)))]


def ring_gathered(own, axis, order, hold=()):
    n = len(order)
    up_pairs, down_pairs = ring_pairs(order, 1), ring_pairs(order, -1)
    out = [own]
    up = down = own
    half = half_of(own.shape[0])
    for _ in range(1, n // 2):
        up, down = lax.ppermute(up, axis, up_pairs), lax.ppermute(down, axis, down_pairs)
        out += [up, down]
    up, down = after(up[:half], *hold), after(down[half:], *hold)
    return out + [lax.ppermute(up, axis, up_pairs), lax.ppermute(down, axis, down_pairs)]


def ring_sum(parts, axis, order, hold=(), tail=0):
    n = len(order)
    up_pairs, down_pairs = ring_pairs(order, 1), ring_pairs(order, -1)
    low, high = lax.ppermute(parts[n - 1], axis, down_pairs), lax.ppermute(parts[n], axis, up_pairs)
    sent = ()
    for step in range(n // 2 - 1, 0, -1):
        sent = pass_on(parts[2 * step - 1], parts[2 * step], after(low, *hold), high, tail)
        low, high = lax.ppermute(sent[0], axis, down_pairs), lax.ppermute(sent[1], axis, up_pairs)
    return [parts[0], low, high], sent


def in_two(values):
    first = values.astype(BF)
    return first, (values - first.astype(F32)).astype(BF)


def add_rows(part, arrived, tail):
    total = part.astype(F32) + arrived.astype(F32)
    if not tail:
        return total.astype(BF)
    cut, half = total.shape[0] - tail, tail // 2
    values = total[cut : cut + half, :] + total[cut + half :, :]
    return jnp.concatenate([total[:cut, :].astype(BF), *in_two(values)], 0)


def pass_on_kernel(tail, low_part_ref, high_part_ref, low_ref, high_ref, to_low_ref, to_high_ref):
    rows = low_part_ref.shape[0]
    cut = low_ref.shape[0]
    if cut < rows:
        to_low_ref[0:cut, :] = add_rows(low_part_ref[0:cut, :], low_ref[...], 0)
        to_low_ref[cut:, :] = low_part_ref[cut:, :]
        to_high_ref[0:cut, :] = high_part_ref[0:cut, :]
        to_high_ref[cut:, :] = add_rows(high_part_ref[cut:, :], high_ref[...], tail)
    else:
        to_low_ref[...] = add_rows(low_part_ref[...], low_ref[...], tail)
        to_high_ref[...] = add_rows(high_part_ref[...], high_ref[...], tail)


def pass_on(low_part, high_part, low, high, tail):
    rows, columns = low_part.shape
    wide = math.gcd(columns, 512)

    def block(array):
        return pl.BlockSpec((array.shape[0], wide), lambda i: (0, i))

    arrays = [low_part, high_part, low, high]
    return pl.pallas_call(
        partial(pass_on_kernel, tail),
        grid=(columns // wide,),
        in_specs=[block(array) for array in arrays],
        out_specs=[block(low_part)] * 2,
        out_shape=[jax.ShapeDtypeStruct((rows, columns), BF)] * 2,
        cost_estimate=cost(2 * rows * columns, 12 * rows * columns),
        name="pass_on",
    )(*arrays)


def swap(value):
    return lax.ppermute(value, "core", [(0, 1), (1, 0)])


def turn(values, cosine, sine_a, sine_b):
    width = values.shape[1]
    cosine, sine_a, sine_b = (jnp.concatenate([v] * (width // 128), 1) for v in (cosine, sine_a, sine_b))
    return (
        values * cosine
        + pltpu.roll(values, width - ROT // 2, 1) * sine_a
        + pltpu.roll(values, ROT // 2, 1) * sine_b
    )


def head_mask(shape, head, head_dim):
    lane = lax.broadcasted_iota(jnp.int32, shape, 1)
    return (lane >= head * head_dim) & (lane < (head + 1) * head_dim)


def attend_kernel(heads, head_dim, span, order_ref, qkv_ref, cos_ref, sin_a_ref, sin_b_ref, att_ref, sorted_ref, out_scr):
    seq_len = qkv_ref.shape[1]
    width = heads * head_dim
    for slot in range(seq_len // span):
        rows = pl.ds(pl.multiple_of(order_ref[slot] * span, span), span)
        here = pl.ds(slot * span, span)
        tables = (cos_ref[here, :], sin_a_ref[here, :], sin_b_ref[here, :])
        query = turn(qkv_ref[0, rows, 0:width], *tables).astype(BF)
        sorted_ref[0, here, 0:width] = (query.astype(F32) * (head_dim**-0.5)).astype(BF)
        sorted_ref[0, here, width : 2 * width] = turn(qkv_ref[0, rows, width : 2 * width], *tables).astype(BF)
        sorted_ref[0, here, 2 * width :] = qkv_ref[0, rows, 2 * width :].astype(BF)
    block = min(BLOCK_Q, seq_len)
    for i in range(seq_len // block):
        extent = (i + 1) * block
        here = pl.ds(i * block, block)
        queries = sorted_ref[0, here, 0:width]
        keys = sorted_ref[0, 0:extent, width : 2 * width]
        values = sorted_ref[0, 0:extent, 2 * width :]
        row = lax.broadcasted_iota(jnp.int32, (block, extent), 0) + i * block
        col = lax.broadcasted_iota(jnp.int32, (block, extent), 1)
        total = jnp.zeros((block, width), F32)
        for head in range(heads):
            mask = head_mask((block, width), head, head_dim)
            scores = dot_t(jnp.where(mask, queries, jnp.zeros_like(queries)), keys)
            scores = jnp.where(col <= row, scores, NEG)
            top = jnp.max(scores, 1, keepdims=True)
            weights = jnp.exp(scores - top)
            norm = 1.0 / jnp.sum(weights, 1, keepdims=True)
            probs = (weights * norm).astype(BF)
            total = jnp.where(mask, dot(probs, values), total)
        out_scr[here, :] = total.astype(BF)
    for slot in range(seq_len // span):
        rows = pl.ds(pl.multiple_of(order_ref[slot] * span, span), span)
        att_ref[0, rows, :] = out_scr[slot * span : (slot + 1) * span, :]


def attend_back_kernel(
    heads, head_dim, span, order_ref, kept_a_ref, kept_b_ref, grad_ref, cos_ref, sin_a_ref, sin_b_ref, out_ref, grad_scr, key_scr, value_scr, sorted_ref
):
    seq_len = sorted_ref.shape[1]

    @pl.when(pl.program_id(0) == 0)
    def _():
        sorted_ref[...] = kept_a_ref[...]

    @pl.when(pl.program_id(0) == 1)
    def _():
        sorted_ref[...] = kept_b_ref[...]

    width = heads * head_dim
    for slot in range(seq_len // span):
        rows = pl.ds(pl.multiple_of(order_ref[slot] * span, span), span)
        grad_scr[slot * span : (slot + 1) * span, :] = grad_ref[0, rows, :]
    key_scr[...] = jnp.zeros_like(key_scr)
    value_scr[...] = jnp.zeros_like(value_scr)
    block = min(BLOCK_Q, seq_len)

    def put(slot, first, values):
        rows = pl.ds(pl.multiple_of(order_ref[slot] * span, span), span)
        out_ref[0, rows, first : first + width] = values.astype(BF)

    def tables(here):
        return (cos_ref[here, :], -sin_a_ref[here, :], -sin_b_ref[here, :])

    for i in range(seq_len // block):
        extent = (i + 1) * block
        here = pl.ds(i * block, block)
        queries = sorted_ref[0, here, 0:width]
        grads = grad_scr[here, :]
        keys = sorted_ref[0, 0:extent, width : 2 * width]
        values = sorted_ref[0, 0:extent, 2 * width :]
        key = lax.broadcasted_iota(jnp.int32, (extent, block), 0)
        query = lax.broadcasted_iota(jnp.int32, (extent, block), 1) + i * block
        query_grad = jnp.zeros((block, width), F32)
        for head in range(heads):
            mask = head_mask((block, width), head, head_dim)
            own_queries = jnp.where(mask, queries, jnp.zeros_like(queries))
            own_grads = jnp.where(mask, grads, jnp.zeros_like(grads))
            scores = jnp.where(key <= query, dot_t(keys, own_queries), NEG)
            weights = jnp.exp(scores - jnp.max(scores, 0, keepdims=True))
            probs = weights * (1.0 / jnp.sum(weights, 0, keepdims=True))
            probs_grad = dot_t(values, own_grads)
            delta = jnp.sum(probs * probs_grad, 0, keepdims=True)
            score_grad = (probs * (probs_grad - delta)).astype(BF)
            value_scr[0:extent, :] += dot(probs.astype(BF), own_grads)
            key_scr[0:extent, :] += dot(score_grad, own_queries)
            query_grad = jnp.where(mask, t_dot(score_grad, keys), query_grad)
        query_grad = turn(query_grad * (head_dim**-0.5), *tables(here))
        for j in range(block // span):
            put(i * (block // span) + j, 0, query_grad[j * span : (j + 1) * span])
    for slot in range(seq_len // span):
        here = pl.ds(slot * span, span)
        put(slot, width, turn(key_scr[here, :], *tables(here)))
        put(slot, 2 * width, value_scr[here, :])


def attend(order, qkv, tables, heads, head_dim, span, part):
    seq_len, wide = qkv.shape[0] // 2, qkv.shape[1]
    width = wide // 3
    whole = pl.BlockSpec((seq_len, 128), lambda s, o: (0, 0))
    return pl.pallas_call(
        partial(attend_kernel, heads, head_dim, span),
        grid_spec=pltpu.PrefetchScalarGridSpec(
            num_scalar_prefetch=1,
            grid=(1,),
            in_specs=[pl.BlockSpec((1, seq_len, wide), lambda s, o: (part, 0, 0)), whole, whole, whole],
            out_specs=[
                pl.BlockSpec((1, seq_len, width), lambda s, o: (0, 0, 0)),
                pl.BlockSpec((1, seq_len, wide), lambda s, o: (0, 0, 0)),
            ],
            scratch_shapes=[pltpu.VMEM((seq_len, width), BF)],
        ),
        out_shape=[
            jax.ShapeDtypeStruct((1, seq_len, width), BF),
            jax.ShapeDtypeStruct((1, seq_len, wide), BF),
        ],
        compiler_params=pltpu.CompilerParams(vmem_limit_bytes=40 * 2**20),
        cost_estimate=cost(8 * heads * seq_len * seq_len * head_dim, 8 * seq_len * wide),
        name="attend",
    )(order, qkv.reshape(2, seq_len, wide), *tables)


def attend_back(order, kept, grads, tables, heads, head_dim, span):
    count, (_, seq_len, wide) = len(kept), kept[0].shape
    width = wide // 3
    whole = pl.BlockSpec((seq_len, 128), lambda s, o: (0, 0))
    return pl.pallas_call(
        partial(attend_back_kernel, heads, head_dim, span),
        grid_spec=pltpu.PrefetchScalarGridSpec(
            num_scalar_prefetch=1,
            grid=(count,),
            in_specs=[
                pl.BlockSpec((1, seq_len, wide), lambda s, o: (0, 0, 0)),
                pl.BlockSpec((1, seq_len, wide), lambda s, o: (0, 0, 0)),
                pl.BlockSpec((1, seq_len, width), lambda s, o: (s, 0, 0)),
                whole,
                whole,
                whole,
            ],
            out_specs=pl.BlockSpec((1, seq_len, wide), lambda s, o: (s, 0, 0)),
            scratch_shapes=[
                pltpu.VMEM((seq_len, width), BF),
                pltpu.VMEM((seq_len, width), F32),
                pltpu.VMEM((seq_len, width), F32),
                pltpu.VMEM((1, seq_len, wide), BF),
            ],
        ),
        out_shape=jax.ShapeDtypeStruct((count, seq_len, wide), BF),
        compiler_params=pltpu.CompilerParams(vmem_limit_bytes=40 * 2**20),
        cost_estimate=cost(20 * count * heads * seq_len * seq_len * head_dim, 6 * count * seq_len * wide),
        name="attend_back",
    )(order, *kept, grads, *tables)


def after(value, *others):
    return lax.optimization_barrier((value,) + others)[0]


def whole_block(shape):
    return pl.BlockSpec(shape, lambda *_: (0,) * len(shape))


def params(limit):
    return pltpu.CompilerParams(vmem_limit_bytes=limit * 2**20)


ANYWHERE = pl.BlockSpec(memory_space=pl.ANY)
SCALARS = pl.BlockSpec(memory_space=pltpu.SMEM)
VMEM = pl.BlockSpec(memory_space=pltpu.VMEM)
ROWS = 256


def to_blocks_kernel(n_q, n_t, heads, head_dim, units, at_ref, qkv_ref, up_ref, *out_refs):
    n_z = n_t // 2
    width = heads * head_dim
    core, z = at_ref[0], at_ref[1]
    rows = qkv_ref.shape[0]
    low = lax.broadcasted_iota(jnp.int32, (rows, 128), 1) < head_dim
    per = 128 // head_dim
    for c in range(2):
        for s in range(n_z):
            out_ref = out_refs[s].at[pl.ds(c * rows, rows)]
            t = lax.rem(core + c, 2) * n_z + (z ^ s)
            odd = lax.rem(t, per)
            for which in range(3):
                for j in range(0, heads, per):
                    tiles = []
                    for i in range(per):
                        first = (which * heads + j + i) * n_t * head_dim + (t // per) * 128
                        tile = qkv_ref[:, pl.ds(pl.multiple_of(first, 128), 128)].astype(F32)
                        tiles.append(tile)
                    even = jnp.where(low, tiles[0], pltpu.roll(tiles[1], head_dim, 1))
                    uneven = jnp.where(low, pltpu.roll(tiles[0], head_dim, 1), tiles[1])
                    at = which * width + j * head_dim
                    out_ref[:, at : at + 128] = jnp.where(odd == 0, even, uneven).astype(BF)
            for q in range(n_q):
                at = 3 * width + q * units
                if units % 128 == 0:
                    first = pl.multiple_of((q * n_t + t) * units, 128)
                    out_ref[:, at : at + units] = up_ref[:, pl.ds(first, units)]
                else:
                    for k in range(n_t):

                        @pl.when(t == k)
                        def _(at=at, q=q, k=k):
                            first = (q * n_t + k) * units
                            out_ref[:, at : at + units] = up_ref[:, first : first + units]


def to_blocks(at, qkv, up, n_q, n_t, heads, head_dim, units):
    rows = qkv.shape[0]
    wide = 3 * heads * head_dim + n_q * units
    return pl.pallas_call(
        partial(to_blocks_kernel, n_q, n_t, heads, head_dim, units),
        in_specs=[SCALARS, VMEM, VMEM],
        out_specs=[VMEM] * (n_t // 2),
        out_shape=[jax.ShapeDtypeStruct((2 * rows, wide), BF)] * (n_t // 2),
        compiler_params=params(16),
        cost_estimate=cost(0, 4 * rows * wide * n_t),
        name="to_blocks",
    )(at, qkv, up)


def theirs_kernel(*refs):
    pieces, out_ref = refs[:-1], refs[-1]
    rows = pieces[0].shape[0] // 2
    for s, piece in enumerate(pieces):
        out_ref[s * rows : (s + 1) * rows, :] = piece[rows:, :]


def theirs(pieces):
    rows, columns = pieces[0].shape
    return pl.pallas_call(
        theirs_kernel,
        in_specs=[VMEM] * len(pieces),
        out_specs=VMEM,
        out_shape=jax.ShapeDtypeStruct((len(pieces) * rows // 2, columns), BF),
        compiler_params=params(16),
        cost_estimate=cost(0, 2 * len(pieces) * rows * columns),
        name="theirs",
    )(*pieces)


def piece_rows(came_refs, got_ref, at_ref):
    n_z = len(came_refs)
    rows = came_refs[0].shape[0] // 2
    core, z = at_ref[0], at_ref[1]
    for s in range(n_z):
        yield core * n_z + (z ^ s), came_refs[s][0:rows, :]
        yield (1 - core) * n_z + (z ^ s), got_ref[s * rows : (s + 1) * rows, :]


def stack_rows_kernel(at_ref, *refs):
    out_ref = refs[-1]
    for block, values in piece_rows(refs[:-2], refs[-2], at_ref):
        rows = values.shape[0]
        out_ref[pl.ds(pl.multiple_of(block * rows, 16), rows), :] = values


def stack_rows(at, came, got):
    rows, columns = came[0].shape
    return pl.pallas_call(
        stack_rows_kernel,
        in_specs=[SCALARS] + [VMEM] * (len(came) + 1),
        out_specs=VMEM,
        out_shape=jax.ShapeDtypeStruct((len(came) * rows, columns), BF),
        compiler_params=params(16),
        cost_estimate=cost(0, 4 * len(came) * rows * columns),
        name="stack_rows",
    )(at, *came, got)


def last_sum_kernel(n_z, n_parts, tail, at_ref, *refs):
    part_refs, out_refs = refs[:n_parts], refs[n_parts:]
    n_t = 2 * n_z
    below = 16 if tail else 0
    count = part_refs[0].shape[0] - tail
    rows = count // n_t
    core, z = at_ref[0], at_ref[1]
    if tail:
        total = part_refs[0][count:, :].astype(F32)
        for part_ref in part_refs[1:]:
            total = total + part_ref[count:, :].astype(F32)
        values = total[: tail // 2, :] + total[tail // 2 :, :]
        index = lax.broadcasted_iota(jnp.int32, values.shape, 0)
    for c in range(2):
        for s in range(n_z):
            block = lax.rem(core + c, 2) * n_z + (z ^ s)
            here = pl.ds(pl.multiple_of(block * rows, 16), rows)
            total = part_refs[0][here, :].astype(F32)
            for part_ref in part_refs[1:]:
                total = total + part_ref[here, :].astype(F32)
            first = c * (rows + below)
            out_refs[s][first : first + rows, :] = total.astype(BF)
            if tail:
                own = jnp.sum(jnp.where(index == block, values, 0.0), 0, keepdims=True)
                high, low = in_two(own)
                row = lax.broadcasted_iota(jnp.int32, (below, own.shape[1]), 0)
                both = jnp.where(row == 0, high.astype(F32), jnp.where(row == 1, low.astype(F32), 0.0))
                out_refs[s][first + rows : first + rows + below, :] = both.astype(BF)


def last_sum(at, parts, n_t, tail=0):
    columns = parts[0].shape[1]
    rows = 2 * ((parts[0].shape[0] - tail) // n_t + (16 if tail else 0))
    return pl.pallas_call(
        partial(last_sum_kernel, n_t // 2, len(parts), tail),
        in_specs=[SCALARS] + [VMEM] * len(parts),
        out_specs=[VMEM] * (n_t // 2),
        out_shape=[jax.ShapeDtypeStruct((rows, columns), BF)] * (n_t // 2),
        compiler_params=params(24),
        cost_estimate=cost(0, 8 * rows * n_t * columns),
        name="last_sum",
    )(at, *parts)


def from_blocks_kernel(groups, piece, below, at_ref, *refs):
    came_refs, got_ref, refs = refs[: -3 - (below > 0)], refs[-3 - (below > 0)], refs[-2 - (below > 0) :]
    out_ref, held_ref = refs[0], refs[-1]
    n_t = held_ref.shape[0]
    rows = out_ref.shape[0]
    total = 0.0
    for block, values in piece_rows(came_refs, got_ref, at_ref):
        held_ref[block] = values[0:rows, :]
        if below:
            under = values[rows:, :].astype(F32)
            total = total + under[0:1, :] + under[1:2, :]
    for t in range(n_t):
        for j in range(groups):
            first = (j * n_t + t) * piece
            out_ref[:, first : first + piece] = held_ref[t, :, j * piece : (j + 1) * piece].astype(F32)
    if below:
        refs[1][...] = jnp.broadcast_to(total, refs[1].shape)


def from_blocks(at, came, got, groups, piece, below=0):
    n_t = 2 * len(came)
    rows = came[0].shape[0] // 2 - below
    columns = groups * piece
    return pl.pallas_call(
        partial(from_blocks_kernel, groups, piece, below),
        in_specs=[SCALARS] + [VMEM] * (len(came) + 1),
        out_specs=[VMEM] * (1 + (below > 0)),
        out_shape=[jax.ShapeDtypeStruct((rows, columns * n_t), F32)]
        + [jax.ShapeDtypeStruct((8, columns), F32)] * (below > 0),
        scratch_shapes=[pltpu.VMEM((n_t, rows, columns), BF)],
        compiler_params=params(16),
        cost_estimate=cost(0, 8 * rows * columns * n_t),
        name="from_blocks",
    )(at, *came, got)


def places_kernel(n_q, n_z, q_order, at_ref, table_ref, turns_ref, order_ref):
    q, z = at_ref[2], at_ref[1]
    place = 0
    for i, index in enumerate(q_order):
        place = place + jnp.where(q == index, i, 0)
    for k, offset in enumerate(ring_offsets(n_q)):
        at = lax.rem(place + offset + n_q, n_q)
        turn_of = 0
        for i, index in enumerate(q_order):
            turn_of = turn_of + jnp.where(at == i, index, 0)
        turns_ref[k] = turn_of
    for k, offset in enumerate(ring_offsets(n_z)):
        row = lax.rem(z + offset + n_z, n_z)
        for j in range(2):
            order_ref[table_ref[row, j]] = 2 * k + j


def find_places(at, span_table, n_q, n_z, q_order):
    return pl.pallas_call(
        partial(places_kernel, n_q, n_z, q_order),
        in_specs=[SCALARS, SCALARS],
        out_specs=[SCALARS, SCALARS],
        out_shape=[jax.ShapeDtypeStruct((n_q,), jnp.int32), jax.ShapeDtypeStruct((2 * n_z,), jnp.int32)],
        cost_estimate=cost(0, 1000),
        name="places",
    )(at, span_table)


def pack_small_kernel(*refs):
    out_ref = refs[-1]
    row = 0
    for ref in refs[:-1]:
        size = ref.shape[1]
        for first in range(0, size, 128):
            count = min(128, size - first)
            out_ref[row : row + 1, 0:count] = ref[:, first : first + count].astype(F32).astype(BF)
            row += 1


def pack_small(vectors):
    return pl.pallas_call(
        pack_small_kernel,
        in_specs=[VMEM] * len(vectors),
        out_specs=VMEM,
        out_shape=jax.ShapeDtypeStruct((256, 128), BF),
        cost_estimate=cost(0, 65536),
        name="pack_small",
    )(*[v.reshape(1, -1) for v in vectors])


def pack_vectors_kernel(shape, widths, at_ref, norm_a_ref, norm_b_ref, g_ref, up_ref, out_ref):
    n_q, n_t, heads, head_dim, units = shape
    part, biases = widths
    t_here = at_ref[0] * (n_t // 2) + at_ref[1]
    gain = norm_a_ref[0:1, :] + norm_b_ref[0:1, :]
    shift = norm_a_ref[1:2, :] + norm_b_ref[1:2, :]
    qkv = norm_a_ref[2:3, :] + norm_b_ref[2:3, :]
    g = g_ref[0:1, :]
    up = up_ref[0:1, :]
    columns = out_ref.shape[2]
    for q in range(n_q):
        lines = []
        for t in range(n_t):
            owner = q * n_t + t
            here = slice(owner * part, (owner + 1) * part)
            cells = [gain[:, here], shift[:, here], g[:, here]]
            first, end = owner * biases, (owner + 1) * biases
            while first < end:
                which, head = first // (HEADS * head_dim), first // head_dim % HEADS
                stop = min(end, (first // head_dim + 1) * head_dim)
                source = (which * heads + head // n_t) * head_dim + first % head_dim
                cells.append(jnp.where(t_here == head % n_t, qkv[:, source : source + stop - first], 0.0))
                first = stop
            cells.append(jnp.where(t_here == t, up[:, q * units : (q + 1) * units], 0.0))
            used = 3 * part + biases + units
            cells.append(jnp.zeros((1, columns - used), F32))
            lines.append(jnp.concatenate(cells, 1))
        high, low = in_two(jnp.concatenate(lines, 0))
        out_ref[q, 0:n_t, :] = high
        out_ref[q, n_t:, :] = low


def pack_vectors(at, norm_a, norm_b, g, up, shape, widths, columns):
    n_q, n_t = shape[:2]
    return pl.pallas_call(
        partial(pack_vectors_kernel, shape, widths),
        in_specs=[SCALARS] + [VMEM] * 4,
        out_specs=VMEM,
        out_shape=jax.ShapeDtypeStruct((n_q, 2 * n_t, columns), BF),
        cost_estimate=cost(0, 4 * n_q * n_t * columns),
        name="pack_vectors",
    )(at, norm_a, norm_b, g, up)


def load_pieces(plan, turns_ref, piece_refs, target, sem):
    copies = []
    for i, (piece, first, rows, slot, scale, base) in enumerate(plan):
        start = pl.multiple_of(turns_ref[slot] * scale + base, 16)
        copies.append(pltpu.make_async_copy(piece_refs[piece].at[pl.ds(first, rows)], target.at[pl.ds(start, rows)], sem.at[i]))
    return copies


def fetch_slots(plan, slot_refs, buffers, sems):
    i = pl.program_id(0)

    def copies(k):
        return [
            pltpu.make_async_copy(slot_refs[which], buffers.at[k % 2, pl.ds(first, rows)], sems.at[k % 2, part])
            for part, (which, first, rows) in enumerate(plan[k])
        ]

    for k in range(len(plan)):

        @pl.when(i == k)
        def _(k=k):
            for copy in (copies(0) if k == 0 else []) + (copies(k + 1) if k + 1 < len(plan) else []):
                copy.start()
            for copy in copies(k):
                copy.wait()


class Gathered:
    def __init__(self, arrays, plan, turns):
        self.arrays = arrays
        self.plan = tuple(plan)
        self.starts = turns
        self.rows = sum(piece[2] for piece in plan)
        self.columns = arrays[0].shape[1]

    def scratch(self):
        return [pltpu.VMEM((self.rows, self.columns), BF), pltpu.SemaphoreType.DMA((len(self.plan),))]

    def specs(self):
        return [ANYWHERE] * len(self.arrays)


def put_block(plan, block, held_ref, out_refs, sem):
    i = pl.program_id(0)
    held_ref[i] = block

    def copies(k):
        return [
            pltpu.make_async_copy(held_ref.at[k, pl.ds(first, rows)], out_refs[which], sem.at[which])
            for which, first, rows in plan[k]
        ]

    for k in range(len(plan)):

        @pl.when(i == k)
        def _(k=k):
            for copy in copies(k):
                copy.start()

    @pl.when(i == len(plan) - 1)
    def _():
        for k in range(len(plan)):
            for copy in copies(k):
                copy.wait()


def normed(rows):
    mean = jnp.mean(rows, -1, keepdims=True)
    centred = rows - mean
    scale = lax.rsqrt(jnp.mean(centred * centred, -1, keepdims=True) + EPS)
    return centred * scale, scale


def project_kernel(split, x_plan, n_x, w_plan, n_w, starts_ref, *refs):
    x_refs, refs = refs[:n_x], refs[n_x:]
    w_refs, refs = refs[:n_w], refs[n_w:]
    gain_ref, shift_ref, b_ref, x_out_ref, hidden_ref, qkv_ref, act_ref, slope_ref, w_ref, w_sem, x_buf, x_sem = refs

    @pl.when(pl.program_id(0) == 0)
    def _():
        for copy in load_pieces(w_plan, starts_ref, w_refs, w_ref, w_sem):
            copy.start()

    fetch_slots(x_plan, x_refs, x_buf, x_sem)
    x = x_buf[lax.rem(pl.program_id(0), 2)]
    x_out_ref[...] = x
    xhat, _ = normed(x.astype(F32))
    hidden = (xhat * gain_ref[...] + shift_ref[...]).astype(BF)
    hidden_ref[...] = hidden

    @pl.when(pl.program_id(0) == 0)
    def _():
        for copy in load_pieces(w_plan, starts_ref, w_refs, w_ref, w_sem):
            copy.wait()

    pre = dot(hidden, w_ref[:, split:]) + b_ref[:, split:]
    root = math.sqrt(2.0 / math.pi)
    square = pre * pre
    turned = jnp.tanh(root * pre * (1.0 + 0.044715 * square))
    act_ref[...] = (0.5 * pre * (1.0 + turned)).astype(BF)
    slope = 0.5 * (1.0 + turned) + 0.5 * pre * (1.0 - turned * turned) * (root * (1.0 + 3 * 0.044715 * square))
    slope_ref[...] = slope.astype(BF)
    qkv_ref[...] = dot(hidden, w_ref[:, :split]) + b_ref[:, :split]


def project(x_arrays, x_plan, gain, shift, w, b, split):
    rows, width = x_arrays[0].shape
    count = rows * len(x_plan)
    wide = w.columns

    def block(columns):
        return pl.BlockSpec((rows, columns), lambda i, s: (i, 0))

    return pl.pallas_call(
        partial(project_kernel, split, x_plan, len(x_arrays), w.plan, len(w.arrays)),
        grid_spec=pltpu.PrefetchScalarGridSpec(
            num_scalar_prefetch=1,
            grid=(len(x_plan),),
            in_specs=[ANYWHERE] * len(x_arrays) + w.specs() + [whole_block((1, width))] * 2 + [whole_block(b.shape)],
            out_specs=[block(width), block(width), block(split), block(wide - split), block(wide - split)],
            scratch_shapes=w.scratch() + [pltpu.VMEM((2, rows, width), BF), pltpu.SemaphoreType.DMA((2, 2))],
        ),
        out_shape=[
            jax.ShapeDtypeStruct((count, width), BF),
            jax.ShapeDtypeStruct((count, width), BF),
            jax.ShapeDtypeStruct((count, split), F32),
            jax.ShapeDtypeStruct((count, wide - split), BF),
            jax.ShapeDtypeStruct((count, wide - split), BF),
        ],
        compiler_params=params(36),
        cost_estimate=cost(2 * count * width * wide, 8 * count * width + 2 * width * wide),
        name="project",
    )(w.starts, *x_arrays, *w.arrays, gain, shift, b)


def combine_kernel(split, w_plan, n_w, plan, n_arrived, starts_ref, act_ref, att_ref, *refs):
    w_refs, refs = refs[:n_w], refs[n_w:]
    arrived_refs, refs = refs[:n_arrived], refs[n_arrived:]
    out_refs, (w_ref, w_sem, held, held_sem, buf, buf_sem) = refs[:-6], refs[-6:]

    @pl.when(pl.program_id(0) == 0)
    def _():
        copies = load_pieces(w_plan, starts_ref, w_refs, w_ref, w_sem)
        for copy in copies:
            copy.start()
        for copy in copies:
            copy.wait()

    total = dot(act_ref[...], w_ref[:split, :]) + dot(att_ref[...], w_ref[split:, :])
    if n_arrived:
        fetch_slots([((k, 0, total.shape[0]),) for k in range(n_arrived)], arrived_refs, buf, buf_sem)
        total = total + buf[lax.rem(pl.program_id(0), 2)].astype(F32)
    put_block(plan, total.astype(BF), held, out_refs, held_sem)


def held_blocks(steps, rows, width):
    return [pltpu.VMEM((steps, rows, width), BF), pltpu.SemaphoreType.DMA((steps + 1,))]


def combine(act, att, w, part, rows, arrived=()):
    count, split = act.shape[0] // 2, act.shape[1]
    own_width = att.shape[-1]
    att = att.reshape(count, own_width)
    width = w.columns
    steps = count // rows
    base = part * steps
    plan = slot_plan(steps, rows) if arrived else [((k, 0, rows),) for k in range(steps)]
    shapes = [jax.ShapeDtypeStruct((r, width), BF) for slot in plan for _, _, r in slot]
    return pl.pallas_call(
        partial(combine_kernel, split, w.plan, len(w.arrays), plan, len(arrived)),
        grid_spec=pltpu.PrefetchScalarGridSpec(
            num_scalar_prefetch=1,
            grid=(steps,),
            in_specs=[
                pl.BlockSpec((rows, split), lambda i, s: (i + base, 0)),
                pl.BlockSpec((rows, own_width), lambda i, s: (i, 0)),
            ]
            + w.specs()
            + [ANYWHERE] * len(arrived),
            out_specs=[ANYWHERE] * len(shapes),
            scratch_shapes=w.scratch()
            + held_blocks(steps, rows, width)
            + [pltpu.VMEM((2, rows, width), BF), pltpu.SemaphoreType.DMA((2, 2))],
        ),
        out_shape=shapes,
        compiler_params=params(32),
        cost_estimate=cost(2 * count * width * w.rows, 4 * count * width + 2 * width * w.rows),
        name="combine",
    )(w.starts, act, att, *w.arrays, *arrived)


def combine_back_kernel(split, g_plan, n_g, w_plan, n_w, starts_ref, *refs):
    g_refs, refs = refs[:n_g], refs[n_g:]
    w_refs, refs = refs[:n_w], refs[n_w:]
    slope_ref, g_out_ref, pre_grad_ref, att_grad_ref, sums_ref, w_ref, w_sem, g_buf, g_sem = refs

    @pl.when(pl.program_id(0) == 0)
    def _():
        for copy in load_pieces(w_plan, starts_ref, w_refs, w_ref, w_sem):
            copy.start()

    fetch_slots(g_plan, g_refs, g_buf, g_sem)

    @pl.when(pl.program_id(0) == 0)
    def _():
        for copy in load_pieces(w_plan, starts_ref, w_refs, w_ref, w_sem):
            copy.wait()

    grad = g_buf[lax.rem(pl.program_id(0), 2)]
    g_out_ref[...] = grad

    @pl.when(pl.program_id(0) == 0)
    def _():
        sums_ref[...] = jnp.zeros_like(sums_ref)
        sums_ref[0:1, :] = jnp.sum(grad.astype(F32), 0, keepdims=True)

    pre_grad_ref[...] = (dot_t(grad, w_ref[:split, :]) * slope_ref[...].astype(F32)).astype(BF)
    att_grad_ref[...] = dot_t(grad, w_ref[split:, :]).astype(BF)


def combine_back(g_arrays, g_plan, w, slope):
    rows, width = g_arrays[0].shape
    count = rows * len(g_plan)
    split = slope.shape[1]
    rest = w.rows - split

    def block(columns):
        return pl.BlockSpec((rows, columns), lambda i, s: (i, 0))

    return pl.pallas_call(
        partial(combine_back_kernel, split, g_plan, len(g_arrays), w.plan, len(w.arrays)),
        grid_spec=pltpu.PrefetchScalarGridSpec(
            num_scalar_prefetch=1,
            grid=(len(g_plan),),
            in_specs=[ANYWHERE] * len(g_arrays) + w.specs() + [block(split)],
            out_specs=[block(width), block(split), block(rest), whole_block((8, width))],
            scratch_shapes=w.scratch() + [pltpu.VMEM((2, rows, width), BF), pltpu.SemaphoreType.DMA((2, 2))],
        ),
        out_shape=[
            jax.ShapeDtypeStruct((count, width), BF),
            jax.ShapeDtypeStruct((count, split), BF),
            jax.ShapeDtypeStruct((count, rest), BF),
            jax.ShapeDtypeStruct((8, width), F32),
        ],
        compiler_params=params(32),
        cost_estimate=cost(2 * count * width * w.rows, 6 * count * width + 2 * width * w.rows),
        name="combine_back",
    )(w.starts, *g_arrays, *w.arrays, slope)


def project_back_kernel(split, w_plan, n_w, plan, n_arrived, starts_ref, qkv_grad_ref, pre_grad_ref, x_ref, *refs):
    w_refs, refs = refs[:n_w], refs[n_w:]
    arrived_refs, refs = refs[:n_arrived], refs[n_arrived:]
    out_refs, (sums_ref, w_ref, w_sem, held, held_sem, buf, buf_sem) = refs[:-7], refs[-7:]

    @pl.when(pl.program_id(0) == 0)
    def _():
        copies = load_pieces(w_plan, starts_ref, w_refs, w_ref, w_sem)
        for copy in copies:
            copy.start()
        sums_ref[...] = jnp.zeros_like(sums_ref)
        for copy in copies:
            copy.wait()

    grad = dot_t(qkv_grad_ref[...], w_ref[:, :split]) + dot_t(pre_grad_ref[...], w_ref[:, split:])
    xhat, _ = normed(x_ref[...].astype(F32))
    sums_ref[0:1, :] += jnp.sum(grad * xhat, 0, keepdims=True)
    sums_ref[1:2, :] += jnp.sum(grad, 0, keepdims=True)
    sums_ref[2:3, 0:split] += jnp.sum(qkv_grad_ref[...].astype(F32), 0, keepdims=True)
    if n_arrived:
        fetch_slots([((k, 0, grad.shape[0]),) for k in range(n_arrived)], arrived_refs, buf, buf_sem)
        grad = grad + buf[lax.rem(pl.program_id(0), 2)].astype(F32)
    put_block(plan, grad.astype(BF), held, out_refs, held_sem)


def project_back(qkv_grad, pre_grad, w, x, part, rows, arrived=()):
    count, width = x.shape[0] // 2, x.shape[1]
    split = qkv_grad.shape[1]
    steps = count // rows
    base = part * steps
    plan = slot_plan(steps, rows) if arrived else [((k, 0, rows),) for k in range(steps)]
    shapes = [jax.ShapeDtypeStruct((r, width), BF) for slot in plan for _, _, r in slot]

    def block(columns):
        return pl.BlockSpec((rows, columns), lambda i, s: (i + base, 0))

    *out, sums = pl.pallas_call(
        partial(project_back_kernel, split, w.plan, len(w.arrays), plan, len(arrived)),
        grid_spec=pltpu.PrefetchScalarGridSpec(
            num_scalar_prefetch=1,
            grid=(steps,),
            in_specs=[block(split), block(pre_grad.shape[1]), block(width)] + w.specs() + [ANYWHERE] * len(arrived),
            out_specs=[ANYWHERE] * len(shapes) + [whole_block((8, width))],
            scratch_shapes=w.scratch()
            + held_blocks(steps, rows, width)
            + [pltpu.VMEM((2, rows, width), BF), pltpu.SemaphoreType.DMA((2, 2))],
        ),
        out_shape=shapes + [jax.ShapeDtypeStruct((8, width), F32)],
        compiler_params=params(36),
        cost_estimate=cost(2 * count * width * w.columns, 6 * count * width + 2 * width * w.columns),
        name="project_back",
    )(w.starts, qkv_grad, pre_grad, x, *w.arrays, *arrived)
    return out, sums


def weight_grad_kernel(with_tail, turns_ref, left_ref, right_ref, *refs):
    tail_refs, refs = refs[:with_tail], refs[with_tail:]
    out_refs, (sums_ref, held, sem) = refs[:-3], refs[-3:]

    @pl.when(pl.program_id(0) == 0)
    def _():
        sums_ref[...] = jnp.zeros_like(sums_ref)
        sums_ref[0:1, :] = jnp.sum(right_ref[...].astype(F32), 0, keepdims=True)

    block = t_dot(left_ref[...], right_ref[...]).astype(BF)
    if with_tail:
        block = jnp.concatenate([block, tail_refs[0][0]], 0)
    put_block(slot_plan(held.shape[0], held.shape[1]), block, held, out_refs, sem)


def slot_shapes(n, rows, columns):
    return [jax.ShapeDtypeStruct((r, columns), BF) for slot in slot_plan(n, rows) for _, _, r in slot]


def weight_grad(turns, left, right, tail=None):
    n_q = turns.shape[0]
    count, wide = left.shape
    columns = right.shape[1]
    part = wide // n_q
    rows = part + (0 if tail is None else tail.shape[1])
    extra = [] if tail is None else [tail]
    shapes = slot_shapes(n_q, rows, columns)
    *out, sums = pl.pallas_call(
        partial(weight_grad_kernel, len(extra)),
        grid_spec=pltpu.PrefetchScalarGridSpec(
            num_scalar_prefetch=1,
            grid=(n_q,),
            in_specs=[pl.BlockSpec((count, part), lambda k, s: (0, s[k])), whole_block(right.shape)]
            + [pl.BlockSpec((1,) + v.shape[1:], lambda k, s: (s[k], 0, 0)) for v in extra],
            out_specs=[ANYWHERE] * len(shapes) + [whole_block((8, columns))],
            scratch_shapes=held_blocks(n_q, rows, columns),
        ),
        out_shape=shapes + [jax.ShapeDtypeStruct((8, columns), F32)],
        compiler_params=params(40),
        cost_estimate=cost(2 * count * wide * columns, 2 * count * (wide + columns) + 2 * wide * columns),
        name="weight_grad",
    )(turns, left, right, *extra)
    return out, sums


def down_grad_kernel(head_rows, turns_ref, act_ref, att_a_ref, att_b_ref, g_ref, *refs):
    out_refs, (heads_ref, held, sem) = refs[:-3], refs[-3:]
    units = act_ref.shape[1]
    k = pl.program_id(0)

    @pl.when(k == 0)
    def _():
        half = att_a_ref.shape[0]
        heads_ref[...] = (t_dot(att_a_ref[...], g_ref[0:half, :]) + t_dot(att_b_ref[...], g_ref[half:, :])).astype(BF)

    rows = pl.ds(pl.multiple_of(turns_ref[k] * head_rows, head_rows), head_rows)
    block = jnp.concatenate([t_dot(act_ref[...], g_ref[...]).astype(BF), heads_ref[rows, :]], 0)
    put_block(slot_plan(held.shape[0], held.shape[1]), block, held, out_refs, sem)


def down_grad(turns, act, att, g, head_rows):
    n_q = turns.shape[0]
    count, wide = act.shape
    own_width = att[0].shape[-1]
    att = [a.reshape(count // 2, own_width) for a in att]
    width = g.shape[1]
    units = wide // n_q
    if not head_rows:
        whole = t_dot(act, g).astype(BF).reshape(n_q, units, width)[turns]
        blocks = [whole[k][first : first + r] for k, slot in enumerate(slot_plan(n_q, units)) for _, first, r in slot]
        return blocks, t_dot(jnp.concatenate(att, 0), g)
    out = pl.pallas_call(
        partial(down_grad_kernel, head_rows),
        grid_spec=pltpu.PrefetchScalarGridSpec(
            num_scalar_prefetch=1,
            grid=(n_q,),
            in_specs=[pl.BlockSpec((count, units), lambda k, s: (0, s[k]))] + [whole_block(v.shape) for v in (*att, g)],
            out_specs=[ANYWHERE] * (n_q + 1),
            scratch_shapes=[pltpu.VMEM((own_width, width), BF)] + held_blocks(n_q, units + head_rows, width),
        ),
        out_shape=slot_shapes(n_q, units + head_rows, width),
        compiler_params=params(40),
        cost_estimate=cost(2 * count * (wide + own_width) * width, 2 * count * (wide + width) + 2 * wide * width),
        name="down_grad",
    )(turns, act, *att, g)
    return list(out), None


def finish_kernel(x_ref, g_ref, gain_ref, *refs):
    part_refs, out_ref = refs[:-1], refs[-1]
    grad = part_refs[0][...].astype(F32)
    for part_ref in part_refs[1:]:
        grad = grad + part_ref[...].astype(F32)
    xhat, scale = normed(x_ref[...].astype(F32))
    m = grad * gain_ref[...]
    x_grad = (m - jnp.mean(m, -1, keepdims=True) - xhat * jnp.mean(m * xhat, -1, keepdims=True)) * scale
    out_ref[...] = (g_ref[...].astype(F32) + x_grad).astype(BF)


def finish(parts, x, g, gain):
    count, width = x.shape
    rows = math.gcd(count, 64)
    block = pl.BlockSpec((rows, width), lambda i: (i, 0))
    return pl.pallas_call(
        finish_kernel,
        grid=(count // rows,),
        in_specs=[block] * 2 + [whole_block((1, width))] + [block] * len(parts),
        out_specs=block,
        out_shape=jax.ShapeDtypeStruct((count, width), BF),
        cost_estimate=cost(20 * count * width, 12 * count * width),
        name="finish",
    )(x, g, gain, *parts)


def output_kernel(x_ref, bias_ref, *refs):
    part_refs, out_ref = refs[:-1], refs[-1]
    total = x_ref[...].astype(F32) + bias_ref[...]
    for part_ref in part_refs:
        total = total + part_ref[...].astype(F32)
    out_ref[...] = total.astype(BF)


def output_sum(x, bias, parts):
    count, width = x.shape
    rows = math.gcd(count, 64)
    block = pl.BlockSpec((rows, width), lambda i: (i, 0))
    return pl.pallas_call(
        output_kernel,
        grid=(count // rows,),
        in_specs=[block, whole_block((1, width))] + [block] * len(parts),
        out_specs=block,
        out_shape=jax.ShapeDtypeStruct((count, width), BF),
        cost_estimate=cost(4 * count * width, 10 * count * width),
        name="output_sum",
    )(x, bias, *parts)


def split_sum(parts, cuts):
    count, width = parts[0].shape
    wide = math.gcd(width, 512)
    ends = [sum(cuts[: i + 1]) for i in range(len(cuts))]

    def kernel(*refs):
        part_refs, out_refs = refs[: len(parts)], refs[len(parts) :]
        total = part_refs[0][...].astype(F32)
        for part_ref in part_refs[1:]:
            total = total + part_ref[...].astype(F32)
        for end, rows, out_ref in zip(ends, cuts, out_refs):
            out_ref[...] = total[end - rows : end, :]

    return pl.pallas_call(
        kernel,
        grid=(width // wide,),
        in_specs=[pl.BlockSpec((count, wide), lambda i: (0, i))] * len(parts),
        out_specs=[pl.BlockSpec((rows, wide), lambda i: (0, i)) for rows in cuts],
        out_shape=[jax.ShapeDtypeStruct((rows, width), F32) for rows in cuts],
        cost_estimate=cost(4 * count * width, 12 * count * width),
        name="split_sum",
    )(*parts)


def tables_kernel(head_dim, cos_ref, sin_a_ref, sin_b_ref):
    rows = cos_ref.shape[0]
    half = ROT // 2
    lane = lax.broadcasted_iota(jnp.int32, (1, 128), 1) % head_dim
    step = (lane % half).astype(F32) * (-2.0 * math.log(10000.0) / ROT)
    freqs = jnp.where(lane < ROT, jnp.exp(step), 0.0)
    position = lax.broadcasted_iota(jnp.int32, (rows, 128), 0) + pl.program_id(0) * rows
    angles = position.astype(F32) * freqs
    cosine, sine = jnp.cos(angles), jnp.sin(angles)
    cos_ref[...] = cosine
    sin_a_ref[...] = jnp.where(lane < half, -sine, 0.0)
    sin_b_ref[...] = jnp.where((lane >= half) & (lane < ROT), sine, 0.0)


def rotary_tables(seq_len, head_dim):
    width = 128
    block = pl.BlockSpec((128, width), lambda i: (i, 0))
    return pl.pallas_call(
        partial(tables_kernel, head_dim),
        grid=(seq_len // 128,),
        out_specs=[block] * 3,
        out_shape=[jax.ShapeDtypeStruct((seq_len, width), F32)] * 3,
        cost_estimate=cost(100 * seq_len * width, 12 * seq_len * width),
        name="rotary_tables",
    )()


def per_device(
    inputs,
    span_table,
    ln_gain,
    ln_bias,
    qkv_weight,
    qkv_bias,
    out_weight,
    out_bias,
    fc1_weight,
    fc1_bias,
    fc2_weight,
    fc2_bias,
    cotangent,
):
    rows, width = inputs.shape
    head_dim = width // HEADS
    n_q, n_z = lax.axis_size("q"), lax.axis_size("ctx")
    n_t = 2 * n_z
    n_all = n_q * n_t
    q, core, z = lax.axis_index("q"), lax.axis_index("core"), lax.axis_index("ctx")
    t = core * n_z + z
    at = jnp.stack([core, z, q]).astype(jnp.int32)
    span = rows // 2
    seq_len = rows * n_z
    heads = HEADS // n_t
    own_width = heads * head_dim
    split = 3 * own_width
    units = fc2_weight.shape[0]
    own_units = units * n_q
    d_rows = qkv_weight.shape[0]
    every = ("q", "core", "ctx")
    z_order = list(range(n_z))
    q_order = [0, 1, 3, 2] if n_q == 4 else list(range(n_q))
    turns, order = find_places(at, span_table, n_q, n_z, q_order)
    whole_heads = out_weight.shape[0] == head_dim

    tables = rotary_tables(seq_len, head_dim)

    owned = [ln_gain, ln_bias, out_bias, fc2_bias, qkv_bias, fc1_bias]
    small = lax.all_gather(pack_small(owned), every, axis=0, tiled=True)

    came = scattered(to_blocks(at, qkv_weight, fc1_weight, n_q, n_t, heads, head_dim, units), "ctx")
    w2_block = jnp.concatenate([fc2_weight, out_weight], 0) if whole_heads else fc2_weight
    w2_arrays = ring_gathered(w2_block, "q", q_order)
    plan = []
    for slot, pieces in enumerate(slot_plan(n_q, w2_block.shape[0])):
        for which, first, count in pieces:
            if first < units:
                plan.append((which, 0, min(first + count, units) - first, slot, units, first))
            if first + count > units:
                begin = max(first, units)
                plan.append((which, begin - first, first + count - begin, slot, head_dim, own_units + begin - units))
    w2_sent = w2_arrays[1:]
    if not whole_heads:
        w_out = lax.all_gather(out_weight, every, axis=0, tiled=True).reshape(heads, n_t, head_dim, width)
        w2_arrays = w2_arrays + [lax.dynamic_index_in_dim(w_out, t, 1, False).reshape(own_width, width)]
        plan.append((len(w2_arrays) - 1, 0, own_width, 0, 0, own_units))
    w2 = Gathered(w2_arrays, plan, turns)

    got = swap(theirs([after(came[0], *w2_sent[:-2], turns, order)] + came[1:]))
    w1_block = stack_rows(at, came, got)
    w1_arrays = ring_gathered(w1_block, "q", q_order)
    block_rows = n_t * d_rows
    w1_plan = [
        (which, 0, count, slot, block_rows, first)
        for slot, pieces in enumerate(slot_plan(n_q, block_rows))
        for which, first, count in pieces
    ]
    w1 = Gathered(w1_arrays, w1_plan, turns)

    token_plan = slot_plan(n_z, rows) + slot_plan(n_z, rows, n_z + 1)
    x_line = ring_gathered(after(inputs, *w2_sent[:-2]), "ctx", z_order, w1_arrays[1:-2])
    x_arrays = x_line + [swap(p) for p in x_line[:-2]] + [swap(after(p, *w1_arrays[-2:])) for p in x_line[-2:]]

    small = after(small, *x_line[-2:])
    small = small.reshape(n_all, 256, 128)[:, :16]
    lists, row = [], 0
    for vector in owned:
        used = -(-vector.shape[0] // 128)
        lists.append(small[:, row : row + used].reshape(n_all, used * 128)[:, : vector.shape[0]].astype(F32))
        row += used
    gain, shift, b_out, b_down = (v.reshape(1, width) for v in lists[:4])
    b_qkv = lax.dynamic_index_in_dim(lists[4].reshape(3, heads, n_t, head_dim), t, 2, False).reshape(1, split)
    b_up = lax.dynamic_index_in_dim(lists[5].reshape(n_q, n_t, units), t, 1, False).reshape(1, own_units)
    b_project = jnp.concatenate([b_qkv, b_up], 1)

    x_all, hidden, qkv, act, slope = project(x_arrays, token_plan, gain, shift, w1, b_project, split)
    att_other, kept_other = attend(order, qkv, tables, heads, head_dim, span, 1)
    out_other = combine(act, att_other, w2, 1, rows)
    g_line = ring_gathered(after(cotangent, *x_line[-2:]), "ctx", z_order, out_other)
    att_own, kept_own = attend(order, after(qkv, *out_other, *g_line[1:-2]), tables, heads, head_dim, span, 0)
    out_own = combine(act, att_own, w2, 0, rows, [swap(p) for p in out_other])
    g_arrays = g_line + [swap(p) for p in g_line[:-2]] + [swap(after(p, *out_own)) for p in g_line[-2:]]

    g_all, pre_grad, att_grad, g_sums = combine_back(g_arrays, token_plan, w2, after(slope, *out_own))
    up_own, up_sums = weight_grad(turns, hidden, pre_grad)
    out_parts, out_sent = ring_sum(out_own, "ctx", z_order, up_own)
    att_grad = after(att_grad, *up_own, *out_sent).reshape(2, seq_len, own_width)
    qkv_grad = attend_back(order, (kept_own, kept_other), att_grad, tables, heads, head_dim, span).reshape(2 * seq_len, split)
    up_parts, up_sent = ring_sum(up_own, "q", q_order, [qkv_grad])
    normed_other, sums_other = project_back(after(qkv_grad, *up_sent), pre_grad, w1, x_all, 1, rows)
    down, out_apart = down_grad(turns, after(act, *normed_other, *out_parts[1:]), (att_own, att_other), g_all, head_dim if whole_heads else 0)
    up_came = scattered(last_sum(at, [after(up_parts[0], *down)] + up_parts[1:], n_t), "ctx")
    normed_own, sums_own = project_back(
        after(qkv_grad, *down), pre_grad, w1, x_all, 0, rows, [swap(p) for p in normed_other]
    )
    down_parts, _ = ring_sum(down, "q", q_order, normed_own)
    vectors = pack_vectors(
        at, sums_own, sums_other, g_sums, up_sums, (n_q, n_t, heads, head_dim, units), (d_rows, qkv_bias.shape[0]), split
    )
    qkv_own, _ = weight_grad(turns, after(hidden, *normed_own), qkv_grad, vectors)
    normed_parts, normed_sent = ring_sum([after(p, *up_came[1:]) for p in normed_own], "ctx", z_order, qkv_own)
    qkv_parts, qkv_sent = ring_sum(qkv_own, "q", q_order, normed_sent, 2 * n_t)
    output = output_sum(inputs, b_out + b_down, [after(out_parts[0], *normed_sent)] + out_parts[1:])

    qkv_came = scattered(last_sum(at, qkv_parts, n_t, 2 * n_t), "ctx")
    up_got = swap(theirs([after(up_came[0], *normed_parts[1:], output)] + up_came[1:]))
    (fc1_weight_grad,) = from_blocks(at, up_came, up_got, n_q, units)
    qkv_got = swap(theirs([after(qkv_came[0], up_got)] + qkv_came[1:]))
    qkv_weight_grad, total = from_blocks(at, qkv_came, qkv_got, 3 * heads, head_dim, 16)
    total = total[0]
    if whole_heads:
        fc2_weight_grad, out_weight_grad = split_sum(down_parts, [units, head_dim])
    else:
        (fc2_weight_grad,) = split_sum(down_parts, [units])
        spread = jnp.zeros((heads, n_t, head_dim, width), F32)
        spread = lax.dynamic_update_slice(spread, out_apart.reshape(heads, 1, head_dim, width), (0, t, 0, 0))
        out_weight_grad = lax.psum_scatter(spread.reshape(width, width), every, scatter_dimension=0, tiled=True)

    input_grad = finish(normed_parts, inputs, cotangent, gain)

    cuts = [ln_gain.shape[0], ln_bias.shape[0], out_bias.shape[0], qkv_bias.shape[0], fc1_bias.shape[0]]
    starts = [sum(cuts[:i]) for i in range(len(cuts))]
    gain_grad, shift_grad, bias_grad, qkv_bias_grad, fc1_bias_grad = (total[s : s + c] for s, c in zip(starts, cuts))
    return (
        output,
        input_grad,
        gain_grad,
        shift_grad,
        qkv_weight_grad,
        qkv_bias_grad,
        out_weight_grad,
        bias_grad,
        fc1_weight_grad,
        fc1_bias_grad,
        fc2_weight_grad,
        bias_grad,
    )


def solution(mesh):
    n_dp, n_ctx = mesh.devices.shape
    inner = Mesh(mesh.devices.reshape(n_dp // 2, 2, n_ctx), ("q", "core", "ctx"))
    every = ("q", "core", "ctx")
    matrix, vector = P(every, None), P(every)
    return jax.shard_map(
        per_device,
        mesh=inner,
        in_specs=(
            matrix,
            P(),
            vector,
            vector,
            matrix,
            vector,
            matrix,
            vector,
            matrix,
            vector,
            matrix,
            vector,
            matrix,
        ),
        out_specs=(matrix, matrix, vector, vector, matrix, vector, matrix, vector, matrix, vector, matrix, vector),
        check_vma=False,
    )
```

time: 647 us -> 557 us (0.86)
  waiting for transfers between devices: 243 us -> 153 us
  Pallas kernels: 205 us -> 238 us
  other arithmetic: 19.9 us -> 1.05 us
  between operations: 26.9 us -> 15.2 us
  starting transfers between devices: 81.1 us -> 71.2 us
  local copies, waits for them, and re-layouts: 65.1 us -> 73.2 us
    ppermute x60 -> x45, waiting for transfers between devices: 243 us -> 147 us  [the longest x8 45.5 us: ring_gathered(): lax.ppermute(down, axis, down_pairs)]
    pallas_call x17 -> x26, Pallas kernels: 99.9 us -> 129 us  [the longest x2 31.4 us: project_back(): pl.pallas_call(partial(project_back_kernel, split, w.plan, len(w.arrays),...]
    unnamed x130 -> x204, local copies, waits for them, and re-layouts: 34.4 us -> 54 us
    ppermute x60 -> x45, starting transfers between devices: 78.8 us -> 68 us  [the longest x8 17.4 us: ring_gathered(): lax.ppermute(down, axis, down_pairs)]
    pallas_call x1 -> x2, Pallas kernels: 14.5 us -> 14.8 us  [attend(): pl.pallas_call(partial(attend_kernel, heads, head_dim, span), grid_spec=p...]
    slice x17 -> x9, local copies, waits for them, and re-layouts: 15 us -> 15.2 us  [the longest x8 13.5 us: ring_gathered(): up, down = (after(up[:half], *hold), after(down[half:], *hold))]
  transfers between devices with their start and end apart: 77 -> 67, of which waited for: 22 -> 22; matrix products, arithmetic and copies ran while one was open for 7% -> 3% of each run, Pallas kernels for 28% -> 42%
where the time goes in v3:
time: 557 us; the launch traced here: 551 us
  Pallas kernels  238 us (43%)
  waiting for transfers between devices  153 us (27%)
  local copies, waits for them, and re-layouts  73.2 us (13%)
  starting transfers between devices  71.2 us (13%)
  between operations  15.2 us (3%)
    unnamed x204, local copies, waits for them, and re-layouts  54 us
    ppermute x8, waiting for transfers between devices, ring_gathered(): lax.ppermute(down, axis, down_pairs)  45.5 us
    ppermute x8, waiting for transfers between devices, ring_gathered(): lax.ppermute(up, axis, up_pairs)  32 us
    pallas_call x2, Pallas kernels, project_back(): pl.pallas_call(partial(project_back_kernel, split, w.plan, len(w.arrays),...  31.4 us
    pallas_call x1, Pallas kernels, project(): pl.pallas_call(partial(project_kernel, split, x_plan, len(x_arrays), w.pl...  30.5 us
    pallas_call x2, Pallas kernels, weight_grad(): pl.pallas_call(partial(weight_grad_kernel, len(extra)), grid_spec=pltpu.P...  26.4 us
    pallas_call x1, Pallas kernels, attend_back(): pl.pallas_call(partial(attend_back_kernel, heads, head_dim, span), grid_s...  25.8 us
    ppermute x9, waiting for transfers between devices, across(): return lax.ppermute(value, axis, [(i, i ^ e) for i in range(n)])  25.5 us
  transfers between devices with their start and end apart: 67, of which 22 were waited for; matrix products, arithmetic and copies ran while one was open for 3% of the time, Pallas kernels for 42%

profile of v3, /device:TPU:0, one launch (start us, length us, event | category | flops | bytes accessed | tf_op | source)
XLA Modules:
  0.0 550.9 jit_solution(6044756416235047871)
XLA Ops:
  25.7 15.2 %collective-permute-done.1.refs_2_.refs_12_ = bf16[320,2048]{1,0:T(8,128)(2,1)S(1)} collective-permute-done((bf16[320,2048]{1,0:T(8,128)(2,1)S(1)}, bf16[320,2048]{1,0:T(8,128)(2,1)S(1)}, u32[]{:S(2)}, u32[]{:S(2)}) %collective-permute-start.1) | collective-permute-done | bytes 1310752 | tf_op jit(solution)/shard_map/ppermute | solution.py:71
  42.5 14.4 %collective-permute-done.4.refs_2_ = bf16[128,1792]{1,0:T(8,128)(2,1)} collective-permute-done((bf16[128,1792]{1,0:T(8,128)(2,1)}, bf16[128,1792]{1,0:T(8,128)(2,1)}, u32[]{:S(2)}, u32[]{:S(2)}) %collective-permute-start.4) | collective-permute-done | bytes 458784 | tf_op jit(solution)/shard_map/ppermute | solution.py:39
  68.5 6.8 %collective-permute-start.2 = (bf16[256,2048]{1,0:T(8,128)(2,1)}, bf16[256,2048]{1,0:T(8,128)(2,1)}, u32[]{:S(2)}, u32[]{:S(2)}) collective-permute-start(bf16[256,2048]{1,0:T(8,128)(2,1)} %x_ref.3), channel_id=1, source_target_pairs={{0,1},{1,2},{2,3},{3,0},{4,5},{5,6},{6,7},{7,4},{8,9},{9,10},{10,1... | collective-permute-start | bytes 3145736 | tf_op jit(solution)/shard_map/ppermute | solution.py:71
  75.4 23.2 %collective-permute-done.10.refs_2_ = bf16[256,2048]{1,0:T(8,128)(2,1)} collective-permute-done((bf16[256,2048]{1,0:T(8,128)(2,1)}, bf16[256,2048]{1,0:T(8,128)(2,1)}, u32[]{:S(2)}, u32[]{:S(2)}) %collective-permute-start.10) | collective-permute-done | bytes 1048608 | tf_op jit(solution)/shard_map/ppermute | solution.py:71
  100.5 28.6 %collective-permute-done.2.refs_1_ = bf16[256,2048]{1,0:T(8,128)(2,1)} collective-permute-done((bf16[256,2048]{1,0:T(8,128)(2,1)}, bf16[256,2048]{1,0:T(8,128)(2,1)}, u32[]{:S(2)}, u32[]{:S(2)}) %collective-permute-start.2) | collective-permute-done | bytes 1048608 | tf_op jit(solution)/shard_map/ppermute | solution.py:71
  148.0 7.1 %collective-permute-done.11.refs_4_ = bf16[128,2048]{1,0:T(8,128)(2,1)} collective-permute-done((bf16[128,2048]{1,0:T(8,128)(2,1)}, bf16[128,2048]{1,0:T(8,128)(2,1)}, u32[]{:S(2)}, u32[]{:S(2)}) %collective-permute-start.11) | collective-permute-done | bytes 524320 | tf_op jit(solution)/shard_map/ppermute | solution.py:74
  168.9 30.5 %project.1 = (bf16[2048,2048]{1,0:T(8,128)(2,1)}, bf16[2048,2048]{1,0:T(8,128)(2,1)}, f32[2048,768]{1,0:T(8,128)}, bf16[2048,1024]{1,0:T(8,128)(2,1)}, bf16[2048,1024]{1,0:T(8,128)(2,1)}) custom-call(s32[4]{0:T(128)S(1)} %copy-done.74, bf16[256,2048]{1,0:T(8,128)(2,1)} %x_ref.3, bf16[256,2048]{1,0:T(8,128)(2,1)} %collective-permute-done.2.refs_1_, ...), custom_call_target="tpu_custom_call" | custom-call | flops 15032385 | bytes 40894 | tf_op jit(solution)/shard_map/project/pallas_call | solution.py:712
  202.2 7.4 %attend.2 = (bf16[1,1024,256]{2,1,0:T(8,128)(2,1)S(1)}, bf16[1,1024,768]{2,1,0:T(8,128)(2,1)S(1)}) custom-call(s32[8]{0:T(128)S(1)} %copy-done.79, f32[2,1024,768]{2,1,0:T(8,128)S(1)} %bitcast.38, f32[1024,128]{1,0:T(8,128)S(1)} %copy-done.19, f32[1024,128]{1,0:T(8,128)S(1)} %copy-done.21, f32[1024,128]{1,0:T(8,128)S(1)} %copy-done.23), custom_call_target="tpu_custom_call" | custom-call | flops 2147483 | bytes 6291 | tf_op jit(solution)/shard_map/attend/pallas_call | solution.py:253
  210.9 9.5 %combine.2 = (bf16[256,2048]{1,0:T(8,128)(2,1)S(1)}, bf16[256,2048]{1,0:T(8,128)(2,1)S(1)}, bf16[256,2048]{1,0:T(8,128)(2,1)S(1)}, bf16[256,2048]{1,0:T(8,128)(2,1)S(1)}) custom-call(s32[4]{0:T(128)S(1)} %copy-done.74, bf16[2048,1024]{1,0:T(8,128)(2,1)S(1)} %copy-done.3, bf16[1024,256]{1,0:T(8,128)(2,1)S(1)} %bitcast.42, ...), custom_call_target="tpu_custom_call" | custom-call | flops 5368709 | bytes 13631 | tf_op jit(solution)/shard_map/combine/pallas_call | solution.py:767
  231.1 7.4 %attend.3 = (bf16[1,1024,256]{2,1,0:T(8,128)(2,1)S(1)}, bf16[1,1024,768]{2,1,0:T(8,128)(2,1)S(1)}) custom-call(s32[8]{0:T(128)S(1)} %copy-done.79, f32[2,1024,768]{2,1,0:T(8,128)S(1)} %bitcast.41, f32[1024,128]{1,0:T(8,128)S(1)} %copy-done.19, f32[1024,128]{1,0:T(8,128)S(1)} %copy-done.21, f32[1024,128]{1,0:T(8,128)S(1)} %copy-done.23), custom_call_target="tpu_custom_call" | custom-call | flops 2147483 | bytes 6291 | tf_op jit(solution)/shard_map/attend/pallas_call | solution.py:253
  240.5 10.0 %combine.3 = (bf16[256,2048]{1,0:T(8,128)(2,1)S(1)}, bf16[256,2048]{1,0:T(8,128)(2,1)S(1)}, bf16[256,2048]{1,0:T(8,128)(2,1)S(1)}, bf16[128,2048]{1,0:T(8,128)(2,1)S(1)}, bf16[128,2048]{1,0:T(8,128)(2,1)S(1)}) custom-call(s32[4]{0:T(128)S(1)} %copy-done.74, bf16[2048,1024]{1,0:T(8,128)(2,1)S(1)} %copy-done.3, bf16[1024,256]{1,0:T(8,128)(2,1)S(1)} %bitcast.44, ...), custom_call_target="tpu_custom_call" | custom-call | flops 5368709 | bytes 13631 | tf_op jit(solution)/shard_map/combine/pallas_call | solution.py:767
  257.8 18.1 %combine_back.1 = (bf16[2048,2048]{1,0:T(8,128)(2,1)}, bf16[2048,1024]{1,0:T(8,128)(2,1)S(1)}, bf16[2048,256]{1,0:T(8,128)(2,1)S(1)}, f32[8,2048]{1,0:T(8,128)S(1)}) custom-call(s32[4]{0:T(128)S(1)} %copy-done.74, bf16[256,2048]{1,0:T(8,128)(2,1)S(1)} %copy-done.25, bf16[256,2048]{1,0:T(8,128)(2,1)} %collective-permute-done.21.refs_1_, ...), custom_call_target="tpu_custom_call" | custom-call | flops 10737418 | bytes 30408 | tf_op jit(solution)/shard_map/combine_back/pallas_call | solution.py:828
  277.5 14.6 %weight_grad.2 = (bf16[512,1024]{1,0:T(8,128)(2,1)S(1)}, bf16[512,1024]{1,0:T(8,128)(2,1)S(1)}, bf16[512,1024]{1,0:T(8,128)(2,1)S(1)}, bf16[256,1024]{1,0:T(8,12...) custom-call(s32[4]{0:T(128)S(1)} %copy-done.74, bf16[2048,2048]{1,0:T(8,128)(2,1)} %get-tuple-element.205.left_ref, ...), custom_call_target="tpu_custom_call" | custom-call | flops 8589934 | bytes 16777 | tf_op jit(solution)/shard_map/weight_grad/pallas_call | solution.py:931
  313.7 25.8 %attend_back.1 = bf16[2,1024,768]{2,1,0:T(8,128)(2,1)S(1)} custom-call(s32[8]{0:T(128)S(1)} %copy-done.79, bf16[1,1024,768]{2,1,0:T(8,128)(2,1)S(1)} %copy-done.37, bf16[1,1024,768]{2,1,0:T(8,128)(2,1)S(1)} %copy-done.35, bf16[2,1024,256]{2,1,0:T(8,128)(2,1)S(1)} %bitcast.46, f32[1024,128]{1,0:T(8,128)S(1)} %copy-done.20, f32[1024,128]{1,0:T(8,128)S(1)} %copy-done.22, ...), custom_call_target="tpu_custom_call" | custom-call | flops 10737418 | bytes 9437 | tf_op jit(solution)/shard_map/attend_back/pallas_call | solution.py:279
  339.6 4.2 pass_on.6
  350.4 15.0 %project_back.2 = (bf16[256,2048]{1,0:T(8,128)(2,1)}, bf16[256,2048]{1,0:T(8,128)(2,1)}, bf16[256,2048]{1,0:T(8,128)(2,1)}, bf16[256,2048]{1,0:T(8,128)(2,1)}, f32[8,2048]{1,0:T(8,128)S(1)}) custom-call(s32[4]{0:T(128)S(1)} %copy-done.74, bf16[2048,768]{1,0:T(8,128)(2,1)S(1)} %bitcast.35, bf16[2048,1024]{1,0:T(8,128)(2,1)} %copy-done.2, ...), custom_call_target="tpu_custom_call" | custom-call | flops 7516192 | bytes 19922 | tf_op jit(solution)/shard_map/project_back/pallas_call | solution.py:885
  368.2 17.4 %down_grad.1 = (bf16[320,2048]{1,0:T(8,128)(2,1)S(1)}, bf16[320,2048]{1,0:T(8,128)(2,1)S(1)}, bf16[320,2048]{1,0:T(8,128)(2,1)S(1)}, bf16[160,2048]{1,0:T(8,128)(2,1)S(1)}, bf16[160,2048]{1,0:T(8,128)(2,1)S(1)}) custom-call(s32[4]{0:T(128)S(1)} %copy-done.74, bf16[2048,1024]{1,0:T(8,128)(2,1)S(1)} %copy-done.4, bf16[1024,256]{1,0:T(8,128)(2,1)S(1)} %bitcast.45, ...), custom_call_target="tpu_custom_call" | custom-call | flops 10737418 | bytes 16777 | tf_op jit(solution)/shard_map/down_grad/pallas_call | solution.py:975
  389.9 4.1 collective-permute-start.47
  394.3 16.3 %project_back.3 = (bf16[256,2048]{1,0:T(8,128)(2,1)S(1)}, bf16[256,2048]{1,0:T(8,128)(2,1)S(1)}, bf16[256,2048]{1,0:T(8,128)(2,1)S(1)}, bf16[128,2048]{1,0:T(8,1...) custom-call(s32[4]{0:T(128)S(1)} %copy-done.74, bf16[2048,768]{1,0:T(8,128)(2,1)} %bitcast.36, ...), custom_call_target="tpu_custom_call" | custom-call | flops 7516192 | bytes 19922 | tf_op jit(solution)/shard_map/project_back/pallas_call | solution.py:885
  422.6 11.8 %weight_grad.3 = (bf16[528,768]{1,0:T(8,128)(2,1)S(1)}, bf16[528,768]{1,0:T(8,128)(2,1)S(1)}, bf16[528,768]{1,0:T(8,128)(2,1)S(1)}, bf16[256,768]{1,0:T(8,128)(2...) custom-call(s32[4]{0:T(128)S(1)} %copy-done.74, bf16[2048,2048]{1,0:T(8,128)(2,1)} %get-tuple-element.205.left_ref, ...), custom_call_target="tpu_custom_call" | custom-call | flops 6442450 | bytes 14680 | tf_op jit(solution)/shard_map/weight_grad/pallas_call | solution.py:931
  438.6 5.7 %collective-permute-done.50.high_ref = bf16[128,2048]{1,0:T(8,128)(2,1)} collective-permute-done((bf16[128,2048]{1,0:T(8,128)(2,1)}, bf16[128,2048]{1,0:T(8,128)(2,1)}, u32[]{:S(2)}, u32[]{:S(2)}) %collective-permute-start.50) | collective-permute-done | bytes 524320 | tf_op jit(solution)/shard_map/ppermute | solution.py:80
  444.3 4.1 pass_on.7
  454.0 8.2 %collective-permute-done.53.low_ref = bf16[256,768]{1,0:T(8,128)(2,1)S(1)} collective-permute-done((bf16[256,768]{1,0:T(8,128)(2,1)S(1)}, bf16[256,768]{1,0:T(8,128)(2,1)S(1)}, u32[]{:S(2)}, u32[]{:S(2)}) %collective-permute-start.53) | collective-permute-done | bytes 393248 | tf_op jit(solution)/shard_map/ppermute | solution.py:80
  463.7 13.5 %collective-permute-done.54.high_ref = bf16[272,768]{1,0:T(8,128)(2,1)S(1)} collective-permute-done((bf16[272,768]{1,0:T(8,128)(2,1)S(1)}, bf16[272,768]{1,0:T(8,128)(2,1)S(1)}, u32[]{:S(2)}, u32[]{:S(2)}) %collective-permute-start.54) | collective-permute-done | bytes 417824 | tf_op jit(solution)/shard_map/ppermute | solution.py:80
  483.6 4.2 pass_on.9
  490.5 4.2 output_sum.1
  495.9 6.8 %collective-permute-done.55.refs_1_ = bf16[528,768]{1,0:T(8,128)(2,1)S(1)} collective-permute-done((bf16[528,768]{1,0:T(8,128)(2,1)}, bf16[528,768]{1,0:T(8,128)(2,1)S(1)}, u32[]{:S(2)}, u32[]{:S(2)}) %collective-permute-start.55) | collective-permute-done | bytes 811040 | tf_op jit(solution)/shard_map/ppermute | solution.py:84
  509.5 4.5 collective-permute-done.57.refs_1_
  513.9 6.7 %collective-permute-done.58.refs_2_ = bf16[160,768]{1,0:T(8,128)(2,1)S(1)} collective-permute-done((bf16[160,768]{1,0:T(8,128)(2,1)S(1)}, bf16[160,768]{1,0:T(8,128)(2,1)S(1)}, u32[]{:S(2)}, u32[]{:S(2)}) %collective-permute-start.58) | collective-permute-done | bytes 245792 | tf_op jit(solution)/shard_map/ppermute | solution.py:39
  520.7 6.4 %collective-permute-done.64.refs_1_ = bf16[320,2048]{1,0:T(8,128)(2,1)} collective-permute-done((bf16[320,2048]{1,0:T(8,128)(2,1)}, bf16[320,2048]{1,0:T(8,128)(2,1)}, u32[]{:S(2)}, u32[]{:S(2)}) %collective-permute-start.64) | collective-permute-done | bytes 1310752 | tf_op jit(solution)/shard_map/ppermute | solution.py:84
  527.4 4.3 split_sum.1
  531.6 5.1 finish.1
  (373 shorter events, 174.6 us)
Async XLA Ops:
  7.2 148.0 %all-gather.2.cloned.1.call-start = ((), (), s32[]{:S(2)}) async-start(), calls=%async_computation | async-start | bytes 2162688 | tf_op jit(solution)/shard_map/all_gather | solution.py:1132
  8.6 32.2 %collective-permute-start.1 = (bf16[320,2048]{1,0:T(8,128)(2,1)S(1)}, bf16[320,2048]{1,0:T(8,128)(2,1)S(1)}, u32[]{:S(2)}, u32[]{:S(2)}) collective-permute-start(bf16[320,2048]{1,0:T(8,128)(2,1)S(1)} %constant_dynamic-update-slice_fusion.refs_0_.refs_10_), channel_id=1, source_target_pairs={{0,16},{8,0},{24,8},{16,24},{1,17},{9,1},{25,9},{17,25},{2,18},{10... | collective-permute-start | bytes 3932168 | tf_op jit(solution)/shard_map/ppermute | solution.py:71
  11.7 30.8 %collective-permute-start = (bf16[320,2048]{1,0:T(8,128)(2,1)S(1)}, bf16[320,2048]{1,0:T(8,128)(2,1)}, u32[]{:S(2)}, u32[]{:S(2)}) collective-permute-start(bf16[320,2048]{1,0:T(8,128)(2,1)S(1)} %constant_dynamic-update-slice_fusion.refs_0_.refs_10_), channel_id=1, source_target_pairs={{0,8},{8,24},{24,16},{16,0},{1,9},{9,25},{25,17},{17,1},{2,10},{10... | collective-permute-start | bytes 3932168 | tf_op jit(solution)/shard_map/ppermute | solution.py:71
  21.1 35.7 %collective-permute-start.4 = (bf16[128,1792]{1,0:T(8,128)(2,1)}, bf16[128,1792]{1,0:T(8,128)(2,1)}, u32[]{:S(2)}, u32[]{:S(2)}) collective-permute-start(bf16[128,1792]{1,0:T(8,128)(2,1)} %get-tuple-element.128), channel_id=1, source_target_pairs={{0,2},{1,3},{2,0},{3,1},{4,6},{5,7},{6,4},{7,5},{8,10},{9,11},{10,... | collective-permute-start | bytes 1376264 | tf_op jit(solution)/shard_map/ppermute | solution.py:39
  23.7 33.1 %collective-permute-start.5 = (bf16[128,1792]{1,0:T(8,128)(2,1)}, bf16[128,1792]{1,0:T(8,128)(2,1)}, u32[]{:S(2)}, u32[]{:S(2)}) collective-permute-start(bf16[128,1792]{1,0:T(8,128)(2,1)} %get-tuple-element.129), channel_id=1, source_target_pairs={{0,3},{1,2},{2,1},{3,0},{4,7},{5,6},{6,5},{7,4},{8,11},{9,10},{10,... | collective-permute-start | bytes 1376264 | tf_op jit(solution)/shard_map/ppermute | solution.py:39
  64.0 67.0 %collective-permute-start.8 = (bf16[512,1792]{1,0:T(8,128)(2,1)S(1)}, bf16[512,1792]{1,0:T(8,128)(2,1)S(1)}, u32[]{:S(2)}, u32[]{:S(2)}) collective-permute-start(bf16[512,1792]{1,0:T(8,128)(2,1)S(1)} %stack_rows.1.refs_10_.refs_0_), channel_id=1, source_target_pairs={{0,16},{8,0},{24,8},{16,24},{1,17},{9,1},{25,9},{17,25},{2,18},{10... | collective-permute-start | bytes 5505032 | tf_op jit(solution)/shard_map/ppermute | solution.py:71
  65.5 65.4 %collective-permute-start.7 = (bf16[512,1792]{1,0:T(8,128)(2,1)S(1)}, bf16[512,1792]{1,0:T(8,128)(2,1)S(1)}, u32[]{:S(2)}, u32[]{:S(2)}) collective-permute-start(bf16[512,1792]{1,0:T(8,128)(2,1)S(1)} %stack_rows.1.refs_10_.refs_0_), channel_id=1, source_target_pairs={{0,8},{8,24},{24,16},{16,0},{1,9},{9,25},{25,17},{17,1},{2,10},{10... | collective-permute-start | bytes 5505032 | tf_op jit(solution)/shard_map/ppermute | solution.py:71
  66.0 32.5 %collective-permute-start.10 = (bf16[256,2048]{1,0:T(8,128)(2,1)}, bf16[256,2048]{1,0:T(8,128)(2,1)}, u32[]{:S(2)}, u32[]{:S(2)}) collective-permute-start(bf16[256,2048]{1,0:T(8,128)(2,1)} %x_ref.3), channel_id=1, source_target_pairs={{0,3},{1,0},{2,1},{3,2},{4,7},{5,4},{6,5},{7,6},{8,11},{9,8},{10,9... | collective-permute-start | bytes 3145736 | tf_op jit(solution)/shard_map/ppermute | solution.py:71
  68.5 60.6 %collective-permute-start.2 = (bf16[256,2048]{1,0:T(8,128)(2,1)}, bf16[256,2048]{1,0:T(8,128)(2,1)}, u32[]{:S(2)}, u32[]{:S(2)}) collective-permute-start(bf16[256,2048]{1,0:T(8,128)(2,1)} %x_ref.3), channel_id=1, source_target_pairs={{0,1},{1,2},{2,3},{3,0},{4,5},{5,6},{6,7},{7,4},{8,9},{9,10},{10,1... | collective-permute-start | bytes 3145736 | tf_op jit(solution)/shard_map/ppermute | solution.py:71
  157.9 53.0 %collective-permute-start.20 = (bf16[160,2048]{1,0:T(8,128)(2,1)}, bf16[160,2048]{1,0:T(8,128)(2,1)}, u32[]{:S(2)}, u32[]{:S(2)}) collective-permute-start(bf16[160,2048]{1,0:T(8,128)(2,1)} %slice.145), channel_id=1, source_target_pairs={{0,16},{8,0},{24,8},{16,24},{1,17},{9,1},{25,9},{17,25},{2,18},{10... | collective-permute-start | bytes 1966088 | tf_op jit(solution)/shard_map/ppermute | solution.py:74
  159.5 51.4 %collective-permute-start.19 = (bf16[160,2048]{1,0:T(8,128)(2,1)}, bf16[160,2048]{1,0:T(8,128)(2,1)}, u32[]{:S(2)}, u32[]{:S(2)}) collective-permute-start(bf16[160,2048]{1,0:T(8,128)(2,1)} %slice.144), channel_id=1, source_target_pairs={{0,8},{8,24},{24,16},{16,0},{1,9},{9,25},{25,17},{17,1},{2,10},{10... | collective-permute-start | bytes 1966088 | tf_op jit(solution)/shard_map/ppermute | solution.py:74
  161.2 59.9 %collective-permute-start.22 = (bf16[256,2048]{1,0:T(8,128)(2,1)}, bf16[256,2048]{1,0:T(8,128)(2,1)}, u32[]{:S(2)}, u32[]{:S(2)}) collective-permute-start(bf16[256,2048]{1,0:T(8,128)(2,1)} %g_ref.1), channel_id=1, source_target_pairs={{0,3},{1,0},{2,1},{3,2},{4,7},{5,4},{6,5},{7,6},{8,11},{9,8},{10,9... | collective-permute-start | bytes 3145736 | tf_op jit(solution)/shard_map/ppermute | solution.py:71
  164.5 57.0 %collective-permute-start.21 = (bf16[256,2048]{1,0:T(8,128)(2,1)}, bf16[256,2048]{1,0:T(8,128)(2,1)}, u32[]{:S(2)}, u32[]{:S(2)}) collective-permute-start(bf16[256,2048]{1,0:T(8,128)(2,1)} %g_ref.1), channel_id=1, source_target_pairs={{0,1},{1,2},{2,3},{3,0},{4,5},{5,6},{6,7},{7,4},{8,9},{9,10},{10,1... | collective-permute-start | bytes 3145736 | tf_op jit(solution)/shard_map/ppermute | solution.py:71
  221.5 32.5 %collective-permute-start.29 = (bf16[256,2048]{1,0:T(8,128)(2,1)S(1)}, bf16[256,2048]{1,0:T(8,128)(2,1)S(1)}, u32[]{:S(2)}, u32[]{:S(2)}) collective-permute-start(bf16[256,2048]{1,0:T(8,128)(2,1)S(1)} %copy-done.25), channel_id=1, source_target_pairs={{0,4},{4,0},{1,5},{5,1},{2,6},{6,2},{3,7},{7,3},{8,12},{12,8},{9,1... | collective-permute-start | bytes 3145736 | tf_op jit(solution)/shard_map/ppermute | solution.py:135
  223.1 34.7 %collective-permute-start.31 = (bf16[256,2048]{1,0:T(8,128)(2,1)}, bf16[256,2048]{1,0:T(8,128)(2,1)S(1)}, u32[]{:S(2)}, u32[]{:S(2)}) collective-permute-start(bf16[256,2048]{1,0:T(8,128)(2,1)} %collective-permute-done.22.refs_2_), channel_id=1, source_target_pairs={{0,4},{4,0},{1,5},{5,1},{2,6},{6,2},{3,7},{7,3},{8,12},{12,8},{9,1... | collective-permute-start | bytes 3145736 | tf_op jit(solution)/shard_map/ppermute | solution.py:135
  225.2 28.3 %collective-permute-start.28 = (bf16[128,2048]{1,0:T(8,128)(2,1)}, bf16[128,2048]{1,0:T(8,128)(2,1)S(1)}, u32[]{:S(2)}, u32[]{:S(2)}) collective-permute-start(bf16[128,2048]{1,0:T(8,128)(2,1)} %slice.147), channel_id=1, source_target_pairs={{0,3},{1,0},{2,1},{3,2},{4,7},{5,4},{6,5},{7,6},{8,11},{9,8},{10,9... | collective-permute-start | bytes 1572872 | tf_op jit(solution)/shard_map/ppermute | solution.py:74
  231.0 26.8 %collective-permute-start.30 = (bf16[256,2048]{1,0:T(8,128)(2,1)}, bf16[256,2048]{1,0:T(8,128)(2,1)S(1)}, u32[]{:S(2)}, u32[]{:S(2)}) collective-permute-start(bf16[256,2048]{1,0:T(8,128)(2,1)} %collective-permute-done.21.refs_1_), channel_id=1, source_target_pairs={{0,4},{4,0},{1,5},{5,1},{2,6},{6,2},{3,7},{7,3},{8,12},{12,8},{9,1... | collective-permute-start | bytes 3145736 | tf_op jit(solution)/shard_map/ppermute | solution.py:135
  254.0 43.1 %collective-permute-start.34 = (bf16[128,2048]{1,0:T(8,128)(2,1)S(1)}, bf16[128,2048]{1,0:T(8,128)(2,1)S(1)}, u32[]{:S(2)}, u32[]{:S(2)}) collective-permute-start(bf16[128,2048]{1,0:T(8,128)(2,1)S(1)} %get-tuple-element.158), channel_id=1, source_target_pairs={{0,3},{1,0},{2,1},{3,2},{4,7},{5,4},{6,5},{7,6},{8,11},{9,8},{10,9... | collective-permute-start | bytes 1572872 | tf_op jit(solution)/shard_map/ppermute | solution.py:80
  257.8 39.3 %collective-permute-start.35 = (bf16[128,2048]{1,0:T(8,128)(2,1)S(1)}, bf16[128,2048]{1,0:T(8,128)(2,1)S(1)}, u32[]{:S(2)}, u32[]{:S(2)}) collective-permute-start(bf16[128,2048]{1,0:T(8,128)(2,1)S(1)} %get-tuple-element.159), channel_id=1, source_target_pairs={{0,1},{1,2},{2,3},{3,0},{4,5},{5,6},{6,7},{7,4},{8,9},{9,10},{10,1... | collective-permute-start | bytes 1572872 | tf_op jit(solution)/shard_map/ppermute | solution.py:80
  295.1 44.5 %collective-permute-start.36 = (bf16[256,1024]{1,0:T(8,128)(2,1)}, bf16[256,1024]{1,0:T(8,128)(2,1)}, u32[]{:S(2)}, u32[]{:S(2)}) collective-permute-start(bf16[256,1024]{1,0:T(8,128)(2,1)} %get-tuple-element.170), channel_id=1, source_target_pairs={{0,16},{8,0},{24,8},{16,24},{1,17},{9,1},{25,9},{17,25},{2,18},{10... | collective-permute-start | bytes 1572872 | tf_op jit(solution)/shard_map/ppermute | solution.py:80
  296.6 43.0 %collective-permute-start.37 = (bf16[256,1024]{1,0:T(8,128)(2,1)}, bf16[256,1024]{1,0:T(8,128)(2,1)}, u32[]{:S(2)}, u32[]{:S(2)}) collective-permute-start(bf16[256,1024]{1,0:T(8,128)(2,1)} %get-tuple-element.171), channel_id=1, source_target_pairs={{0,8},{8,24},{24,16},{16,0},{1,9},{9,25},{25,17},{17,1},{2,10},{10... | collective-permute-start | bytes 1572872 | tf_op jit(solution)/shard_map/ppermute | solution.py:80
  302.7 63.3 %collective-permute-start.38 = (bf16[256,2048]{1,0:T(8,128)(2,1)}, bf16[256,2048]{1,0:T(8,128)(2,1)}, u32[]{:S(2)}, u32[]{:S(2)}) collective-permute-start(bf16[256,2048]{1,0:T(8,128)(2,1)} %get-tuple-element.173), channel_id=1, source_target_pairs={{0,3},{1,0},{2,1},{3,2},{4,7},{5,4},{6,5},{7,6},{8,11},{9,8},{10,9... | collective-permute-start | bytes 3145736 | tf_op jit(solution)/shard_map/ppermute | solution.py:84
  306.6 60.0 %collective-permute-start.39 = (bf16[256,2048]{1,0:T(8,128)(2,1)}, bf16[256,2048]{1,0:T(8,128)(2,1)}, u32[]{:S(2)}, u32[]{:S(2)}) collective-permute-start(bf16[256,2048]{1,0:T(8,128)(2,1)} %get-tuple-element.174), channel_id=1, source_target_pairs={{0,1},{1,2},{2,3},{3,0},{4,5},{5,6},{6,7},{7,4},{8,9},{9,10},{10,1... | collective-permute-start | bytes 3145736 | tf_op jit(solution)/shard_map/ppermute | solution.py:84
  345.4 43.0 %collective-permute-start.45 = (bf16[512,1024]{1,0:T(8,128)(2,1)}, bf16[512,1024]{1,0:T(8,128)(2,1)S(1)}, u32[]{:S(2)}, u32[]{:S(2)}) collective-permute-start(bf16[512,1024]{1,0:T(8,128)(2,1)} %get-tuple-element.178), channel_id=1, source_target_pairs={{0,8},{8,24},{24,16},{16,0},{1,9},{9,25},{25,17},{17,1},{2,10},{10... | collective-permute-start | bytes 3145736 | tf_op jit(solution)/shard_map/ppermute | solution.py:84
  366.1 27.9 %collective-permute-start.41 = (bf16[256,2048]{1,0:T(8,128)(2,1)}, bf16[256,2048]{1,0:T(8,128)(2,1)S(1)}, u32[]{:S(2)}, u32[]{:S(2)}) collective-permute-start(bf16[256,2048]{1,0:T(8,128)(2,1)} %get-tuple-element.182), channel_id=1, source_target_pairs={{0,4},{4,0},{1,5},{5,1},{2,6},{6,2},{3,7},{7,3},{8,12},{12,8},{9,1... | collective-permute-start | bytes 3145736 | tf_op jit(solution)/shard_map/ppermute | solution.py:135
  366.6 27.7 %collective-permute-start.42 = (bf16[256,2048]{1,0:T(8,128)(2,1)}, bf16[256,2048]{1,0:T(8,128)(2,1)S(1)}, u32[]{:S(2)}, u32[]{:S(2)}) collective-permute-start(bf16[256,2048]{1,0:T(8,128)(2,1)} %get-tuple-element.183), channel_id=1, source_target_pairs={{0,4},{4,0},{1,5},{5,1},{2,6},{6,2},{3,7},{7,3},{8,12},{12,8},{9,1... | collective-permute-start | bytes 3145736 | tf_op jit(solution)/shard_map/ppermute | solution.py:135
  448.4 39.8 %collective-permute-start.51 = (bf16[256,2048]{1,0:T(8,128)(2,1)}, bf16[256,2048]{1,0:T(8,128)(2,1)}, u32[]{:S(2)}, u32[]{:S(2)}) collective-permute-start(bf16[256,2048]{1,0:T(8,128)(2,1)} %get-tuple-element.217), channel_id=1, source_target_pairs={{0,3},{1,0},{2,1},{3,2},{4,7},{5,4},{6,5},{7,6},{8,11},{9,8},{10,9... | collective-permute-start | bytes 3145736 | tf_op jit(solution)/shard_map/ppermute | solution.py:84
  451.7 30.3 %collective-permute-start.62 = (bf16[160,2048]{1,0:T(8,128)(2,1)S(1)}, bf16[160,2048]{1,0:T(8,128)(2,1)}, u32[]{:S(2)}, u32[]{:S(2)}) collective-permute-start(bf16[160,2048]{1,0:T(8,128)(2,1)S(1)} %copy-done.83), channel_id=1, source_target_pairs={{0,16},{8,0},{24,8},{16,24},{1,17},{9,1},{25,9},{17,25},{2,18},{10... | collective-permute-start | bytes 1966088 | tf_op jit(solution)/shard_map/ppermute | solution.py:80
  453.2 42.6 %collective-permute-start.52 = (bf16[256,2048]{1,0:T(8,128)(2,1)}, bf16[256,2048]{1,0:T(8,128)(2,1)}, u32[]{:S(2)}, u32[]{:S(2)}) collective-permute-start(bf16[256,2048]{1,0:T(8,128)(2,1)} %get-tuple-element.218), channel_id=1, source_target_pairs={{0,1},{1,2},{2,3},{3,0},{4,5},{5,6},{6,7},{7,4},{8,9},{9,10},{10,1... | collective-permute-start | bytes 3145736 | tf_op jit(solution)/shard_map/ppermute | solution.py:84
  453.5 30.1 %collective-permute-start.63 = (bf16[160,2048]{1,0:T(8,128)(2,1)S(1)}, bf16[160,2048]{1,0:T(8,128)(2,1)}, u32[]{:S(2)}, u32[]{:S(2)}) collective-permute-start(bf16[160,2048]{1,0:T(8,128)(2,1)S(1)} %copy-done.81), channel_id=1, source_target_pairs={{0,8},{8,24},{24,16},{16,0},{1,9},{9,25},{25,17},{17,1},{2,10},{10... | collective-permute-start | bytes 1966088 | tf_op jit(solution)/shard_map/ppermute | solution.py:80
  487.8 39.3 %collective-permute-start.64 = (bf16[320,2048]{1,0:T(8,128)(2,1)}, bf16[320,2048]{1,0:T(8,128)(2,1)}, u32[]{:S(2)}, u32[]{:S(2)}) collective-permute-start(bf16[320,2048]{1,0:T(8,128)(2,1)} %get-tuple-element.234), channel_id=1, source_target_pairs={{0,16},{8,0},{24,8},{16,24},{1,17},{9,1},{25,9},{17,25},{2,18},{10... | collective-permute-start | bytes 3932168 | tf_op jit(solution)/shard_map/ppermute | solution.py:84
  488.2 39.1 %collective-permute-start.65 = (bf16[320,2048]{1,0:T(8,128)(2,1)}, bf16[320,2048]{1,0:T(8,128)(2,1)}, u32[]{:S(2)}, u32[]{:S(2)}) collective-permute-start(bf16[320,2048]{1,0:T(8,128)(2,1)} %get-tuple-element.235), channel_id=1, source_target_pairs={{0,8},{8,24},{24,16},{16,0},{1,9},{9,25},{25,17},{17,1},{2,10},{10... | collective-permute-start | bytes 3932168 | tf_op jit(solution)/shard_map/ppermute | solution.py:84
  (135 other events, 1490.2 us)
Sparse Core Ops, SparseCore 0:
  14.4 102.7 all-gather.1

commit v4 on v3

--- a/solution.py
+++ b/solution.py
@@ -61,7 +61,7 @@
     return plan + [((first + n - 1, 0, half_of(rows)), (first + n, half_of(rows), rows - half_of(rows)))]
 
 
-def ring_gathered(own, axis, order, hold=()):
+def ring_halves(own, axis, order):
     n = len(order)
     up_pairs, down_pairs = ring_pairs(order, 1), ring_pairs(order, -1)
     out = [own]
@@ -70,19 +70,36 @@
     for _ in range(1, n // 2):
         up, down = lax.ppermute(up, axis, up_pairs), lax.ppermute(down, axis, down_pairs)
         out += [up, down]
-    up, down = after(up[:half], *hold), after(down[half:], *hold)
-    return out + [lax.ppermute(up, axis, up_pairs), lax.ppermute(down, axis, down_pairs)]
-
-
-def ring_sum(parts, axis, order, hold=(), tail=0):
+    return out, (up[:half], down[half:])
+
+
+def ring_gathered(own, axis, order, hold=()):
+    out, (up, down) = ring_halves(own, axis, order)
+    up, down = after(up, *hold), after(down, *hold)
+    return out + [lax.ppermute(up, axis, ring_pairs(order, 1)), lax.ppermute(down, axis, ring_pairs(order, -1))]
+
+
+def ring_first(parts, axis, order):
     n = len(order)
-    up_pairs, down_pairs = ring_pairs(order, 1), ring_pairs(order, -1)
-    low, high = lax.ppermute(parts[n - 1], axis, down_pairs), lax.ppermute(parts[n], axis, up_pairs)
+    return [
+        lax.ppermute(parts[n - 1], axis, ring_pairs(order, -1)),
+        lax.ppermute(parts[n], axis, ring_pairs(order, 1)),
+    ]
+
+
+def ring_rest(parts, arrived, axis, order, hold=(), tail=0):
+    n = len(order)
+    low, high = arrived
     sent = ()
     for step in range(n // 2 - 1, 0, -1):
         sent = pass_on(parts[2 * step - 1], parts[2 * step], after(low, *hold), high, tail)
-        low, high = lax.ppermute(sent[0], axis, down_pairs), lax.ppermute(sent[1], axis, up_pairs)
+        low = lax.ppermute(sent[0], axis, ring_pairs(order, -1))
+        high = lax.ppermute(sent[1], axis, ring_pairs(order, 1))
     return [parts[0], low, high], sent
+
+
+def ring_sum(parts, axis, order, hold=()):
+    return ring_rest(parts, ring_first(parts, axis, order), axis, order, hold)
 
 
 def in_two(values):
@@ -114,7 +131,7 @@
 
 def pass_on(low_part, high_part, low, high, tail):
     rows, columns = low_part.shape
-    wide = math.gcd(columns, 512)
+    wide = math.gcd(columns, 1024)
 
     def block(array):
         return pl.BlockSpec((array.shape[0], wide), lambda i: (0, i))
@@ -298,7 +315,7 @@
             ],
         ),
         out_shape=jax.ShapeDtypeStruct((count, seq_len, wide), BF),
-        compiler_params=pltpu.CompilerParams(vmem_limit_bytes=40 * 2**20),
+        compiler_params=params(58),
         cost_estimate=cost(20 * count * heads * seq_len * seq_len * head_dim, 6 * count * seq_len * wide),
         name="attend_back",
     )(order, *kept, grads, *tables)
@@ -725,7 +742,7 @@
             jax.ShapeDtypeStruct((count, wide - split), BF),
             jax.ShapeDtypeStruct((count, wide - split), BF),
         ],
-        compiler_params=params(36),
+        compiler_params=params(58),
         cost_estimate=cost(2 * count * width * wide, 8 * count * width + 2 * width * wide),
         name="project",
     )(w.starts, *x_arrays, *w.arrays, gain, shift, b)
@@ -840,7 +857,7 @@
             jax.ShapeDtypeStruct((count, rest), BF),
             jax.ShapeDtypeStruct((8, width), F32),
         ],
-        compiler_params=params(32),
+        compiler_params=params(58),
         cost_estimate=cost(2 * count * width * w.rows, 6 * count * width + 2 * width * w.rows),
         name="combine_back",
     )(w.starts, *g_arrays, *w.arrays, slope)
@@ -894,7 +911,7 @@
             + [pltpu.VMEM((2, rows, width), BF), pltpu.SemaphoreType.DMA((2, 2))],
         ),
         out_shape=shapes + [jax.ShapeDtypeStruct((8, width), F32)],
-        compiler_params=params(36),
+        compiler_params=params(58),
         cost_estimate=cost(2 * count * width * w.columns, 6 * count * width + 2 * width * w.columns),
         name="project_back",
     )(w.starts, qkv_grad, pre_grad, x, *w.arrays, *arrived)
@@ -939,7 +956,7 @@
             scratch_shapes=held_blocks(n_q, rows, columns),
         ),
         out_shape=shapes + [jax.ShapeDtypeStruct((8, columns), F32)],
-        compiler_params=params(40),
+        compiler_params=params(58),
         cost_estimate=cost(2 * count * wide * columns, 2 * count * (wide + columns) + 2 * wide * columns),
         name="weight_grad",
     )(turns, left, right, *extra)
@@ -982,7 +999,7 @@
             scratch_shapes=[pltpu.VMEM((own_width, width), BF)] + held_blocks(n_q, units + head_rows, width),
         ),
         out_shape=slot_shapes(n_q, units + head_rows, width),
-        compiler_params=params(40),
+        compiler_params=params(58),
         cost_estimate=cost(2 * count * (wide + own_width) * width, 2 * count * (wide + width) + 2 * wide * width),
         name="down_grad",
     )(turns, act, *att, g)
@@ -1002,7 +1019,7 @@
 
 def finish(parts, x, g, gain):
     count, width = x.shape
-    rows = math.gcd(count, 64)
+    rows = math.gcd(count, 128)
     block = pl.BlockSpec((rows, width), lambda i: (i, 0))
     return pl.pallas_call(
         finish_kernel,
@@ -1025,7 +1042,7 @@
 
 def output_sum(x, bias, parts):
     count, width = x.shape
-    rows = math.gcd(count, 64)
+    rows = math.gcd(count, 128)
     block = pl.BlockSpec((rows, width), lambda i: (i, 0))
     return pl.pallas_call(
         output_kernel,
@@ -1040,7 +1057,7 @@
 
 def split_sum(parts, cuts):
     count, width = parts[0].shape
-    wide = math.gcd(width, 512)
+    wide = math.gcd(width, 1024)
     ends = [sum(cuts[: i + 1]) for i in range(len(cuts))]
 
     def kernel(*refs):
@@ -1133,7 +1150,11 @@
 
     came = scattered(to_blocks(at, qkv_weight, fc1_weight, n_q, n_t, heads, head_dim, units), "ctx")
     w2_block = jnp.concatenate([fc2_weight, out_weight], 0) if whole_heads else fc2_weight
-    w2_arrays = ring_gathered(w2_block, "q", q_order)
+    w2_arrays, w2_halves = ring_halves(w2_block, "q", q_order)
+    w2_halves = lax.optimization_barrier(w2_halves)
+    w2_arrays = w2_arrays + [
+        lax.ppermute(half, "q", ring_pairs(q_order, step)) for half, step in zip(w2_halves, (1, -1))
+    ]
     plan = []
     for slot, pieces in enumerate(slot_plan(n_q, w2_block.shape[0])):
         for which, first, count in pieces:
@@ -1161,8 +1182,8 @@
     w1 = Gathered(w1_arrays, w1_plan, turns)
 
     token_plan = slot_plan(n_z, rows) + slot_plan(n_z, rows, n_z + 1)
-    x_line = ring_gathered(after(inputs, *w2_sent[:-2]), "ctx", z_order, w1_arrays[1:-2])
-    x_arrays = x_line + [swap(p) for p in x_line[:-2]] + [swap(after(p, *w1_arrays[-2:])) for p in x_line[-2:]]
+    x_line = ring_gathered(after(inputs, *w2_halves), "ctx", z_order)
+    x_arrays = x_line + [swap(x_line[0])] + [swap(after(p, *w1_arrays[-2:])) for p in x_line[1:]]
 
     small = after(small, *x_line[-2:])
     small = small.reshape(n_all, 256, 128)[:, :16]
@@ -1192,25 +1213,24 @@
     up_parts, up_sent = ring_sum(up_own, "q", q_order, [qkv_grad])
     normed_other, sums_other = project_back(after(qkv_grad, *up_sent), pre_grad, w1, x_all, 1, rows)
     down, out_apart = down_grad(turns, after(act, *normed_other, *out_parts[1:]), (att_own, att_other), g_all, head_dim if whole_heads else 0)
-    up_came = scattered(last_sum(at, [after(up_parts[0], *down)] + up_parts[1:], n_t), "ctx")
+    up_rows = last_sum(at, [after(up_parts[0], *down)] + up_parts[1:], n_t)
+    up_came = scattered(up_rows, "ctx")
     normed_own, sums_own = project_back(
         after(qkv_grad, *down), pre_grad, w1, x_all, 0, rows, [swap(p) for p in normed_other]
     )
-    down_parts, _ = ring_sum(down, "q", q_order, normed_own)
+    down_parts, down_sent = ring_sum(down, "q", q_order, normed_own)
     vectors = pack_vectors(
         at, sums_own, sums_other, g_sums, up_sums, (n_q, n_t, heads, head_dim, units), (d_rows, qkv_bias.shape[0]), split
     )
-    qkv_own, _ = weight_grad(turns, after(hidden, *normed_own), qkv_grad, vectors)
-    normed_parts, normed_sent = ring_sum([after(p, *up_came[1:]) for p in normed_own], "ctx", z_order, qkv_own)
-    qkv_parts, qkv_sent = ring_sum(qkv_own, "q", q_order, normed_sent, 2 * n_t)
+    qkv_own, _ = weight_grad(turns, after(hidden, *normed_own, *down_sent), qkv_grad, vectors)
+    qkv_first = ring_first(qkv_own, "q", q_order)
+    normed_own = [after(p, *up_came[1:]) for p in normed_own]
+    normed_first = ring_first(normed_own, "ctx", z_order)
+    normed_parts, normed_sent = ring_rest(normed_own, normed_first, "ctx", z_order, qkv_own)
+    qkv_parts, qkv_sent = ring_rest(qkv_own, qkv_first, "q", q_order, normed_sent, 2 * n_t)
     output = output_sum(inputs, b_out + b_down, [after(out_parts[0], *normed_sent)] + out_parts[1:])
 
     qkv_came = scattered(last_sum(at, qkv_parts, n_t, 2 * n_t), "ctx")
-    up_got = swap(theirs([after(up_came[0], *normed_parts[1:], output)] + up_came[1:]))
-    (fc1_weight_grad,) = from_blocks(at, up_came, up_got, n_q, units)
-    qkv_got = swap(theirs([after(qkv_came[0], up_got)] + qkv_came[1:]))
-    qkv_weight_grad, total = from_blocks(at, qkv_came, qkv_got, 3 * heads, head_dim, 16)
-    total = total[0]
     if whole_heads:
         fc2_weight_grad, out_weight_grad = split_sum(down_parts, [units, head_dim])
     else:
@@ -1218,8 +1238,12 @@
         spread = jnp.zeros((heads, n_t, head_dim, width), F32)
         spread = lax.dynamic_update_slice(spread, out_apart.reshape(heads, 1, head_dim, width), (0, t, 0, 0))
         out_weight_grad = lax.psum_scatter(spread.reshape(width, width), every, scatter_dimension=0, tiled=True)
-
     input_grad = finish(normed_parts, inputs, cotangent, gain)
+    up_got = swap(theirs([after(up_came[0], *normed_parts[1:], output)] + up_came[1:]))
+    (fc1_weight_grad,) = from_blocks(at, up_came, up_got, n_q, units)
+    qkv_got = swap(theirs([after(qkv_came[0], up_got, fc1_weight_grad, input_grad, fc2_weight_grad)] + qkv_came[1:]))
+    qkv_weight_grad, total = from_blocks(at, qkv_came, qkv_got, 3 * heads, head_dim, 16)
+    total = total[0]
 
     cuts = [ln_gain.shape[0], ln_bias.shape[0], out_bias.shape[0], qkv_bias.shape[0], fc1_bias.shape[0]]
     starts = [sum(cuts[:i]) for i in range(len(cuts))]

time: 557 us -> 542 us (0.973)
  local copies, waits for them, and re-layouts: 73.2 us -> 44.3 us
  Pallas kernels: 238 us -> 248 us
  waiting for transfers between devices: 153 us -> 159 us
    unnamed x204 -> x138, local copies, waits for them, and re-layouts: 54 us -> 25.3 us
    ppermute x36, waiting for transfers between devices: 122 us -> 131 us  [the longest x4 46.7 us: ring_halves(): lax.ppermute(down, axis, down_pairs)]
  transfers between devices with their start and end apart: 67 -> 67, of which waited for: 22 -> 21; matrix products, arithmetic and copies ran while one was open for 3% -> 4% of each run, Pallas kernels for 42% -> 45%
where the time goes in v4:
time: 542 us; the launch traced here: 536 us
  Pallas kernels  248 us (46%)
  waiting for transfers between devices  159 us (29%)
  starting transfers between devices  68.8 us (13%)
  local copies, waits for them, and re-layouts  44.3 us (8%)
  between operations  15.2 us (3%)
    ppermute x4, waiting for transfers between devices, ring_halves(): lax.ppermute(down, axis, down_pairs)  46.7 us
    pallas_call x2, Pallas kernels, project_back(): pl.pallas_call(partial(project_back_kernel, split, w.plan, len(w.arrays),...  35.6 us
    pallas_call x1, Pallas kernels, project(): pl.pallas_call(partial(project_kernel, split, x_plan, len(x_arrays), w.pl...  32 us
    pallas_call x1, Pallas kernels, attend_back(): pl.pallas_call(partial(attend_back_kernel, heads, head_dim, span), grid_s...  29.6 us
    pallas_call x2, Pallas kernels, weight_grad(): pl.pallas_call(partial(weight_grad_kernel, len(extra)), grid_spec=pltpu.P...  28.3 us
    unnamed x138, local copies, waits for them, and re-layouts  25.3 us
    ppermute x9, waiting for transfers between devices, across(): return lax.ppermute(value, axis, [(i, i ^ e) for i in range(n)])  20.8 us
    pallas_call x1, Pallas kernels, combine_back(): pl.pallas_call(partial(combine_back_kernel, split, g_plan, len(g_arrays),...  20.4 us
  transfers between devices with their start and end apart: 67, of which 21 were waited for; matrix products, arithmetic and copies ran while one was open for 4% of the time, Pallas kernels for 45%

profile of v4, /device:TPU:0, one launch (start us, length us, event | category | flops | bytes accessed | tf_op | source)
XLA Modules:
  0.0 536.2 jit_solution(881818015766566312)
XLA Ops:
  25.7 15.2 %collective-permute-done.1.refs_2_.refs_12_ = bf16[320,2048]{1,0:T(8,128)(2,1)S(1)} collective-permute-done((bf16[320,2048]{1,0:T(8,128)(2,1)S(1)}, bf16[320,2048]{1,0:T(8,128)(2,1)S(1)}, u32[]{:S(2)}, u32[]{:S(2)}) %collective-permute-start.1) | collective-permute-done | bytes 1310752 | tf_op jit(solution)/shard_map/ppermute | solution.py:71
  42.5 14.4 %collective-permute-done.8.refs_2_ = bf16[128,1792]{1,0:T(8,128)(2,1)} collective-permute-done((bf16[128,1792]{1,0:T(8,128)(2,1)}, bf16[128,1792]{1,0:T(8,128)(2,1)}, u32[]{:S(2)}, u32[]{:S(2)}) %collective-permute-start.8) | collective-permute-done | bytes 458784 | tf_op jit(solution)/shard_map/ppermute | solution.py:39
  70.8 6.8 %collective-permute-start.2 = (bf16[256,2048]{1,0:T(8,128)(2,1)}, bf16[256,2048]{1,0:T(8,128)(2,1)}, u32[]{:S(2)}, u32[]{:S(2)}) collective-permute-start(bf16[256,2048]{1,0:T(8,128)(2,1)} %x_ref.3), channel_id=1, source_target_pairs={{0,1},{1,2},{2,3},{3,0},{4,5},{5,6},{6,7},{7,4},{8,9},{9,10},{10,1... | collective-permute-start | bytes 3145736 | tf_op jit(solution)/shard_map/ppermute | solution.py:71
  77.6 31.5 %collective-permute-done.13.refs_12_.refs_2_ = bf16[512,1792]{1,0:T(8,128)(2,1)S(1)} collective-permute-done((bf16[512,1792]{1,0:T(8,128)(2,1)S(1)}, bf16[512,1792]{1,0:T(8,128)(2,1)S(1)}, u32[]{:S(2)}, u32[]{:S(2)}) %collective-permute-start.13) | collective-permute-done | bytes 1835040 | tf_op jit(solution)/shard_map/ppermute | solution.py:71
  117.6 14.0 %collective-permute-done.2.refs_1_ = bf16[256,2048]{1,0:T(8,128)(2,1)} collective-permute-done((bf16[256,2048]{1,0:T(8,128)(2,1)}, bf16[256,2048]{1,0:T(8,128)(2,1)}, u32[]{:S(2)}, u32[]{:S(2)}) %collective-permute-start.2) | collective-permute-done | bytes 1048608 | tf_op jit(solution)/shard_map/ppermute | solution.py:71
  133.6 4.0 rotary_tables.1
  137.6 5.2 collective-permute-done.5.refs_4_
  142.8 10.9 %collective-permute-done.3.refs_3_ = bf16[128,2048]{1,0:T(8,128)(2,1)} collective-permute-done((bf16[128,2048]{1,0:T(8,128)(2,1)}, bf16[128,2048]{1,0:T(8,128)(2,1)}, u32[]{:S(2)}, u32[]{:S(2)}) %collective-permute-start.3) | collective-permute-done | bytes 524320 | tf_op jit(solution)/shard_map/ppermute | solution.py:79
  163.9 32.0 %project.1 = (bf16[2048,2048]{1,0:T(8,128)(2,1)}, bf16[2048,2048]{1,0:T(8,128)(2,1)}, f32[2048,768]{1,0:T(8,128)}, bf16[2048,1024]{1,0:T(8,128)(2,1)}, bf16[2048,1024]{1,0:T(8,128)(2,1)}) custom-call(s32[4]{0:T(128)} %get-tuple-element.131.starts_ref.turns_ref, bf16[256,2048]{1,0:T(8,128)(2,1)} %x_ref.3, bf16[256,2048]{1,0:T(8,128)(2,1)} %collective-permute-done.2.refs_1_, ...), custom_call_target="tpu_custom_call" | custom-call | flops 15032385 | bytes 40894 | tf_op jit(solution)/shard_map/project/pallas_call | solution.py:729
  198.7 7.5 %attend.2 = (bf16[1,1024,256]{2,1,0:T(8,128)(2,1)S(1)}, bf16[1,1024,768]{2,1,0:T(8,128)(2,1)S(1)}) custom-call(s32[8]{0:T(128)S(1)} %copy-done.37, f32[2,1024,768]{2,1,0:T(8,128)S(1)} %bitcast.35, f32[1024,128]{1,0:T(8,128)S(1)} %copy-done.9, f32[1024,128]{1,0:T(8,128)S(1)} %copy-done.11, f32[1024,128]{1,0:T(8,128)S(1)} %copy-done.13), custom_call_target="tpu_custom_call" | custom-call | flops 2147483 | bytes 6291 | tf_op jit(solution)/shard_map/attend/pallas_call | solution.py:270
  206.2 10.0 %combine.2 = (bf16[256,2048]{1,0:T(8,128)(2,1)S(1)}, bf16[256,2048]{1,0:T(8,128)(2,1)S(1)}, bf16[256,2048]{1,0:T(8,128)(2,1)S(1)}, bf16[256,2048]{1,0:T(8,128)(2,1)S(1)}) custom-call(s32[4]{0:T(128)S(1)} %copy-done.33, bf16[2048,1024]{1,0:T(8,128)(2,1)S(1)} %copy-done, bf16[1024,256]{1,0:T(8,128)(2,1)S(1)} %bitcast.39, ...), custom_call_target="tpu_custom_call" | custom-call | flops 5368709 | bytes 13631 | tf_op jit(solution)/shard_map/combine/pallas_call | solution.py:784
  226.8 7.4 %attend.3 = (bf16[1,1024,256]{2,1,0:T(8,128)(2,1)S(1)}, bf16[1,1024,768]{2,1,0:T(8,128)(2,1)S(1)}) custom-call(s32[8]{0:T(128)S(1)} %copy-done.37, f32[2,1024,768]{2,1,0:T(8,128)S(1)} %bitcast.38, f32[1024,128]{1,0:T(8,128)S(1)} %copy-done.10, f32[1024,128]{1,0:T(8,128)S(1)} %copy-done.12, f32[1024,128]{1,0:T(8,128)S(1)} %copy-done.14), custom_call_target="tpu_custom_call" | custom-call | flops 2147483 | bytes 6291 | tf_op jit(solution)/shard_map/attend/pallas_call | solution.py:270
  239.7 9.6 %combine.3 = (bf16[256,2048]{1,0:T(8,128)(2,1)S(1)}, bf16[256,2048]{1,0:T(8,128)(2,1)S(1)}, bf16[256,2048]{1,0:T(8,128)(2,1)S(1)}, bf16[128,2048]{1,0:T(8,128)(2,1)S(1)}, bf16[128,2048]{1,0:T(8,128)(2,1)S(1)}) custom-call(s32[4]{0:T(128)S(1)} %copy-done.33, bf16[2048,1024]{1,0:T(8,128)(2,1)S(1)} %copy-done, bf16[1024,256]{1,0:T(8,128)(2,1)S(1)} %bitcast.42, ...), custom_call_target="tpu_custom_call" | custom-call | flops 5368709 | bytes 13631 | tf_op jit(solution)/shard_map/combine/pallas_call | solution.py:784
  257.9 20.4 %combine_back.1 = (bf16[2048,2048]{1,0:T(8,128)(2,1)}, bf16[2048,1024]{1,0:T(8,128)(2,1)}, bf16[2048,256]{1,0:T(8,128)(2,1)}, f32[8,2048]{1,0:T(8,128)}) custom-call(s32[4]{0:T(128)} %get-tuple-element.131.starts_ref.turns_ref, bf16[256,2048]{1,0:T(8,128)(2,1)} %g_ref.1, bf16[256,2048]{1,0:T(8,128)(2,1)} %collective-permute-done.21.refs_1_, ...), custom_call_target="tpu_custom_call" | custom-call | flops 10737418 | bytes 30408 | tf_op jit(solution)/shard_map/combine_back/pallas_call | solution.py:845
  278.3 15.4 %weight_grad.2 = (bf16[512,1024]{1,0:T(8,128)(2,1)}, bf16[512,1024]{1,0:T(8,128)(2,1)}, bf16[512,1024]{1,0:T(8,128)(2,1)}, bf16[256,1024]{1,0:T(8,128)(2,1)}, bf...) custom-call(s32[4]{0:T(128)} %get-tuple-element.131.starts_ref.turns_ref, bf16[2048,2048]{1,0:T(8,128)(2,1)} %get-tuple-element.212.left_ref, ...), custom_call_target="tpu_custom_call" | custom-call | flops 8589934 | bytes 16777 | tf_op jit(solution)/shard_map/weight_grad/pallas_call | solution.py:948
  300.5 3.8 collective-permute-start.38
  304.5 29.6 %attend_back.1 = bf16[2,1024,768]{2,1,0:T(8,128)(2,1)} custom-call(s32[8]{0:T(128)} %get-tuple-element.136.order_ref, bf16[1,1024,768]{2,1,0:T(8,128)(2,1)} %copy-done.21, bf16[1,1024,768]{2,1,0:T(8,128)(2,1)} %copy-done.20, bf16[2,1024,256]{2,1,0:T(8,128)(2,1)} %bitcast.46, f32[1024,128]{1,0:T(8,128)} %get-tuple-element.144.cos_ref, ...), custom_call_target="tpu_custom_call" | custom-call | flops 10737418 | bytes 9437 | tf_op jit(solution)/shard_map/attend_back/pallas_call | solution.py:296
  341.0 17.0 %project_back.2 = (bf16[256,2048]{1,0:T(8,128)(2,1)}, bf16[256,2048]{1,0:T(8,128)(2,1)}, bf16[256,2048]{1,0:T(8,128)(2,1)}, bf16[256,2048]{1,0:T(8,128)(2,1)}, f32[8,2048]{1,0:T(8,128)}) custom-call(s32[4]{0:T(128)} %get-tuple-element.131.starts_ref.turns_ref, bf16[2048,768]{1,0:T(8,128)(2,1)} %bitcast.43, ...), custom_call_target="tpu_custom_call" | custom-call | flops 7516192 | bytes 19922 | tf_op jit(solution)/shard_map/project_back/pallas_call | solution.py:902
  358.7 4.6 collective-permute-done.44.refs_1_
  363.3 18.0 %down_grad.1 = (bf16[320,2048]{1,0:T(8,128)(2,1)}, bf16[320,2048]{1,0:T(8,128)(2,1)}, bf16[320,2048]{1,0:T(8,128)(2,1)}, bf16[160,2048]{1,0:T(8,128)(2,1)}, bf16[160,2048]{1,0:T(8,128)(2,1)}) custom-call(s32[4]{0:T(128)} %get-tuple-element.131.starts_ref.turns_ref, bf16[2048,1024]{1,0:T(8,128)(2,1)} %get-tuple-element.189.act_ref, ...), custom_call_target="tpu_custom_call" | custom-call | flops 10737418 | bytes 16777 | tf_op jit(solution)/shard_map/down_grad/pallas_call | solution.py:992
  382.3 4.0 collective-permute-start.47
  388.7 18.6 %project_back.3 = (bf16[256,2048]{1,0:T(8,128)(2,1)}, bf16[256,2048]{1,0:T(8,128)(2,1)}, bf16[256,2048]{1,0:T(8,128)(2,1)}, bf16[128,2048]{1,0:T(8,128)(2,1)}, b...) custom-call(s32[4]{0:T(128)} %get-tuple-element.131.starts_ref.turns_ref, bf16[2048,768]{1,0:T(8,128)(2,1)} %bitcast.44, ...), custom_call_target="tpu_custom_call" | custom-call | flops 7516192 | bytes 19922 | tf_op jit(solution)/shard_map/project_back/pallas_call | solution.py:902
  417.0 12.8 %weight_grad.3 = (bf16[528,768]{1,0:T(8,128)(2,1)}, bf16[528,768]{1,0:T(8,128)(2,1)}, bf16[528,768]{1,0:T(8,128)(2,1)}, bf16[256,768]{1,0:T(8,128)(2,1)}, bf16[272,768]{1,0:T(8,128)(2,1)}, /*index=5*/f32[8,768]{1,0:T(8,128)}) custom-call(s32[4]{0:T(128)} %get-tuple-element.131.starts_ref.turns_ref, bf16[2048,2048]{1,0:T(8,128)(2,1)} %get-tuple-element.212.left_ref, ...), custom_call_target="tpu_custom_call" | custom-call | flops 6442450 | bytes 14680 | tf_op jit(solution)/shard_map/weight_grad/pallas_call | solution.py:948
  429.8 6.1 %collective-permute-done.52.high_ref = bf16[128,2048]{1,0:T(8,128)(2,1)S(1)} collective-permute-done((bf16[128,2048]{1,0:T(8,128)(2,1)}, bf16[128,2048]{1,0:T(8,128)(2,1)S(1)}, u32[]{:S(2)}, u32[]{:S(2)}) %collective-permute-start.52) | collective-permute-done | bytes 524320 | tf_op jit(solution)/shard_map/ppermute | solution.py:86
  445.2 7.8 %collective-permute-done.55.low_ref = bf16[256,768]{1,0:T(8,128)(2,1)S(1)} collective-permute-done((bf16[256,768]{1,0:T(8,128)(2,1)}, bf16[256,768]{1,0:T(8,128)(2,1)S(1)}, u32[]{:S(2)}, u32[]{:S(2)}) %collective-permute-start.55) | collective-permute-done | bytes 393248 | tf_op jit(solution)/shard_map/ppermute | solution.py:85
  456.0 3.7 pass_on.9
  459.8 4.9 collective-permute-done.53.refs_1_
  470.9 16.3 %collective-permute-done.54.refs_2_ = bf16[256,2048]{1,0:T(8,128)(2,1)} collective-permute-done((bf16[256,2048]{1,0:T(8,128)(2,1)}, bf16[256,2048]{1,0:T(8,128)(2,1)}, u32[]{:S(2)}, u32[]{:S(2)}) %collective-permute-start.54) | collective-permute-done | bytes 1048608 | tf_op jit(solution)/shard_map/ppermute | solution.py:97
  488.1 9.1 %collective-permute-done.57.refs_1_ = bf16[528,768]{1,0:T(8,128)(2,1)S(1)} collective-permute-done((bf16[528,768]{1,0:T(8,128)(2,1)}, bf16[528,768]{1,0:T(8,128)(2,1)S(1)}, u32[]{:S(2)}, u32[]{:S(2)}) %collective-permute-start.57) | collective-permute-done | bytes 811040 | tf_op jit(solution)/shard_map/ppermute | solution.py:96
  501.4 4.1 collective-permute-start.60
  509.1 4.6 finish.1
  516.3 6.4 %collective-permute-done.60.refs_2_ = bf16[160,768]{1,0:T(8,128)(2,1)S(1)} collective-permute-done((bf16[160,768]{1,0:T(8,128)(2,1)}, bf16[160,768]{1,0:T(8,128)(2,1)S(1)}, u32[]{:S(2)}, u32[]{:S(2)}) %collective-permute-start.60) | collective-permute-done | bytes 245792 | tf_op jit(solution)/shard_map/ppermute | solution.py:39
  (307 shorter events, 145.0 us)
Async XLA Ops:
  7.2 146.5 %all-gather.2.cloned.1.call-start = ((), (), s32[]{:S(2)}) async-start(), calls=%async_computation | async-start | bytes 2162688 | tf_op jit(solution)/shard_map/all_gather | solution.py:1149
  8.6 32.2 %collective-permute-start.1 = (bf16[320,2048]{1,0:T(8,128)(2,1)S(1)}, bf16[320,2048]{1,0:T(8,128)(2,1)S(1)}, u32[]{:S(2)}, u32[]{:S(2)}) collective-permute-start(bf16[320,2048]{1,0:T(8,128)(2,1)S(1)} %constant_dynamic-update-slice_fusion.refs_0_.refs_10_), channel_id=1, source_target_pairs={{0,16},{8,0},{24,8},{16,24},{1,17},{9,1},{25,9},{17,25},{2,18},{10... | collective-permute-start | bytes 3932168 | tf_op jit(solution)/shard_map/ppermute | solution.py:71
  11.7 30.8 %collective-permute-start = (bf16[320,2048]{1,0:T(8,128)(2,1)S(1)}, bf16[320,2048]{1,0:T(8,128)(2,1)}, u32[]{:S(2)}, u32[]{:S(2)}) collective-permute-start(bf16[320,2048]{1,0:T(8,128)(2,1)S(1)} %constant_dynamic-update-slice_fusion.refs_0_.refs_10_), channel_id=1, source_target_pairs={{0,8},{8,24},{24,16},{16,0},{1,9},{9,25},{25,17},{17,1},{2,10},{10... | collective-permute-start | bytes 3932168 | tf_op jit(solution)/shard_map/ppermute | solution.py:71
  21.1 35.7 %collective-permute-start.8 = (bf16[128,1792]{1,0:T(8,128)(2,1)}, bf16[128,1792]{1,0:T(8,128)(2,1)}, u32[]{:S(2)}, u32[]{:S(2)}) collective-permute-start(bf16[128,1792]{1,0:T(8,128)(2,1)} %get-tuple-element.134), channel_id=1, source_target_pairs={{0,2},{1,3},{2,0},{3,1},{4,6},{5,7},{6,4},{7,5},{8,10},{9,11},{10,... | collective-permute-start | bytes 1376264 | tf_op jit(solution)/shard_map/ppermute | solution.py:39
  23.7 33.1 %collective-permute-start.9 = (bf16[128,1792]{1,0:T(8,128)(2,1)}, bf16[128,1792]{1,0:T(8,128)(2,1)}, u32[]{:S(2)}, u32[]{:S(2)}) collective-permute-start(bf16[128,1792]{1,0:T(8,128)(2,1)} %get-tuple-element.135), channel_id=1, source_target_pairs={{0,3},{1,2},{2,1},{3,0},{4,7},{5,6},{6,5},{7,4},{8,11},{9,10},{10,... | collective-permute-start | bytes 1376264 | tf_op jit(solution)/shard_map/ppermute | solution.py:39
  63.3 45.8 %collective-permute-start.13 = (bf16[512,1792]{1,0:T(8,128)(2,1)S(1)}, bf16[512,1792]{1,0:T(8,128)(2,1)S(1)}, u32[]{:S(2)}, u32[]{:S(2)}) collective-permute-start(bf16[512,1792]{1,0:T(8,128)(2,1)S(1)} %stack_rows.1.refs_10_.refs_0_), channel_id=1, source_target_pairs={{0,16},{8,0},{24,8},{16,24},{1,17},{9,1},{25,9},{17,25},{2,18},{10... | collective-permute-start | bytes 5505032 | tf_op jit(solution)/shard_map/ppermute | solution.py:71
  64.9 46.8 %collective-permute-start.11 = (bf16[512,1792]{1,0:T(8,128)(2,1)S(1)}, bf16[512,1792]{1,0:T(8,128)(2,1)S(1)}, u32[]{:S(2)}, u32[]{:S(2)}) collective-permute-start(bf16[512,1792]{1,0:T(8,128)(2,1)S(1)} %stack_rows.1.refs_10_.refs_0_), channel_id=1, source_target_pairs={{0,8},{8,24},{24,16},{16,0},{1,9},{9,25},{25,17},{17,1},{2,10},{10... | collective-permute-start | bytes 5505032 | tf_op jit(solution)/shard_map/ppermute | solution.py:71
  68.3 45.0 %collective-permute-start.4 = (bf16[256,2048]{1,0:T(8,128)(2,1)}, bf16[256,2048]{1,0:T(8,128)(2,1)}, u32[]{:S(2)}, u32[]{:S(2)}) collective-permute-start(bf16[256,2048]{1,0:T(8,128)(2,1)} %x_ref.3), channel_id=1, source_target_pairs={{0,3},{1,0},{2,1},{3,2},{4,7},{5,4},{6,5},{7,6},{8,11},{9,8},{10,9... | collective-permute-start | bytes 3145736 | tf_op jit(solution)/shard_map/ppermute | solution.py:71
  70.8 60.9 %collective-permute-start.2 = (bf16[256,2048]{1,0:T(8,128)(2,1)}, bf16[256,2048]{1,0:T(8,128)(2,1)}, u32[]{:S(2)}, u32[]{:S(2)}) collective-permute-start(bf16[256,2048]{1,0:T(8,128)(2,1)} %x_ref.3), channel_id=1, source_target_pairs={{0,1},{1,2},{2,3},{3,0},{4,5},{5,6},{6,7},{7,4},{8,9},{9,10},{10,1... | collective-permute-start | bytes 3145736 | tf_op jit(solution)/shard_map/ppermute | solution.py:71
  110.2 44.6 %collective-permute-start.14 = (bf16[256,1792]{1,0:T(8,128)(2,1)}, bf16[256,1792]{1,0:T(8,128)(2,1)}, u32[]{:S(2)}, u32[]{:S(2)}) collective-permute-start(bf16[256,1792]{1,0:T(8,128)(2,1)} %slice.138), channel_id=1, source_target_pairs={{0,16},{8,0},{24,8},{16,24},{1,17},{9,1},{25,9},{17,25},{2,18},{10... | collective-permute-start | bytes 2752520 | tf_op jit(solution)/shard_map/ppermute | solution.py:79
  112.8 42.1 %collective-permute-start.12 = (bf16[256,1792]{1,0:T(8,128)(2,1)}, bf16[256,1792]{1,0:T(8,128)(2,1)S(1)}, u32[]{:S(2)}, u32[]{:S(2)}) collective-permute-start(bf16[256,1792]{1,0:T(8,128)(2,1)} %slice.137), channel_id=1, source_target_pairs={{0,8},{8,24},{24,16},{16,0},{1,9},{9,25},{25,17},{17,1},{2,10},{10... | collective-permute-start | bytes 2752520 | tf_op jit(solution)/shard_map/ppermute | solution.py:79
  157.0 60.0 %collective-permute-start.22 = (bf16[256,2048]{1,0:T(8,128)(2,1)}, bf16[256,2048]{1,0:T(8,128)(2,1)}, u32[]{:S(2)}, u32[]{:S(2)}) collective-permute-start(bf16[256,2048]{1,0:T(8,128)(2,1)} %g_ref.1), channel_id=1, source_target_pairs={{0,3},{1,0},{2,1},{3,2},{4,7},{5,4},{6,5},{7,6},{8,11},{9,8},{10,9... | collective-permute-start | bytes 3145736 | tf_op jit(solution)/shard_map/ppermute | solution.py:71
  157.1 49.1 %collective-permute-start.19 = (bf16[160,2048]{1,0:T(8,128)(2,1)}, bf16[160,2048]{1,0:T(8,128)(2,1)S(1)}, u32[]{:S(2)}, u32[]{:S(2)}) collective-permute-start(bf16[160,2048]{1,0:T(8,128)(2,1)} %slice.129), channel_id=1, source_target_pairs={{0,8},{8,24},{24,16},{16,0},{1,9},{9,25},{25,17},{17,1},{2,10},{10... | collective-permute-start | bytes 1966088 | tf_op jit(solution)/shard_map/ppermute | solution.py:1156
  158.6 47.5 %collective-permute-start.20 = (bf16[160,2048]{1,0:T(8,128)(2,1)}, bf16[160,2048]{1,0:T(8,128)(2,1)S(1)}, u32[]{:S(2)}, u32[]{:S(2)}) collective-permute-start(bf16[160,2048]{1,0:T(8,128)(2,1)} %slice.130), channel_id=1, source_target_pairs={{0,16},{8,0},{24,8},{16,24},{1,17},{9,1},{25,9},{17,25},{2,18},{10... | collective-permute-start | bytes 1966088 | tf_op jit(solution)/shard_map/ppermute | solution.py:1156
  161.8 55.6 %collective-permute-start.21 = (bf16[256,2048]{1,0:T(8,128)(2,1)}, bf16[256,2048]{1,0:T(8,128)(2,1)}, u32[]{:S(2)}, u32[]{:S(2)}) collective-permute-start(bf16[256,2048]{1,0:T(8,128)(2,1)} %g_ref.1), channel_id=1, source_target_pairs={{0,1},{1,2},{2,3},{3,0},{4,5},{5,6},{6,7},{7,4},{8,9},{9,10},{10,1... | collective-permute-start | bytes 3145736 | tf_op jit(solution)/shard_map/ppermute | solution.py:71
  217.4 35.3 %collective-permute-start.29 = (bf16[256,2048]{1,0:T(8,128)(2,1)}, bf16[256,2048]{1,0:T(8,128)(2,1)}, u32[]{:S(2)}, u32[]{:S(2)}) collective-permute-start(bf16[256,2048]{1,0:T(8,128)(2,1)} %g_ref.1), channel_id=1, source_target_pairs={{0,4},{4,0},{1,5},{5,1},{2,6},{6,2},{3,7},{7,3},{8,12},{12,8},{9,1... | collective-permute-start | bytes 3145736 | tf_op jit(solution)/shard_map/ppermute | solution.py:152
  219.1 37.2 %collective-permute-start.31 = (bf16[256,2048]{1,0:T(8,128)(2,1)}, bf16[256,2048]{1,0:T(8,128)(2,1)}, u32[]{:S(2)}, u32[]{:S(2)}) collective-permute-start(bf16[256,2048]{1,0:T(8,128)(2,1)} %collective-permute-done.22.refs_2_), channel_id=1, source_target_pairs={{0,4},{4,0},{1,5},{5,1},{2,6},{6,2},{3,7},{7,3},{8,12},{12,8},{9,1... | collective-permute-start | bytes 3145736 | tf_op jit(solution)/shard_map/ppermute | solution.py:152
  222.1 30.1 %collective-permute-start.28 = (bf16[128,2048]{1,0:T(8,128)(2,1)}, bf16[128,2048]{1,0:T(8,128)(2,1)S(1)}, u32[]{:S(2)}, u32[]{:S(2)}) collective-permute-start(bf16[128,2048]{1,0:T(8,128)(2,1)} %slice.147), channel_id=1, source_target_pairs={{0,3},{1,0},{2,1},{3,2},{4,7},{5,4},{6,5},{7,6},{8,11},{9,8},{10,9... | collective-permute-start | bytes 1572872 | tf_op jit(solution)/shard_map/ppermute | solution.py:79
  226.6 29.7 %collective-permute-start.30 = (bf16[256,2048]{1,0:T(8,128)(2,1)}, bf16[256,2048]{1,0:T(8,128)(2,1)}, u32[]{:S(2)}, u32[]{:S(2)}) collective-permute-start(bf16[256,2048]{1,0:T(8,128)(2,1)} %collective-permute-done.21.refs_1_), channel_id=1, source_target_pairs={{0,4},{4,0},{1,5},{5,1},{2,6},{6,2},{3,7},{7,3},{8,12},{12,8},{9,1... | collective-permute-start | bytes 3145736 | tf_op jit(solution)/shard_map/ppermute | solution.py:152
  252.7 43.1 %collective-permute-start.34 = (bf16[128,2048]{1,0:T(8,128)(2,1)S(1)}, bf16[128,2048]{1,0:T(8,128)(2,1)S(1)}, u32[]{:S(2)}, u32[]{:S(2)}) collective-permute-start(bf16[128,2048]{1,0:T(8,128)(2,1)S(1)} %get-tuple-element.162), channel_id=1, source_target_pairs={{0,3},{1,0},{2,1},{3,2},{4,7},{5,4},{6,5},{7,6},{8,11},{9,8},{10,9... | collective-permute-start | bytes 1572872 | tf_op jit(solution)/shard_map/ppermute | solution.py:85
  256.3 39.5 %collective-permute-start.35 = (bf16[128,2048]{1,0:T(8,128)(2,1)S(1)}, bf16[128,2048]{1,0:T(8,128)(2,1)S(1)}, u32[]{:S(2)}, u32[]{:S(2)}) collective-permute-start(bf16[128,2048]{1,0:T(8,128)(2,1)S(1)} %get-tuple-element.163), channel_id=1, source_target_pairs={{0,1},{1,2},{2,3},{3,0},{4,5},{5,6},{6,7},{7,4},{8,9},{9,10},{10,1... | collective-permute-start | bytes 1572872 | tf_op jit(solution)/shard_map/ppermute | solution.py:86
  293.7 40.3 %collective-permute-start.36 = (bf16[256,1024]{1,0:T(8,128)(2,1)}, bf16[256,1024]{1,0:T(8,128)(2,1)S(1)}, u32[]{:S(2)}, u32[]{:S(2)}) collective-permute-start(bf16[256,1024]{1,0:T(8,128)(2,1)} %get-tuple-element.174), channel_id=1, source_target_pairs={{0,16},{8,0},{24,8},{16,24},{1,17},{9,1},{25,9},{17,25},{2,18},{10... | collective-permute-start | bytes 1572872 | tf_op jit(solution)/shard_map/ppermute | solution.py:85
  295.3 38.8 %collective-permute-start.37 = (bf16[256,1024]{1,0:T(8,128)(2,1)}, bf16[256,1024]{1,0:T(8,128)(2,1)S(1)}, u32[]{:S(2)}, u32[]{:S(2)}) collective-permute-start(bf16[256,1024]{1,0:T(8,128)(2,1)} %get-tuple-element.175), channel_id=1, source_target_pairs={{0,8},{8,24},{24,16},{16,0},{1,9},{9,25},{25,17},{17,1},{2,10},{10... | collective-permute-start | bytes 1572872 | tf_op jit(solution)/shard_map/ppermute | solution.py:86
  300.5 57.6 %collective-permute-start.38 = (bf16[256,2048]{1,0:T(8,128)(2,1)}, bf16[256,2048]{1,0:T(8,128)(2,1)S(1)}, u32[]{:S(2)}, u32[]{:S(2)}) collective-permute-start(bf16[256,2048]{1,0:T(8,128)(2,1)} %get-tuple-element.177), channel_id=1, source_target_pairs={{0,3},{1,0},{2,1},{3,2},{4,7},{5,4},{6,5},{7,6},{8,11},{9,8},{10,9... | collective-permute-start | bytes 3145736 | tf_op jit(solution)/shard_map/ppermute | solution.py:96
  304.3 54.3 %collective-permute-start.39 = (bf16[256,2048]{1,0:T(8,128)(2,1)}, bf16[256,2048]{1,0:T(8,128)(2,1)S(1)}, u32[]{:S(2)}, u32[]{:S(2)}) collective-permute-start(bf16[256,2048]{1,0:T(8,128)(2,1)} %get-tuple-element.178), channel_id=1, source_target_pairs={{0,1},{1,2},{2,3},{3,0},{4,5},{5,6},{6,7},{7,4},{8,9},{9,10},{10,1... | collective-permute-start | bytes 3145736 | tf_op jit(solution)/shard_map/ppermute | solution.py:97
  340.4 40.9 %collective-permute-start.45 = (bf16[512,1024]{1,0:T(8,128)(2,1)}, bf16[512,1024]{1,0:T(8,128)(2,1)S(1)}, u32[]{:S(2)}, u32[]{:S(2)}) collective-permute-start(bf16[512,1024]{1,0:T(8,128)(2,1)} %get-tuple-element.182), channel_id=1, source_target_pairs={{0,8},{8,24},{24,16},{16,0},{1,9},{9,25},{25,17},{17,1},{2,10},{10... | collective-permute-start | bytes 3145736 | tf_op jit(solution)/shard_map/ppermute | solution.py:97
  358.1 28.3 %collective-permute-start.41 = (bf16[256,2048]{1,0:T(8,128)(2,1)}, bf16[256,2048]{1,0:T(8,128)(2,1)}, u32[]{:S(2)}, u32[]{:S(2)}) collective-permute-start(bf16[256,2048]{1,0:T(8,128)(2,1)} %get-tuple-element.186), channel_id=1, source_target_pairs={{0,4},{4,0},{1,5},{5,1},{2,6},{6,2},{3,7},{7,3},{8,12},{12,8},{9,1... | collective-permute-start | bytes 3145736 | tf_op jit(solution)/shard_map/ppermute | solution.py:152
  442.3 44.9 %collective-permute-start.54 = (bf16[256,2048]{1,0:T(8,128)(2,1)}, bf16[256,2048]{1,0:T(8,128)(2,1)}, u32[]{:S(2)}, u32[]{:S(2)}) collective-permute-start(bf16[256,2048]{1,0:T(8,128)(2,1)} %get-tuple-element.225), channel_id=1, source_target_pairs={{0,1},{1,2},{2,3},{3,0},{4,5},{5,6},{6,7},{7,4},{8,9},{9,10},{10,1... | collective-permute-start | bytes 3145736 | tf_op jit(solution)/shard_map/ppermute | solution.py:97
  443.2 62.3 %collective-permute-start.63 = (bf16[320,2048]{1,0:T(8,128)(2,1)}, bf16[320,2048]{1,0:T(8,128)(2,1)}, u32[]{:S(2)}, u32[]{:S(2)}) collective-permute-start(bf16[320,2048]{1,0:T(8,128)(2,1)} %get-tuple-element.210), channel_id=1, source_target_pairs={{0,16},{8,0},{24,8},{16,24},{1,17},{9,1},{25,9},{17,25},{2,18},{10... | collective-permute-start | bytes 3932168 | tf_op jit(solution)/shard_map/ppermute | solution.py:96
  453.1 52.7 %collective-permute-start.64 = (bf16[320,2048]{1,0:T(8,128)(2,1)}, bf16[320,2048]{1,0:T(8,128)(2,1)}, u32[]{:S(2)}, u32[]{:S(2)}) collective-permute-start(bf16[320,2048]{1,0:T(8,128)(2,1)} %get-tuple-element.211), channel_id=1, source_target_pairs={{0,8},{8,24},{24,16},{16,0},{1,9},{9,25},{25,17},{17,1},{2,10},{10... | collective-permute-start | bytes 3932168 | tf_op jit(solution)/shard_map/ppermute | solution.py:97
  459.7 37.5 %collective-permute-start.57 = (bf16[528,768]{1,0:T(8,128)(2,1)}, bf16[528,768]{1,0:T(8,128)(2,1)S(1)}, u32[]{:S(2)}, u32[]{:S(2)}) collective-permute-start(bf16[528,768]{1,0:T(8,128)(2,1)} %get-tuple-element.229), channel_id=1, source_target_pairs={{0,16},{8,0},{24,8},{16,24},{1,17},{9,1},{25,9},{17,25},{2,18},{10... | collective-permute-start | bytes 2433032 | tf_op jit(solution)/shard_map/ppermute | solution.py:96
  465.7 34.1 %collective-permute-start.58 = (bf16[528,768]{1,0:T(8,128)(2,1)}, bf16[528,768]{1,0:T(8,128)(2,1)S(1)}, u32[]{:S(2)}, u32[]{:S(2)}) collective-permute-start(bf16[528,768]{1,0:T(8,128)(2,1)} %get-tuple-element.230), channel_id=1, source_target_pairs={{0,8},{8,24},{24,16},{16,0},{1,9},{9,25},{25,17},{17,1},{2,10},{10... | collective-permute-start | bytes 2433032 | tf_op jit(solution)/shard_map/ppermute | solution.py:97
  (102 other events, 1481.6 us)
Sparse Core Ops, SparseCore 0:
  14.4 81.3 all-gather.1

commit v5 on v4

--- a/solution.py
+++ b/solution.py
@@ -204,18 +204,9 @@
 
 
 def attend_back_kernel(
-    heads, head_dim, span, order_ref, kept_a_ref, kept_b_ref, grad_ref, cos_ref, sin_a_ref, sin_b_ref, out_ref, grad_scr, key_scr, value_scr, sorted_ref
+    heads, head_dim, span, order_ref, sorted_ref, grad_ref, cos_ref, sin_a_ref, sin_b_ref, out_ref, grad_scr, key_scr, value_scr
 ):
     seq_len = sorted_ref.shape[1]
-
-    @pl.when(pl.program_id(0) == 0)
-    def _():
-        sorted_ref[...] = kept_a_ref[...]
-
-    @pl.when(pl.program_id(0) == 1)
-    def _():
-        sorted_ref[...] = kept_b_ref[...]
-
     width = heads * head_dim
     for slot in range(seq_len // span):
         rows = pl.ds(pl.multiple_of(order_ref[slot] * span, span), span)
@@ -289,36 +280,29 @@
     )(order, qkv.reshape(2, seq_len, wide), *tables)
 
 
-def attend_back(order, kept, grads, tables, heads, head_dim, span):
-    count, (_, seq_len, wide) = len(kept), kept[0].shape
+def attend_back(order, kept, grads, tables, heads, head_dim, span, part):
+    _, seq_len, wide = kept.shape
     width = wide // 3
     whole = pl.BlockSpec((seq_len, 128), lambda s, o: (0, 0))
+    one = pl.BlockSpec((1, seq_len, wide), lambda s, o: (0, 0, 0))
     return pl.pallas_call(
         partial(attend_back_kernel, heads, head_dim, span),
         grid_spec=pltpu.PrefetchScalarGridSpec(
             num_scalar_prefetch=1,
-            grid=(count,),
-            in_specs=[
-                pl.BlockSpec((1, seq_len, wide), lambda s, o: (0, 0, 0)),
-                pl.BlockSpec((1, seq_len, wide), lambda s, o: (0, 0, 0)),
-                pl.BlockSpec((1, seq_len, width), lambda s, o: (s, 0, 0)),
-                whole,
-                whole,
-                whole,
-            ],
-            out_specs=pl.BlockSpec((1, seq_len, wide), lambda s, o: (s, 0, 0)),
+            grid=(1,),
+            in_specs=[one, pl.BlockSpec((1, seq_len, width), lambda s, o: (part, 0, 0)), whole, whole, whole],
+            out_specs=one,
             scratch_shapes=[
                 pltpu.VMEM((seq_len, width), BF),
                 pltpu.VMEM((seq_len, width), F32),
                 pltpu.VMEM((seq_len, width), F32),
-                pltpu.VMEM((1, seq_len, wide), BF),
             ],
         ),
-        out_shape=jax.ShapeDtypeStruct((count, seq_len, wide), BF),
-        compiler_params=params(58),
-        cost_estimate=cost(20 * count * heads * seq_len * seq_len * head_dim, 6 * count * seq_len * wide),
+        out_shape=jax.ShapeDtypeStruct((1, seq_len, wide), BF),
+        compiler_params=params(40),
+        cost_estimate=cost(20 * heads * seq_len * seq_len * head_dim, 6 * seq_len * wide),
         name="attend_back",
-    )(order, *kept, grads, *tables)
+    )(order, kept, grads, *tables).reshape(seq_len, wide)
 
 
 def after(value, *others):
@@ -889,8 +873,8 @@
 
 
 def project_back(qkv_grad, pre_grad, w, x, part, rows, arrived=()):
-    count, width = x.shape[0] // 2, x.shape[1]
-    split = qkv_grad.shape[1]
+    count, split = qkv_grad.shape
+    width = x.shape[1]
     steps = count // rows
     base = part * steps
     plan = slot_plan(steps, rows) if arrived else [((k, 0, rows),) for k in range(steps)]
@@ -904,7 +888,7 @@
         grid_spec=pltpu.PrefetchScalarGridSpec(
             num_scalar_prefetch=1,
             grid=(steps,),
-            in_specs=[block(split), block(pre_grad.shape[1]), block(width)] + w.specs() + [ANYWHERE] * len(arrived),
+            in_specs=[pl.BlockSpec((rows, split), lambda i, s: (i, 0)), block(pre_grad.shape[1]), block(width)] + w.specs() + [ANYWHERE] * len(arrived),
             out_specs=[ANYWHERE] * len(shapes) + [whole_block((8, width))],
             scratch_shapes=w.scratch()
             + held_blocks(steps, rows, width)
@@ -918,16 +902,21 @@
     return out, sums
 
 
-def weight_grad_kernel(with_tail, turns_ref, left_ref, right_ref, *refs):
+def weight_grad_kernel(n_right, with_tail, turns_ref, left_ref, *refs):
+    right_refs, refs = refs[:n_right], refs[n_right:]
     tail_refs, refs = refs[:with_tail], refs[with_tail:]
     out_refs, (sums_ref, held, sem) = refs[:-3], refs[-3:]
 
     @pl.when(pl.program_id(0) == 0)
     def _():
         sums_ref[...] = jnp.zeros_like(sums_ref)
-        sums_ref[0:1, :] = jnp.sum(right_ref[...].astype(F32), 0, keepdims=True)
-
-    block = t_dot(left_ref[...], right_ref[...]).astype(BF)
+        sums_ref[0:1, :] = sum(jnp.sum(right_ref[...].astype(F32), 0, keepdims=True) for right_ref in right_refs)
+
+    count = right_refs[0].shape[0]
+    total = t_dot(left_ref[0:count, :], right_refs[0][...])
+    for k in range(1, n_right):
+        total = total + t_dot(left_ref[k * count : (k + 1) * count, :], right_refs[k][...])
+    block = total.astype(BF)
     if with_tail:
         block = jnp.concatenate([block, tail_refs[0][0]], 0)
     put_block(slot_plan(held.shape[0], held.shape[1]), block, held, out_refs, sem)
@@ -937,20 +926,21 @@
     return [jax.ShapeDtypeStruct((r, columns), BF) for slot in slot_plan(n, rows) for _, _, r in slot]
 
 
-def weight_grad(turns, left, right, tail=None):
+def weight_grad(turns, left, rights, tail=None):
     n_q = turns.shape[0]
     count, wide = left.shape
-    columns = right.shape[1]
+    columns = rights[0].shape[1]
     part = wide // n_q
     rows = part + (0 if tail is None else tail.shape[1])
     extra = [] if tail is None else [tail]
     shapes = slot_shapes(n_q, rows, columns)
     *out, sums = pl.pallas_call(
-        partial(weight_grad_kernel, len(extra)),
+        partial(weight_grad_kernel, len(rights), len(extra)),
         grid_spec=pltpu.PrefetchScalarGridSpec(
             num_scalar_prefetch=1,
             grid=(n_q,),
-            in_specs=[pl.BlockSpec((count, part), lambda k, s: (0, s[k])), whole_block(right.shape)]
+            in_specs=[pl.BlockSpec((count, part), lambda k, s: (0, s[k]))]
+            + [whole_block(right.shape) for right in rights]
             + [pl.BlockSpec((1,) + v.shape[1:], lambda k, s: (s[k], 0, 0)) for v in extra],
             out_specs=[ANYWHERE] * len(shapes) + [whole_block((8, columns))],
             scratch_shapes=held_blocks(n_q, rows, columns),
@@ -959,7 +949,7 @@
         compiler_params=params(58),
         cost_estimate=cost(2 * count * wide * columns, 2 * count * (wide + columns) + 2 * wide * columns),
         name="weight_grad",
-    )(turns, left, right, *extra)
+    )(turns, left, *rights, *extra)
     return out, sums
 
 
@@ -1206,31 +1196,35 @@
     g_arrays = g_line + [swap(p) for p in g_line[:-2]] + [swap(after(p, *out_own)) for p in g_line[-2:]]
 
     g_all, pre_grad, att_grad, g_sums = combine_back(g_arrays, token_plan, w2, after(slope, *out_own))
-    up_own, up_sums = weight_grad(turns, hidden, pre_grad)
+    up_own, up_sums = weight_grad(turns, hidden, [pre_grad])
     out_parts, out_sent = ring_sum(out_own, "ctx", z_order, up_own)
+    up_first = ring_first(up_own, "q", q_order)
     att_grad = after(att_grad, *up_own, *out_sent).reshape(2, seq_len, own_width)
-    qkv_grad = attend_back(order, (kept_own, kept_other), att_grad, tables, heads, head_dim, span).reshape(2 * seq_len, split)
-    up_parts, up_sent = ring_sum(up_own, "q", q_order, [qkv_grad])
-    normed_other, sums_other = project_back(after(qkv_grad, *up_sent), pre_grad, w1, x_all, 1, rows)
-    down, out_apart = down_grad(turns, after(act, *normed_other, *out_parts[1:]), (att_own, att_other), g_all, head_dim if whole_heads else 0)
-    up_rows = last_sum(at, [after(up_parts[0], *down)] + up_parts[1:], n_t)
+    grad_other = attend_back(order, kept_other, att_grad, tables, heads, head_dim, span, 1)
+    up_parts, up_sent = ring_rest(up_own, up_first, "q", q_order, [grad_other])
+    normed_other, sums_other = project_back(after(grad_other, *up_sent), pre_grad, w1, x_all, 1, rows)
+    att_grad = after(att_grad, *normed_other)
+    grad_own = attend_back(order, kept_own, att_grad, tables, heads, head_dim, span, 0)
+    up_rows = last_sum(at, [after(up_parts[0], grad_own)] + up_parts[1:], n_t)
     up_came = scattered(up_rows, "ctx")
     normed_own, sums_own = project_back(
-        after(qkv_grad, *down), pre_grad, w1, x_all, 0, rows, [swap(p) for p in normed_other]
+        after(grad_own, *out_parts[1:], *up_rows), pre_grad, w1, x_all, 0, rows, [swap(p) for p in normed_other]
     )
-    down_parts, down_sent = ring_sum(down, "q", q_order, normed_own)
     vectors = pack_vectors(
         at, sums_own, sums_other, g_sums, up_sums, (n_q, n_t, heads, head_dim, units), (d_rows, qkv_bias.shape[0]), split
     )
-    qkv_own, _ = weight_grad(turns, after(hidden, *normed_own, *down_sent), qkv_grad, vectors)
+    qkv_own, _ = weight_grad(turns, after(hidden, *normed_own), [grad_own, grad_other], vectors)
     qkv_first = ring_first(qkv_own, "q", q_order)
     normed_own = [after(p, *up_came[1:]) for p in normed_own]
     normed_first = ring_first(normed_own, "ctx", z_order)
     normed_parts, normed_sent = ring_rest(normed_own, normed_first, "ctx", z_order, qkv_own)
     qkv_parts, qkv_sent = ring_rest(qkv_own, qkv_first, "q", q_order, normed_sent, 2 * n_t)
-    output = output_sum(inputs, b_out + b_down, [after(out_parts[0], *normed_sent)] + out_parts[1:])
-
-    qkv_came = scattered(last_sum(at, qkv_parts, n_t, 2 * n_t), "ctx")
+    qkv_rows = last_sum(at, qkv_parts, n_t, 2 * n_t)
+    down, out_apart = down_grad(turns, after(act, *qkv_sent), (att_own, att_other), g_all, head_dim if whole_heads else 0)
+    down_parts, down_sent = ring_sum([after(p, *qkv_parts[1:]) for p in down], "q", q_order, [normed_parts[1], *qkv_rows])
+    output = output_sum(inputs, b_out + b_down, [after(out_parts[0], *normed_sent, *down)] + out_parts[1:])
+
+    qkv_came = scattered(qkv_rows, "ctx")
     if whole_heads:
         fc2_weight_grad, out_weight_grad = split_sum(down_parts, [units, head_dim])
     else:

time: 542 us -> 521 us (0.961)
  waiting for transfers between devices: 159 us -> 136 us
    ppermute x5, waiting for transfers between devices: 18.9 us -> 2.55 us  [ring_rest(): high = lax.ppermute(sent[1], axis, ring_pairs(order, 1))]
    ppermute x9, waiting for transfers between devices: 20.8 us -> 14.4 us  [across(): return lax.ppermute(value, axis, [(i, i ^ e) for i in range(n)])]
    unnamed x138 -> x140, local copies, waits for them, and re-layouts: 25.3 us -> 29.1 us
    pallas_call x1 -> x2, Pallas kernels: 29.6 us -> 26.5 us  [attend_back(): pl.pallas_call(partial(attend_back_kernel, heads, head_dim, span), grid_s...]
  transfers between devices with their start and end apart: 67 -> 67, of which waited for: 21 -> 20; matrix products, arithmetic and copies ran while one was open for 4% -> 4% of each run, Pallas kernels for 45% -> 47%
where the time goes in v5:
time: 521 us; the launch traced here: 515 us
  Pallas kernels  246 us (47%)
  waiting for transfers between devices  136 us (26%)
  starting transfers between devices  68.9 us (13%)
  local copies, waits for them, and re-layouts  48 us (9%)
  between operations  15.2 us (3%)
    ppermute x4, waiting for transfers between devices, ring_halves(): lax.ppermute(down, axis, down_pairs)  46.7 us
    pallas_call x2, Pallas kernels, project_back(): pl.pallas_call(partial(project_back_kernel, split, w.plan, len(w.arrays),...  36.4 us
    pallas_call x1, Pallas kernels, project(): pl.pallas_call(partial(project_kernel, split, x_plan, len(x_arrays), w.pl...  32 us
    unnamed x140, local copies, waits for them, and re-layouts  29.1 us
    pallas_call x2, Pallas kernels, weight_grad(): pl.pallas_call(partial(weight_grad_kernel, len(rights), len(extra)), grid...  28.3 us
    pallas_call x2, Pallas kernels, attend_back(): pl.pallas_call(partial(attend_back_kernel, heads, head_dim, span), grid_s...  26.5 us
    pallas_call x1, Pallas kernels, combine_back(): pl.pallas_call(partial(combine_back_kernel, split, g_plan, len(g_arrays),...  20.4 us
    pallas_call x2, Pallas kernels, combine(): pl.pallas_call(partial(combine_kernel, split, w.plan, len(w.arrays), plan...  20.4 us
  transfers between devices with their start and end apart: 67, of which 20 were waited for; matrix products, arithmetic and copies ran while one was open for 4% of the time, Pallas kernels for 47%

profile of v5, /device:TPU:0, one launch (start us, length us, event | category | flops | bytes accessed | tf_op | source)
XLA Modules:
  0.0 515.4 jit_solution(4274394222756737008)
XLA Ops:
  25.7 15.2 %collective-permute-done.1.refs_2_.refs_12_ = bf16[320,2048]{1,0:T(8,128)(2,1)S(1)} collective-permute-done((bf16[320,2048]{1,0:T(8,128)(2,1)S(1)}, bf16[320,2048]{1,0:T(8,128)(2,1)S(1)}, u32[]{:S(2)}, u32[]{:S(2)}) %collective-permute-start.1) | collective-permute-done | bytes 1310752 | tf_op jit(solution)/shard_map/ppermute | solution.py:71
  42.5 14.4 %collective-permute-done.8.refs_2_ = bf16[128,1792]{1,0:T(8,128)(2,1)} collective-permute-done((bf16[128,1792]{1,0:T(8,128)(2,1)}, bf16[128,1792]{1,0:T(8,128)(2,1)}, u32[]{:S(2)}, u32[]{:S(2)}) %collective-permute-start.8) | collective-permute-done | bytes 458784 | tf_op jit(solution)/shard_map/ppermute | solution.py:39
  70.8 6.8 %collective-permute-start.2 = (bf16[256,2048]{1,0:T(8,128)(2,1)}, bf16[256,2048]{1,0:T(8,128)(2,1)}, u32[]{:S(2)}, u32[]{:S(2)}) collective-permute-start(bf16[256,2048]{1,0:T(8,128)(2,1)} %x_ref.3), channel_id=1, source_target_pairs={{0,1},{1,2},{2,3},{3,0},{4,5},{5,6},{6,7},{7,4},{8,9},{9,10},{10,1... | collective-permute-start | bytes 3145736 | tf_op jit(solution)/shard_map/ppermute | solution.py:71
  77.6 31.5 %collective-permute-done.13.refs_12_.refs_2_ = bf16[512,1792]{1,0:T(8,128)(2,1)S(1)} collective-permute-done((bf16[512,1792]{1,0:T(8,128)(2,1)S(1)}, bf16[512,1792]{1,0:T(8,128)(2,1)S(1)}, u32[]{:S(2)}, u32[]{:S(2)}) %collective-permute-start.13) | collective-permute-done | bytes 1835040 | tf_op jit(solution)/shard_map/ppermute | solution.py:71
  117.7 14.0 %collective-permute-done.2.refs_1_ = bf16[256,2048]{1,0:T(8,128)(2,1)} collective-permute-done((bf16[256,2048]{1,0:T(8,128)(2,1)}, bf16[256,2048]{1,0:T(8,128)(2,1)}, u32[]{:S(2)}, u32[]{:S(2)}) %collective-permute-start.2) | collective-permute-done | bytes 1048608 | tf_op jit(solution)/shard_map/ppermute | solution.py:71
  133.6 4.1 rotary_tables.1
  137.7 5.2 collective-permute-done.5.refs_4_
  142.8 10.9 %collective-permute-done.3.refs_3_ = bf16[128,2048]{1,0:T(8,128)(2,1)} collective-permute-done((bf16[128,2048]{1,0:T(8,128)(2,1)}, bf16[128,2048]{1,0:T(8,128)(2,1)}, u32[]{:S(2)}, u32[]{:S(2)}) %collective-permute-start.3) | collective-permute-done | bytes 524320 | tf_op jit(solution)/shard_map/ppermute | solution.py:79
  163.7 32.0 %project.1 = (bf16[2048,2048]{1,0:T(8,128)(2,1)}, bf16[2048,2048]{1,0:T(8,128)(2,1)}, f32[2048,768]{1,0:T(8,128)}, bf16[2048,1024]{1,0:T(8,128)(2,1)}, bf16[2048,1024]{1,0:T(8,128)(2,1)}) custom-call(s32[4]{0:T(128)} %get-tuple-element.137.starts_ref.turns_ref, bf16[256,2048]{1,0:T(8,128)(2,1)} %x_ref.3, bf16[256,2048]{1,0:T(8,128)(2,1)} %collective-permute-done.2.refs_1_, ...), custom_call_target="tpu_custom_call" | custom-call | flops 15032385 | bytes 40894 | tf_op jit(solution)/shard_map/project/pallas_call | solution.py:713
  198.5 7.9 %attend.2 = (bf16[1,1024,256]{2,1,0:T(8,128)(2,1)S(1)}, bf16[1,1024,768]{2,1,0:T(8,128)(2,1)S(1)}) custom-call(s32[8]{0:T(128)S(1)} %copy-done.43, f32[2,1024,768]{2,1,0:T(8,128)S(1)} %bitcast.36, f32[1024,128]{1,0:T(8,128)S(1)} %copy-done.9, f32[1024,128]{1,0:T(8,128)S(1)} %copy-done.10, f32[1024,128]{1,0:T(8,128)S(1)} %copy-done.11), custom_call_target="tpu_custom_call" | custom-call | flops 2147483 | bytes 6291 | tf_op jit(solution)/shard_map/attend/pallas_call | solution.py:261
  206.5 10.1 %combine.2 = (bf16[256,2048]{1,0:T(8,128)(2,1)S(1)}, bf16[256,2048]{1,0:T(8,128)(2,1)S(1)}, bf16[256,2048]{1,0:T(8,128)(2,1)S(1)}, bf16[256,2048]{1,0:T(8,128)(2,1)S(1)}) custom-call(s32[4]{0:T(128)S(1)} %copy-done.39, bf16[2048,1024]{1,0:T(8,128)(2,1)S(1)} %copy-done, bf16[1024,256]{1,0:T(8,128)(2,1)S(1)} %bitcast.46, ...), custom_call_target="tpu_custom_call" | custom-call | flops 5368709 | bytes 13631 | tf_op jit(solution)/shard_map/combine/pallas_call | solution.py:768
  228.9 7.9 %attend.3 = (bf16[1,1024,256]{2,1,0:T(8,128)(2,1)S(1)}, bf16[1,1024,768]{2,1,0:T(8,128)(2,1)S(1)}) custom-call(s32[8]{0:T(128)S(1)} %copy-done.43, f32[2,1024,768]{2,1,0:T(8,128)S(1)} %bitcast.39, f32[1024,128]{1,0:T(8,128)S(1)} %copy-done.9, f32[1024,128]{1,0:T(8,128)S(1)} %copy-done.10, f32[1024,128]{1,0:T(8,128)S(1)} %copy-done.11), custom_call_target="tpu_custom_call" | custom-call | flops 2147483 | bytes 6291 | tf_op jit(solution)/shard_map/attend/pallas_call | solution.py:261
  241.0 10.3 %combine.3 = (bf16[256,2048]{1,0:T(8,128)(2,1)S(1)}, bf16[256,2048]{1,0:T(8,128)(2,1)S(1)}, bf16[256,2048]{1,0:T(8,128)(2,1)S(1)}, bf16[128,2048]{1,0:T(8,128)(2,1)S(1)}, bf16[128,2048]{1,0:T(8,128)(2,1)S(1)}) custom-call(s32[4]{0:T(128)S(1)} %copy-done.39, bf16[2048,1024]{1,0:T(8,128)(2,1)S(1)} %copy-done, bf16[1024,256]{1,0:T(8,128)(2,1)S(1)} %bitcast.49, ...), custom_call_target="tpu_custom_call" | custom-call | flops 5368709 | bytes 13631 | tf_op jit(solution)/shard_map/combine/pallas_call | solution.py:768
  254.8 3.8 collective-permute-start.34
  260.3 20.4 %combine_back.1 = (bf16[2048,2048]{1,0:T(8,128)(2,1)}, bf16[2048,1024]{1,0:T(8,128)(2,1)}, bf16[2048,256]{1,0:T(8,128)(2,1)}, f32[8,2048]{1,0:T(8,128)}) custom-call(s32[4]{0:T(128)} %get-tuple-element.137.starts_ref.turns_ref, bf16[256,2048]{1,0:T(8,128)(2,1)} %g_ref.1, bf16[256,2048]{1,0:T(8,128)(2,1)} %collective-permute-done.21.refs_1_, ...), custom_call_target="tpu_custom_call" | custom-call | flops 10737418 | bytes 30408 | tf_op jit(solution)/shard_map/combine_back/pallas_call | solution.py:829
  280.7 15.6 %weight_grad.2 = (bf16[512,1024]{1,0:T(8,128)(2,1)}, bf16[512,1024]{1,0:T(8,128)(2,1)}, bf16[512,1024]{1,0:T(8,128)(2,1)}, bf16[256,1024]{1,0:T(8,128)(2,1)}, bf...) custom-call(s32[4]{0:T(128)} %get-tuple-element.137.starts_ref.turns_ref, bf16[2048,2048]{1,0:T(8,128)(2,1)} %get-tuple-element.210.left_ref, ...), custom_call_target="tpu_custom_call" | custom-call | flops 8589934 | bytes 16777 | tf_op jit(solution)/shard_map/weight_grad/pallas_call | solution.py:937
  302.1 4.0 collective-permute-start.38
  307.5 13.3 %attend_back.2 = bf16[1,1024,768]{2,1,0:T(8,128)(2,1)S(1)} custom-call(s32[8]{0:T(128)S(1)} %copy-done.43, bf16[1,1024,768]{2,1,0:T(8,128)(2,1)S(1)} %copy-done.19, bf16[2,1024,256]{2,1,0:T(8,128)(2,1)S(1)} %bitcast.44, f32[1024,128]{1,0:T(8,128)S(1)} %copy-done.9, f32[1024,128]{1,0:T(8,128)S(1)} %copy-done.10, f32[1024,128]{1,0:T(8,128)S(1)} %copy-done.11), custom_call_target="tpu_custom_call" | custom-call | flops 5368709 | bytes 4718 | tf_op jit(solution)/shard_map/attend_back/pallas_call | solution.py:288
  322.8 3.3 pass_on.6
  328.1 17.5 %project_back.2 = (bf16[256,2048]{1,0:T(8,128)(2,1)}, bf16[256,2048]{1,0:T(8,128)(2,1)}, bf16[256,2048]{1,0:T(8,128)(2,1)}, bf16[256,2048]{1,0:T(8,128)(2,1)}, f32[8,2048]{1,0:T(8,128)}) custom-call(s32[4]{0:T(128)} %get-tuple-element.137.starts_ref.turns_ref, bf16[1024,768]{1,0:T(8,128)(2,1)} %bitcast.40, ...), custom_call_target="tpu_custom_call" | custom-call | flops 7516192 | bytes 19922 | tf_op jit(solution)/shard_map/project_back/pallas_call | solution.py:886
  346.3 4.2 collective-permute-done.40.refs_1_
  351.9 13.3 %attend_back.3 = bf16[1,1024,768]{2,1,0:T(8,128)(2,1)S(1)} custom-call(s32[8]{0:T(128)S(1)} %copy-done.43, bf16[1,1024,768]{2,1,0:T(8,128)(2,1)S(1)} %copy-done.21, bf16[2,1024,256]{2,1,0:T(8,128)(2,1)S(1)} %bitcast.45, f32[1024,128]{1,0:T(8,128)S(1)} %copy-done.9, f32[1024,128]{1,0:T(8,128)S(1)} %copy-done.10, f32[1024,128]{1,0:T(8,128)S(1)} %copy-done.11), custom_call_target="tpu_custom_call" | custom-call | flops 5368709 | bytes 4718 | tf_op jit(solution)/shard_map/attend_back/pallas_call | solution.py:288
  368.4 3.5 collective-permute-start.48
  372.9 18.8 %project_back.3 = (bf16[256,2048]{1,0:T(8,128)(2,1)}, bf16[256,2048]{1,0:T(8,128)(2,1)}, bf16[256,2048]{1,0:T(8,128)(2,1)}, bf16[128,2048]{1,0:T(8,128)(2,1)}, b...) custom-call(s32[4]{0:T(128)} %get-tuple-element.137.starts_ref.turns_ref, bf16[1024,768]{1,0:T(8,128)(2,1)} %bitcast.42, ...), custom_call_target="tpu_custom_call" | custom-call | flops 7516192 | bytes 19922 | tf_op jit(solution)/shard_map/project_back/pallas_call | solution.py:886
  396.3 12.7 %weight_grad.3 = (bf16[528,768]{1,0:T(8,128)(2,1)}, bf16[528,768]{1,0:T(8,128)(2,1)}, bf16[528,768]{1,0:T(8,128)(2,1)}, bf16[256,768]{1,0:T(8,128)(2,1)}, bf16[272,768]{1,0:T(8,128)(2,1)}, /*index=5*/f32[8,768]{1,0:T(8,128)}) custom-call(s32[4]{0:T(128)} %get-tuple-element.137.starts_ref.turns_ref, bf16[2048,2048]{1,0:T(8,128)(2,1)} %get-tuple-element.210.left_ref, ...), custom_call_target="tpu_custom_call" | custom-call | flops 6442450 | bytes 14680 | tf_op jit(solution)/shard_map/weight_grad/pallas_call | solution.py:937
  411.1 7.6 %collective-permute-done.50.high_ref = bf16[128,2048]{1,0:T(8,128)(2,1)S(1)} collective-permute-done((bf16[128,2048]{1,0:T(8,128)(2,1)}, bf16[128,2048]{1,0:T(8,128)(2,1)S(1)}, u32[]{:S(2)}, u32[]{:S(2)}) %collective-permute-start.50) | collective-permute-done | bytes 524320 | tf_op jit(solution)/shard_map/ppermute | solution.py:86
  423.9 3.6 pass_on.8
  430.4 17.9 %down_grad.1 = (bf16[320,2048]{1,0:T(8,128)(2,1)}, bf16[320,2048]{1,0:T(8,128)(2,1)}, bf16[320,2048]{1,0:T(8,128)(2,1)}, bf16[160,2048]{1,0:T(8,128)(2,1)}, bf16[160,2048]{1,0:T(8,128)(2,1)}) custom-call(s32[4]{0:T(128)} %get-tuple-element.137.starts_ref.turns_ref, bf16[2048,1024]{1,0:T(8,128)(2,1)} %get-tuple-element.227.act_ref, ...), custom_call_target="tpu_custom_call" | custom-call | flops 10737418 | bytes 16777 | tf_op jit(solution)/shard_map/down_grad/pallas_call | solution.py:982
  454.4 10.1 %collective-permute-done.61.low_ref = bf16[160,2048]{1,0:T(8,128)(2,1)} collective-permute-done((bf16[160,2048]{1,0:T(8,128)(2,1)}, bf16[160,2048]{1,0:T(8,128)(2,1)}, u32[]{:S(2)}, u32[]{:S(2)}) %collective-permute-start.61) | collective-permute-done | bytes 655392 | tf_op jit(solution)/shard_map/ppermute | solution.py:85
  471.5 3.5 output_sum.1
  481.5 4.5 finish.1
  488.1 9.5 %collective-permute-done.63.refs_1_ = bf16[320,2048]{1,0:T(8,128)(2,1)} collective-permute-done((bf16[320,2048]{1,0:T(8,128)(2,1)}, bf16[320,2048]{1,0:T(8,128)(2,1)}, u32[]{:S(2)}, u32[]{:S(2)}) %collective-permute-start.63) | collective-permute-done | bytes 1310752 | tf_op jit(solution)/shard_map/ppermute | solution.py:96
  (310 shorter events, 142.8 us)
Async XLA Ops:
  7.2 146.5 %all-gather.2.cloned.1.call-start = ((), (), s32[]{:S(2)}) async-start(), calls=%async_computation | async-start | bytes 2162688 | tf_op jit(solution)/shard_map/all_gather | solution.py:1139
  8.6 32.2 %collective-permute-start.1 = (bf16[320,2048]{1,0:T(8,128)(2,1)S(1)}, bf16[320,2048]{1,0:T(8,128)(2,1)S(1)}, u32[]{:S(2)}, u32[]{:S(2)}) collective-permute-start(bf16[320,2048]{1,0:T(8,128)(2,1)S(1)} %constant_dynamic-update-slice_fusion.refs_0_.refs_10_), channel_id=1, source_target_pairs={{0,16},{8,0},{24,8},{16,24},{1,17},{9,1},{25,9},{17,25},{2,18},{10... | collective-permute-start | bytes 3932168 | tf_op jit(solution)/shard_map/ppermute | solution.py:71
  11.7 30.8 %collective-permute-start = (bf16[320,2048]{1,0:T(8,128)(2,1)S(1)}, bf16[320,2048]{1,0:T(8,128)(2,1)}, u32[]{:S(2)}, u32[]{:S(2)}) collective-permute-start(bf16[320,2048]{1,0:T(8,128)(2,1)S(1)} %constant_dynamic-update-slice_fusion.refs_0_.refs_10_), channel_id=1, source_target_pairs={{0,8},{8,24},{24,16},{16,0},{1,9},{9,25},{25,17},{17,1},{2,10},{10... | collective-permute-start | bytes 3932168 | tf_op jit(solution)/shard_map/ppermute | solution.py:71
  21.1 35.7 %collective-permute-start.8 = (bf16[128,1792]{1,0:T(8,128)(2,1)}, bf16[128,1792]{1,0:T(8,128)(2,1)}, u32[]{:S(2)}, u32[]{:S(2)}) collective-permute-start(bf16[128,1792]{1,0:T(8,128)(2,1)} %get-tuple-element.140), channel_id=1, source_target_pairs={{0,2},{1,3},{2,0},{3,1},{4,6},{5,7},{6,4},{7,5},{8,10},{9,11},{10,... | collective-permute-start | bytes 1376264 | tf_op jit(solution)/shard_map/ppermute | solution.py:39
  23.7 33.1 %collective-permute-start.9 = (bf16[128,1792]{1,0:T(8,128)(2,1)}, bf16[128,1792]{1,0:T(8,128)(2,1)}, u32[]{:S(2)}, u32[]{:S(2)}) collective-permute-start(bf16[128,1792]{1,0:T(8,128)(2,1)} %get-tuple-element.141), channel_id=1, source_target_pairs={{0,3},{1,2},{2,1},{3,0},{4,7},{5,6},{6,5},{7,4},{8,11},{9,10},{10,... | collective-permute-start | bytes 1376264 | tf_op jit(solution)/shard_map/ppermute | solution.py:39
  63.3 45.8 %collective-permute-start.13 = (bf16[512,1792]{1,0:T(8,128)(2,1)S(1)}, bf16[512,1792]{1,0:T(8,128)(2,1)S(1)}, u32[]{:S(2)}, u32[]{:S(2)}) collective-permute-start(bf16[512,1792]{1,0:T(8,128)(2,1)S(1)} %stack_rows.1.refs_10_.refs_0_), channel_id=1, source_target_pairs={{0,16},{8,0},{24,8},{16,24},{1,17},{9,1},{25,9},{17,25},{2,18},{10... | collective-permute-start | bytes 5505032 | tf_op jit(solution)/shard_map/ppermute | solution.py:71
  64.9 46.8 %collective-permute-start.11 = (bf16[512,1792]{1,0:T(8,128)(2,1)S(1)}, bf16[512,1792]{1,0:T(8,128)(2,1)S(1)}, u32[]{:S(2)}, u32[]{:S(2)}) collective-permute-start(bf16[512,1792]{1,0:T(8,128)(2,1)S(1)} %stack_rows.1.refs_10_.refs_0_), channel_id=1, source_target_pairs={{0,8},{8,24},{24,16},{16,0},{1,9},{9,25},{25,17},{17,1},{2,10},{10... | collective-permute-start | bytes 5505032 | tf_op jit(solution)/shard_map/ppermute | solution.py:71
  68.3 45.0 %collective-permute-start.4 = (bf16[256,2048]{1,0:T(8,128)(2,1)}, bf16[256,2048]{1,0:T(8,128)(2,1)}, u32[]{:S(2)}, u32[]{:S(2)}) collective-permute-start(bf16[256,2048]{1,0:T(8,128)(2,1)} %x_ref.3), channel_id=1, source_target_pairs={{0,3},{1,0},{2,1},{3,2},{4,7},{5,4},{6,5},{7,6},{8,11},{9,8},{10,9... | collective-permute-start | bytes 3145736 | tf_op jit(solution)/shard_map/ppermute | solution.py:71
  70.8 60.9 %collective-permute-start.2 = (bf16[256,2048]{1,0:T(8,128)(2,1)}, bf16[256,2048]{1,0:T(8,128)(2,1)}, u32[]{:S(2)}, u32[]{:S(2)}) collective-permute-start(bf16[256,2048]{1,0:T(8,128)(2,1)} %x_ref.3), channel_id=1, source_target_pairs={{0,1},{1,2},{2,3},{3,0},{4,5},{5,6},{6,7},{7,4},{8,9},{9,10},{10,1... | collective-permute-start | bytes 3145736 | tf_op jit(solution)/shard_map/ppermute | solution.py:71
  110.2 44.7 %collective-permute-start.14 = (bf16[256,1792]{1,0:T(8,128)(2,1)}, bf16[256,1792]{1,0:T(8,128)(2,1)}, u32[]{:S(2)}, u32[]{:S(2)}) collective-permute-start(bf16[256,1792]{1,0:T(8,128)(2,1)} %slice.138), channel_id=1, source_target_pairs={{0,16},{8,0},{24,8},{16,24},{1,17},{9,1},{25,9},{17,25},{2,18},{10... | collective-permute-start | bytes 2752520 | tf_op jit(solution)/shard_map/ppermute | solution.py:79
  112.8 42.1 %collective-permute-start.12 = (bf16[256,1792]{1,0:T(8,128)(2,1)}, bf16[256,1792]{1,0:T(8,128)(2,1)S(1)}, u32[]{:S(2)}, u32[]{:S(2)}) collective-permute-start(bf16[256,1792]{1,0:T(8,128)(2,1)} %slice.137), channel_id=1, source_target_pairs={{0,8},{8,24},{24,16},{16,0},{1,9},{9,25},{25,17},{17,1},{2,10},{10... | collective-permute-start | bytes 2752520 | tf_op jit(solution)/shard_map/ppermute | solution.py:79
  115.2 27.6 %collective-permute-start.5 = (bf16[128,2048]{1,0:T(8,128)(2,1)}, bf16[128,2048]{1,0:T(8,128)(2,1)}, u32[]{:S(2)}, u32[]{:S(2)}) collective-permute-start(bf16[128,2048]{1,0:T(8,128)(2,1)} %slice.132), channel_id=1, source_target_pairs={{0,3},{1,0},{2,1},{3,2},{4,7},{5,4},{6,5},{7,6},{8,11},{9,8},{10,9... | collective-permute-start | bytes 1572872 | tf_op jit(solution)/shard_map/ppermute | solution.py:79
  157.0 60.2 %collective-permute-start.22 = (bf16[256,2048]{1,0:T(8,128)(2,1)}, bf16[256,2048]{1,0:T(8,128)(2,1)}, u32[]{:S(2)}, u32[]{:S(2)}) collective-permute-start(bf16[256,2048]{1,0:T(8,128)(2,1)} %g_ref.1), channel_id=1, source_target_pairs={{0,3},{1,0},{2,1},{3,2},{4,7},{5,4},{6,5},{7,6},{8,11},{9,8},{10,9... | collective-permute-start | bytes 3145736 | tf_op jit(solution)/shard_map/ppermute | solution.py:71
  157.2 49.2 %collective-permute-start.19 = (bf16[160,2048]{1,0:T(8,128)(2,1)}, bf16[160,2048]{1,0:T(8,128)(2,1)}, u32[]{:S(2)}, u32[]{:S(2)}) collective-permute-start(bf16[160,2048]{1,0:T(8,128)(2,1)} %slice.129), channel_id=1, source_target_pairs={{0,8},{8,24},{24,16},{16,0},{1,9},{9,25},{25,17},{17,1},{2,10},{10... | collective-permute-start | bytes 1966088 | tf_op jit(solution)/shard_map/ppermute | solution.py:1146
  158.7 47.8 %collective-permute-start.20 = (bf16[160,2048]{1,0:T(8,128)(2,1)}, bf16[160,2048]{1,0:T(8,128)(2,1)}, u32[]{:S(2)}, u32[]{:S(2)}) collective-permute-start(bf16[160,2048]{1,0:T(8,128)(2,1)} %slice.130), channel_id=1, source_target_pairs={{0,16},{8,0},{24,8},{16,24},{1,17},{9,1},{25,9},{17,25},{2,18},{10... | collective-permute-start | bytes 1966088 | tf_op jit(solution)/shard_map/ppermute | solution.py:1146
  161.7 56.0 %collective-permute-start.21 = (bf16[256,2048]{1,0:T(8,128)(2,1)}, bf16[256,2048]{1,0:T(8,128)(2,1)}, u32[]{:S(2)}, u32[]{:S(2)}) collective-permute-start(bf16[256,2048]{1,0:T(8,128)(2,1)} %g_ref.1), channel_id=1, source_target_pairs={{0,1},{1,2},{2,3},{3,0},{4,5},{5,6},{6,7},{7,4},{8,9},{9,10},{10,1... | collective-permute-start | bytes 3145736 | tf_op jit(solution)/shard_map/ppermute | solution.py:71
  217.7 37.1 %collective-permute-start.29 = (bf16[256,2048]{1,0:T(8,128)(2,1)}, bf16[256,2048]{1,0:T(8,128)(2,1)}, u32[]{:S(2)}, u32[]{:S(2)}) collective-permute-start(bf16[256,2048]{1,0:T(8,128)(2,1)} %g_ref.1), channel_id=1, source_target_pairs={{0,4},{4,0},{1,5},{5,1},{2,6},{6,2},{3,7},{7,3},{8,12},{12,8},{9,1... | collective-permute-start | bytes 3145736 | tf_op jit(solution)/shard_map/ppermute | solution.py:152
  220.3 38.3 %collective-permute-start.31 = (bf16[256,2048]{1,0:T(8,128)(2,1)}, bf16[256,2048]{1,0:T(8,128)(2,1)}, u32[]{:S(2)}, u32[]{:S(2)}) collective-permute-start(bf16[256,2048]{1,0:T(8,128)(2,1)} %collective-permute-done.22.refs_2_), channel_id=1, source_target_pairs={{0,4},{4,0},{1,5},{5,1},{2,6},{6,2},{3,7},{7,3},{8,12},{12,8},{9,1... | collective-permute-start | bytes 3145736 | tf_op jit(solution)/shard_map/ppermute | solution.py:152
  222.4 31.9 %collective-permute-start.28 = (bf16[128,2048]{1,0:T(8,128)(2,1)}, bf16[128,2048]{1,0:T(8,128)(2,1)S(1)}, u32[]{:S(2)}, u32[]{:S(2)}) collective-permute-start(bf16[128,2048]{1,0:T(8,128)(2,1)} %slice.147), channel_id=1, source_target_pairs={{0,3},{1,0},{2,1},{3,2},{4,7},{5,4},{6,5},{7,6},{8,11},{9,8},{10,9... | collective-permute-start | bytes 1572872 | tf_op jit(solution)/shard_map/ppermute | solution.py:79
  227.4 26.9 %collective-permute-start.27 = (bf16[128,2048]{1,0:T(8,128)(2,1)}, bf16[128,2048]{1,0:T(8,128)(2,1)}, u32[]{:S(2)}, u32[]{:S(2)}) collective-permute-start(bf16[128,2048]{1,0:T(8,128)(2,1)} %slice.146), channel_id=1, source_target_pairs={{0,1},{1,2},{2,3},{3,0},{4,5},{5,6},{6,7},{7,4},{8,9},{9,10},{10,1... | collective-permute-start | bytes 1572872 | tf_op jit(solution)/shard_map/ppermute | solution.py:79
  228.8 29.9 %collective-permute-start.30 = (bf16[256,2048]{1,0:T(8,128)(2,1)}, bf16[256,2048]{1,0:T(8,128)(2,1)}, u32[]{:S(2)}, u32[]{:S(2)}) collective-permute-start(bf16[256,2048]{1,0:T(8,128)(2,1)} %collective-permute-done.21.refs_1_), channel_id=1, source_target_pairs={{0,4},{4,0},{1,5},{5,1},{2,6},{6,2},{3,7},{7,3},{8,12},{12,8},{9,1... | collective-permute-start | bytes 3145736 | tf_op jit(solution)/shard_map/ppermute | solution.py:152
  254.8 43.5 %collective-permute-start.34 = (bf16[128,2048]{1,0:T(8,128)(2,1)S(1)}, bf16[128,2048]{1,0:T(8,128)(2,1)S(1)}, u32[]{:S(2)}, u32[]{:S(2)}) collective-permute-start(bf16[128,2048]{1,0:T(8,128)(2,1)S(1)} %get-tuple-element.167), channel_id=1, source_target_pairs={{0,3},{1,0},{2,1},{3,2},{4,7},{5,4},{6,5},{7,6},{8,11},{9,8},{10,9... | collective-permute-start | bytes 1572872 | tf_op jit(solution)/shard_map/ppermute | solution.py:85
  258.6 40.5 %collective-permute-start.35 = (bf16[128,2048]{1,0:T(8,128)(2,1)S(1)}, bf16[128,2048]{1,0:T(8,128)(2,1)}, u32[]{:S(2)}, u32[]{:S(2)}) collective-permute-start(bf16[128,2048]{1,0:T(8,128)(2,1)S(1)} %get-tuple-element.168), channel_id=1, source_target_pairs={{0,1},{1,2},{2,3},{3,0},{4,5},{5,6},{6,7},{7,4},{8,9},{9,10},{10,1... | collective-permute-start | bytes 1572872 | tf_op jit(solution)/shard_map/ppermute | solution.py:86
  296.3 25.7 %collective-permute-start.36 = (bf16[256,1024]{1,0:T(8,128)(2,1)}, bf16[256,1024]{1,0:T(8,128)(2,1)S(1)}, u32[]{:S(2)}, u32[]{:S(2)}) collective-permute-start(bf16[256,1024]{1,0:T(8,128)(2,1)} %get-tuple-element.179), channel_id=1, source_target_pairs={{0,16},{8,0},{24,8},{16,24},{1,17},{9,1},{25,9},{17,25},{2,18},{10... | collective-permute-start | bytes 1572872 | tf_op jit(solution)/shard_map/ppermute | solution.py:85
  302.1 43.6 %collective-permute-start.38 = (bf16[256,2048]{1,0:T(8,128)(2,1)}, bf16[256,2048]{1,0:T(8,128)(2,1)}, u32[]{:S(2)}, u32[]{:S(2)}) collective-permute-start(bf16[256,2048]{1,0:T(8,128)(2,1)} %get-tuple-element.182), channel_id=1, source_target_pairs={{0,3},{1,0},{2,1},{3,2},{4,7},{5,4},{6,5},{7,6},{8,11},{9,8},{10,9... | collective-permute-start | bytes 3145736 | tf_op jit(solution)/shard_map/ppermute | solution.py:96
  328.1 39.3 %collective-permute-start.39 = (bf16[256,2048]{1,0:T(8,128)(2,1)}, bf16[256,2048]{1,0:T(8,128)(2,1)}, u32[]{:S(2)}, u32[]{:S(2)}) collective-permute-start(bf16[256,2048]{1,0:T(8,128)(2,1)} %get-tuple-element.183), channel_id=1, source_target_pairs={{0,1},{1,2},{2,3},{3,0},{4,5},{5,6},{6,7},{7,4},{8,9},{9,10},{10,1... | collective-permute-start | bytes 3145736 | tf_op jit(solution)/shard_map/ppermute | solution.py:97
  392.8 25.9 %collective-permute-start.50 = (bf16[128,2048]{1,0:T(8,128)(2,1)}, bf16[128,2048]{1,0:T(8,128)(2,1)S(1)}, u32[]{:S(2)}, u32[]{:S(2)}) collective-permute-start(bf16[128,2048]{1,0:T(8,128)(2,1)} %get-tuple-element.221), channel_id=1, source_target_pairs={{0,1},{1,2},{2,3},{3,0},{4,5},{5,6},{6,7},{7,4},{8,9},{9,10},{10,1... | collective-permute-start | bytes 1572872 | tf_op jit(solution)/shard_map/ppermute | solution.py:86
  429.5 24.9 %collective-permute-start.53 = (bf16[256,2048]{1,0:T(8,128)(2,1)}, bf16[256,2048]{1,0:T(8,128)(2,1)S(1)}, u32[]{:S(2)}, u32[]{:S(2)}) collective-permute-start(bf16[256,2048]{1,0:T(8,128)(2,1)} %get-tuple-element.222), channel_id=1, source_target_pairs={{0,3},{1,0},{2,1},{3,2},{4,7},{5,4},{6,5},{7,6},{8,11},{9,8},{10,9... | collective-permute-start | bytes 3145736 | tf_op jit(solution)/shard_map/ppermute | solution.py:96
  450.4 25.8 %collective-permute-start.54 = (bf16[256,2048]{1,0:T(8,128)(2,1)}, bf16[256,2048]{1,0:T(8,128)(2,1)}, u32[]{:S(2)}, u32[]{:S(2)}) collective-permute-start(bf16[256,2048]{1,0:T(8,128)(2,1)} %get-tuple-element.223), channel_id=1, source_target_pairs={{0,1},{1,2},{2,3},{3,0},{4,5},{5,6},{6,7},{7,4},{8,9},{9,10},{10,1... | collective-permute-start | bytes 3145736 | tf_op jit(solution)/shard_map/ppermute | solution.py:97
  468.7 28.9 %collective-permute-start.63 = (bf16[320,2048]{1,0:T(8,128)(2,1)}, bf16[320,2048]{1,0:T(8,128)(2,1)}, u32[]{:S(2)}, u32[]{:S(2)}) collective-permute-start(bf16[320,2048]{1,0:T(8,128)(2,1)} %get-tuple-element.247), channel_id=1, source_target_pairs={{0,16},{8,0},{24,8},{16,24},{1,17},{9,1},{25,9},{17,25},{2,18},{10... | collective-permute-start | bytes 3932168 | tf_op jit(solution)/shard_map/ppermute | solution.py:96
  469.9 28.6 %collective-permute-start.64 = (bf16[320,2048]{1,0:T(8,128)(2,1)}, bf16[320,2048]{1,0:T(8,128)(2,1)}, u32[]{:S(2)}, u32[]{:S(2)}) collective-permute-start(bf16[320,2048]{1,0:T(8,128)(2,1)} %get-tuple-element.248), channel_id=1, source_target_pairs={{0,8},{8,24},{24,16},{16,0},{1,9},{9,25},{25,17},{17,1},{2,10},{10... | collective-permute-start | bytes 3932168 | tf_op jit(solution)/shard_map/ppermute | solution.py:97
  476.4 25.5 %collective-permute-start.57 = (bf16[160,768]{1,0:T(8,128)(2,1)S(1)}, bf16[160,768]{1,0:T(8,128)(2,1)S(1)}, u32[]{:S(2)}, u32[]{:S(2)}) collective-permute-start(bf16[160,768]{1,0:T(8,128)(2,1)S(1)} %get-tuple-element.237), channel_id=1, source_target_pairs={{0,1},{1,0},{2,3},{3,2},{4,5},{5,4},{6,7},{7,6},{8,9},{9,8},{10,11... | collective-permute-start | bytes 737288 | tf_op jit(solution)/shard_map/ppermute | solution.py:39
  (103 other events, 1390.2 us)
Sparse Core Ops, SparseCore 0:
  14.4 81.3 all-gather.1

commit v6 on v5

--- a/solution.py
+++ b/solution.py
@@ -59,6 +59,12 @@
 def slot_plan(n, rows, first=0):
     plan = [((first + k, 0, rows),) for k in range(n - 1)]
     return plan + [((first + n - 1, 0, half_of(rows)), (first + n, half_of(rows), rows - half_of(rows)))]
+
+
+def direct_scattered(parts, axis, order):
+    return [parts[0]] + [
+        lax.ppermute(part, axis, ring_pairs(order, o)) for part, o in zip(parts[1:], ring_offsets(len(order))[1:])
+    ]
 
 
 def ring_halves(own, axis, order):
@@ -919,7 +925,11 @@
     block = total.astype(BF)
     if with_tail:
         block = jnp.concatenate([block, tail_refs[0][0]], 0)
-    put_block(slot_plan(held.shape[0], held.shape[1]), block, held, out_refs, sem)
+    if with_tail:
+        plan = [((k, 0, held.shape[1]),) for k in range(held.shape[0])]
+    else:
+        plan = slot_plan(held.shape[0], held.shape[1])
+    put_block(plan, block, held, out_refs, sem)
 
 
 def slot_shapes(n, rows, columns):
@@ -933,7 +943,7 @@
     part = wide // n_q
     rows = part + (0 if tail is None else tail.shape[1])
     extra = [] if tail is None else [tail]
-    shapes = slot_shapes(n_q, rows, columns)
+    shapes = slot_shapes(n_q, rows, columns) if tail is None else [jax.ShapeDtypeStruct((rows, columns), BF)] * n_q
     *out, sums = pl.pallas_call(
         partial(weight_grad_kernel, len(rights), len(extra)),
         grid_spec=pltpu.PrefetchScalarGridSpec(
@@ -1214,14 +1224,13 @@
         at, sums_own, sums_other, g_sums, up_sums, (n_q, n_t, heads, head_dim, units), (d_rows, qkv_bias.shape[0]), split
     )
     qkv_own, _ = weight_grad(turns, after(hidden, *normed_own), [grad_own, grad_other], vectors)
-    qkv_first = ring_first(qkv_own, "q", q_order)
+    qkv_parts = direct_scattered(qkv_own, "q", q_order)
     normed_own = [after(p, *up_came[1:]) for p in normed_own]
     normed_first = ring_first(normed_own, "ctx", z_order)
     normed_parts, normed_sent = ring_rest(normed_own, normed_first, "ctx", z_order, qkv_own)
-    qkv_parts, qkv_sent = ring_rest(qkv_own, qkv_first, "q", q_order, normed_sent, 2 * n_t)
     qkv_rows = last_sum(at, qkv_parts, n_t, 2 * n_t)
-    down, out_apart = down_grad(turns, after(act, *qkv_sent), (att_own, att_other), g_all, head_dim if whole_heads else 0)
-    down_parts, down_sent = ring_sum([after(p, *qkv_parts[1:]) for p in down], "q", q_order, [normed_parts[1], *qkv_rows])
+    down, out_apart = down_grad(turns, after(act, *normed_sent), (att_own, att_other), g_all, head_dim if whole_heads else 0)
+    down_parts, down_sent = ring_sum([after(p, *qkv_parts[1:-1]) for p in down], "q", q_order, [normed_parts[1], *qkv_rows])
     output = output_sum(inputs, b_out + b_down, [after(out_parts[0], *normed_sent, *down)] + out_parts[1:])
 
     qkv_came = scattered(qkv_rows, "ctx")

time: 521 us -> 518 us (level)
    pallas_call x5 -> x4, Pallas kernels: 16 us -> 12.5 us  [pass_on(): pl.pallas_call(partial(pass_on_kernel, tail), grid=(columns // wide,), in...]
    unnamed x140 -> x136, local copies, waits for them, and re-layouts: 29.1 us -> 28.3 us
    ppermute x5 -> x4, waiting for transfers between devices: 15.6 us -> 16.4 us  [ring_rest(): low = lax.ppermute(sent[0], axis, ring_pairs(order, -1))]
  transfers between devices with their start and end apart: 67 -> 66, of which waited for: 20 -> 19; matrix products, arithmetic and copies ran while one was open for 4% -> 4% of each run, Pallas kernels for 47% -> 47%
where the time goes in v6:
time: 518 us; the launch traced here: 512 us
  Pallas kernels  242 us (47%)
  waiting for transfers between devices  138 us (27%)
  starting transfers between devices  67.7 us (13%)
  local copies, waits for them, and re-layouts  47.1 us (9%)
  between operations  15.2 us (3%)
    ppermute x4, waiting for transfers between devices, ring_halves(): lax.ppermute(down, axis, down_pairs)  46.7 us
    pallas_call x2, Pallas kernels, project_back(): pl.pallas_call(partial(project_back_kernel, split, w.plan, len(w.arrays),...  36.3 us
    pallas_call x1, Pallas kernels, project(): pl.pallas_call(partial(project_kernel, split, x_plan, len(x_arrays), w.pl...  32 us
    pallas_call x2, Pallas kernels, weight_grad(): pl.pallas_call(partial(weight_grad_kernel, len(rights), len(extra)), grid...  28.3 us
    unnamed x136, local copies, waits for them, and re-layouts  28.3 us
    pallas_call x2, Pallas kernels, attend_back(): pl.pallas_call(partial(attend_back_kernel, heads, head_dim, span), grid_s...  26.5 us
    pallas_call x1, Pallas kernels, combine_back(): pl.pallas_call(partial(combine_back_kernel, split, g_plan, len(g_arrays),...  20.4 us
    pallas_call x2, Pallas kernels, combine(): pl.pallas_call(partial(combine_kernel, split, w.plan, len(w.arrays), plan...  20.3 us
  transfers between devices with their start and end apart: 66, of which 19 were waited for; matrix products, arithmetic and copies ran while one was open for 4% of the time, Pallas kernels for 47%

profile of v6, /device:TPU:0, one launch (start us, length us, event | category | flops | bytes accessed | tf_op | source)
XLA Modules:
  0.0 512.0 jit_solution(11176606293456902260)
XLA Ops:
  25.7 15.2 %collective-permute-done.1.refs_2_.refs_12_ = bf16[320,2048]{1,0:T(8,128)(2,1)S(1)} collective-permute-done((bf16[320,2048]{1,0:T(8,128)(2,1)S(1)}, bf16[320,2048]{1,0:T(8,128)(2,1)S(1)}, u32[]{:S(2)}, u32[]{:S(2)}) %collective-permute-start.1) | collective-permute-done | bytes 1310752 | tf_op jit(solution)/shard_map/ppermute | solution.py:77
  42.5 14.4 %collective-permute-done.8.refs_2_ = bf16[128,1792]{1,0:T(8,128)(2,1)} collective-permute-done((bf16[128,1792]{1,0:T(8,128)(2,1)}, bf16[128,1792]{1,0:T(8,128)(2,1)}, u32[]{:S(2)}, u32[]{:S(2)}) %collective-permute-start.8) | collective-permute-done | bytes 458784 | tf_op jit(solution)/shard_map/ppermute | solution.py:39
  70.8 6.8 %collective-permute-start.2 = (bf16[256,2048]{1,0:T(8,128)(2,1)}, bf16[256,2048]{1,0:T(8,128)(2,1)}, u32[]{:S(2)}, u32[]{:S(2)}) collective-permute-start(bf16[256,2048]{1,0:T(8,128)(2,1)} %x_ref.3), channel_id=1, source_target_pairs={{0,1},{1,2},{2,3},{3,0},{4,5},{5,6},{6,7},{7,4},{8,9},{9,10},{10,1... | collective-permute-start | bytes 3145736 | tf_op jit(solution)/shard_map/ppermute | solution.py:77
  77.6 31.5 %collective-permute-done.13.refs_12_.refs_2_ = bf16[512,1792]{1,0:T(8,128)(2,1)S(1)} collective-permute-done((bf16[512,1792]{1,0:T(8,128)(2,1)S(1)}, bf16[512,1792]{1,0:T(8,128)(2,1)S(1)}, u32[]{:S(2)}, u32[]{:S(2)}) %collective-permute-start.13) | collective-permute-done | bytes 1835040 | tf_op jit(solution)/shard_map/ppermute | solution.py:77
  117.7 14.0 %collective-permute-done.2.refs_1_ = bf16[256,2048]{1,0:T(8,128)(2,1)} collective-permute-done((bf16[256,2048]{1,0:T(8,128)(2,1)}, bf16[256,2048]{1,0:T(8,128)(2,1)}, u32[]{:S(2)}, u32[]{:S(2)}) %collective-permute-start.2) | collective-permute-done | bytes 1048608 | tf_op jit(solution)/shard_map/ppermute | solution.py:77
  133.6 4.1 rotary_tables.1
  137.7 5.2 %collective-permute-done.5.refs_4_ = bf16[128,2048]{1,0:T(8,128)(2,1)} collective-permute-done((bf16[128,2048]{1,0:T(8,128)(2,1)}, bf16[128,2048]{1,0:T(8,128)(2,1)}, u32[]{:S(2)}, u32[]{:S(2)}) %collective-permute-start.5) | collective-permute-done | bytes 524320 | tf_op jit(solution)/shard_map/ppermute | solution.py:85
  142.8 10.9 %collective-permute-done.3.refs_3_ = bf16[128,2048]{1,0:T(8,128)(2,1)} collective-permute-done((bf16[128,2048]{1,0:T(8,128)(2,1)}, bf16[128,2048]{1,0:T(8,128)(2,1)}, u32[]{:S(2)}, u32[]{:S(2)}) %collective-permute-start.3) | collective-permute-done | bytes 524320 | tf_op jit(solution)/shard_map/ppermute | solution.py:85
  163.6 32.0 %project.1 = (bf16[2048,2048]{1,0:T(8,128)(2,1)}, bf16[2048,2048]{1,0:T(8,128)(2,1)}, f32[2048,768]{1,0:T(8,128)}, bf16[2048,1024]{1,0:T(8,128)(2,1)}, bf16[2048,1024]{1,0:T(8,128)(2,1)}) custom-call(s32[4]{0:T(128)} %get-tuple-element.133.starts_ref.turns_ref, bf16[256,2048]{1,0:T(8,128)(2,1)} %x_ref.3, bf16[256,2048]{1,0:T(8,128)(2,1)} %collective-permute-done.2.refs_1_, ...), custom_call_target="tpu_custom_call" | custom-call | flops 15032385 | bytes 40894 | tf_op jit(solution)/shard_map/project/pallas_call | solution.py:719
  198.4 7.9 %attend.2 = (bf16[1,1024,256]{2,1,0:T(8,128)(2,1)S(1)}, bf16[1,1024,768]{2,1,0:T(8,128)(2,1)S(1)}) custom-call(s32[8]{0:T(128)S(1)} %copy-done.43, f32[2,1024,768]{2,1,0:T(8,128)S(1)} %bitcast.36, f32[1024,128]{1,0:T(8,128)S(1)} %copy-done.9, f32[1024,128]{1,0:T(8,128)S(1)} %copy-done.10, f32[1024,128]{1,0:T(8,128)S(1)} %copy-done.11), custom_call_target="tpu_custom_call" | custom-call | flops 2147483 | bytes 6291 | tf_op jit(solution)/shard_map/attend/pallas_call | solution.py:267
  206.4 10.1 %combine.2 = (bf16[256,2048]{1,0:T(8,128)(2,1)S(1)}, bf16[256,2048]{1,0:T(8,128)(2,1)S(1)}, bf16[256,2048]{1,0:T(8,128)(2,1)S(1)}, bf16[256,2048]{1,0:T(8,128)(2,1)S(1)}) custom-call(s32[4]{0:T(128)S(1)} %copy-done.39, bf16[2048,1024]{1,0:T(8,128)(2,1)S(1)} %copy-done, bf16[1024,256]{1,0:T(8,128)(2,1)S(1)} %bitcast.46, ...), custom_call_target="tpu_custom_call" | custom-call | flops 5368709 | bytes 13631 | tf_op jit(solution)/shard_map/combine/pallas_call | solution.py:774
  228.8 7.9 %attend.3 = (bf16[1,1024,256]{2,1,0:T(8,128)(2,1)S(1)}, bf16[1,1024,768]{2,1,0:T(8,128)(2,1)S(1)}) custom-call(s32[8]{0:T(128)S(1)} %copy-done.43, f32[2,1024,768]{2,1,0:T(8,128)S(1)} %bitcast.39, f32[1024,128]{1,0:T(8,128)S(1)} %copy-done.9, f32[1024,128]{1,0:T(8,128)S(1)} %copy-done.10, f32[1024,128]{1,0:T(8,128)S(1)} %copy-done.11), custom_call_target="tpu_custom_call" | custom-call | flops 2147483 | bytes 6291 | tf_op jit(solution)/shard_map/attend/pallas_call | solution.py:267
  240.9 10.3 %combine.3 = (bf16[256,2048]{1,0:T(8,128)(2,1)S(1)}, bf16[256,2048]{1,0:T(8,128)(2,1)S(1)}, bf16[256,2048]{1,0:T(8,128)(2,1)S(1)}, bf16[128,2048]{1,0:T(8,128)(2,1)S(1)}, bf16[128,2048]{1,0:T(8,128)(2,1)S(1)}) custom-call(s32[4]{0:T(128)S(1)} %copy-done.39, bf16[2048,1024]{1,0:T(8,128)(2,1)S(1)} %copy-done, bf16[1024,256]{1,0:T(8,128)(2,1)S(1)} %bitcast.49, ...), custom_call_target="tpu_custom_call" | custom-call | flops 5368709 | bytes 13631 | tf_op jit(solution)/shard_map/combine/pallas_call | solution.py:774
  254.7 3.8 collective-permute-start.34
  260.1 20.4 %combine_back.1 = (bf16[2048,2048]{1,0:T(8,128)(2,1)}, bf16[2048,1024]{1,0:T(8,128)(2,1)}, bf16[2048,256]{1,0:T(8,128)(2,1)}, f32[8,2048]{1,0:T(8,128)}) custom-call(s32[4]{0:T(128)} %get-tuple-element.133.starts_ref.turns_ref, bf16[256,2048]{1,0:T(8,128)(2,1)} %g_ref.1, bf16[256,2048]{1,0:T(8,128)(2,1)} %collective-permute-done.21.refs_1_, ...), custom_call_target="tpu_custom_call" | custom-call | flops 10737418 | bytes 30408 | tf_op jit(solution)/shard_map/combine_back/pallas_call | solution.py:835
  280.6 15.6 %weight_grad.2 = (bf16[512,1024]{1,0:T(8,128)(2,1)}, bf16[512,1024]{1,0:T(8,128)(2,1)}, bf16[512,1024]{1,0:T(8,128)(2,1)}, bf16[256,1024]{1,0:T(8,128)(2,1)}, bf...) custom-call(s32[4]{0:T(128)} %get-tuple-element.133.starts_ref.turns_ref, bf16[2048,2048]{1,0:T(8,128)(2,1)} %get-tuple-element.206.left_ref, ...), custom_call_target="tpu_custom_call" | custom-call | flops 8589934 | bytes 16777 | tf_op jit(solution)/shard_map/weight_grad/pallas_call | solution.py:947
  302.0 4.0 collective-permute-start.38
  307.4 13.3 %attend_back.2 = bf16[1,1024,768]{2,1,0:T(8,128)(2,1)S(1)} custom-call(s32[8]{0:T(128)S(1)} %copy-done.43, bf16[1,1024,768]{2,1,0:T(8,128)(2,1)S(1)} %copy-done.19, bf16[2,1024,256]{2,1,0:T(8,128)(2,1)S(1)} %bitcast.44, f32[1024,128]{1,0:T(8,128)S(1)} %copy-done.9, f32[1024,128]{1,0:T(8,128)S(1)} %copy-done.10, f32[1024,128]{1,0:T(8,128)S(1)} %copy-done.11), custom_call_target="tpu_custom_call" | custom-call | flops 5368709 | bytes 4718 | tf_op jit(solution)/shard_map/attend_back/pallas_call | solution.py:294
  322.7 3.3 pass_on.5
  328.0 17.5 %project_back.2 = (bf16[256,2048]{1,0:T(8,128)(2,1)}, bf16[256,2048]{1,0:T(8,128)(2,1)}, bf16[256,2048]{1,0:T(8,128)(2,1)}, bf16[256,2048]{1,0:T(8,128)(2,1)}, f32[8,2048]{1,0:T(8,128)}) custom-call(s32[4]{0:T(128)} %get-tuple-element.133.starts_ref.turns_ref, bf16[1024,768]{1,0:T(8,128)(2,1)} %bitcast.40, ...), custom_call_target="tpu_custom_call" | custom-call | flops 7516192 | bytes 19922 | tf_op jit(solution)/shard_map/project_back/pallas_call | solution.py:892
  346.1 4.2 collective-permute-done.40.refs_1_
  351.8 13.3 %attend_back.3 = bf16[1,1024,768]{2,1,0:T(8,128)(2,1)S(1)} custom-call(s32[8]{0:T(128)S(1)} %copy-done.43, bf16[1,1024,768]{2,1,0:T(8,128)(2,1)S(1)} %copy-done.21, bf16[2,1024,256]{2,1,0:T(8,128)(2,1)S(1)} %bitcast.45, f32[1024,128]{1,0:T(8,128)S(1)} %copy-done.9, f32[1024,128]{1,0:T(8,128)S(1)} %copy-done.10, f32[1024,128]{1,0:T(8,128)S(1)} %copy-done.11), custom_call_target="tpu_custom_call" | custom-call | flops 5368709 | bytes 4718 | tf_op jit(solution)/shard_map/attend_back/pallas_call | solution.py:294
  368.2 3.5 collective-permute-start.48
  372.7 18.8 %project_back.3 = (bf16[256,2048]{1,0:T(8,128)(2,1)}, bf16[256,2048]{1,0:T(8,128)(2,1)}, bf16[256,2048]{1,0:T(8,128)(2,1)}, bf16[128,2048]{1,0:T(8,128)(2,1)}, b...) custom-call(s32[4]{0:T(128)} %get-tuple-element.133.starts_ref.turns_ref, bf16[1024,768]{1,0:T(8,128)(2,1)} %bitcast.42, ...), custom_call_target="tpu_custom_call" | custom-call | flops 7516192 | bytes 19922 | tf_op jit(solution)/shard_map/project_back/pallas_call | solution.py:892
  396.1 12.8 %weight_grad.3 = (bf16[528,768]{1,0:T(8,128)(2,1)}, bf16[528,768]{1,0:T(8,128)(2,1)}, bf16[528,768]{1,0:T(8,128)(2,1)}, bf16[528,768]{1,0:T(8,128)(2,1)}, f32[8,768]{1,0:T(8,128)}) custom-call(s32[4]{0:T(128)} %get-tuple-element.133.starts_ref.turns_ref, bf16[2048,2048]{1,0:T(8,128)(2,1)} %get-tuple-element.206.left_ref, bf16[1024,768]{1,0:T(8,128)(2,1)} %bitcast.43, ...), custom_call_target="tpu_custom_call" | custom-call | flops 6442450 | bytes 14680 | tf_op jit(solution)/shard_map/weight_grad/pallas_call | solution.py:947
  411.0 7.7 %collective-permute-done.50.high_ref = bf16[128,2048]{1,0:T(8,128)(2,1)} collective-permute-done((bf16[128,2048]{1,0:T(8,128)(2,1)}, bf16[128,2048]{1,0:T(8,128)(2,1)}, u32[]{:S(2)}, u32[]{:S(2)}) %collective-permute-start.50) | collective-permute-done | bytes 524320 | tf_op jit(solution)/shard_map/ppermute | solution.py:92
  424.4 17.9 %down_grad.1 = (bf16[320,2048]{1,0:T(8,128)(2,1)}, bf16[320,2048]{1,0:T(8,128)(2,1)}, bf16[320,2048]{1,0:T(8,128)(2,1)}, bf16[160,2048]{1,0:T(8,128)(2,1)}, bf16[160,2048]{1,0:T(8,128)(2,1)}) custom-call(s32[4]{0:T(128)} %get-tuple-element.133.starts_ref.turns_ref, bf16[2048,1024]{1,0:T(8,128)(2,1)} %get-tuple-element.219.act_ref, ...), custom_call_target="tpu_custom_call" | custom-call | flops 10737418 | bytes 16777 | tf_op jit(solution)/shard_map/down_grad/pallas_call | solution.py:992
  445.2 3.5 collective-permute-done.55.refs_3_
  450.5 9.4 %collective-permute-done.60.low_ref = bf16[160,2048]{1,0:T(8,128)(2,1)} collective-permute-done((bf16[160,2048]{1,0:T(8,128)(2,1)}, bf16[160,2048]{1,0:T(8,128)(2,1)}, u32[]{:S(2)}, u32[]{:S(2)}) %collective-permute-start.60) | collective-permute-done | bytes 655392 | tf_op jit(solution)/shard_map/ppermute | solution.py:91
  467.2 3.5 output_sum.1
  476.0 4.5 finish.1
  482.6 12.3 %collective-permute-done.62.refs_1_ = bf16[320,2048]{1,0:T(8,128)(2,1)} collective-permute-done((bf16[320,2048]{1,0:T(8,128)(2,1)}, bf16[320,2048]{1,0:T(8,128)(2,1)}, u32[]{:S(2)}, u32[]{:S(2)}) %collective-permute-start.62) | collective-permute-done | bytes 1310752 | tf_op jit(solution)/shard_map/ppermute | solution.py:102
  (303 shorter events, 137.4 us)
Async XLA Ops:
  7.2 146.6 %all-gather.2.cloned.1.call-start = ((), (), s32[]{:S(2)}) async-start(), calls=%async_computation | async-start | bytes 2162688 | tf_op jit(solution)/shard_map/all_gather | solution.py:1149
  8.6 32.2 %collective-permute-start.1 = (bf16[320,2048]{1,0:T(8,128)(2,1)S(1)}, bf16[320,2048]{1,0:T(8,128)(2,1)S(1)}, u32[]{:S(2)}, u32[]{:S(2)}) collective-permute-start(bf16[320,2048]{1,0:T(8,128)(2,1)S(1)} %constant_dynamic-update-slice_fusion.refs_0_.refs_10_), channel_id=1, source_target_pairs={{0,16},{8,0},{24,8},{16,24},{1,17},{9,1},{25,9},{17,25},{2,18},{10... | collective-permute-start | bytes 3932168 | tf_op jit(solution)/shard_map/ppermute | solution.py:77
  11.7 30.8 %collective-permute-start = (bf16[320,2048]{1,0:T(8,128)(2,1)S(1)}, bf16[320,2048]{1,0:T(8,128)(2,1)}, u32[]{:S(2)}, u32[]{:S(2)}) collective-permute-start(bf16[320,2048]{1,0:T(8,128)(2,1)S(1)} %constant_dynamic-update-slice_fusion.refs_0_.refs_10_), channel_id=1, source_target_pairs={{0,8},{8,24},{24,16},{16,0},{1,9},{9,25},{25,17},{17,1},{2,10},{10... | collective-permute-start | bytes 3932168 | tf_op jit(solution)/shard_map/ppermute | solution.py:77
  21.2 35.7 %collective-permute-start.8 = (bf16[128,1792]{1,0:T(8,128)(2,1)}, bf16[128,1792]{1,0:T(8,128)(2,1)}, u32[]{:S(2)}, u32[]{:S(2)}) collective-permute-start(bf16[128,1792]{1,0:T(8,128)(2,1)} %get-tuple-element.136), channel_id=1, source_target_pairs={{0,2},{1,3},{2,0},{3,1},{4,6},{5,7},{6,4},{7,5},{8,10},{9,11},{10,... | collective-permute-start | bytes 1376264 | tf_op jit(solution)/shard_map/ppermute | solution.py:39
  23.7 33.1 %collective-permute-start.9 = (bf16[128,1792]{1,0:T(8,128)(2,1)}, bf16[128,1792]{1,0:T(8,128)(2,1)}, u32[]{:S(2)}, u32[]{:S(2)}) collective-permute-start(bf16[128,1792]{1,0:T(8,128)(2,1)} %get-tuple-element.137), channel_id=1, source_target_pairs={{0,3},{1,2},{2,1},{3,0},{4,7},{5,6},{6,5},{7,4},{8,11},{9,10},{10,... | collective-permute-start | bytes 1376264 | tf_op jit(solution)/shard_map/ppermute | solution.py:39
  63.3 45.8 %collective-permute-start.13 = (bf16[512,1792]{1,0:T(8,128)(2,1)S(1)}, bf16[512,1792]{1,0:T(8,128)(2,1)S(1)}, u32[]{:S(2)}, u32[]{:S(2)}) collective-permute-start(bf16[512,1792]{1,0:T(8,128)(2,1)S(1)} %stack_rows.1.refs_10_.refs_0_), channel_id=1, source_target_pairs={{0,16},{8,0},{24,8},{16,24},{1,17},{9,1},{25,9},{17,25},{2,18},{10... | collective-permute-start | bytes 5505032 | tf_op jit(solution)/shard_map/ppermute | solution.py:77
  64.9 46.8 %collective-permute-start.11 = (bf16[512,1792]{1,0:T(8,128)(2,1)S(1)}, bf16[512,1792]{1,0:T(8,128)(2,1)S(1)}, u32[]{:S(2)}, u32[]{:S(2)}) collective-permute-start(bf16[512,1792]{1,0:T(8,128)(2,1)S(1)} %stack_rows.1.refs_10_.refs_0_), channel_id=1, source_target_pairs={{0,8},{8,24},{24,16},{16,0},{1,9},{9,25},{25,17},{17,1},{2,10},{10... | collective-permute-start | bytes 5505032 | tf_op jit(solution)/shard_map/ppermute | solution.py:77
  68.3 45.0 %collective-permute-start.4 = (bf16[256,2048]{1,0:T(8,128)(2,1)}, bf16[256,2048]{1,0:T(8,128)(2,1)}, u32[]{:S(2)}, u32[]{:S(2)}) collective-permute-start(bf16[256,2048]{1,0:T(8,128)(2,1)} %x_ref.3), channel_id=1, source_target_pairs={{0,3},{1,0},{2,1},{3,2},{4,7},{5,4},{6,5},{7,6},{8,11},{9,8},{10,9... | collective-permute-start | bytes 3145736 | tf_op jit(solution)/shard_map/ppermute | solution.py:77
  70.8 60.9 %collective-permute-start.2 = (bf16[256,2048]{1,0:T(8,128)(2,1)}, bf16[256,2048]{1,0:T(8,128)(2,1)}, u32[]{:S(2)}, u32[]{:S(2)}) collective-permute-start(bf16[256,2048]{1,0:T(8,128)(2,1)} %x_ref.3), channel_id=1, source_target_pairs={{0,1},{1,2},{2,3},{3,0},{4,5},{5,6},{6,7},{7,4},{8,9},{9,10},{10,1... | collective-permute-start | bytes 3145736 | tf_op jit(solution)/shard_map/ppermute | solution.py:77
  110.2 44.6 %collective-permute-start.14 = (bf16[256,1792]{1,0:T(8,128)(2,1)}, bf16[256,1792]{1,0:T(8,128)(2,1)}, u32[]{:S(2)}, u32[]{:S(2)}) collective-permute-start(bf16[256,1792]{1,0:T(8,128)(2,1)} %slice.138), channel_id=1, source_target_pairs={{0,16},{8,0},{24,8},{16,24},{1,17},{9,1},{25,9},{17,25},{2,18},{10... | collective-permute-start | bytes 2752520 | tf_op jit(solution)/shard_map/ppermute | solution.py:85
  112.8 42.1 %collective-permute-start.12 = (bf16[256,1792]{1,0:T(8,128)(2,1)}, bf16[256,1792]{1,0:T(8,128)(2,1)S(1)}, u32[]{:S(2)}, u32[]{:S(2)}) collective-permute-start(bf16[256,1792]{1,0:T(8,128)(2,1)} %slice.137), channel_id=1, source_target_pairs={{0,8},{8,24},{24,16},{16,0},{1,9},{9,25},{25,17},{17,1},{2,10},{10... | collective-permute-start | bytes 2752520 | tf_op jit(solution)/shard_map/ppermute | solution.py:85
  115.2 27.6 %collective-permute-start.5 = (bf16[128,2048]{1,0:T(8,128)(2,1)}, bf16[128,2048]{1,0:T(8,128)(2,1)}, u32[]{:S(2)}, u32[]{:S(2)}) collective-permute-start(bf16[128,2048]{1,0:T(8,128)(2,1)} %slice.132), channel_id=1, source_target_pairs={{0,3},{1,0},{2,1},{3,2},{4,7},{5,4},{6,5},{7,6},{8,11},{9,8},{10,9... | collective-permute-start | bytes 1572872 | tf_op jit(solution)/shard_map/ppermute | solution.py:85
  157.0 60.2 %collective-permute-start.22 = (bf16[256,2048]{1,0:T(8,128)(2,1)}, bf16[256,2048]{1,0:T(8,128)(2,1)}, u32[]{:S(2)}, u32[]{:S(2)}) collective-permute-start(bf16[256,2048]{1,0:T(8,128)(2,1)} %g_ref.1), channel_id=1, source_target_pairs={{0,3},{1,0},{2,1},{3,2},{4,7},{5,4},{6,5},{7,6},{8,11},{9,8},{10,9... | collective-permute-start | bytes 3145736 | tf_op jit(solution)/shard_map/ppermute | solution.py:77
  157.2 49.2 %collective-permute-start.19 = (bf16[160,2048]{1,0:T(8,128)(2,1)}, bf16[160,2048]{1,0:T(8,128)(2,1)}, u32[]{:S(2)}, u32[]{:S(2)}) collective-permute-start(bf16[160,2048]{1,0:T(8,128)(2,1)} %slice.129), channel_id=1, source_target_pairs={{0,8},{8,24},{24,16},{16,0},{1,9},{9,25},{25,17},{17,1},{2,10},{10... | collective-permute-start | bytes 1966088 | tf_op jit(solution)/shard_map/ppermute | solution.py:1156
  158.6 47.7 %collective-permute-start.20 = (bf16[160,2048]{1,0:T(8,128)(2,1)}, bf16[160,2048]{1,0:T(8,128)(2,1)}, u32[]{:S(2)}, u32[]{:S(2)}) collective-permute-start(bf16[160,2048]{1,0:T(8,128)(2,1)} %slice.130), channel_id=1, source_target_pairs={{0,16},{8,0},{24,8},{16,24},{1,17},{9,1},{25,9},{17,25},{2,18},{10... | collective-permute-start | bytes 1966088 | tf_op jit(solution)/shard_map/ppermute | solution.py:1156
  161.7 56.0 %collective-permute-start.21 = (bf16[256,2048]{1,0:T(8,128)(2,1)}, bf16[256,2048]{1,0:T(8,128)(2,1)}, u32[]{:S(2)}, u32[]{:S(2)}) collective-permute-start(bf16[256,2048]{1,0:T(8,128)(2,1)} %g_ref.1), channel_id=1, source_target_pairs={{0,1},{1,2},{2,3},{3,0},{4,5},{5,6},{6,7},{7,4},{8,9},{9,10},{10,1... | collective-permute-start | bytes 3145736 | tf_op jit(solution)/shard_map/ppermute | solution.py:77
  217.6 37.1 %collective-permute-start.29 = (bf16[256,2048]{1,0:T(8,128)(2,1)}, bf16[256,2048]{1,0:T(8,128)(2,1)}, u32[]{:S(2)}, u32[]{:S(2)}) collective-permute-start(bf16[256,2048]{1,0:T(8,128)(2,1)} %g_ref.1), channel_id=1, source_target_pairs={{0,4},{4,0},{1,5},{5,1},{2,6},{6,2},{3,7},{7,3},{8,12},{12,8},{9,1... | collective-permute-start | bytes 3145736 | tf_op jit(solution)/shard_map/ppermute | solution.py:158
  220.2 38.3 %collective-permute-start.31 = (bf16[256,2048]{1,0:T(8,128)(2,1)}, bf16[256,2048]{1,0:T(8,128)(2,1)}, u32[]{:S(2)}, u32[]{:S(2)}) collective-permute-start(bf16[256,2048]{1,0:T(8,128)(2,1)} %collective-permute-done.22.refs_2_), channel_id=1, source_target_pairs={{0,4},{4,0},{1,5},{5,1},{2,6},{6,2},{3,7},{7,3},{8,12},{12,8},{9,1... | collective-permute-start | bytes 3145736 | tf_op jit(solution)/shard_map/ppermute | solution.py:158
  222.3 31.9 %collective-permute-start.28 = (bf16[128,2048]{1,0:T(8,128)(2,1)}, bf16[128,2048]{1,0:T(8,128)(2,1)S(1)}, u32[]{:S(2)}, u32[]{:S(2)}) collective-permute-start(bf16[128,2048]{1,0:T(8,128)(2,1)} %slice.147), channel_id=1, source_target_pairs={{0,3},{1,0},{2,1},{3,2},{4,7},{5,4},{6,5},{7,6},{8,11},{9,8},{10,9... | collective-permute-start | bytes 1572872 | tf_op jit(solution)/shard_map/ppermute | solution.py:85
  227.3 26.9 %collective-permute-start.27 = (bf16[128,2048]{1,0:T(8,128)(2,1)}, bf16[128,2048]{1,0:T(8,128)(2,1)}, u32[]{:S(2)}, u32[]{:S(2)}) collective-permute-start(bf16[128,2048]{1,0:T(8,128)(2,1)} %slice.146), channel_id=1, source_target_pairs={{0,1},{1,2},{2,3},{3,0},{4,5},{5,6},{6,7},{7,4},{8,9},{9,10},{10,1... | collective-permute-start | bytes 1572872 | tf_op jit(solution)/shard_map/ppermute | solution.py:85
  228.7 29.9 %collective-permute-start.30 = (bf16[256,2048]{1,0:T(8,128)(2,1)}, bf16[256,2048]{1,0:T(8,128)(2,1)}, u32[]{:S(2)}, u32[]{:S(2)}) collective-permute-start(bf16[256,2048]{1,0:T(8,128)(2,1)} %collective-permute-done.21.refs_1_), channel_id=1, source_target_pairs={{0,4},{4,0},{1,5},{5,1},{2,6},{6,2},{3,7},{7,3},{8,12},{12,8},{9,1... | collective-permute-start | bytes 3145736 | tf_op jit(solution)/shard_map/ppermute | solution.py:158
  254.7 43.5 %collective-permute-start.34 = (bf16[128,2048]{1,0:T(8,128)(2,1)S(1)}, bf16[128,2048]{1,0:T(8,128)(2,1)S(1)}, u32[]{:S(2)}, u32[]{:S(2)}) collective-permute-start(bf16[128,2048]{1,0:T(8,128)(2,1)S(1)} %get-tuple-element.163), channel_id=1, source_target_pairs={{0,3},{1,0},{2,1},{3,2},{4,7},{5,4},{6,5},{7,6},{8,11},{9,8},{10,9... | collective-permute-start | bytes 1572872 | tf_op jit(solution)/shard_map/ppermute | solution.py:91
  258.5 40.5 %collective-permute-start.35 = (bf16[128,2048]{1,0:T(8,128)(2,1)S(1)}, bf16[128,2048]{1,0:T(8,128)(2,1)}, u32[]{:S(2)}, u32[]{:S(2)}) collective-permute-start(bf16[128,2048]{1,0:T(8,128)(2,1)S(1)} %get-tuple-element.164), channel_id=1, source_target_pairs={{0,1},{1,2},{2,3},{3,0},{4,5},{5,6},{6,7},{7,4},{8,9},{9,10},{10,1... | collective-permute-start | bytes 1572872 | tf_op jit(solution)/shard_map/ppermute | solution.py:92
  302.0 43.6 %collective-permute-start.38 = (bf16[256,2048]{1,0:T(8,128)(2,1)}, bf16[256,2048]{1,0:T(8,128)(2,1)}, u32[]{:S(2)}, u32[]{:S(2)}) collective-permute-start(bf16[256,2048]{1,0:T(8,128)(2,1)} %get-tuple-element.178), channel_id=1, source_target_pairs={{0,3},{1,0},{2,1},{3,2},{4,7},{5,4},{6,5},{7,6},{8,11},{9,8},{10,9... | collective-permute-start | bytes 3145736 | tf_op jit(solution)/shard_map/ppermute | solution.py:102
  328.0 39.3 %collective-permute-start.39 = (bf16[256,2048]{1,0:T(8,128)(2,1)}, bf16[256,2048]{1,0:T(8,128)(2,1)}, u32[]{:S(2)}, u32[]{:S(2)}) collective-permute-start(bf16[256,2048]{1,0:T(8,128)(2,1)} %get-tuple-element.179), channel_id=1, source_target_pairs={{0,1},{1,2},{2,3},{3,0},{4,5},{5,6},{6,7},{7,4},{8,9},{9,10},{10,1... | collective-permute-start | bytes 3145736 | tf_op jit(solution)/shard_map/ppermute | solution.py:103
  408.9 33.4 %collective-permute-start.53 = (bf16[528,768]{1,0:T(8,128)(2,1)}, bf16[528,768]{1,0:T(8,128)(2,1)S(1)}, u32[]{:S(2)}, u32[]{:S(2)}) collective-permute-start(bf16[528,768]{1,0:T(8,128)(2,1)} %get-tuple-element.212), channel_id=1, source_target_pairs={{0,16},{8,0},{24,8},{16,24},{1,17},{9,1},{25,9},{17,25},{2,18},{10... | collective-permute-start | bytes 2433032 | tf_op jit(solution)/shard_map/ppermute | solution.py:66
  410.3 32.1 %collective-permute-start.54 = (bf16[528,768]{1,0:T(8,128)(2,1)}, bf16[528,768]{1,0:T(8,128)(2,1)S(1)}, u32[]{:S(2)}, u32[]{:S(2)}) collective-permute-start(bf16[528,768]{1,0:T(8,128)(2,1)} %get-tuple-element.213), channel_id=1, source_target_pairs={{0,8},{8,24},{24,16},{16,0},{1,9},{9,25},{25,17},{17,1},{2,10},{10... | collective-permute-start | bytes 2433032 | tf_op jit(solution)/shard_map/ppermute | solution.py:66
  421.6 38.3 %collective-permute-start.51 = (bf16[256,2048]{1,0:T(8,128)(2,1)}, bf16[256,2048]{1,0:T(8,128)(2,1)}, u32[]{:S(2)}, u32[]{:S(2)}) collective-permute-start(bf16[256,2048]{1,0:T(8,128)(2,1)} %get-tuple-element.217), channel_id=1, source_target_pairs={{0,3},{1,0},{2,1},{3,2},{4,7},{5,4},{6,5},{7,6},{8,11},{9,8},{10,9... | collective-permute-start | bytes 3145736 | tf_op jit(solution)/shard_map/ppermute | solution.py:102
  422.5 26.3 %collective-permute-start.55 = (bf16[528,768]{1,0:T(8,128)(2,1)}, bf16[528,768]{1,0:T(8,128)(2,1)S(1)}, u32[]{:S(2)}, u32[]{:S(2)}) collective-permute-start(bf16[528,768]{1,0:T(8,128)(2,1)} %get-tuple-element.214), channel_id=1, source_target_pairs={{0,24},{8,16},{24,0},{16,8},{1,25},{9,17},{25,1},{17,9},{2,26},{10... | collective-permute-start | bytes 2433032 | tf_op jit(solution)/shard_map/ppermute | solution.py:66
  464.5 30.4 %collective-permute-start.62 = (bf16[320,2048]{1,0:T(8,128)(2,1)}, bf16[320,2048]{1,0:T(8,128)(2,1)}, u32[]{:S(2)}, u32[]{:S(2)}) collective-permute-start(bf16[320,2048]{1,0:T(8,128)(2,1)} %get-tuple-element.239), channel_id=1, source_target_pairs={{0,16},{8,0},{24,8},{16,24},{1,17},{9,1},{25,9},{17,25},{2,18},{10... | collective-permute-start | bytes 3932168 | tf_op jit(solution)/shard_map/ppermute | solution.py:102
  465.1 30.1 %collective-permute-start.63 = (bf16[320,2048]{1,0:T(8,128)(2,1)}, bf16[320,2048]{1,0:T(8,128)(2,1)}, u32[]{:S(2)}, u32[]{:S(2)}) collective-permute-start(bf16[320,2048]{1,0:T(8,128)(2,1)} %get-tuple-element.240), channel_id=1, source_target_pairs={{0,8},{8,24},{24,16},{16,0},{1,9},{9,25},{25,17},{17,1},{2,10},{10... | collective-permute-start | bytes 3932168 | tf_op jit(solution)/shard_map/ppermute | solution.py:103
  471.6 26.9 %collective-permute-start.56 = (bf16[160,768]{1,0:T(8,128)(2,1)S(1)}, bf16[160,768]{1,0:T(8,128)(2,1)S(1)}, u32[]{:S(2)}, u32[]{:S(2)}) collective-permute-start(bf16[160,768]{1,0:T(8,128)(2,1)S(1)} %copy-done.45), channel_id=1, source_target_pairs={{0,1},{1,0},{2,3},{3,2},{4,5},{5,4},{6,7},{7,6},{8,9},{9,8},{10,11... | collective-permute-start | bytes 737288 | tf_op jit(solution)/shard_map/ppermute | solution.py:39
  (100 other events, 1400.1 us)
Sparse Core Ops, SparseCore 0:
  14.4 81.3 all-gather.1
